TPU v7x, 32 devices: a whole 2x2x4 slice. The times are simulated.
32 devices in a mesh: ep: 8 (over z, x), tp: 4 (over y, core).
Axes of the slice: x: 2, y: 2, z: 4, core: 2. Of those that a mesh axis runs over, the one named last changes fastest.
Arguments:
- hidden: bfloat16 [5120, 2048], P('ep'), may hold values from -6 to 6
- attn_gain: float32 [2048], replicated, may hold values from 0.5 to 1.5
- qkv_weight: bfloat16 [2048, 3, 2048], P(None, None, 'tp'), may hold values from -0.125 to 0.125
- qkv_bias: float32 [3, 2048], P(None, 'tp'), may hold values from -3 to 3
- out_weight: bfloat16 [2048, 2048], P(None, 'tp'), may hold values from -0.5 to 0.5
- mlp_gain: float32 [2048], replicated, may hold values from 0.5 to 1.5
- router_weight: bfloat16 [2048, 8], replicated, may hold values from -0.0625 to 0.0625
- share_gate: bfloat16 [2048], replicated, may hold values from -0.125 to 0.125
- shared_gate_up: bfloat16 [2048, 2, 5632], P(None, None, 'tp'), may hold values from -0.125 to 0.125
- shared_down: bfloat16 [2048, 5632], P(None, 'tp'), may hold values from -0.15625 to 0.15625
- expert_gate_up: bfloat16 [8, 2048, 2, 1408], P('ep', None, None, 'tp'), may hold values from -0.125 to 0.125
- expert_down: bfloat16 [8, 2048, 1408], P('ep', None, 'tp'), may hold values from -1.25 to 1.25
- routes: int32 [5120, 4], P('ep'), may hold values from 0 to 7, all different within a row
- priority: int32 [5120, 4], P('ep'), may hold values from 0 to 2559, as said below
- prefix: int32 [8], P('ep'), may hold values from 64 to 320
- cotangent: bfloat16 [5120, 2048], P('ep'), may hold values from -6 to 6
Outputs:
- output: bfloat16 [5120, 2048], P('ep', 'tp')
- input_grad: bfloat16 [5120, 2048], P('ep', 'tp')
- attn_gain_grad: float32 [2048], replicated
- qkv_weight_grad: float32 [2048, 3, 2048], P('ep', None, 'tp')
- qkv_bias_grad: float32 [3, 2048], P(None, 'tp')
- out_weight_grad: float32 [2048, 2048], P('ep', 'tp')
- mlp_gain_grad: float32 [2048], replicated
- router_grad: float32 [2048, 8], replicated
- share_gate_grad: float32 [2048], replicated
- shared_gate_up_grad: float32 [2048, 2, 5632], P('ep', None, 'tp')
- shared_down_grad: float32 [2048, 5632], P('ep', 'tp')
- expert_gate_up_grad: float32 [8, 2048, 2, 1408], P('ep', None, None, 'tp')
- expert_down_grad: float32 [8, 2048, 1408], P('ep', None, 'tp')
Inputs may be any that keep to these rules, and one draw needn't show every extreme that they name: `priority`: within each sequence's 640 rows the 2560 values are all different. `routes`: each row names 4 different experts.
All inputs are finite; a program needn't handle non-finite values.
Results may differ from a plain program's by a relative error of at most 0.035.
Values may be sent and summed in bfloat16 or wider, within the bound.
A program may use at most 320 MiB of HBM per device.

v0:
```python
import jax
import jax.numpy as jnp
from jax import lax
from jax.sharding import PartitionSpec as P

HEAD_DIM = 128


EPSILON = 1e-06
THETA = 1000000.0
CONTRACT_LAST = (((1,), (1,)), ((), ()))
CONTRACT_FIRST = (((0,), (0,)), ((), ()))


def norm_factor(values):
    return lax.rsqrt(jnp.mean(values * values, axis=-1, keepdims=True) + EPSILON)


def norm_backward(grad_out, values, factor, gain_vec):
    scaled = grad_out * gain_vec
    gain_grad = jnp.sum(grad_out * values * factor, axis=0)
    value_grad = factor * scaled - values * (factor * factor * factor) * jnp.mean(
        scaled * values, axis=-1, keepdims=True
    )
    return (gain_grad, value_grad)


def swiglu_backward(hidden_grad, gate_pre, up_pre):
    sigmoid_val = jax.nn.sigmoid(gate_pre)
    gate_grad = hidden_grad * up_pre * sigmoid_val * (1.0 + gate_pre * (1.0 - sigmoid_val))
    up_grad = hidden_grad * gate_pre * sigmoid_val
    return (gate_grad, up_grad)


def angle_tables(length, head_size):
    half_size = head_size // 2
    frequency = THETA ** (-jnp.arange(half_size, dtype=jnp.float32) * 2.0 / head_size)
    angles = jnp.arange(length, dtype=jnp.float32)[:, None] * frequency[None, :]
    return (jnp.cos(angles)[:, None, :], jnp.sin(angles)[:, None, :])


def rotate_forward(values, cosine, sine_val):
    half_size = values.shape[-1] // 2
    first_half = values[..., :half_size]
    second_half = values[..., half_size:]
    return jnp.concatenate(
        [
            first_half * cosine - second_half * sine_val,
            second_half * cosine + first_half * sine_val,
        ],
        axis=-1,
    )


def rotate_backward(grad_in, cosine, sine_val):
    half_size = grad_in.shape[-1] // 2
    first_half = grad_in[..., :half_size]
    second_half = grad_in[..., half_size:]
    return jnp.concatenate(
        [
            first_half * cosine + second_half * sine_val,
            second_half * cosine - first_half * sine_val,
        ],
        axis=-1,
    )


def masked_scores(queries, key_rows, prefix_len, head_size):
    length = queries.shape[0]
    scores = jnp.einsum(
        "qhd,khd->hqk", queries, key_rows, preferred_element_type=jnp.float32
    ) * head_size ** (-0.5)
    row_index = jnp.arange(length, dtype=jnp.int32)[:, None]
    col_index = jnp.arange(length, dtype=jnp.int32)[None, :]
    visible = (col_index <= row_index) | (col_index < prefix_len)
    return jnp.where(visible[None], scores, -1e30)


def slots_of(route_rows, order_rows, expert_count):
    assign_count = route_rows.shape[0] * route_rows.shape[1]
    flat_route = route_rows.reshape(assign_count)
    flat_order = order_rows.reshape(assign_count)
    by_order = jnp.zeros((assign_count,), jnp.int32).at[flat_order].set(flat_route)
    expert_hits = (by_order[:, None] == jnp.arange(expert_count, dtype=jnp.int32)[None, :]).astype(
        jnp.int32
    )
    before = jnp.cumsum(expert_hits, axis=0) - expert_hits
    sorted_slot = jnp.sum(before * expert_hits, axis=1)
    return sorted_slot[flat_order].reshape(route_rows.shape)


def body(
    hidden,
    attn_gain,
    qkv_weight,
    qkv_bias,
    out_weight,
    mlp_gain,
    router_weight,
    share_gate,
    shared_gate_up,
    shared_down,
    expert_gate_up,
    expert_down,
    routes,
    priority,
    prefix,
    cotangent,
):
    token_count, model_width = hidden.shape
    ep_count = lax.axis_size("ep")
    tp_count = lax.axis_size("tp")
    col_width = model_width // tp_count
    col_start = lax.axis_index("tp") * col_width
    head_size = HEAD_DIM
    local_width = qkv_weight.shape[2]
    local_heads = local_width // head_size
    expert_local = expert_gate_up.shape[0]
    expert_count = expert_local * ep_count
    route_count = routes.shape[1]
    capacity = (5 * token_count * route_count + 4 * expert_count - 1) // (4 * expert_count)
    slot_total = expert_count * capacity
    residual_in = hidden.astype(jnp.float32)
    factor_one = norm_factor(residual_in)
    normed_one = (residual_in * factor_one * attn_gain).astype(jnp.bfloat16)
    linear = jnp.einsum("td,dkh->tkh", normed_one, qkv_weight, preferred_element_type=jnp.float32)
    mixed_heads = (linear + qkv_bias[None]).reshape(token_count, 3, local_heads, head_size)
    cosine, sine_val = angle_tables(token_count, head_size)
    queries = rotate_forward(mixed_heads[:, 0], cosine, sine_val).astype(jnp.bfloat16)
    key_rows = rotate_forward(mixed_heads[:, 1], cosine, sine_val).astype(jnp.bfloat16)
    value_rows = mixed_heads[:, 2].astype(jnp.bfloat16)
    scores = masked_scores(queries, key_rows, prefix[0], head_size)
    row_max = jnp.max(scores, axis=-1, keepdims=True)
    log_total = row_max + jnp.log(jnp.sum(jnp.exp(scores - row_max), axis=-1, keepdims=True))
    attn_probs = jnp.exp(scores - log_total).astype(jnp.bfloat16)
    context = (
        jnp.einsum("hqk,khd->qhd", attn_probs, value_rows, preferred_element_type=jnp.float32)
        .astype(jnp.bfloat16)
        .reshape(token_count, local_width)
    )
    attn_part = lax.dot_general(
        context, out_weight, CONTRACT_LAST, preferred_element_type=jnp.float32
    )
    attn_out = lax.psum(attn_part.astype(jnp.bfloat16), "tp").astype(jnp.float32)
    middle = residual_in + attn_out
    factor_two = norm_factor(middle)
    normed_two = (middle * factor_two * mlp_gain).astype(jnp.bfloat16)
    logits = jnp.dot(normed_two, router_weight, preferred_element_type=jnp.float32)
    router_probs = jax.nn.softmax(logits, axis=-1)
    route_hits = (
        routes[:, :, None] == jnp.arange(expert_count, dtype=jnp.int32)[None, None, :]
    ).astype(jnp.float32)
    gate_values = jnp.sum(route_hits * router_probs[:, None, :], axis=2)
    slot_index = slots_of(routes, priority, expert_count)
    kept_mask = slot_index < capacity
    kept_float = kept_mask.astype(jnp.float32)
    weighted = gate_values * kept_float
    destination = jnp.where(kept_mask, routes * capacity + slot_index, slot_total)
    token_ids = jnp.broadcast_to(
        jnp.arange(token_count, dtype=jnp.int32)[:, None], (token_count, route_count)
    )
    send_token = (
        jnp.full((slot_total + 1,), token_count, jnp.int32)
        .at[destination.reshape(-1)]
        .set(token_ids.reshape(-1))[:slot_total]
    )
    padded_rows = jnp.concatenate([normed_two, jnp.zeros((1, model_width), jnp.bfloat16)], axis=0)
    send_rows = padded_rows[send_token].reshape(ep_count, expert_local, capacity, model_width)
    gate_in = jnp.dot(normed_two, share_gate, preferred_element_type=jnp.float32)
    share_scale = jax.nn.sigmoid(gate_in)
    shared_pre = jnp.einsum(
        "td,dkf->tkf", normed_two, shared_gate_up, preferred_element_type=jnp.float32
    )
    shared_hidden = (jax.nn.silu(shared_pre[:, 0]) * shared_pre[:, 1]).astype(jnp.bfloat16)
    shared_part = lax.dot_general(
        shared_hidden, shared_down, CONTRACT_LAST, preferred_element_type=jnp.float32
    )
    send_part = lax.dynamic_slice_in_dim(send_rows, col_start, col_width, 3)
    whole_rows = lax.all_gather(
        lax.all_to_all(send_part, "ep", split_axis=0, concat_axis=0, tiled=True),
        "tp",
        axis=3,
        tiled=True,
    )
    inner_pre = jnp.einsum(
        "secd,edkf->seckf", whole_rows, expert_gate_up, preferred_element_type=jnp.float32
    )
    hidden_units = (jax.nn.silu(inner_pre[..., 0, :]) * inner_pre[..., 1, :]).astype(jnp.bfloat16)
    partial_out = jnp.einsum(
        "secf,edf->secd", hidden_units, expert_down, preferred_element_type=jnp.float32
    )
    returned_rows = lax.all_to_all(
        partial_out.astype(jnp.bfloat16), "ep", split_axis=0, concat_axis=0, tiled=True
    )
    flat_back = returned_rows.reshape(slot_total, returned_rows.shape[3])
    flat_back = jnp.concatenate(
        [flat_back, jnp.zeros((1, flat_back.shape[1]), flat_back.dtype)], axis=0
    )
    picked = flat_back[destination]
    routed = jnp.einsum("tk,tkd->td", weighted, picked, preferred_element_type=jnp.float32)
    upstream = cotangent.astype(jnp.float32)
    mlp_out = lax.psum(
        (share_scale[:, None] * shared_part + routed).astype(jnp.bfloat16), "tp"
    ).astype(jnp.float32)
    output = lax.dynamic_slice_in_dim(middle + mlp_out, col_start, col_width, 1).astype(
        jnp.bfloat16
    )
    gate_grad_part = jnp.einsum("td,tkd->tk", upstream, picked, preferred_element_type=jnp.float32)
    slot_weight = (
        jnp.zeros((slot_total + 1,), jnp.float32)
        .at[destination.reshape(-1)]
        .set(weighted.reshape(-1))[:slot_total]
    )
    padded_up = jnp.concatenate([upstream, jnp.zeros((1, model_width), jnp.float32)], axis=0)
    grad_send = (
        (padded_up[send_token] * slot_weight[:, None])
        .astype(jnp.bfloat16)
        .reshape(ep_count, expert_local, capacity, model_width)
    )
    grad_part = lax.dynamic_slice_in_dim(grad_send, col_start, col_width, 3)
    grad_recv_part = lax.all_to_all(grad_part, "ep", split_axis=0, concat_axis=0, tiled=True)
    grad_recv = lax.all_gather(grad_recv_part, "tp", axis=3, tiled=True)
    gate_pre = inner_pre[..., 0, :]
    up_pre = inner_pre[..., 1, :]
    expert_hidden = (jax.nn.silu(gate_pre) * up_pre).astype(jnp.bfloat16)
    hidden_grad = jnp.einsum(
        "secd,edf->secf", grad_recv, expert_down, preferred_element_type=jnp.float32
    )
    gate_grad, up_grad = swiglu_backward(hidden_grad, gate_pre, up_pre)
    expert_pre_grad = jnp.stack([gate_grad, up_grad], axis=-2).astype(jnp.bfloat16)
    row_grad = jnp.einsum(
        "seckf,edkf->secd", expert_pre_grad, expert_gate_up, preferred_element_type=jnp.float32
    ).astype(jnp.bfloat16)
    back_rows = lax.all_to_all(row_grad, "ep", split_axis=0, concat_axis=0, tiled=True)
    expert_down_grad = jnp.einsum(
        "secd,secf->edf", grad_recv, expert_hidden, preferred_element_type=jnp.float32
    )
    expert_gate_up_grad = jnp.einsum(
        "secd,seckf->edkf", whole_rows, expert_pre_grad, preferred_element_type=jnp.float32
    )
    flat_grad = jnp.concatenate(
        [back_rows.reshape(slot_total, model_width), jnp.zeros((1, model_width), jnp.bfloat16)],
        axis=0,
    )
    routed_row_grad = jnp.sum(flat_grad[destination], axis=1, dtype=jnp.float32)
    shared_out_grad = (share_scale[:, None] * upstream).astype(jnp.bfloat16)
    scale_grad_part = jnp.sum(upstream * shared_part, axis=1)
    shared_hidden_grad = jnp.dot(shared_out_grad, shared_down, preferred_element_type=jnp.float32)
    shared_gate_grad, shared_up_grad = swiglu_backward(
        shared_hidden_grad, shared_pre[:, 0], shared_pre[:, 1]
    )
    shared_pre_grad = jnp.stack([shared_gate_grad, shared_up_grad], axis=1).astype(jnp.bfloat16)
    normed_two_part = (
        jnp.einsum(
            "tkf,dkf->td", shared_pre_grad, shared_gate_up, preferred_element_type=jnp.float32
        )
        + routed_row_grad
    )
    normed_two_grad, scale_grad, gate_grad_sum = (
        lax.psum(normed_two_part.astype(jnp.bfloat16), "tp").astype(jnp.float32),
        lax.psum(scale_grad_part.astype(jnp.bfloat16), "tp").astype(jnp.float32),
        lax.psum(gate_grad_part.astype(jnp.bfloat16), "tp").astype(jnp.float32),
    )
    gate_in_grad = (scale_grad * share_scale * (1.0 - share_scale)).astype(jnp.bfloat16)
    prob_grad = jnp.sum(route_hits * (gate_grad_sum * kept_float)[:, :, None], axis=1)
    logit_grad = (
        router_probs * (prob_grad - jnp.sum(router_probs * prob_grad, axis=1, keepdims=True))
    ).astype(jnp.bfloat16)
    normed_two_grad = normed_two_grad + lax.dot_general(
        logit_grad, router_weight, CONTRACT_LAST, preferred_element_type=jnp.float32
    )
    normed_two_grad = (
        normed_two_grad
        + gate_in_grad.astype(jnp.float32)[:, None] * share_gate.astype(jnp.float32)[None, :]
    )
    router_grad = lax.dot_general(
        normed_two, logit_grad, CONTRACT_FIRST, preferred_element_type=jnp.float32
    )
    share_gate_grad = jnp.dot(gate_in_grad, normed_two, preferred_element_type=jnp.float32)
    mlp_gain_grad, middle_norm_grad = norm_backward(normed_two_grad, middle, factor_two, mlp_gain)
    middle_grad = upstream + middle_norm_grad
    attn_grad = middle_grad.astype(jnp.bfloat16)
    context_grad = (
        jnp.dot(attn_grad, out_weight, preferred_element_type=jnp.float32)
        .astype(jnp.bfloat16)
        .reshape(token_count, local_heads, head_size)
    )
    scores = masked_scores(queries, key_rows, prefix[0], head_size)
    attn_weights = jnp.exp(scores - log_total)
    prob_grad_att = jnp.einsum(
        "qhd,khd->hqk", context_grad, value_rows, preferred_element_type=jnp.float32
    )
    value_grad = jnp.einsum(
        "hqk,qhd->khd",
        attn_weights.astype(jnp.bfloat16),
        context_grad,
        preferred_element_type=jnp.float32,
    )
    row_delta = jnp.sum(attn_weights * prob_grad_att, axis=-1, keepdims=True)
    score_grad = (attn_weights * (prob_grad_att - row_delta)).astype(jnp.bfloat16)
    query_grad = jnp.einsum(
        "hqk,khd->qhd", score_grad, key_rows, preferred_element_type=jnp.float32
    ) * head_size ** (-0.5)
    key_grad = jnp.einsum(
        "hqk,qhd->khd", score_grad, queries, preferred_element_type=jnp.float32
    ) * head_size ** (-0.5)
    query_grad = rotate_backward(query_grad, cosine, sine_val)
    key_grad = rotate_backward(key_grad, cosine, sine_val)
    mixed_grad = jnp.stack([query_grad, key_grad, value_grad], axis=1).reshape(
        token_count, 3, local_width
    )
    bias_grad = jnp.sum(mixed_grad, axis=0)
    linear_grad = mixed_grad.astype(jnp.bfloat16)
    normed_one_part = jnp.einsum(
        "tkh,dkh->td", linear_grad, qkv_weight, preferred_element_type=jnp.float32
    )
    normed_one_grad = lax.psum(normed_one_part.astype(jnp.bfloat16), "tp").astype(jnp.float32)
    attn_gain_grad, input_norm_grad = norm_backward(
        normed_one_grad, residual_in, factor_one, attn_gain
    )
    input_grad = lax.dynamic_slice_in_dim(
        middle_grad + input_norm_grad, col_start, col_width, 1
    ).astype(jnp.bfloat16)
    normed_rows = normed_one
    grad_rows = attn_grad
    qkv_term = jnp.einsum(
        "td,tkh->dkh", normed_rows, linear_grad, preferred_element_type=jnp.float32
    ).reshape(lax.axis_size("ep") * (model_width // ep_count), 3 * local_width)
    out_term = jnp.einsum("td,th->dh", grad_rows, context, preferred_element_type=jnp.float32)
    attention_slab = lax.psum_scatter(
        jnp.concatenate([qkv_term, out_term], axis=1).astype(jnp.bfloat16),
        "ep",
        scatter_dimension=0,
        tiled=True,
    ).astype(jnp.float32)
    qkv_weight_grad = attention_slab[:, : 3 * local_width].reshape(-1, 3, local_width)
    out_weight_grad = attention_slab[:, 3 * local_width :]
    shared_local = shared_hidden.shape[1]
    normed_rows = normed_two
    grad_rows = shared_out_grad
    gate_up_term = jnp.einsum(
        "td,tkf->dkf", normed_rows, shared_pre_grad, preferred_element_type=jnp.float32
    ).reshape(lax.axis_size("ep") * (model_width // ep_count), 2 * shared_local)
    down_term = jnp.einsum(
        "td,tf->df", grad_rows, shared_hidden, preferred_element_type=jnp.float32
    )
    shared_slab = lax.psum_scatter(
        jnp.concatenate([gate_up_term, down_term], axis=1).astype(jnp.bfloat16),
        "ep",
        scatter_dimension=0,
        tiled=True,
    ).astype(jnp.float32)
    shared_gate_up_grad = shared_slab[:, : 2 * shared_local].reshape(-1, 2, shared_local)
    shared_down_grad = shared_slab[:, 2 * shared_local :]
    router_sum, share_gate_sum, gain_one_sum, gain_two_sum, bias_sum = (
        lax.psum(router_grad.astype(jnp.bfloat16), "ep").astype(jnp.float32),
        lax.psum(share_gate_grad.astype(jnp.bfloat16), "ep").astype(jnp.float32),
        lax.psum(attn_gain_grad.astype(jnp.bfloat16), "ep").astype(jnp.float32),
        lax.psum(mlp_gain_grad.astype(jnp.bfloat16), "ep").astype(jnp.float32),
        lax.psum(bias_grad.astype(jnp.bfloat16), "ep").astype(jnp.float32),
    )
    return (
        output,
        input_grad,
        gain_one_sum,
        qkv_weight_grad,
        bias_sum,
        out_weight_grad,
        gain_two_sum,
        router_sum,
        share_gate_sum,
        shared_gate_up_grad,
        shared_down_grad,
        expert_gate_up_grad,
        expert_down_grad,
    )


def solution(mesh):
    return jax.shard_map(
        body,
        mesh=mesh,
        in_specs=(
            P("ep", None),
            P(),
            P(None, None, "tp"),
            P(None, "tp"),
            P(None, "tp"),
            P(),
            P(),
            P(),
            P(None, None, "tp"),
            P(None, "tp"),
            P("ep", None, None, "tp"),
            P("ep", None, "tp"),
            P("ep", None),
            P("ep", None),
            P("ep"),
            P("ep", None),
        ),
        out_specs=(
            P("ep", "tp"),
            P("ep", "tp"),
            P(),
            P("ep", None, "tp"),
            P(None, "tp"),
            P("ep", "tp"),
            P(),
            P(),
            P(),
            P("ep", None, "tp"),
            P("ep", "tp"),
            P("ep", None, None, "tp"),
            P("ep", None, "tp"),
        ),
        check_vma=False,
    )
```

profile of v0, /device:TPU:0, one launch (start us, length us, event | category | flops | bytes accessed | tf_op | source)
XLA Modules:
  0.0 1913.4 jit_solution(13546523864264514845)
XLA Ops:
  13.2 8.4 broadcast_add_fusion
  47.5 9.9 scatter_custom_fusion
  60.4 13.6 gather_fusion
  75.8 9.9 scatter_custom_fusion.1
  85.8 23.4 %all-reduce.11.cloned.1.call-done = bf16[640,2048]{1,0:T(8,128)(2,1)} async-done(((bf16[640,2048]{1,0:T(8,128)(2,1)}), bf16[640,2048]{1,0:T(8,128)(2,1)}) %all-reduce.11.cloned.1.call-update) | async-done | bytes 2621456 | tf_op jit(solution)/shard_map/psum | solution.py:144
  118.3 27.7 %gather_fusion.1 = bf16[3200,2048]{1,0:T(8,128)(2,1)} fusion(bf16[641,2048]{1,0:T(8,128)(2,1)} %concatenate.42, s32[4096]{0:T(1024)S(1)} %pad_clamp_fusion), kind=kCustom, calls=%fused_computation.1 | custom fusion | bytes 26227200 | tf_op jit(solution)/shard_map/gather | solution.py:168
  148.1 79.6 %all_to_all.20 = bf16[8,1,400,512]{3,2,1,0:T(8,128)(2,1)} all-to-all(bf16[8,1,400,512]{3,2,1,0:T(8,128)(2,1)S(1)} %constant_dynamic-slice_fusion), channel_id=1, replica_groups=mesh['ep'=8,'tp'=4] {'ep'}, dimensions={0} | all-to-all | bytes 6553600 | tf_op jit(solution)/shard_map/all_to_all | solution.py:180
  227.7 83.2 %all-gather.3.cloned.1.call-done = bf16[8,1,400,2048]{3,2,0,1:T(8,128)(2,1)} async-done(((bf16[8,1,400,512]{3,2,0,1:T(8,128)(2,1)}), bf16[8,1,400,2048]{3,2,0,1:T(8,128)(2,1)}) %all-gather.3.cloned.1.call-update) | async-done | bytes 13107216 | tf_op jit(solution)/shard_map/all_gather | solution.py:179
  311.0 14.6 fusion.47
  329.3 10.1 convert_bitcast_fusion
  350.4 27.4 %gather_fusion.3 = f32[3200,2048]{1,0:T(8,128)} fusion(f32[641,2048]{1,0:T(8,128)} %concatenate.44, s32[4096]{0:T(1024)S(1)} %pad_clamp_fusion), kind=kCustom, calls=%fused_computation.3 | custom fusion | bytes 52441600 | tf_op jit(solution)/shard_map/gather | solution.py:216
  383.7 12.0 fusion.10
  395.8 6.9 fusion.73
  403.9 6.2 multiply_reduce_fusion.3
  410.1 219.7 %all-to-all-done.1 = bf16[8,1,400,2048]{3,2,1,0:T(8,128)(2,1)} async-done(((bf16[8,1,400,2048]{3,2,1,0:T(8,128)(2,1)}), bf16[8,1,400,2048]{3,2,1,0:T(8,128)(2,1)}, u32[]{:S(2)}, u32[]{:S(2)}) %all-to-all-start.1) | async-done | bytes 13107232 | tf_op jit(solution)/shard_map/all_to_all | solution.py:192
  629.8 11.2 concatenate.43
  641.0 27.0 %gather_fusion.2 = bf16[2560,2048]{1,0:T(8,128)(2,1)} fusion(bf16[3201,2048]{1,0:T(8,128)(2,1)} %concatenate.43, s32[3072]{0:T(1024)S(1)} %pad_clamp_fusion.1), kind=kCustom, calls=%fused_computation.2 | custom fusion | bytes 20981760 | tf_op jit(solution)/shard_map/gather | solution.py:199
  668.0 16.1 reshape.452
  684.1 11.3 fusion.22
  695.6 6.7 all-reduce.5
  703.3 10.1 scatter_custom_fusion.2
  716.8 77.1 %all_to_all.21 = bf16[8,1,400,512]{3,2,1,0:T(8,128)(2,1)} all-to-all(bf16[8,1,400,512]{3,2,1,0:T(8,128)(2,1)S(1)} %fusion.13), channel_id=1, replica_groups=mesh['ep'=8,'tp'=4] {'ep'}, dimensions={0} | all-to-all | bytes 6553600 | tf_op jit(solution)/shard_map/all_to_all | solution.py:221
  793.9 83.0 %all-gather.5.cloned.1.call-done = bf16[8,1,400,2048]{3,2,0,1:T(8,128)(2,1)} async-done(((bf16[8,1,400,512]{3,2,0,1:T(8,128)(2,1)}), bf16[8,1,400,2048]{3,2,0,1:T(8,128)(2,1)}) %all-gather.5.cloned.1.call-update) | async-done | bytes 13107216 | tf_op jit(solution)/shard_map/all_gather | solution.py:222
  876.8 13.4 fusion.69
  892.5 13.5 fusion.12
  911.8 8.4 convolution_convert_fusion.2
  920.2 8.5 copy.169
  928.6 13.9 convolution_convert_fusion
  942.5 15.2 copy.168
  957.8 238.8 %all-to-all-done.3 = bf16[8,1,400,2048]{3,2,1,0:T(8,128)(2,1)} async-done(((bf16[8,1,400,2048]{3,2,1,0:T(8,128)(2,1)}), bf16[8,1,400,2048]{3,2,1,0:T(8,128)(2,1)}, u32[]{:S(2)}, u32[]{:S(2)}) %all-to-all-start.3) | async-done | bytes 13107232 | tf_op jit(solution)/shard_map/all_to_all | solution.py:234
  1196.6 11.0 concatenate.45
  1207.6 26.6 %gather_fusion.4 = bf16[2560,2048]{1,0:T(8,128)(2,1)} fusion(bf16[3201,2048]{1,0:T(8,128)(2,1)} %concatenate.45, s32[3072]{0:T(1024)S(1)} %pad_clamp_fusion.1), kind=kCustom, calls=%fused_computation.4 | custom fusion | bytes 20981760 | tf_op jit(solution)/shard_map/gather | solution.py:245
  1234.2 19.2 %reshape.505 = f32[640,4,2048]{2,1,0:T(4,128)} reshape(bf16[2560,2048]{1,0:T(8,128)(2,1)} %gather_fusion.4) | data formatting | bytes 31457280 | tf_op jit(solution)/shard_map/convert_element_type | solution.py:245
  1253.4 18.6 reduce_sum.153
  1272.0 13.2 fusion.20
  1285.3 14.1 pad_maximum_fusion
  1300.5 8.2 fusion.130
  1308.8 6.9 fusion.21
  1315.6 27.8 %all-reduce.13.cloned.1.call-done = bf16[640,2048]{1,0:T(8,128)(2,1)} async-done(((bf16[640,2048]{1,0:T(8,128)(2,1)}), bf16[640,2048]{1,0:T(8,128)(2,1)}) %all-reduce.13.cloned.1.call-update) | async-done | bytes 2621456 | tf_op jit(solution)/shard_map/psum | solution.py:260
  1391.6 10.1 bitcast_convert_fusion.1
  1415.7 7.2 convolution_convert_fusion.1
  1422.9 8.6 pad_maximum_fusion.1
  1434.5 205.4 %reduce-scatter.5.cloned.1.call-done = bf16[256,4224]{1,0:T(8,128)(2,1)} async-done(((bf16[2048,4224]{1,0:T(8,128)(2,1)}), bf16[256,4224]{1,0:T(8,128)(2,1)}) %reduce-scatter.5.cloned.1.call-update) | async-done | bytes 2162704 | tf_op jit(solution)/shard_map/reduce_scatter | solution.py:347
  1651.4 15.0 fusion.53
  1666.4 13.0 fusion.44
  1679.8 64.3 %all-reduce.15.cloned.1.call-done = (bf16[640,2048]{1,0:T(8,128)(2,1)}, bf16[640,2048]{1,0:T(8,128)(2,1)}) async-done(((bf16[640,2048]{1,0:T(8,128)(2,1)}, bf16[640,2048]{1,0:T(8,128)(2,1)}), (bf16[640,2048]{1,0:T(8,128)(2,1)}, bf16[640,2048]{1,0:T(8,128)(2,1)})) %all-reduce.15.cloned.1.call-update) | async-done | bytes 5242896 | tf_op jit(solution)/shard_map/psum | solution.py:202
  1749.9 39.9 %all-reduce.4 = (bf16[2048]{0:T(1024)(128)(2,1)S(1)}, bf16[3,512]{1,0:T(4,128)(2,1)S(1)}, bf16[2048]{0:T(1024)(128)(2,1)S(1)}, bf16[2048,8]{0,1:T(8,128)(2,1)S(1)}, bf16[2048]{0:T(1024)(128)(2,1)S(1)}) all-reduce(bf16[2048]{0:T(1024)(128)(2,1)S(1)} %get-tuple-element.67, ...), channel_id=1, replica_groups=mesh['ep'=8,'tp'=4] {'ep'}, use_global_device_ids=true, to_apply=%region_27.28 | all-reduce | flops 24064 | bytes 96256 | tf_op jit(solution)/shard_map/psum | solution.py:358
  1797.1 101.4 %reduce-scatter.3.cloned.1.call-done = bf16[256,2048]{0,1:T(8,128)(2,1)} async-done(((bf16[2048,2048]{0,1:T(8,128)(2,1)}), bf16[256,2048]{0,1:T(8,128)(2,1)}) %reduce-scatter.3.cloned.1.call-update) | async-done | bytes 1048592 | tf_op jit(solution)/shard_map/reduce_scatter | solution.py:330
  (304 shorter events, 179.5 us)
Async XLA Ops:
  7.2 303.8 %copy-start = (bf16[1,2048,2,352]{1,3,2,0:T(8,128)(2,1)S(1)}, bf16[1,2048,2,352]{1,3,2,0:T(8,128)(2,1)}, u32[]{:S(2)}) copy-start(bf16[1,2048,2,352]{1,3,2,0:T(8,128)(2,1)} %param.26) | copy-start | bytes 8650756
  7.2 101.9 %all-reduce.11.cloned.1.call-start = ((), (), s32[]{:S(2)}) async-start(), calls=%async_computation.6 | async-start | bytes 5242880 | tf_op jit(solution)/shard_map/psum | solution.py:144
  11.0 10.6 copy-start.52
  11.2 26.9 %copy-start.18 = (pred[640,640]{0,1:T(8,128)(4,1)}, pred[640,640]{0,1:T(8,128)(4,1)S(1)}, u32[]{:S(2)}) copy-start(pred[640,640]{0,1:T(8,128)(4,1)S(1)} %fusion.74) | copy-start | bytes 1228804
  46.4 264.6 %all-gather.3.cloned.1.call-start = ((), (), s32[]{:S(2)}) async-start(), calls=%async_computation.7 | async-start | bytes 16384000 | tf_op jit(solution)/shard_map/all_gather | solution.py:179
  74.6 38.7 %copy-start.60 = (f32[2048]{0:T(1024)S(1)}, f32[2048]{0:T(1024)}, u32[]{:S(2)}) copy-start(f32[2048]{0:T(1024)} %param.21) | copy-start | bytes 24580
  75.1 39.9 %copy-start.37 = (s32[640,4]{0,1:T(4,128)}, s32[640,4]{0,1:T(4,128)S(1)}, u32[]{:S(2)}) copy-start(s32[640,4]{0,1:T(4,128)S(1)} %copy.138) | copy-start | bytes 30724
  75.8 10.0 copy-start.66
  311.0 18.4 copy-start.72
  339.4 290.4 %all-to-all-start.1 = ((bf16[8,1,400,2048]{3,2,1,0:T(8,128)(2,1)}), bf16[8,1,400,2048]{3,2,1,0:T(8,128)(2,1)}, u32[]{:S(2)}, u32[]{:S(2)}) async-start(bf16[8,1,400,2048]{3,2,1,0:T(8,128)(2,1)} %convert_bitcast_fusion), calls=%async_computation.1 | async-start | bytes 26214400 | tf_op jit(solution)/shard_map/all_to_all | solution.py:192
  345.1 531.8 %all-gather.5.cloned.1.call-start = ((), (), s32[]{:S(2)}) async-start(), calls=%async_computation.8 | async-start | bytes 16384000 | tf_op jit(solution)/shard_map/all_gather | solution.py:222
  350.4 27.4 %copy-start.58 = (bf16[2048,8]{0,1:T(8,128)(2,1)S(1)}, bf16[2048,8]{0,1:T(8,128)(2,1)}, u32[]{:S(2)}) copy-start(bf16[2048,8]{0,1:T(8,128)(2,1)} %param.22) | copy-start | bytes 98308
  377.7 5.9 copy-start.3
  377.8 18.0 slice-start.6
  380.5 15.2 copy-start.50
  383.7 12.1 copy-start.15
  383.7 12.1 slice-start.7
  684.1 18.1 copy-start.38
  684.1 18.1 copy-start.47
  684.1 19.2 %copy-start.41 = (s32[2560]{0:T(1024)S(1)}, s32[2560]{0:T(1024)}, u32[]{:S(2)}) copy-start(s32[2560]{0:T(1024)} %copy-done.40) | copy-start | bytes 30724
  702.9 13.9 copy-start.48
  906.0 290.6 %all-to-all-start.3 = ((bf16[8,1,400,2048]{3,2,1,0:T(8,128)(2,1)}), bf16[8,1,400,2048]{3,2,1,0:T(8,128)(2,1)}, u32[]{:S(2)}, u32[]{:S(2)}) async-start(bf16[8,1,400,2048]{3,2,1,0:T(8,128)(2,1)} %fusion.12), calls=%async_computation.3 | async-start | bytes 26214400 | tf_op jit(solution)/shard_map/all_to_all | solution.py:234
  911.7 431.7 %all-reduce.13.cloned.1.call-start = ((), (), s32[]{:S(2)}) async-start(), calls=%async_computation.9 | async-start | bytes 5242880 | tf_op jit(solution)/shard_map/psum | solution.py:260
  920.2 8.5 copy-start.4
  1253.4 18.6 copy-start.77
  1285.2 354.7 %reduce-scatter.5.cloned.1.call-start = ((), (), s32[]{:S(2)}) async-start(), calls=%async_computation.11 | async-start | bytes 19464192 | tf_op jit(solution)/shard_map/reduce_scatter | solution.py:347
  1299.5 444.6 %all-reduce.15.cloned.1.call-start = ((), (), s32[]{:S(2)}) async-start(), calls=%async_computation.12 | async-start | bytes 10485760 | tf_op jit(solution)/shard_map/psum | solution.py:202
  1308.7 34.7 %copy-start.8 = (bf16[640,2048]{1,0:T(8,128)(2,1)S(1)}, bf16[640,2048]{1,0:T(8,128)(2,1)}, u32[]{:S(2)}) copy-start(bf16[640,2048]{1,0:T(8,128)(2,1)} %param.16) | copy-start | bytes 7864324
  1308.7 34.7 %copy-start.57 = (f32[640]{0:T(1024)S(1)}, f32[640]{0:T(1024)}, u32[]{:S(2)}) copy-start(f32[640]{0:T(1024)} %copy-done.56) | copy-start | bytes 7684
  1308.7 34.7 %copy-start.59 = (bf16[2048,8]{0,1:T(8,128)(2,1)S(1)}, bf16[2048,8]{0,1:T(8,128)(2,1)}, u32[]{:S(2)}) copy-start(bf16[2048,8]{0,1:T(8,128)(2,1)} %param.22) | copy-start | bytes 98308
  1308.8 34.7 %copy-start.61 = (f32[2048]{0:T(1024)S(1)}, f32[2048]{0:T(1024)}, u32[]{:S(2)}) copy-start(f32[2048]{0:T(1024)} %param.21) | copy-start | bytes 24580
  1343.5 11.6 slice-start
  1348.2 6.8 slice-start.1
  1401.7 8.1 copy-start.74
  1401.7 496.7 %reduce-scatter.3.cloned.1.call-start = ((), (), s32[]{:S(2)}) async-start(), calls=%async_computation.10 | async-start | bytes 9437184 | tf_op jit(solution)/shard_map/reduce_scatter | solution.py:330
  1409.9 5.8 copy-start.53
  1643.1 7.4 copy-start.5
  1650.5 15.9 slice-start.2
  1651.4 15.0 slice-start.3
  1651.4 15.0 slice-start.4
  1651.4 15.0 slice-start.5
  1651.4 15.0 copy-start.79
  1666.4 13.0 copy-start.12
  1666.4 13.0 copy-start.13
  1666.4 13.0 copy-start.14
  1679.5 64.6 %copy-start.9 = (bf16[640,2048]{1,0:T(8,128)(2,1)S(1)}, bf16[640,2048]{1,0:T(8,128)(2,1)}, u32[]{:S(2)}) copy-start(bf16[640,2048]{1,0:T(8,128)(2,1)} %param.16) | copy-start | bytes 7864324
  1744.1 48.7 %copy-start.62 = (f32[640]{0:T(1024)S(1)}, f32[640]{0:T(1024)}, u32[]{:S(2)}) copy-start(f32[640]{0:T(1024)} %get-tuple-element.106) | copy-start | bytes 7684
  1898.5 7.6 copy-start.1
  (50 other events, 134.4 us)
Sparse Core Ops, SparseCore 0:
  46.5 62.6 all-reduce.10
  227.9 83.0 all-gather.2
  794.0 82.7 all-gather.4
  1285.4 58.0 all-reduce.12
  1347.1 292.7 reduce-scatter.4
  1642.3 101.7 all-reduce.14
  1748.2 150.2 reduce-scatter.2
where the time goes:
time: 1930 us; the launch traced here: 1910 us
  waiting for transfers between devices  1050 us (54%)
  local copies, waits for them, and re-layouts  303 us (16%)
  matrix products  225 us (12%)
  blocking collectives  203 us (11%)
  other arithmetic  107 us (6%)
    all_to_all x1, waiting for transfers between devices, body(): lax.all_to_all(row_grad, 'ep', split_axis=0, concat_axis=0, tiled=True)  239 us
    all_to_all x1, waiting for transfers between devices, body(): lax.all_to_all(partial_out.astype(jnp.bfloat16), 'ep', split_axis=0, conc...  220 us
    reduce_scatter x1, waiting for transfers between devices, body(): lax.psum_scatter(jnp.concatenate([gate_up_term, down_term], axis=1).astyp...  205 us
    reduce_scatter x1, waiting for transfers between devices, body(): lax.psum_scatter(jnp.concatenate([qkv_term, out_term], axis=1).astype(jnp...  101 us
    all_gather x1, waiting for transfers between devices, body(): lax.all_gather(lax.all_to_all(send_part, 'ep', split_axis=0, concat_axis=...  83.2 us
    all_gather x1, waiting for transfers between devices, body(): grad_recv = lax.all_gather(grad_recv_part, 'tp', axis=3, tiled=True)  83 us
    all_to_all x1, blocking collectives, body(): lax.all_to_all(send_part, 'ep', split_axis=0, concat_axis=0, tiled=True)  79.6 us
    all_to_all x1, blocking collectives, body(): lax.all_to_all(grad_part, 'ep', split_axis=0, concat_axis=0, tiled=True)  77.1 us
  transfers between devices with their start and end apart: 9, of which 9 were waited for; matrix products, arithmetic and copies ran while one was open for 17% of the time, Pallas kernels for 0%

commit v1 on v0

v1 whole, which is shorter than its diff:
```python
import jax
import jax.numpy as jnp
from jax import lax
from jax.sharding import PartitionSpec as P

HEAD_DIM = 128
EPSILON = 1e-06
THETA = 1000000.0
BF = jnp.bfloat16
F32 = jnp.float32


def mm(a, b, ca, cb):
    return lax.dot_general(a, b, (((ca,), (cb,)), ((), ())), preferred_element_type=F32)


def norm_factor(values):
    return lax.rsqrt(jnp.mean(values * values, axis=-1, keepdims=True) + EPSILON)


def swiglu_backward(hidden_grad, gate_pre, up_pre):
    sig = jax.nn.sigmoid(gate_pre)
    gate_grad = hidden_grad * up_pre * sig * (1.0 + gate_pre * (1.0 - sig))
    up_grad = hidden_grad * gate_pre * sig
    return gate_grad, up_grad


def angle_tables(length, head_size):
    half_size = head_size // 2
    frequency = THETA ** (-jnp.arange(half_size, dtype=F32) * 2.0 / head_size)
    angles = jnp.arange(length, dtype=F32)[:, None] * frequency[None, :]
    return jnp.cos(angles)[:, None, :], jnp.sin(angles)[:, None, :]


def rotate_forward(values, cosine, sine_val):
    half = values.shape[-1] // 2
    a, b = values[..., :half], values[..., half:]
    return jnp.concatenate([a * cosine - b * sine_val, b * cosine + a * sine_val], axis=-1)


def rotate_backward(grad_in, cosine, sine_val):
    half = grad_in.shape[-1] // 2
    a, b = grad_in[..., :half], grad_in[..., half:]
    return jnp.concatenate([a * cosine + b * sine_val, b * cosine - a * sine_val], axis=-1)


def masked_scores(queries, key_rows, prefix_len, head_size):
    length = queries.shape[0]
    scores = jnp.einsum(
        "qhd,khd->hqk", queries, key_rows, preferred_element_type=F32
    ) * head_size ** (-0.5)
    row_index = jnp.arange(length, dtype=jnp.int32)[:, None]
    col_index = jnp.arange(length, dtype=jnp.int32)[None, :]
    visible = (col_index <= row_index) | (col_index < prefix_len)
    return jnp.where(visible[None], scores, -1e30)


def swap(x, bit, n):
    return lax.ppermute(x, "tp", [(i, i ^ bit) for i in range(n)])


def tp_sum(x, n):
    half = x.shape[1] // 2
    low = (lax.axis_index("tp") % 2) == 0
    a, b = x[:, :half], x[:, half:]
    mine = jnp.where(low, a, b)
    theirs = jnp.where(low, b, a).astype(BF)
    one = (mine.astype(F32) + swap(theirs, 1, n).astype(F32)).astype(BF)
    two = (one.astype(F32) + swap(one, 2, n).astype(F32)).astype(BF)
    other = swap(two, 1, n)
    return jnp.concatenate([jnp.where(low, two, other), jnp.where(low, other, two)], axis=1).astype(F32)


def exchange(x, n):
    rows = x.shape[0] // n
    me = lax.axis_index("ep")
    out = jnp.zeros_like(x)
    out = lax.dynamic_update_slice_in_dim(
        out, lax.dynamic_slice_in_dim(x, me * rows, rows, 0), me * rows, 0
    )
    for shift in range(1, n):
        to = lax.rem(me + shift, n)
        came = lax.rem(me + n - shift, n)
        got = lax.ppermute(
            lax.dynamic_slice_in_dim(x, to * rows, rows, 0),
            "ep",
            [(i, (i + shift) % n) for i in range(n)],
        )
        out = lax.dynamic_update_slice_in_dim(out, got, came * rows, 0)
    return out


def body(
    hidden,
    attn_gain,
    qkv_weight,
    qkv_bias,
    out_weight,
    mlp_gain,
    router_weight,
    share_gate,
    shared_gate_up,
    shared_down,
    expert_gate_up,
    expert_down,
    routes,
    priority,
    prefix,
    cotangent,
):
    tokens, width = hidden.shape
    n_ep = lax.axis_size("ep")
    n_tp = lax.axis_size("tp")
    tp_i = lax.axis_index("tp")
    cols = width // n_tp
    col_start = tp_i * cols
    head_size = HEAD_DIM
    local_width = qkv_weight.shape[2]
    heads = local_width // head_size
    expert_local = expert_gate_up.shape[0]
    n_exp = expert_local * n_ep
    top = routes.shape[1]
    capacity = (5 * tokens * top + 4 * n_exp - 1) // (4 * n_exp)
    part = -(-capacity // n_tp)
    part_pad = -(-part // 16) * 16
    rows = n_exp * part_pad

    gu_t = jnp.transpose(expert_gate_up[0], (1, 2, 0))
    w_gate = lax.all_gather(gu_t[0], "tp", axis=0, tiled=True)
    w_up = lax.all_gather(gu_t[1], "tp", axis=0, tiled=True)
    w_down = lax.all_gather(jnp.transpose(expert_down[0], (1, 0)), "tp", axis=0, tiled=True)

    flat_route = routes.T.reshape(-1)
    flat_order = priority.T.reshape(-1)
    hits = (flat_route[:, None] == jnp.arange(n_exp, dtype=jnp.int32)[None, :]).astype(BF)
    smaller = (flat_order[None, :] < flat_order[:, None]).astype(BF)
    counts = mm(smaller, hits, 1, 0)
    slot = jnp.sum(counts * hits.astype(F32), axis=1).astype(jnp.int32).reshape(top, tokens)
    kept = slot < capacity
    in_part = slot - tp_i * part
    mine = kept & (in_part >= 0) & (in_part < part)
    dest = jnp.where(mine, routes.T * part_pad + in_part, -1)
    row_ids = jnp.arange(rows, dtype=jnp.int32)[:, None]
    place = (dest[0][None, :] == row_ids)
    for k in range(1, top):
        place = place | (dest[k][None, :] == row_ids)
    place = place.astype(BF)

    up_sent = mm(place, cotangent, 1, 0).astype(BF)
    up_rows = exchange(up_sent, n_ep)

    upstream = cotangent.astype(F32)
    residual_in = hidden.astype(F32)
    factor_one = norm_factor(residual_in)
    normed_one = (residual_in * factor_one * attn_gain).astype(BF)
    linear = jnp.einsum("td,dkh->tkh", normed_one, qkv_weight, preferred_element_type=F32)
    mixed_heads = (linear + qkv_bias[None]).reshape(tokens, 3, heads, head_size)
    cosine, sine_val = angle_tables(tokens, head_size)
    queries = rotate_forward(mixed_heads[:, 0], cosine, sine_val).astype(BF)
    key_rows = rotate_forward(mixed_heads[:, 1], cosine, sine_val).astype(BF)
    value_rows = mixed_heads[:, 2].astype(BF)
    scores = masked_scores(queries, key_rows, prefix[0], head_size)
    row_max = jnp.max(scores, axis=-1, keepdims=True)
    log_total = row_max + jnp.log(jnp.sum(jnp.exp(scores - row_max), axis=-1, keepdims=True))
    attn_probs = jnp.exp(scores - log_total).astype(BF)
    context = (
        jnp.einsum("hqk,khd->qhd", attn_probs, value_rows, preferred_element_type=F32)
        .astype(BF)
        .reshape(tokens, local_width)
    )
    attn_out = tp_sum(mm(context, out_weight, 1, 1), n_tp)
    middle = residual_in + attn_out
    factor_two = norm_factor(middle)
    normed_two = (middle * factor_two * mlp_gain).astype(BF)

    logits = mm(normed_two, router_weight, 1, 0)
    router_probs = jax.nn.softmax(logits, axis=-1)
    probs_hi = router_probs.astype(BF)
    probs_lo = (router_probs - probs_hi.astype(F32)).astype(BF)
    own = (row_ids // part_pad == jnp.arange(n_exp, dtype=jnp.int32)[None, :]).astype(F32)
    sent_rows = mm(place, normed_two, 1, 0).astype(BF)
    gate_hi = jnp.sum(mm(place, probs_hi, 1, 0) * own, axis=1, keepdims=True)
    gate_lo = jnp.sum(mm(place, probs_lo, 1, 0) * own, axis=1, keepdims=True)
    gate_sent = gate_hi + gate_lo
    lane = jnp.arange(128, dtype=jnp.int32)[None, :]
    gate_cols = jnp.where(lane == 0, gate_hi, jnp.where(lane == 1, gate_lo, 0.0)).astype(BF)
    got = exchange(jnp.concatenate([sent_rows, gate_cols], axis=1), n_ep)
    whole_rows = got[:, :width]
    gate_row = got[:, width : width + 1].astype(F32) + got[:, width + 1 : width + 2].astype(F32)

    gate_in = mm(normed_two, share_gate, 1, 0)
    share_scale = jax.nn.sigmoid(gate_in)
    shared_pre = jnp.einsum("td,dkf->tkf", normed_two, shared_gate_up, preferred_element_type=F32)
    shared_hidden = (jax.nn.silu(shared_pre[:, 0]) * shared_pre[:, 1]).astype(BF)
    shared_part = mm(shared_hidden, shared_down, 1, 1)
    shared_out_grad = (share_scale[:, None] * upstream).astype(BF)
    scale_grad_part = jnp.sum(upstream * shared_part, axis=1)
    shared_hidden_grad = mm(shared_out_grad, shared_down, 1, 0)
    sg, su = swiglu_backward(shared_hidden_grad, shared_pre[:, 0], shared_pre[:, 1])
    shared_pre_grad = jnp.stack([sg, su], axis=1).astype(BF)
    shared_back = jnp.einsum("tkf,dkf->td", shared_pre_grad, shared_gate_up, preferred_element_type=F32)
    sg, su = sg.astype(BF), su.astype(BF)
    shared_slab = lax.psum_scatter(
        jnp.concatenate(
            [
                mm(normed_two, sg, 0, 0).astype(BF),
                mm(normed_two, su, 0, 0).astype(BF),
                mm(shared_out_grad, shared_hidden, 0, 0).astype(BF),
            ],
            axis=1,
        ),
        "ep",
        scatter_dimension=0,
        tiled=True,
    ).astype(F32)
    sf = shared_hidden.shape[1]
    shared_gate_up_grad = jnp.stack([shared_slab[:, :sf], shared_slab[:, sf : 2 * sf]], axis=1)
    shared_down_grad = shared_slab[:, 2 * sf :]

    e_gate = mm(whole_rows, w_gate, 1, 1)
    e_up = mm(whole_rows, w_up, 1, 1)
    e_hidden = (jax.nn.silu(e_gate) * e_up).astype(BF)
    e_out = mm(e_hidden, w_down, 1, 0).astype(BF)
    row_grad = (gate_row * up_rows.astype(F32)).astype(BF)
    e_hidden_grad = mm(row_grad, w_down, 1, 1)
    eg, eu = swiglu_backward(e_hidden_grad, e_gate, e_up)
    eg, eu = eg.astype(BF), eu.astype(BF)
    back_sent = (mm(eg, w_gate, 1, 0) + mm(eu, w_up, 1, 0)).astype(BF)
    back_rows = exchange(back_sent, n_ep)
    out_rows = exchange(e_out, n_ep)
    d_down = lax.psum_scatter(mm(e_hidden, row_grad, 0, 0).astype(BF), "tp", scatter_dimension=0, tiled=True)
    d_gate = lax.psum_scatter(mm(eg, whole_rows, 0, 0).astype(BF), "tp", scatter_dimension=0, tiled=True)
    d_up = lax.psum_scatter(mm(eu, whole_rows, 0, 0).astype(BF), "tp", scatter_dimension=0, tiled=True)
    expert_down_grad = jnp.transpose(d_down.astype(F32), (1, 0))[None]
    expert_gate_up_grad = jnp.transpose(
        jnp.stack([d_gate, d_up], axis=0).astype(F32), (2, 0, 1)
    )[None]

    weighted_place = (place.astype(F32) * gate_sent).astype(BF)
    routed = mm(weighted_place, out_rows, 0, 0)
    out_cols = lax.psum_scatter(
        (share_scale[:, None] * shared_part + routed).astype(BF), "tp", scatter_dimension=1, tiled=True
    ).astype(F32)
    output = (lax.dynamic_slice_in_dim(middle, col_start, cols, 1) + out_cols).astype(BF)
    gate_grad_row = jnp.sum(up_sent.astype(F32) * out_rows.astype(F32), axis=1, keepdims=True)
    prob_part = mm(place, (gate_grad_row * own).astype(BF), 0, 0)
    pad = -(-(n_exp + 1) // 256) * 256 - n_exp - 1
    summed = tp_sum(
        jnp.concatenate(
            [
                shared_back + mm(place, back_rows, 0, 0),
                prob_part,
                scale_grad_part[:, None],
                jnp.zeros((tokens, pad), F32),
            ],
            axis=1,
        ),
        n_tp,
    )
    normed_two_grad = summed[:, :width]
    prob_grad = summed[:, width : width + n_exp]
    scale_grad = summed[:, width + n_exp]
    gate_in_grad = (scale_grad * share_scale * (1.0 - share_scale)).astype(BF)
    logit_grad = (
        router_probs * (prob_grad - jnp.sum(router_probs * prob_grad, axis=1, keepdims=True))
    ).astype(BF)
    normed_two_grad = (
        normed_two_grad
        + mm(logit_grad, router_weight, 1, 1)
        + gate_in_grad.astype(F32)[:, None] * share_gate.astype(F32)[None, :]
    )
    small_two = mm(
        jnp.concatenate([logit_grad, gate_in_grad[:, None]], axis=1), normed_two, 0, 0
    )
    mlp_gain_grad = jnp.sum(normed_two_grad * middle * factor_two, axis=0)
    scaled = normed_two_grad * mlp_gain
    middle_grad = upstream + factor_two * scaled - middle * (factor_two**3) * jnp.mean(
        scaled * middle, axis=-1, keepdims=True
    )
    small_sum = lax.psum(
        jnp.concatenate([small_two, mlp_gain_grad[None]], axis=0).astype(BF), "ep"
    ).astype(F32)
    router_sum = small_sum[:n_exp].T
    share_gate_sum = small_sum[n_exp]
    gain_two_sum = small_sum[n_exp + 1]

    attn_grad = middle_grad.astype(BF)
    context_grad = mm(attn_grad, out_weight, 1, 0).astype(BF).reshape(tokens, heads, head_size)
    attn_weights = jnp.exp(scores - log_total)
    prob_grad_att = jnp.einsum("qhd,khd->hqk", context_grad, value_rows, preferred_element_type=F32)
    value_grad = jnp.einsum(
        "hqk,qhd->khd", attn_weights.astype(BF), context_grad, preferred_element_type=F32
    )
    row_delta = jnp.sum(attn_weights * prob_grad_att, axis=-1, keepdims=True)
    score_grad = (attn_weights * (prob_grad_att - row_delta)).astype(BF)
    query_grad = jnp.einsum(
        "hqk,khd->qhd", score_grad, key_rows, preferred_element_type=F32
    ) * head_size ** (-0.5)
    key_grad = jnp.einsum(
        "hqk,qhd->khd", score_grad, queries, preferred_element_type=F32
    ) * head_size ** (-0.5)
    query_grad = rotate_backward(query_grad, cosine, sine_val)
    key_grad = rotate_backward(key_grad, cosine, sine_val)
    parts = [g.reshape(tokens, local_width) for g in (query_grad, key_grad, value_grad)]
    bias_grad = jnp.concatenate([jnp.sum(g, axis=0) for g in parts])
    linear_grad = jnp.concatenate([g.astype(BF) for g in parts], axis=1)
    attention_slab = lax.psum_scatter(
        jnp.concatenate(
            [mm(normed_one, linear_grad, 0, 0).astype(BF), mm(attn_grad, context, 0, 0).astype(BF)], axis=1
        ),
        "ep",
        scatter_dimension=0,
        tiled=True,
    ).astype(F32)
    qkv_weight_grad = attention_slab[:, : 3 * local_width].reshape(-1, 3, local_width)
    out_weight_grad = attention_slab[:, 3 * local_width :]
    w_t = jnp.transpose(qkv_weight, (1, 0, 2))
    normed_one_part = sum(
        mm(linear_grad[:, i * local_width : (i + 1) * local_width], w_t[i], 1, 1) for i in range(3)
    )
    normed_one_grad = tp_sum(normed_one_part, n_tp)
    attn_gain_grad = jnp.sum(normed_one_grad * residual_in * factor_one, axis=0)
    scaled = normed_one_grad * attn_gain
    input_grad = lax.dynamic_slice_in_dim(
        middle_grad
        + factor_one * scaled
        - residual_in * (factor_one**3) * jnp.mean(scaled * residual_in, axis=-1, keepdims=True),
        col_start,
        cols,
        1,
    ).astype(BF)
    last_sum = lax.psum(jnp.concatenate([attn_gain_grad, bias_grad]).astype(BF), "ep").astype(F32)
    gain_one_sum = last_sum[:width]
    bias_sum = last_sum[width:].reshape(3, local_width)
    return (
        output,
        input_grad,
        gain_one_sum,
        qkv_weight_grad,
        bias_sum,
        out_weight_grad,
        gain_two_sum,
        router_sum,
        share_gate_sum,
        shared_gate_up_grad,
        shared_down_grad,
        expert_gate_up_grad,
        expert_down_grad,
    )


def solution(mesh):
    return jax.shard_map(
        body,
        mesh=mesh,
        in_specs=(
            P("ep", None),
            P(),
            P(None, None, "tp"),
            P(None, "tp"),
            P(None, "tp"),
            P(),
            P(),
            P(),
            P(None, None, "tp"),
            P(None, "tp"),
            P("ep", None, None, "tp"),
            P("ep", None, "tp"),
            P("ep", None),
            P("ep", None),
            P("ep"),
            P("ep", None),
        ),
        out_specs=(
            P("ep", "tp"),
            P("ep", "tp"),
            P(),
            P("ep", None, "tp"),
            P(None, "tp"),
            P("ep", "tp"),
            P(),
            P(),
            P(),
            P("ep", None, "tp"),
            P("ep", "tp"),
            P("ep", None, None, "tp"),
            P("ep", None, "tp"),
        ),
        check_vma=False,
    )
```

time: 1930 us -> 1170 us (0.61)
  waiting for transfers between devices: 1050 us -> 472 us
  blocking collectives: 203 us -> 46.4 us
  local copies, waits for them, and re-layouts: 303 us -> 165 us
  starting transfers between devices: 11.9 us -> 123 us
    all_to_all x2 -> x0, waiting for transfers between devices: 459 us -> none  [the longest x1 239 us: body(): lax.all_to_all(row_grad, 'ep', split_axis=0, concat_axis=0, tiled=True)]
    ppermute x0 -> x37, waiting for transfers between devices: none -> 179 us  [the longest x9 113 us: swap(): return lax.ppermute(x, 'tp', [(i, i ^ bit) for i in range(n)])]
    all_gather x2 -> x3, waiting for transfers between devices: 166 us -> 0.04 us  [the longest x1 0.02 us: body(): lax.all_gather(jnp.transpose(expert_down[0], (1, 0)), 'tp', axis=0, tiled...]
    all_to_all x2 -> x0, blocking collectives: 157 us -> none  [the longest x1 79.6 us: body(): lax.all_to_all(send_part, 'ep', split_axis=0, concat_axis=0, tiled=True)]
    gather x6 -> x0, local copies, waits for them, and re-layouts: 138 us -> none  [the longest x2 43.1 us: body(): picked = flat_back[destination]]
    ppermute x0 -> x37, starting transfers between devices: none -> 122 us  [the longest x28 116 us: exchange(): lax.ppermute(lax.dynamic_slice_in_dim(x, to * rows, rows, 0), 'ep', [(i,...]
    psum x3 -> x0, waiting for transfers between devices: 115 us -> none  [the longest x1 64.3 us: body(): lax.psum((share_scale[:, None] * shared_part + routed).astype(jnp.bfloat1...]
    dynamic_update_slice x0 -> x29, local copies, waits for them, and re-layouts: none -> 71.7 us  [the longest x28 64.9 us: exchange(): out = lax.dynamic_update_slice_in_dim(out, got, came * rows, 0)]
  transfers between devices with their start and end apart: 9 -> 46, of which waited for: 9 -> 15; matrix products, arithmetic and copies ran while one was open for 17% -> 38% of each run, Pallas kernels for 0% -> 0%
where the time goes in v1:
time: 1170 us; the launch traced here: 1160 us
  waiting for transfers between devices  472 us (40%)
  matrix products  243 us (21%)
  local copies, waits for them, and re-layouts  165 us (14%)
  starting transfers between devices  123 us (11%)
  other arithmetic  98.7 us (8%)
  blocking collectives  46.4 us (4%)
  between operations  17.1 us (1%)
    reduce_scatter x1, waiting for transfers between devices, body(): lax.psum_scatter(jnp.concatenate([mm(normed_two, sg, 0, 0).astype(BF), mm...  289 us
    dot_general x33, matrix products, mm(): lax.dot_general(a, b, (((ca,), (cb,)), ((), ())), preferred_element_type=...  194 us
    ppermute x28, starting transfers between devices, exchange(): lax.ppermute(lax.dynamic_slice_in_dim(x, to * rows, rows, 0), 'ep', [(i,...  116 us
    ppermute x9, waiting for transfers between devices, swap(): return lax.ppermute(x, 'tp', [(i, i ^ bit) for i in range(n)])  113 us
    ppermute x28, waiting for transfers between devices, exchange(): lax.ppermute(lax.dynamic_slice_in_dim(x, to * rows, rows, 0), 'ep', [(i,...  66.3 us
    dynamic_update_slice x28, local copies, waits for them, and re-layouts, exchange(): out = lax.dynamic_update_slice_in_dim(out, got, came * rows, 0)  64.9 us
    psum x1, blocking collectives, body(): lax.psum(jnp.concatenate([attn_gain_grad, bias_grad]).astype(BF), 'ep')  46.4 us
    unnamed x245, local copies, waits for them, and re-layouts  42.4 us
  transfers between devices with their start and end apart: 46, of which 15 were waited for; matrix products, arithmetic and copies ran while one was open for 38% of the time, Pallas kernels for 0%

profile of v1, /device:TPU:0, one launch (start us, length us, event | category | flops | bytes accessed | tf_op | source)
XLA Modules:
  0.0 1164.7 jit_solution(11135899277597571071)
XLA Ops:
  20.0 9.8 broadcast_add_fusion
  91.6 29.5 %collective-permute-done.1 = bf16[640,1024]{0,1:T(8,128)(2,1)} collective-permute-done((bf16[640,1024]{0,1:T(8,128)(2,1)S(1)}, bf16[640,1024]{0,1:T(8,128)(2,1)}, u32[]{:S(2)}, u32[]{:S(2)}) %collective-permute-start.1) | collective-permute-done | bytes 1310752 | tf_op jit(solution)/shard_map/ppermute | solution.py:59
  133.7 14.1 %collective-permute-done.22 = bf16[112,2048]{1,0:T(8,128)(2,1)S(1)} collective-permute-done((bf16[112,2048]{1,0:T(8,128)(2,1)}, bf16[112,2048]{1,0:T(8,128)(2,1)S(1)}, u32[]{:S(2)}, u32[]{:S(2)}) %collective-permute-start.22) | collective-permute-done | bytes 458784 | tf_op jit(solution)/shard_map/ppermute | solution.py:84
  163.3 10.4 collective-permute-start.3
  175.1 7.8 fusion.6
  191.8 8.2 collective-permute-start.9
  200.1 10.9 multiply_convert_fusion.7
  213.4 6.8 dynamic_update_slice.96
  221.6 6.9 dynamic_update_slice.97
  229.9 7.6 dynamic_update_slice.98
  238.8 7.6 dynamic_update_slice.99
  247.8 7.6 dynamic_update_slice.100
  256.7 7.6 dynamic_update_slice.101
  265.7 7.6 dynamic_update_slice.102
  274.6 7.6 dynamic_update_slice.103
  283.1 10.9 fusion.59
  294.0 10.8 fusion.10
  304.8 16.6 %multiply_convert_fusion.4 = (bf16[896,1408]{1,0:T(8,128)(2,1)}, bf16[896,1408]{1,0:T(8,128)(2,1)S(1)}, bf16[896,1408]{1,0:T(8,128)(2,1)}) fusion(f32[896,1408]{1,0:T(8,128)} %fusion.59, f32[896,1408]{1,0:T(8,128)} %fusion.10, bf16[1,1408,2048]{2,1,0:T(8,128)(2,1)} %all-gather.8.cloned.1.call-done, bf16[896,2176]{0,1:T(8,128)(2,1)} %dynamic_update_slice.103), kind=kOutput, calls=%fused_computation.70 | convolution fusion | flops 5187567616 | bytes 27099136 | tf_op jit(solution)/shard_map/dot_general | solution.py:14
  321.4 9.7 convolution_convert_fusion.9
  333.3 38.1 %collective-permute-start.11 = (bf16[112,2048]{1,0:T(8,128)(2,1)S(1)}, bf16[112,2048]{1,0:T(8,128)(2,1)S(1)}, u32[]{:S(2)}, u32[]{:S(2)}) collective-permute-start(bf16[112,2048]{1,0:T(8,128)(2,1)S(1)} %get-tuple-element.121), channel_id=1, source_target_pairs={{0,8},{4,12},{8,16},{12,20},{16,24},{20,28},{24,0},{28,4},{1,9},{5... | collective-permute-start | bytes 1376264 | tf_op jit(solution)/shard_map/ppermute | solution.py:84
  371.5 7.5 fusion.23
  393.8 11.0 collective-permute-done.12
  404.8 6.7 collective-permute-done.13
  413.7 5.9 add_convert_fusion.1
  419.6 10.3 convolution_convert_fusion.1
  430.1 10.3 convolution_convert_fusion.2
  440.5 9.7 fusion.8
  450.2 9.5 add_convert_fusion
  461.9 6.0 collective-permute-start.24
  467.8 10.3 collective-permute-start.25
  478.2 13.1 %fusion.4 = f32[640,2048,1]{0,1,2:T(8,128)} fusion(bf16[2048,2,1408]{2,1,0:T(2,128)(2,1)S(1)} %bitcast.157, bf16[640,1,1408]{2,0,1:T(8,128)(2,1)} %bitcast.187, bf16[640,1,1408]{2,0,1:T(8,128)(2,1)} %bitcast.186), kind=kOutput, calls=%fused_computation.13 | convolution fusion | flops 7383777280 | bytes 20381696 | tf_op jit(solution)/shard_map/tkf,dkf->td/dot_general | solution.py:201
  501.0 19.6 %collective-permute-done.26 = bf16[112,2048]{1,0:T(8,128)(2,1)S(1)} collective-permute-done((bf16[112,2048]{1,0:T(8,128)(2,1)}, bf16[112,2048]{1,0:T(8,128)(2,1)S(1)}, u32[]{:S(2)}, u32[]{:S(2)}) %collective-permute-start.26) | collective-permute-done | bytes 458784 | tf_op jit(solution)/shard_map/ppermute | solution.py:84
  520.7 5.4 collective-permute-done.27
  532.9 6.1 bitcast_add_fusion
  539.0 16.2 %concatenate.53 = f32[640,2304]{0,1:T(8,128)} concatenate(f32[640,2048]{0,1:T(8,128)} %bitcast_add_fusion, f32[640,8]{0,1:T(8,128)S(1)} %fusion.105, f32[640,1]{0,1:T(1,128)S(1)} %broadcast_in_dim.122, f32[640,247]{0,1:T(8,128)S(1)} %broadcast_in_dim.123), dimensions={1} | concatenate | bytes 11796480 | tf_op jit(solution)/shard_map/concatenate | solution.py:249
  565.9 47.6 %collective-permute-done.32 = bf16[640,1152]{0,1:T(8,128)(2,1)S(1)} collective-permute-done((bf16[640,1152]{0,1:T(8,128)(2,1)S(1)}, bf16[640,1152]{0,1:T(8,128)(2,1)S(1)}, u32[]{:S(2)}, u32[]{:S(2)}) %collective-permute-start.32) | collective-permute-done | bytes 1474592 | tf_op jit(solution)/shard_map/ppermute | solution.py:59
  615.0 8.3 convolution_convert_fusion
  631.8 6.8 fusion.24
  661.8 5.9 convolution_convert_fusion.10
  673.8 9.0 convolution_convert_fusion.6
  682.9 8.5 pad_maximum_fusion.1
  691.7 7.1 convolution_convert_fusion.4
  703.9 6.5 convolution_convert_fusion.3
  710.4 10.5 pad_maximum_fusion
  736.6 30.1 %collective-permute-done.35 = bf16[640,1024]{0,1:T(8,128)(2,1)S(1)} collective-permute-done((bf16[640,1024]{0,1:T(8,128)(2,1)S(1)}, bf16[640,1024]{0,1:T(8,128)(2,1)S(1)}, u32[]{:S(2)}, u32[]{:S(2)}) %collective-permute-start.35) | collective-permute-done | bytes 1310752 | tf_op jit(solution)/shard_map/ppermute | solution.py:59
  785.4 46.4 %all-reduce = (bf16[3584]{0:T(1024)(128)(2,1)S(1)}, bf16[10,2048]{1,0:T(8,128)(2,1)S(1)}) all-reduce(bf16[3584]{0:T(1024)(128)(2,1)S(1)} %pad_maximum_fusion.14, bf16[10,2048]{1,0:T(8,128)(2,1)S(1)} %pad_maximum_fusion.12), channel_id=1, replica_groups=mesh['ep'=8,'tp'=4] {'ep'}, use_global_device_ids=true, to_apply=%region_20.21 | all-reduce | flops 24064 | bytes 96256 | tf_op jit(solution)/shard_map/psum | solution.py:332
  856.5 289.0 %reduce-scatter.11.cloned.1.call-done = bf16[256,4224]{0,1:T(8,128)(2,1)} async-done(((bf16[2048,4224]{0,1:T(8,128)(2,1)}), bf16[256,4224]{0,1:T(8,128)(2,1)}) %reduce-scatter.11.cloned.1.call-update) | async-done | bytes 2162704 | tf_op jit(solution)/shard_map/reduce_scatter | solution.py:203
  1149.4 5.5 copy.160
  (477 shorter events, 282.7 us)
Async XLA Ops:
  7.2 275.9 %all-gather.6.cloned.1.call-start = ((), (), s32[]{:S(2)}) async-start(), calls=%async_computation.6 | async-start | bytes 7208960 | tf_op jit(solution)/shard_map/all_gather | solution.py:131
  7.9 286.1 %all-gather.10.cloned.1.call-start = ((), (), s32[]{:S(2)}) async-start(), calls=%async_computation.14 | async-start | bytes 7208960 | tf_op jit(solution)/shard_map/all_gather | solution.py:130
  11.7 293.1 %all-gather.8.cloned.1.call-start = ((), (), s32[]{:S(2)}) async-start(), calls=%async_computation.13 | async-start | bytes 7208960 | tf_op jit(solution)/shard_map/all_gather | solution.py:129
  53.8 5.0 collective-permute-start
  58.8 96.7 %copy-start.90 = (s32[640]{0:T(1024)}, s32[640]{0:T(1024)S(1)}, u32[]{:S(2)}) copy-start(s32[640]{0:T(1024)S(1)} %get-tuple-element.69) | copy-start | bytes 7684
  62.3 58.8 %collective-permute-start.1 = (bf16[640,1024]{0,1:T(8,128)(2,1)S(1)}, bf16[640,1024]{0,1:T(8,128)(2,1)}, u32[]{:S(2)}, u32[]{:S(2)}) collective-permute-start(bf16[640,1024]{0,1:T(8,128)(2,1)S(1)} %add_convert_fusion.7), channel_id=1, source_target_pairs={{0,2},{1,3},{2,0},{3,1},{4,6},{5,7},{6,4},{7,5},{8,10},{9,11},{10,... | collective-permute-start | bytes 3932168 | tf_op jit(solution)/shard_map/ppermute | solution.py:59
  73.2 16.5 %collective-permute-start.17 = (bf16[112,2048]{1,0:T(8,128)(2,1)}, bf16[112,2048]{1,0:T(8,128)(2,1)}, u32[]{:S(2)}, u32[]{:S(2)}) collective-permute-start(bf16[112,2048]{1,0:T(8,128)(2,1)} %get-tuple-element.114), channel_id=1, source_target_pairs={{0,4},{4,8},{8,12},{12,16},{16,20},{20,24},{24,28},{28,0},{1,5},{5... | collective-permute-start | bytes 1376264 | tf_op jit(solution)/shard_map/ppermute | solution.py:84
  74.7 51.1 %collective-permute-start.18 = (bf16[112,2048]{1,0:T(8,128)(2,1)}, bf16[112,2048]{1,0:T(8,128)(2,1)}, u32[]{:S(2)}, u32[]{:S(2)}) collective-permute-start(bf16[112,2048]{1,0:T(8,128)(2,1)} %get-tuple-element.113), channel_id=1, source_target_pairs={{0,8},{4,12},{8,16},{12,20},{16,24},{20,28},{24,0},{28,4},{1,9},{5... | collective-permute-start | bytes 1376264 | tf_op jit(solution)/shard_map/ppermute | solution.py:84
  76.2 52.0 %collective-permute-start.19 = (bf16[112,2048]{1,0:T(8,128)(2,1)}, bf16[112,2048]{1,0:T(8,128)(2,1)}, u32[]{:S(2)}, u32[]{:S(2)}) collective-permute-start(bf16[112,2048]{1,0:T(8,128)(2,1)} %get-tuple-element.112), channel_id=1, source_target_pairs={{0,12},{4,16},{8,20},{12,24},{16,28},{20,0},{24,4},{28,8},{1,13},{... | collective-permute-start | bytes 1376264 | tf_op jit(solution)/shard_map/ppermute | solution.py:84
  78.6 52.4 %collective-permute-start.20 = (bf16[112,2048]{1,0:T(8,128)(2,1)}, bf16[112,2048]{1,0:T(8,128)(2,1)}, u32[]{:S(2)}, u32[]{:S(2)}) collective-permute-start(bf16[112,2048]{1,0:T(8,128)(2,1)} %get-tuple-element.111), channel_id=1, source_target_pairs={{0,16},{4,20},{8,24},{12,28},{16,0},{20,4},{24,8},{28,12},{1,17},{... | collective-permute-start | bytes 1376264 | tf_op jit(solution)/shard_map/ppermute | solution.py:84
  80.1 695.7 %reduce-scatter.7.cloned.1.call-start = ((), (), s32[]{:S(2)}) async-start(), calls=%async_computation.7 | async-start | bytes 3276800 | tf_op jit(solution)/shard_map/reduce_scatter | solution.py:241
  89.7 43.1 %collective-permute-start.21 = (bf16[112,2048]{1,0:T(8,128)(2,1)}, bf16[112,2048]{1,0:T(8,128)(2,1)S(1)}, u32[]{:S(2)}, u32[]{:S(2)}) collective-permute-start(bf16[112,2048]{1,0:T(8,128)(2,1)} %get-tuple-element.110), channel_id=1, source_target_pairs={{0,20},{4,24},{8,28},{12,0},{16,4},{20,8},{24,12},{28,16},{1,21},{... | collective-permute-start | bytes 1376264 | tf_op jit(solution)/shard_map/ppermute | solution.py:84
  121.1 26.8 %collective-permute-start.22 = (bf16[112,2048]{1,0:T(8,128)(2,1)}, bf16[112,2048]{1,0:T(8,128)(2,1)S(1)}, u32[]{:S(2)}, u32[]{:S(2)}) collective-permute-start(bf16[112,2048]{1,0:T(8,128)(2,1)} %get-tuple-element.109), channel_id=1, source_target_pairs={{0,24},{4,28},{8,0},{12,4},{16,8},{20,12},{24,16},{28,20},{1,25},{... | collective-permute-start | bytes 1376264 | tf_op jit(solution)/shard_map/ppermute | solution.py:84
  125.9 23.6 %collective-permute-start.2 = (bf16[640,1024]{0,1:T(8,128)(2,1)S(1)}, bf16[640,1024]{0,1:T(8,128)(2,1)S(1)}, u32[]{:S(2)}, u32[]{:S(2)}) collective-permute-start(bf16[640,1024]{0,1:T(8,128)(2,1)S(1)} %add_convert_fusion.6), channel_id=1, source_target_pairs={{0,1},{1,0},{2,3},{3,2},{4,5},{5,4},{6,7},{7,6},{8,9},{9,8},{10,11... | collective-permute-start | bytes 3932168 | tf_op jit(solution)/shard_map/ppermute | solution.py:59
  128.2 20.5 %collective-permute-start.23 = (bf16[112,2048]{1,0:T(8,128)(2,1)S(1)}, bf16[112,2048]{1,0:T(8,128)(2,1)S(1)}, u32[]{:S(2)}, u32[]{:S(2)}) collective-permute-start(bf16[112,2048]{1,0:T(8,128)(2,1)S(1)} %copy-done.54), channel_id=1, source_target_pairs={{0,28},{4,0},{8,4},{12,8},{16,12},{20,16},{24,20},{28,24},{1,29},{... | collective-permute-start | bytes 1376264 | tf_op jit(solution)/shard_map/ppermute | solution.py:84
  163.3 28.5 %collective-permute-start.3 = (bf16[112,2176]{1,0:T(8,128)(2,1)}, bf16[112,2176]{1,0:T(8,128)(2,1)}, u32[]{:S(2)}, u32[]{:S(2)}) collective-permute-start(bf16[112,2176]{1,0:T(8,128)(2,1)} %get-tuple-element.94), channel_id=1, source_target_pairs={{0,4},{4,8},{8,12},{12,16},{16,20},{20,24},{24,28},{28,0},{1,5},{5... | collective-permute-start | bytes 1462280 | tf_op jit(solution)/shard_map/ppermute | solution.py:84
  173.7 18.1 %collective-permute-start.4 = (bf16[112,2176]{1,0:T(8,128)(2,1)}, bf16[112,2176]{1,0:T(8,128)(2,1)}, u32[]{:S(2)}, u32[]{:S(2)}) collective-permute-start(bf16[112,2176]{1,0:T(8,128)(2,1)} %get-tuple-element.95), channel_id=1, source_target_pairs={{0,8},{4,12},{8,16},{12,20},{16,24},{20,28},{24,0},{28,4},{1,9},{5... | collective-permute-start | bytes 1462280 | tf_op jit(solution)/shard_map/ppermute | solution.py:84
  183.9 53.5 %collective-permute-start.5 = (bf16[112,2176]{1,0:T(8,128)(2,1)}, bf16[112,2176]{1,0:T(8,128)(2,1)}, u32[]{:S(2)}, u32[]{:S(2)}) collective-permute-start(bf16[112,2176]{1,0:T(8,128)(2,1)} %get-tuple-element.96), channel_id=1, source_target_pairs={{0,12},{4,16},{8,20},{12,24},{16,28},{20,0},{24,4},{28,8},{1,13},{... | collective-permute-start | bytes 1462280 | tf_op jit(solution)/shard_map/ppermute | solution.py:84
  186.2 60.2 %collective-permute-start.6 = (bf16[112,2176]{1,0:T(8,128)(2,1)}, bf16[112,2176]{1,0:T(8,128)(2,1)}, u32[]{:S(2)}, u32[]{:S(2)}) collective-permute-start(bf16[112,2176]{1,0:T(8,128)(2,1)} %get-tuple-element.97), channel_id=1, source_target_pairs={{0,16},{4,20},{8,24},{12,28},{16,0},{20,4},{24,8},{28,12},{1,17},{... | collective-permute-start | bytes 1462280 | tf_op jit(solution)/shard_map/ppermute | solution.py:84
  187.4 67.9 %collective-permute-start.7 = (bf16[112,2176]{1,0:T(8,128)(2,1)}, bf16[112,2176]{1,0:T(8,128)(2,1)}, u32[]{:S(2)}, u32[]{:S(2)}) collective-permute-start(bf16[112,2176]{1,0:T(8,128)(2,1)} %get-tuple-element.99), channel_id=1, source_target_pairs={{0,20},{4,24},{8,28},{12,0},{16,4},{20,8},{24,12},{28,16},{1,21},{... | collective-permute-start | bytes 1462280 | tf_op jit(solution)/shard_map/ppermute | solution.py:84
  191.7 220.1 %copy-start.86 = (f32[640]{0:T(1024)}, f32[640]{0:T(1024)S(1)}, u32[]{:S(2)}) copy-start(f32[640]{0:T(1024)S(1)} %add_divide_fusion.2) | copy-start | bytes 7684
  191.8 72.6 %collective-permute-start.8 = (bf16[112,2176]{1,0:T(8,128)(2,1)}, bf16[112,2176]{1,0:T(8,128)(2,1)}, u32[]{:S(2)}, u32[]{:S(2)}) collective-permute-start(bf16[112,2176]{1,0:T(8,128)(2,1)} %get-tuple-element.98), channel_id=1, source_target_pairs={{0,24},{4,28},{8,0},{12,4},{16,8},{20,12},{24,16},{28,20},{1,25},{... | collective-permute-start | bytes 1462280 | tf_op jit(solution)/shard_map/ppermute | solution.py:84
  191.8 81.4 %collective-permute-start.9 = (bf16[112,2176]{1,0:T(8,128)(2,1)}, bf16[112,2176]{1,0:T(8,128)(2,1)}, u32[]{:S(2)}, u32[]{:S(2)}) collective-permute-start(bf16[112,2176]{1,0:T(8,128)(2,1)} %get-tuple-element.92), channel_id=1, source_target_pairs={{0,28},{4,0},{8,4},{12,8},{16,12},{20,16},{24,20},{28,24},{1,29},{... | collective-permute-start | bytes 1462280 | tf_op jit(solution)/shard_map/ppermute | solution.py:84
  332.2 54.3 %collective-permute-start.10 = (bf16[112,2048]{1,0:T(8,128)(2,1)S(1)}, bf16[112,2048]{1,0:T(8,128)(2,1)S(1)}, u32[]{:S(2)}, u32[]{:S(2)}) collective-permute-start(bf16[112,2048]{1,0:T(8,128)(2,1)S(1)} %get-tuple-element.122), channel_id=1, source_target_pairs={{0,4},{4,8},{8,12},{12,16},{16,20},{20,24},{24,28},{28,0},{1,5},{5... | collective-permute-start | bytes 1376264 | tf_op jit(solution)/shard_map/ppermute | solution.py:84
  333.3 55.4 %collective-permute-start.11 = (bf16[112,2048]{1,0:T(8,128)(2,1)S(1)}, bf16[112,2048]{1,0:T(8,128)(2,1)S(1)}, u32[]{:S(2)}, u32[]{:S(2)}) collective-permute-start(bf16[112,2048]{1,0:T(8,128)(2,1)S(1)} %get-tuple-element.121), channel_id=1, source_target_pairs={{0,8},{4,12},{8,16},{12,20},{16,24},{20,28},{24,0},{28,4},{1,9},{5... | collective-permute-start | bytes 1376264 | tf_op jit(solution)/shard_map/ppermute | solution.py:84
  379.1 25.7 %collective-permute-start.12 = (bf16[112,2048]{1,0:T(8,128)(2,1)S(1)}, bf16[112,2048]{1,0:T(8,128)(2,1)S(1)}, u32[]{:S(2)}, u32[]{:S(2)}) collective-permute-start(bf16[112,2048]{1,0:T(8,128)(2,1)S(1)} %get-tuple-element.120), channel_id=1, source_target_pairs={{0,12},{4,16},{8,20},{12,24},{16,28},{20,0},{24,4},{28,8},{1,13},{... | collective-permute-start | bytes 1376264 | tf_op jit(solution)/shard_map/ppermute | solution.py:84
  384.1 27.5 %collective-permute-start.13 = (bf16[112,2048]{1,0:T(8,128)(2,1)S(1)}, bf16[112,2048]{1,0:T(8,128)(2,1)S(1)}, u32[]{:S(2)}, u32[]{:S(2)}) collective-permute-start(bf16[112,2048]{1,0:T(8,128)(2,1)S(1)} %get-tuple-element.119), channel_id=1, source_target_pairs={{0,16},{4,20},{8,24},{12,28},{16,0},{20,4},{24,8},{28,12},{1,17},{... | collective-permute-start | bytes 1376264 | tf_op jit(solution)/shard_map/ppermute | solution.py:84
  384.1 27.5 %collective-permute-start.14 = (bf16[112,2048]{1,0:T(8,128)(2,1)S(1)}, bf16[112,2048]{1,0:T(8,128)(2,1)S(1)}, u32[]{:S(2)}, u32[]{:S(2)}) collective-permute-start(bf16[112,2048]{1,0:T(8,128)(2,1)S(1)} %get-tuple-element.118), channel_id=1, source_target_pairs={{0,20},{4,24},{8,28},{12,0},{16,4},{20,8},{24,12},{28,16},{1,21},{... | collective-permute-start | bytes 1376264 | tf_op jit(solution)/shard_map/ppermute | solution.py:84
  386.5 25.2 %collective-permute-start.15 = (bf16[112,2048]{1,0:T(8,128)(2,1)S(1)}, bf16[112,2048]{1,0:T(8,128)(2,1)S(1)}, u32[]{:S(2)}, u32[]{:S(2)}) collective-permute-start(bf16[112,2048]{1,0:T(8,128)(2,1)S(1)} %get-tuple-element.117), channel_id=1, source_target_pairs={{0,24},{4,28},{8,0},{12,4},{16,8},{20,12},{24,16},{28,20},{1,25},{... | collective-permute-start | bytes 1376264 | tf_op jit(solution)/shard_map/ppermute | solution.py:84
  388.7 23.0 %collective-permute-start.16 = (bf16[112,2048]{1,0:T(8,128)(2,1)S(1)}, bf16[112,2048]{1,0:T(8,128)(2,1)S(1)}, u32[]{:S(2)}, u32[]{:S(2)}) collective-permute-start(bf16[112,2048]{1,0:T(8,128)(2,1)S(1)} %get-tuple-element.116), channel_id=1, source_target_pairs={{0,28},{4,0},{8,4},{12,8},{16,12},{20,16},{24,20},{28,24},{1,29},{... | collective-permute-start | bytes 1376264 | tf_op jit(solution)/shard_map/ppermute | solution.py:84
  419.6 418.1 %reduce-scatter.15.cloned.1.call-start = ((), (), s32[]{:S(2)}) async-start(), calls=%async_computation.11 | async-start | bytes 7208960 | tf_op jit(solution)/shard_map/reduce_scatter | solution.py:233
  430.0 407.7 %reduce-scatter.13.cloned.1.call-start = ((), (), s32[]{:S(2)}) async-start(), calls=%async_computation.10 | async-start | bytes 7208960 | tf_op jit(solution)/shard_map/reduce_scatter | solution.py:232
  440.4 402.1 %reduce-scatter.17.cloned.1.call-start = ((), (), s32[]{:S(2)}) async-start(), calls=%async_computation.12 | async-start | bytes 7208960 | tf_op jit(solution)/shard_map/reduce_scatter | solution.py:231
  461.9 35.3 %collective-permute-start.24 = (bf16[112,2048]{1,0:T(8,128)(2,1)}, bf16[112,2048]{1,0:T(8,128)(2,1)}, u32[]{:S(2)}, u32[]{:S(2)}) collective-permute-start(bf16[112,2048]{1,0:T(8,128)(2,1)} %get-tuple-element.106), channel_id=1, source_target_pairs={{0,4},{4,8},{8,12},{12,16},{16,20},{20,24},{24,28},{28,0},{1,5},{5... | collective-permute-start | bytes 1376264 | tf_op jit(solution)/shard_map/ppermute | solution.py:84
  467.8 30.7 %collective-permute-start.25 = (bf16[112,2048]{1,0:T(8,128)(2,1)}, bf16[112,2048]{1,0:T(8,128)(2,1)}, u32[]{:S(2)}, u32[]{:S(2)}) collective-permute-start(bf16[112,2048]{1,0:T(8,128)(2,1)} %get-tuple-element.105), channel_id=1, source_target_pairs={{0,8},{4,12},{8,16},{12,20},{16,24},{20,28},{24,0},{28,4},{1,9},{5... | collective-permute-start | bytes 1376264 | tf_op jit(solution)/shard_map/ppermute | solution.py:84
  491.3 29.3 %collective-permute-start.26 = (bf16[112,2048]{1,0:T(8,128)(2,1)}, bf16[112,2048]{1,0:T(8,128)(2,1)S(1)}, u32[]{:S(2)}, u32[]{:S(2)}) collective-permute-start(bf16[112,2048]{1,0:T(8,128)(2,1)} %get-tuple-element.104), channel_id=1, source_target_pairs={{0,12},{4,16},{8,20},{12,24},{16,28},{20,0},{24,4},{28,8},{1,13},{... | collective-permute-start | bytes 1376264 | tf_op jit(solution)/shard_map/ppermute | solution.py:84
  491.4 34.7 %collective-permute-start.27 = (bf16[112,2048]{1,0:T(8,128)(2,1)}, bf16[112,2048]{1,0:T(8,128)(2,1)S(1)}, u32[]{:S(2)}, u32[]{:S(2)}) collective-permute-start(bf16[112,2048]{1,0:T(8,128)(2,1)} %get-tuple-element.103), channel_id=1, source_target_pairs={{0,16},{4,20},{8,24},{12,28},{16,0},{20,4},{24,8},{28,12},{1,17},{... | collective-permute-start | bytes 1376264 | tf_op jit(solution)/shard_map/ppermute | solution.py:84
  494.3 32.9 %collective-permute-start.28 = (bf16[112,2048]{1,0:T(8,128)(2,1)}, bf16[112,2048]{1,0:T(8,128)(2,1)S(1)}, u32[]{:S(2)}, u32[]{:S(2)}) collective-permute-start(bf16[112,2048]{1,0:T(8,128)(2,1)} %get-tuple-element.102), channel_id=1, source_target_pairs={{0,20},{4,24},{8,28},{12,0},{16,4},{20,8},{24,12},{28,16},{1,21},{... | collective-permute-start | bytes 1376264 | tf_op jit(solution)/shard_map/ppermute | solution.py:84
  497.2 31.0 %collective-permute-start.29 = (bf16[112,2048]{1,0:T(8,128)(2,1)}, bf16[112,2048]{1,0:T(8,128)(2,1)S(1)}, u32[]{:S(2)}, u32[]{:S(2)}) collective-permute-start(bf16[112,2048]{1,0:T(8,128)(2,1)} %get-tuple-element.101), channel_id=1, source_target_pairs={{0,24},{4,28},{8,0},{12,4},{16,8},{20,12},{24,16},{28,20},{1,25},{... | collective-permute-start | bytes 1376264 | tf_op jit(solution)/shard_map/ppermute | solution.py:84
  498.5 34.3 %collective-permute-start.30 = (bf16[112,2048]{1,0:T(8,128)(2,1)}, bf16[112,2048]{1,0:T(8,128)(2,1)S(1)}, u32[]{:S(2)}, u32[]{:S(2)}) collective-permute-start(bf16[112,2048]{1,0:T(8,128)(2,1)} %get-tuple-element.100), channel_id=1, source_target_pairs={{0,28},{4,0},{8,4},{12,8},{16,12},{20,16},{24,20},{28,24},{1,29},{... | collective-permute-start | bytes 1376264 | tf_op jit(solution)/shard_map/ppermute | solution.py:84
  558.2 3.3 collective-permute-start.31
  565.0 48.5 %collective-permute-start.32 = (bf16[640,1152]{0,1:T(8,128)(2,1)S(1)}, bf16[640,1152]{0,1:T(8,128)(2,1)S(1)}, u32[]{:S(2)}, u32[]{:S(2)}) collective-permute-start(bf16[640,1152]{0,1:T(8,128)(2,1)S(1)} %add_convert_fusion.3), channel_id=1, source_target_pairs={{0,2},{1,3},{2,0},{3,1},{4,6},{5,7},{6,4},{7,5},{8,10},{9,11},{10,... | collective-permute-start | bytes 4423688 | tf_op jit(solution)/shard_map/ppermute | solution.py:59
  615.0 9.0 collective-permute-start.33
  623.4 224.8 %reduce-scatter.9.cloned.1.call-start = ((), (), s32[]{:S(2)}) async-start(), calls=%async_computation.8 | async-start | bytes 9437184 | tf_op jit(solution)/shard_map/reduce_scatter | solution.py:307
  691.4 454.0 %reduce-scatter.11.cloned.1.call-start = ((), (), s32[]{:S(2)}) async-start(), calls=%async_computation.9 | async-start | bytes 19464192 | tf_op jit(solution)/shard_map/reduce_scatter | solution.py:203
  731.9 3.2 collective-permute-start.34
  735.6 31.1 %collective-permute-start.35 = (bf16[640,1024]{0,1:T(8,128)(2,1)S(1)}, bf16[640,1024]{0,1:T(8,128)(2,1)S(1)}, u32[]{:S(2)}, u32[]{:S(2)}) collective-permute-start(bf16[640,1024]{0,1:T(8,128)(2,1)S(1)} %add_convert_fusion.5), channel_id=1, source_target_pairs={{0,2},{1,3},{2,0},{3,1},{4,6},{5,7},{6,4},{7,5},{8,10},{9,11},{10,... | collective-permute-start | bytes 3932168 | tf_op jit(solution)/shard_map/ppermute | solution.py:59
  768.1 10.5 collective-permute-start.36
  (115 other events, 1610.5 us)
Sparse Core Ops, SparseCore 0:
  9.6 46.5 all-gather.5
  58.3 68.4 all-gather.9
  128.9 45.1 all-gather.7
  419.7 48.9 reduce-scatter.6
  471.3 54.8 reduce-scatter.14
  528.6 68.9 reduce-scatter.12
  623.5 61.8 reduce-scatter.16
  691.5 156.5 reduce-scatter.8
  852.6 292.8 reduce-scatter.10

commit v2 on v1

--- a/solution.py
+++ b/solution.py
@@ -1,6 +1,10 @@
+import functools
+
 import jax
 import jax.numpy as jnp
 from jax import lax
+from jax.experimental import pallas as pl
+from jax.experimental.pallas import tpu as pltpu
 from jax.sharding import PartitionSpec as P
 
 HEAD_DIM = 128
@@ -71,23 +75,360 @@
     return jnp.concatenate([jnp.where(low, two, other), jnp.where(low, other, two)], axis=1).astype(F32)
 
 
-def exchange(x, n):
+def exchange(x, n, back=False):
     rows = x.shape[0] // n
-    me = lax.axis_index("ep")
-    out = jnp.zeros_like(x)
-    out = lax.dynamic_update_slice_in_dim(
-        out, lax.dynamic_slice_in_dim(x, me * rows, rows, 0), me * rows, 0
-    )
+    out = [x[:rows]]
     for shift in range(1, n):
-        to = lax.rem(me + shift, n)
-        came = lax.rem(me + n - shift, n)
-        got = lax.ppermute(
-            lax.dynamic_slice_in_dim(x, to * rows, rows, 0),
+        step = n - shift if back else shift
+        out.append(
+            lax.ppermute(
+                x[shift * rows : (shift + 1) * rows], "ep", [(i, (i + step) % n) for i in range(n)]
+            )
+        )
+    return jnp.concatenate(out, axis=0)
+
+def ring_place(e, n):
+    odd = e % 2
+    return (1 - odd) * (e // 2) + odd * (n - 1 - e // 2)
+
+
+def ring_member(p, n):
+    second = p // (n // 2)
+    return (1 - second) * 2 * p + second * (2 * (n - 1 - p) + 1)
+
+
+def remote(src, dst, send_sem, recv_sem, axis, index):
+    return pltpu.make_async_remote_copy(
+        src_ref=src,
+        dst_ref=dst,
+        send_sem=send_sem,
+        recv_sem=recv_sem,
+        device_id={axis: index},
+        device_id_type=pl.DeviceIdType.MESH,
+    )
+
+
+def greet(n, n_tp, ep, tp):
+    barrier = pltpu.get_barrier_semaphore()
+    for shift in range(1, n):
+        pl.semaphore_signal(
+            barrier, 1, device_id={"ep": lax.rem(ep + shift, n)}, device_id_type=pl.DeviceIdType.MESH
+        )
+    for shift in range(1, n_tp):
+        pl.semaphore_signal(
+            barrier, 1, device_id={"tp": lax.rem(tp + shift, n_tp)}, device_id_type=pl.DeviceIdType.MESH
+        )
+    pl.semaphore_wait(barrier, n - 1 + n_tp - 1)
+
+
+def flip(index, bit):
+    if bit == 1:
+        return index + 1 - 2 * (index % 2)
+    return index + 2 - 4 * ((index // 2) % 2)
+
+
+def tail_kernel(
+    n,
+    n_tp,
+    n1t,
+    lg,
+    agt,
+    ctx,
+    w,
+    h_cols,
+    r_one,
+    gain,
+    mid_cols,
+    bias,
+    small,
+    qkv_out,
+    o_out,
+    in_out,
+    gain_out,
+    bias_out,
+    small_out,
+    ring_recv,
+    ring_send,
+    part_own,
+    part_send,
+    part_recv,
+    y_send,
+    y_recv,
+    mean_send,
+    mean_recv,
+    vec_send,
+    vec_recv,
+    small_send,
+    small_recv,
+    gain_send,
+    gain_recv,
+    ring_ss,
+    ring_rs,
+    tp_ss,
+    tp_rs,
+    vec_ss,
+    vec_rs,
+    small_ss,
+    small_rs,
+    gain_ss,
+    gain_rs,
+):
+    ep = lax.axis_index("ep")
+    tp = lax.axis_index("tp")
+    tokens, lw = ctx.shape
+    rows = n1t.shape[0] // n
+    width = n1t.shape[0]
+    p = ring_place(ep, n)
+    nxt = ring_member(lax.rem(p + 1, n), n)
+    prv = ring_member(lax.rem(p + n - 1, n), n)
+    core_peer, y_peer = flip(tp, 1), flip(tp, 2)
+    greet(n, n_tp, ep, tp)
+
+    def small_copy(shift):
+        to = lax.rem(ep + shift, n)
+        return remote(
+            small_send, small_recv.at[ep], small_ss.at[shift], small_rs.at[shift], "ep", to
+        )
+
+    def small_wait(shift):
+        came = lax.rem(ep + n - shift, n)
+        return remote(
+            small_send, small_recv.at[came], small_ss.at[shift], small_rs.at[shift], "ep", came
+        )
+
+    def block_of(ring, step):
+        if ring < 2:
+            return ring_member(lax.rem(p + 2 * n - 1 - step, n), n)
+        return ring_member(lax.rem(p + 1 + step, n), n)
+
+    def term(ring, owner):
+        at = pl.ds(pl.multiple_of(owner * rows, rows), rows)
+        if ring == 1:
+            return jnp.dot(agt[at, :], ctx[...], preferred_element_type=F32)
+        k = {0: 0, 2: 1, 3: 2}[ring]
+        return jnp.dot(n1t[at, :], lg[:, k * lw : (k + 1) * lw], preferred_element_type=F32)
+
+    def ring_copy(ring, step, slot):
+        return remote(
+            ring_send.at[ring, slot],
+            ring_recv.at[ring, step],
+            ring_ss.at[ring, slot],
+            ring_rs.at[ring, step],
             "ep",
-            [(i, (i + shift) % n) for i in range(n)],
+            nxt if ring < 2 else prv,
         )
-        out = lax.dynamic_update_slice_in_dim(out, got, came * rows, 0)
-    return out
+
+    def ring_step(step, first):
+        for ring in range(4):
+            slot = lax.rem(step, 2)
+            mine = term(ring, block_of(ring, step))
+            ring_copy(ring, step - 1, slot).wait_recv()
+            if not first:
+                ring_copy(ring, step - 2, slot).wait_send()
+            ring_send[ring, slot] = (mine + ring_recv[ring, step - 1].astype(F32)).astype(BF)
+            ring_copy(ring, step, slot).start()
+
+    for ring in range(4):
+        ring_send[ring, 0] = term(ring, block_of(ring, 0)).astype(BF)
+        ring_copy(ring, 0, 0).start()
+
+    def part_block(column, store):
+        for m in range(0, tokens, 128):
+            total = None
+            for k in range(3):
+                d = lax.dot_general(
+                    lg[m : m + 128, k * lw : (k + 1) * lw],
+                    w[k, pl.ds(pl.multiple_of(column * lw, lw), lw), :],
+                    (((1,), (1,)), ((), ())),
+                    preferred_element_type=F32,
+                )
+                total = d if total is None else total + d
+            store(m, total)
+
+    def tp_copy(i, src, dst, peer):
+        return remote(src, dst, tp_ss.at[i], tp_rs.at[i], "tp", peer)
+
+    first = [tp_copy(i, part_send.at[i], part_recv.at[i], core_peer) for i in range(2)]
+    for i in range(2):
+
+        def put(m, total, i=i):
+            part_send[i, m : m + 128, :] = total.astype(BF)
+
+        part_block((core_peer % 2) + 2 * i, put)
+        first[i].start()
+
+    ring_step(1, True)
+
+    small_send[...] = small[...]
+    small_recv[ep] = small[...]
+    for shift in range(1, n):
+        small_copy(shift).start()
+
+    def put_own(m, total):
+        part_own[m : m + 128, :] = total
+
+    other = (tp // 2) * -1 + 1
+    part_block((tp % 2) + 2 * other, put_own)
+    for i in range(2):
+        first[i].wait()
+    y_send[...] = (part_own[...] + part_recv[other].astype(F32)).astype(BF)
+    second = tp_copy(2, y_send, y_recv, y_peer)
+    second.start()
+
+    ring_step(2, False)
+
+    part_block(tp, put_own)
+    second.wait()
+    for m in range(0, tokens, 128):
+        at = slice(m, m + 128)
+        grad = (
+            part_own[at, :]
+            + part_recv[tp // 2, at, :].astype(F32)
+            + y_recv[at, :].astype(F32)
+        )
+        part_own[at, :] = grad
+        hid = h_cols[at, :].astype(F32)
+        mean = jnp.sum(grad * gain[...] * hid, axis=1, keepdims=True)
+        mean_send[0, at, :] = jnp.broadcast_to(mean, (128, 128))
+        col = jnp.sum(grad * hid * r_one[at, :], axis=0, keepdims=True)
+        if m == 0:
+            vec_send[:, :lw] = col
+        else:
+            vec_send[:, :lw] += col
+    third = tp_copy(3, mean_send.at[0], mean_recv.at[0], core_peer)
+    third.start()
+    vec_send[:, lw:] = bias[...]
+    vec_recv[ep] = vec_send[...]
+
+    def vec_copy(shift, way):
+        to = lax.rem(ep + shift, n)
+        came = lax.rem(ep + n - shift, n)
+        if way == "out":
+            return remote(vec_send, vec_recv.at[ep], vec_ss.at[shift], vec_rs.at[shift], "ep", to)
+        return remote(vec_send, vec_recv.at[came], vec_ss.at[shift], vec_rs.at[shift], "ep", came)
+
+    for shift in range(1, n):
+        vec_copy(shift, "out").start()
+
+    ring_step(3, False)
+
+    third.wait()
+    mean_send[1] = mean_send[0] + mean_recv[0]
+    fourth = tp_copy(4, mean_send.at[1], mean_recv.at[1], y_peer)
+    fourth.start()
+
+    ring_step(4, False)
+
+    fourth.wait()
+    for m in range(0, tokens, 128):
+        at = slice(m, m + 128)
+        mean = (mean_send[1, at, :1] + mean_recv[1, at, :1]) * (1.0 / width)
+        r = r_one[at, :]
+        in_out[at, :] = (
+            mid_cols[at, :]
+            + r * part_own[at, :] * gain[...]
+            - h_cols[at, :].astype(F32) * (r * r * r) * mean
+        ).astype(BF)
+    for shift in range(1, n):
+        vec_copy(shift, "in").wait()
+    total = vec_recv[0]
+    for e in range(1, n):
+        total = total + vec_recv[e]
+    bias_out[...] = total[:, lw:]
+    gain_send[...] = total[:, :lw]
+    gain_recv[tp] = total[:, :lw]
+
+    def gain_copy(shift, way):
+        to = lax.rem(tp + shift, n_tp)
+        came = lax.rem(tp + n_tp - shift, n_tp)
+        if way == "out":
+            return remote(gain_send, gain_recv.at[tp], gain_ss.at[shift], gain_rs.at[shift], "tp", to)
+        return remote(gain_send, gain_recv.at[came], gain_ss.at[shift], gain_rs.at[shift], "tp", came)
+
+    for shift in range(1, n_tp):
+        gain_copy(shift, "out").start()
+
+    @pl.loop(5, n - 1)
+    def _(step):
+        ring_step(step, False)
+
+    for shift in range(1, n):
+        small_wait(shift).wait()
+    total = small_recv[0].astype(F32)
+    for e in range(1, n):
+        total = total + small_recv[e].astype(F32)
+    small_out[...] = total
+    for shift in range(1, n_tp):
+        gain_copy(shift, "in").wait()
+    for j in range(n_tp):
+        gain_out[:, j * lw : (j + 1) * lw] = gain_recv[j]
+
+    for ring in range(4):
+        mine = term(ring, ep)
+        ring_copy(ring, n - 2, 0).wait_recv()
+        done = mine + ring_recv[ring, n - 2].astype(F32)
+        if ring == 1:
+            o_out[...] = done
+        else:
+            qkv_out[{0: 0, 2: 1, 3: 2}[ring]] = done
+    for ring in range(4):
+        for step in (n - 3, n - 2):
+            ring_copy(ring, step, step % 2).wait_send()
+
+
+def tail(n, n_tp, n1t, lg, agt, ctx, w, h_cols, r_one, gain, mid_cols, bias, small):
+    width, tokens = n1t.shape
+    lw = ctx.shape[1]
+    rows = width // n
+    wide = small.shape[0]
+    vmem = pl.BlockSpec(memory_space=pltpu.VMEM)
+    dma = pltpu.SemaphoreType.DMA
+    return pl.pallas_call(
+        functools.partial(tail_kernel, n, n_tp),
+        out_shape=(
+            jax.ShapeDtypeStruct((3, rows, lw), F32),
+            jax.ShapeDtypeStruct((rows, lw), F32),
+            jax.ShapeDtypeStruct((tokens, lw), BF),
+            jax.ShapeDtypeStruct((1, width), F32),
+            jax.ShapeDtypeStruct((1, 3 * lw), F32),
+            jax.ShapeDtypeStruct((wide, width), F32),
+        ),
+        in_specs=[vmem] * 11,
+        out_specs=[vmem] * 6,
+        scratch_shapes=[
+            pltpu.VMEM((4, n - 1, rows, lw), BF),
+            pltpu.VMEM((4, 2, rows, lw), BF),
+            pltpu.VMEM((tokens, lw), F32),
+            pltpu.VMEM((2, tokens, lw), BF),
+            pltpu.VMEM((2, tokens, lw), BF),
+            pltpu.VMEM((tokens, lw), BF),
+            pltpu.VMEM((tokens, lw), BF),
+            pltpu.VMEM((2, tokens, 128), F32),
+            pltpu.VMEM((2, tokens, 128), F32),
+            pltpu.VMEM((1, 4 * lw), F32),
+            pltpu.VMEM((n, 1, 4 * lw), F32),
+            pltpu.VMEM((wide, width), BF),
+            pltpu.VMEM((n, wide, width), BF),
+            pltpu.VMEM((1, lw), F32),
+            pltpu.VMEM((n_tp, 1, lw), F32),
+            dma((4, 2)),
+            dma((4, n - 1)),
+            dma((5,)),
+            dma((5,)),
+            dma((n,)),
+            dma((n,)),
+            dma((n,)),
+            dma((n,)),
+            dma((n_tp,)),
+            dma((n_tp,)),
+        ],
+        compiler_params=pltpu.CompilerParams(
+            collective_id=0, has_side_effects=True, vmem_limit_bytes=56 * 2**20
+        ),
+        cost_estimate=pl.CostEstimate(
+            flops=2 * tokens * width * 7 * lw, bytes_accessed=30 * 2**20, transcendentals=0
+        ),
+    )(n1t, lg, agt, ctx, w, h_cols, r_one, gain, mid_cols, bias, small)
 
 
 def body(
@@ -139,7 +480,9 @@
     kept = slot < capacity
     in_part = slot - tp_i * part
     mine = kept & (in_part >= 0) & (in_part < part)
-    dest = jnp.where(mine, routes.T * part_pad + in_part, -1)
+    ep_i = lax.axis_index("ep")
+    hop = lax.rem(routes.T + n_exp - ep_i * expert_local, n_exp)
+    dest = jnp.where(mine, hop * part_pad + in_part, -1)
     row_ids = jnp.arange(rows, dtype=jnp.int32)[:, None]
     place = (dest[0][None, :] == row_ids)
     for k in range(1, top):
@@ -177,7 +520,8 @@
     router_probs = jax.nn.softmax(logits, axis=-1)
     probs_hi = router_probs.astype(BF)
     probs_lo = (router_probs - probs_hi.astype(F32)).astype(BF)
-    own = (row_ids // part_pad == jnp.arange(n_exp, dtype=jnp.int32)[None, :]).astype(F32)
+    row_expert = lax.rem(row_ids // part_pad + ep_i * expert_local, n_exp)
+    own = (row_expert == jnp.arange(n_exp, dtype=jnp.int32)[None, :]).astype(F32)
     sent_rows = mm(place, normed_two, 1, 0).astype(BF)
     gate_hi = jnp.sum(mm(place, probs_hi, 1, 0) * own, axis=1, keepdims=True)
     gate_lo = jnp.sum(mm(place, probs_lo, 1, 0) * own, axis=1, keepdims=True)
@@ -200,19 +544,16 @@
     shared_pre_grad = jnp.stack([sg, su], axis=1).astype(BF)
     shared_back = jnp.einsum("tkf,dkf->td", shared_pre_grad, shared_gate_up, preferred_element_type=F32)
     sg, su = sg.astype(BF), su.astype(BF)
-    shared_slab = lax.psum_scatter(
-        jnp.concatenate(
-            [
-                mm(normed_two, sg, 0, 0).astype(BF),
-                mm(normed_two, su, 0, 0).astype(BF),
-                mm(shared_out_grad, shared_hidden, 0, 0).astype(BF),
-            ],
-            axis=1,
-        ),
-        "ep",
-        scatter_dimension=0,
-        tiled=True,
-    ).astype(F32)
+    slab = jnp.concatenate(
+        [
+            mm(normed_two, sg, 0, 0).astype(BF),
+            mm(normed_two, su, 0, 0).astype(BF),
+            mm(shared_out_grad, shared_hidden, 0, 0).astype(BF),
+        ],
+        axis=1,
+    )
+    slab, whole_rows, gate_row = lax.optimization_barrier((slab, whole_rows, gate_row))
+    shared_slab = lax.psum_scatter(slab, "ep", scatter_dimension=0, tiled=True).astype(F32)
     sf = shared_hidden.shape[1]
     shared_gate_up_grad = jnp.stack([shared_slab[:, :sf], shared_slab[:, sf : 2 * sf]], axis=1)
     shared_down_grad = shared_slab[:, 2 * sf :]
@@ -226,8 +567,8 @@
     eg, eu = swiglu_backward(e_hidden_grad, e_gate, e_up)
     eg, eu = eg.astype(BF), eu.astype(BF)
     back_sent = (mm(eg, w_gate, 1, 0) + mm(eu, w_up, 1, 0)).astype(BF)
-    back_rows = exchange(back_sent, n_ep)
-    out_rows = exchange(e_out, n_ep)
+    back_rows = exchange(back_sent, n_ep, True)
+    out_rows = exchange(e_out, n_ep, True)
     d_down = lax.psum_scatter(mm(e_hidden, row_grad, 0, 0).astype(BF), "tp", scatter_dimension=0, tiled=True)
     d_gate = lax.psum_scatter(mm(eg, whole_rows, 0, 0).astype(BF), "tp", scatter_dimension=0, tiled=True)
     d_up = lax.psum_scatter(mm(eu, whole_rows, 0, 0).astype(BF), "tp", scatter_dimension=0, tiled=True)
@@ -277,12 +618,10 @@
     middle_grad = upstream + factor_two * scaled - middle * (factor_two**3) * jnp.mean(
         scaled * middle, axis=-1, keepdims=True
     )
-    small_sum = lax.psum(
-        jnp.concatenate([small_two, mlp_gain_grad[None]], axis=0).astype(BF), "ep"
-    ).astype(F32)
-    router_sum = small_sum[:n_exp].T
-    share_gate_sum = small_sum[n_exp]
-    gain_two_sum = small_sum[n_exp + 1]
+    small_pad = -(-(n_exp + 2) // 16) * 16 - n_exp - 2
+    small = jnp.concatenate(
+        [small_two, mlp_gain_grad[None], jnp.zeros((small_pad, width), F32)], axis=0
+    ).astype(BF)
 
     attn_grad = middle_grad.astype(BF)
     context_grad = mm(attn_grad, out_weight, 1, 0).astype(BF).reshape(tokens, heads, head_size)
@@ -304,34 +643,27 @@
     parts = [g.reshape(tokens, local_width) for g in (query_grad, key_grad, value_grad)]
     bias_grad = jnp.concatenate([jnp.sum(g, axis=0) for g in parts])
     linear_grad = jnp.concatenate([g.astype(BF) for g in parts], axis=1)
-    attention_slab = lax.psum_scatter(
-        jnp.concatenate(
-            [mm(normed_one, linear_grad, 0, 0).astype(BF), mm(attn_grad, context, 0, 0).astype(BF)], axis=1
-        ),
-        "ep",
-        scatter_dimension=0,
-        tiled=True,
-    ).astype(F32)
-    qkv_weight_grad = attention_slab[:, : 3 * local_width].reshape(-1, 3, local_width)
-    out_weight_grad = attention_slab[:, 3 * local_width :]
-    w_t = jnp.transpose(qkv_weight, (1, 0, 2))
-    normed_one_part = sum(
-        mm(linear_grad[:, i * local_width : (i + 1) * local_width], w_t[i], 1, 1) for i in range(3)
-    )
-    normed_one_grad = tp_sum(normed_one_part, n_tp)
-    attn_gain_grad = jnp.sum(normed_one_grad * residual_in * factor_one, axis=0)
-    scaled = normed_one_grad * attn_gain
-    input_grad = lax.dynamic_slice_in_dim(
-        middle_grad
-        + factor_one * scaled
-        - residual_in * (factor_one**3) * jnp.mean(scaled * residual_in, axis=-1, keepdims=True),
-        col_start,
-        cols,
-        1,
-    ).astype(BF)
-    last_sum = lax.psum(jnp.concatenate([attn_gain_grad, bias_grad]).astype(BF), "ep").astype(F32)
-    gain_one_sum = last_sum[:width]
-    bias_sum = last_sum[width:].reshape(3, local_width)
+    qkv_grad, out_weight_grad, input_grad, gain_one, bias_sum, small_sum = tail(
+        n_ep,
+        n_tp,
+        normed_one.T,
+        linear_grad,
+        attn_grad.T,
+        context,
+        jnp.transpose(qkv_weight, (1, 0, 2)),
+        lax.dynamic_slice_in_dim(hidden, col_start, cols, 1),
+        factor_one,
+        lax.dynamic_slice_in_dim(attn_gain, col_start, cols, 0)[None],
+        lax.dynamic_slice_in_dim(middle_grad, col_start, cols, 1),
+        bias_grad[None],
+        small,
+    )
+    qkv_weight_grad = jnp.transpose(qkv_grad, (1, 0, 2))
+    gain_one_sum = gain_one[0]
+    bias_sum = bias_sum.reshape(3, local_width)
+    router_sum = small_sum[:n_exp].T
+    share_gate_sum = small_sum[n_exp]
+    gain_two_sum = small_sum[n_exp + 1]
     return (
         output,
         input_grad,

time: 1170 us -> 1030 us (0.88)
  Pallas kernels: 0 us -> 198 us
  waiting for transfers between devices: 472 us -> 373 us
  local copies, waits for them, and re-layouts: 165 us -> 96.5 us
  starting transfers between devices: 123 us -> 60 us
  blocking collectives: 46.4 us -> 0 us
  matrix products: 243 us -> 207 us
  other arithmetic: 98.7 us -> 72.4 us
    pallas_call x0 -> x1, Pallas kernels: none -> 198 us  [tail(): pl.pallas_call(functools.partial(tail_kernel, n, n_tp), out_shape=(jax.Sh...]
    reduce_scatter x2 -> x1, waiting for transfers between devices: 291 us -> 121 us  [body(): lax.psum_scatter(slab, 'ep', scatter_dimension=0, tiled=True).astype(F32)]
    ppermute x28, waiting for transfers between devices: 66.3 us -> 174 us  [exchange(): lax.ppermute(x[shift * rows:(shift + 1) * rows], 'ep', [(i, (i + step) %...]
    dynamic_update_slice x29 -> x0, local copies, waits for them, and re-layouts: 71.7 us -> none  [the longest x28 64.9 us: exchange(): out = lax.dynamic_update_slice_in_dim(out, got, came * rows, 0)]
    ppermute x28, starting transfers between devices: 116 us -> 55.2 us  [exchange(): lax.ppermute(x[shift * rows:(shift + 1) * rows], 'ep', [(i, (i + step) %...]
    psum x1 -> x0, blocking collectives: 46.4 us -> none  [body(): lax.psum(jnp.concatenate([attn_gain_grad, bias_grad]).astype(BF), 'ep')]
    dot_general x33 -> x28, matrix products: 194 us -> 155 us  [mm(): lax.dot_general(a, b, (((ca,), (cb,)), ((), ())), preferred_element_type=...]
    ppermute x9 -> x6, waiting for transfers between devices: 113 us -> 76.5 us  [swap(): return lax.ppermute(x, 'tp', [(i, i ^ bit) for i in range(n)])]
  transfers between devices with their start and end apart: 46 -> 42, of which waited for: 15 -> 15; matrix products, arithmetic and copies ran while one was open for 38% -> 30% of each run, Pallas kernels for 0% -> 19%
where the time goes in v2:
time: 1030 us; the launch traced here: 1020 us
  waiting for transfers between devices  373 us (36%)
  matrix products  207 us (20%)
  Pallas kernels  198 us (19%)
  local copies, waits for them, and re-layouts  96.5 us (9%)
  other arithmetic  72.4 us (7%)
  starting transfers between devices  60 us (6%)
  between operations  16.8 us (2%)
    pallas_call x1, Pallas kernels, tail(): pl.pallas_call(functools.partial(tail_kernel, n, n_tp), out_shape=(jax.Sh...  198 us
    ppermute x28, waiting for transfers between devices, exchange(): lax.ppermute(x[shift * rows:(shift + 1) * rows], 'ep', [(i, (i + step) %...  174 us
    dot_general x28, matrix products, mm(): lax.dot_general(a, b, (((ca,), (cb,)), ((), ())), preferred_element_type=...  155 us
    reduce_scatter x1, waiting for transfers between devices, body(): lax.psum_scatter(slab, 'ep', scatter_dimension=0, tiled=True).astype(F32)  121 us
    ppermute x6, waiting for transfers between devices, swap(): return lax.ppermute(x, 'tp', [(i, i ^ bit) for i in range(n)])  76.5 us
    ppermute x28, starting transfers between devices, exchange(): lax.ppermute(x[shift * rows:(shift + 1) * rows], 'ep', [(i, (i + step) %...  55.2 us
    unnamed x217, local copies, waits for them, and re-layouts  49.6 us
  transfers between devices with their start and end apart: 42, of which 15 were waited for; matrix products, arithmetic and copies ran while one was open for 30% of the time, Pallas kernels for 19%

profile of v2, /device:TPU:0, one launch (start us, length us, event | category | flops | bytes accessed | tf_op | source)
XLA Modules:
  0.0 1024.0 jit_solution(1618676889952012576)
XLA Ops:
  7.2 3.9 fusion.124
  14.3 8.6 broadcast_add_fusion
  39.0 4.2 convolution_convert_fusion.11
  47.9 4.4 fusion.49
  52.5 3.9 add_convert_fusion.5
  72.7 9.5 collective-permute-done.17
  84.0 23.6 %collective-permute-done.1 = bf16[640,1024]{1,0:T(8,128)(2,1)} collective-permute-done((bf16[640,1024]{1,0:T(8,128)(2,1)S(1)}, bf16[640,1024]{1,0:T(8,128)(2,1)}, u32[]{:S(2)}, u32[]{:S(2)}) %collective-permute-start.1) | collective-permute-done | bytes 1310752 | tf_op jit(solution)/shard_map/ppermute | solution.py:63
  115.1 5.5 collective-permute-done.19
  125.2 15.2 %collective-permute-done.22 = bf16[112,2048]{1,0:T(8,128)(2,1)S(1)} collective-permute-done((bf16[112,2048]{1,0:T(8,128)(2,1)}, bf16[112,2048]{1,0:T(8,128)(2,1)S(1)}, u32[]{:S(2)}, u32[]{:S(2)}) %collective-permute-start.22) | collective-permute-done | bytes 458784 | tf_op jit(solution)/shard_map/ppermute | solution.py:84
  156.5 7.6 collective-permute-start.3
  164.1 4.1 collective-permute-start.4
  171.7 3.8 collective-permute-start.7
  175.5 13.7 %fusion.6 = f32[640,2,1408]{2,0,1:T(8,128)} fusion(bf16[2048,2,1408]{2,1,0:T(2,128)(2,1)} %param.24, bf16[640,2048]{1,0:T(8,128)(2,1)S(1)} %copy-done.5), kind=kOutput, calls=%fused_computation.14 | convolution fusion | flops 7381975040 | bytes 21364736 | tf_op jit(solution)/shard_map/td,dkf->tkf/dot_general | solution.py:537
  190.1 7.8 multiply_convert_fusion.7
  197.9 5.0 convolution_convert_fusion.5
  202.9 5.0 convolution_convert_fusion.4
  207.9 5.6 convolution_convert_fusion.3
  213.4 7.6 pad_maximum_fusion
  229.9 14.2 %collective-permute-done.8 = bf16[112,2176]{1,0:T(8,128)(2,1)S(1)} collective-permute-done((bf16[112,2176]{1,0:T(8,128)(2,1)}, bf16[112,2176]{1,0:T(8,128)(2,1)S(1)}, u32[]{:S(2)}, u32[]{:S(2)}) %collective-permute-start.8) | collective-permute-done | bytes 487456 | tf_op jit(solution)/shard_map/ppermute | solution.py:84
  245.7 4.3 slice.300
  251.6 10.8 %fusion.10 = f32[896,1408]{1,0:T(8,128)} fusion(bf16[896,2048]{1,0:T(8,128)(2,1)} %slice.300, bf16[1,1408,2048]{2,1,0:T(8,128)(2,1)} %all-gather.10.cloned.1.call-done), kind=kOutput, calls=%fused_computation.38 | convolution fusion | flops 5167382528 | bytes 14483456 | tf_op jit(solution)/shard_map/dot_general | solution.py:18
  262.4 10.7 %fusion.14 = f32[896,1408]{1,0:T(8,128)} fusion(bf16[896,2048]{1,0:T(8,128)(2,1)} %slice.300, bf16[1,1408,2048]{2,1,0:T(8,128)(2,1)} %all-gather.8.cloned.1.call-done), kind=kOutput, calls=%fused_computation.42 | convolution fusion | flops 5167382528 | bytes 14483456 | tf_op jit(solution)/shard_map/dot_general | solution.py:18
  273.1 15.0 %multiply_convert_fusion.4 = (bf16[896,1408]{1,0:T(8,128)(2,1)}, bf16[896,1408]{1,0:T(8,128)(2,1)S(1)}, bf16[896,1408]{1,0:T(8,128)(2,1)}) fusion(f32[896,1408]{1,0:T(8,128)} %fusion.14, f32[896,1408]{1,0:T(8,128)} %fusion.10, bf16[1408,2048]{1,0:T(8,128)(2,1)} %all-gather.6.cloned.1.call-done, bf16[896,2048]{1,0:T(8,128)(2,1)} %constant_dynamic-update-slice_fusion.14, ...), kind=kOutput, calls=%fused_computation.60 | convolution fusion | flops 5193072640 | bytes 27102720 | tf_op jit(solution)/shard_map/dot_general | solution.py:18
  288.1 6.0 convolution_convert_fusion.8
  294.7 11.6 %collective-permute-start.10 = (bf16[112,2048]{1,0:T(8,128)(2,1)S(1)}, bf16[112,2048]{1,0:T(8,128)(2,1)S(1)}, u32[]{:S(2)}, u32[]{:S(2)}) collective-permute-start(bf16[112,2048]{1,0:T(8,128)(2,1)S(1)} %get-tuple-element.137), channel_id=1, source_target_pairs={{0,28},{4,0},{8,4},{12,8},{16,12},{20,16},{24,20},{28,24},{1,29},{... | collective-permute-start | bytes 1376264 | tf_op jit(solution)/shard_map/ppermute | solution.py:84
  306.3 6.6 fusion.20
  319.8 7.6 collective-permute-done.11
  327.5 9.6 collective-permute-done.12
  337.1 49.3 %collective-permute-done.13 = bf16[112,2048]{1,0:T(8,128)(2,1)S(1)} collective-permute-done((bf16[112,2048]{1,0:T(8,128)(2,1)S(1)}, bf16[112,2048]{1,0:T(8,128)(2,1)S(1)}, u32[]{:S(2)}, u32[]{:S(2)}) %collective-permute-start.13) | collective-permute-done | bytes 458784 | tf_op jit(solution)/shard_map/ppermute | solution.py:84
  388.5 5.0 add_convert_fusion.1
  393.6 10.3 %convolution_convert_fusion.2 = bf16[1408,2048]{1,0:T(8,128)(2,1)} fusion(bf16[896,1408]{1,0:T(8,128)(2,1)} %get-tuple-element.98, bf16[896,2048]{1,0:T(8,128)(2,1)} %slice.300), kind=kOutput, calls=%fused_computation.24 | convolution fusion | flops 5170266112 | bytes 11960320 | tf_op jit(solution)/shard_map/dot_general | solution.py:18
  404.0 10.3 %convolution_convert_fusion.1 = bf16[1408,2048]{1,0:T(8,128)(2,1)} fusion(bf16[896,1408]{1,0:T(8,128)(2,1)} %get-tuple-element.100, bf16[896,2048]{1,0:T(8,128)(2,1)} %slice.300), kind=kOutput, calls=%fused_computation.23 | convolution fusion | flops 5170266112 | bytes 11960320 | tf_op jit(solution)/shard_map/dot_general | solution.py:18
  414.3 10.8 %convolution_convert_fusion = bf16[1408,2048]{1,0:T(8,128)(2,1)} fusion(bf16[896,1408]{1,0:T(8,128)(2,1)} %copy-done.84, bf16[896,2048]{1,0:T(8,128)(2,1)} %constant_dynamic-update-slice_fusion.14, f32[896]{0:T(1024)S(1)} %reduce.8), kind=kOutput, calls=%fused_computation.22 | convolution fusion | flops 5175771136 | bytes 11963904 | tf_op jit(solution)/shard_map/dot_general | solution.py:18
  425.9 8.8 fusion.8
  434.7 10.1 add_convert_fusion
  446.8 13.5 %fusion.4 = f32[640,2048,1]{1,0,2:T(8,128)} fusion(bf16[2048,2,1408]{2,1,0:T(2,128)(2,1)} %param.24, bf16[640,1,1408]{2,0,1:T(8,128)(2,1)S(1)} %bitcast.177, bf16[640,1,1408]{2,0,1:T(8,128)(2,1)S(1)} %bitcast.176), kind=kOutput, calls=%fused_computation.12 | convolution fusion | flops 7383777280 | bytes 20381696 | tf_op jit(solution)/shard_map/tkf,dkf->td/dot_general | solution.py:545
  467.2 8.9 collective-permute-done.26
  476.1 49.4 %collective-permute-done.27 = bf16[112,2048]{1,0:T(8,128)(2,1)S(1)} collective-permute-done((bf16[112,2048]{1,0:T(8,128)(2,1)S(1)}, bf16[112,2048]{1,0:T(8,128)(2,1)S(1)}, u32[]{:S(2)}, u32[]{:S(2)}) %collective-permute-start.27) | collective-permute-done | bytes 458784 | tf_op jit(solution)/shard_map/ppermute | solution.py:84
  531.3 5.2 bitcast_add_fusion
  536.6 7.4 concatenate.63
  554.7 49.6 %collective-permute-done.32 = bf16[640,1152]{1,0:T(8,128)(2,1)S(1)} collective-permute-done((bf16[640,1152]{1,0:T(8,128)(2,1)S(1)}, bf16[640,1152]{1,0:T(8,128)(2,1)S(1)}, u32[]{:S(2)}, u32[]{:S(2)}) %collective-permute-start.32) | collective-permute-done | bytes 1474592 | tf_op jit(solution)/shard_map/ppermute | solution.py:63
  621.7 6.8 convert_bitcast_fusion.2
  647.1 4.4 copy.134.n1t
  651.5 4.6 copy.135.agt
  663.8 198.4 %shard_map.255 = (f32[3,256,512]{2,1,0:T(8,128)}, f32[256,512]{1,0:T(8,128)}, bf16[640,512]{1,0:T(8,128)(2,1)}, f32[1,2048]{1,0:T(1,128)}, f32[1,1536]{1,0:T(1,128)}, /*index=5*/f32[16,2048]{1,0:T(8,128)}) custom-call(bf16[2048,640]{1,0:T(8,128)(2,1)} %copy.134.n1t, bf16[640,1536]{1,0:T(8,128)(2,1)} %pad_maximum_fusion.2.lg, bf16[2048,640]{1,0:T(8,128)(2,1)} %copy.135.agt, ...), custom_call_target="tpu_custom_call" | custom-call | flops 9395240960 | bytes 31457280 | tf_op jit(solution)/shard_map/pallas_call | solution.py:386
  869.2 4.7 convert_bitcast_fusion
  877.2 121.4 %reduce-scatter.8.cloned.1.call-done = bf16[256,4224]{0,1:T(8,128)(2,1)} async-done(((bf16[2048,4224]{0,1:T(8,128)(2,1)}), bf16[256,4224]{0,1:T(8,128)(2,1)}) %reduce-scatter.8.cloned.1.call-update) | async-done | bytes 2162704 | tf_op jit(solution)/shard_map/reduce_scatter | solution.py:556
  1002.5 5.5 copy.137
  (397 shorter events, 187.0 us)
Async XLA Ops:
  7.2 244.4 %all-gather.10.cloned.1.call-start = ((), (), s32[]{:S(2)}) async-start(), calls=%async_computation.12 | async-start | bytes 7208960 | tf_op jit(solution)/shard_map/all_gather | solution.py:471
  11.2 251.2 %all-gather.8.cloned.1.call-start = ((), (), s32[]{:S(2)}) async-start(), calls=%async_computation.11 | async-start | bytes 7208960 | tf_op jit(solution)/shard_map/all_gather | solution.py:470
  11.9 261.2 %all-gather.6.cloned.1.call-start = ((), (), s32[]{:S(2)}) async-start(), calls=%async_computation.5 | async-start | bytes 7208960 | tf_op jit(solution)/shard_map/all_gather | solution.py:472
  47.4 5.1 collective-permute-start
  56.4 51.3 %collective-permute-start.1 = (bf16[640,1024]{1,0:T(8,128)(2,1)S(1)}, bf16[640,1024]{1,0:T(8,128)(2,1)}, u32[]{:S(2)}, u32[]{:S(2)}) collective-permute-start(bf16[640,1024]{1,0:T(8,128)(2,1)S(1)} %add_convert_fusion.5), channel_id=1, source_target_pairs={{0,2},{1,3},{2,0},{3,1},{4,6},{5,7},{6,4},{7,5},{8,10},{9,11},{10,... | collective-permute-start | bytes 3932168 | tf_op jit(solution)/shard_map/ppermute | solution.py:63
  65.7 16.5 %collective-permute-start.17 = (bf16[112,2048]{1,0:T(8,128)(2,1)}, bf16[112,2048]{1,0:T(8,128)(2,1)}, u32[]{:S(2)}, u32[]{:S(2)}) collective-permute-start(bf16[112,2048]{1,0:T(8,128)(2,1)} %get-tuple-element.129), channel_id=1, source_target_pairs={{0,4},{4,8},{8,12},{12,16},{16,20},{20,24},{24,28},{28,0},{1,5},{5... | collective-permute-start | bytes 1376264 | tf_op jit(solution)/shard_map/ppermute | solution.py:84
  67.2 46.0 %collective-permute-start.18 = (bf16[112,2048]{1,0:T(8,128)(2,1)}, bf16[112,2048]{1,0:T(8,128)(2,1)}, u32[]{:S(2)}, u32[]{:S(2)}) collective-permute-start(bf16[112,2048]{1,0:T(8,128)(2,1)} %get-tuple-element.128), channel_id=1, source_target_pairs={{0,8},{4,12},{8,16},{12,20},{16,24},{20,28},{24,0},{28,4},{1,9},{5... | collective-permute-start | bytes 1376264 | tf_op jit(solution)/shard_map/ppermute | solution.py:84
  68.8 51.9 %collective-permute-start.19 = (bf16[112,2048]{1,0:T(8,128)(2,1)}, bf16[112,2048]{1,0:T(8,128)(2,1)}, u32[]{:S(2)}, u32[]{:S(2)}) collective-permute-start(bf16[112,2048]{1,0:T(8,128)(2,1)} %get-tuple-element.127), channel_id=1, source_target_pairs={{0,12},{4,16},{8,20},{12,24},{16,28},{20,0},{24,4},{28,8},{1,13},{... | collective-permute-start | bytes 1376264 | tf_op jit(solution)/shard_map/ppermute | solution.py:84
  71.4 51.1 %collective-permute-start.20 = (bf16[112,2048]{1,0:T(8,128)(2,1)}, bf16[112,2048]{1,0:T(8,128)(2,1)}, u32[]{:S(2)}, u32[]{:S(2)}) collective-permute-start(bf16[112,2048]{1,0:T(8,128)(2,1)} %get-tuple-element.126), channel_id=1, source_target_pairs={{0,16},{4,20},{8,24},{12,28},{16,0},{20,4},{24,8},{28,12},{1,17},{... | collective-permute-start | bytes 1376264 | tf_op jit(solution)/shard_map/ppermute | solution.py:84
  72.6 794.0 %reduce-scatter.6.cloned.1.call-start = ((), (), s32[]{:S(2)}) async-start(), calls=%async_computation.6 | async-start | bytes 3276800 | tf_op jit(solution)/shard_map/reduce_scatter | solution.py:582
  72.7 76.3 %copy-start.74 = (s32[896]{0:T(1024)}, s32[896]{0:T(1024)S(1)}, u32[]{:S(2)}) copy-start(s32[896]{0:T(1024)S(1)} %negate_select_fusion.2) | copy-start | bytes 10756
  82.2 42.1 %collective-permute-start.21 = (bf16[112,2048]{1,0:T(8,128)(2,1)}, bf16[112,2048]{1,0:T(8,128)(2,1)S(1)}, u32[]{:S(2)}, u32[]{:S(2)}) collective-permute-start(bf16[112,2048]{1,0:T(8,128)(2,1)} %get-tuple-element.125), channel_id=1, source_target_pairs={{0,20},{4,24},{8,28},{12,0},{16,4},{20,8},{24,12},{28,16},{1,21},{... | collective-permute-start | bytes 1376264 | tf_op jit(solution)/shard_map/ppermute | solution.py:84
  107.7 32.7 %collective-permute-start.22 = (bf16[112,2048]{1,0:T(8,128)(2,1)}, bf16[112,2048]{1,0:T(8,128)(2,1)S(1)}, u32[]{:S(2)}, u32[]{:S(2)}) collective-permute-start(bf16[112,2048]{1,0:T(8,128)(2,1)} %get-tuple-element.124), channel_id=1, source_target_pairs={{0,24},{4,28},{8,0},{12,4},{16,8},{20,12},{24,16},{28,20},{1,25},{... | collective-permute-start | bytes 1376264 | tf_op jit(solution)/shard_map/ppermute | solution.py:84
  113.2 28.8 %collective-permute-start.2 = (bf16[640,1024]{1,0:T(8,128)(2,1)S(1)}, bf16[640,1024]{1,0:T(8,128)(2,1)S(1)}, u32[]{:S(2)}, u32[]{:S(2)}) collective-permute-start(bf16[640,1024]{1,0:T(8,128)(2,1)S(1)} %add_convert_fusion.4), channel_id=1, source_target_pairs={{0,1},{1,0},{2,3},{3,2},{4,5},{5,4},{6,7},{7,6},{8,9},{9,8},{10,11... | collective-permute-start | bytes 3932168 | tf_op jit(solution)/shard_map/ppermute | solution.py:63
  120.7 20.6 %collective-permute-start.23 = (bf16[112,2048]{1,0:T(8,128)(2,1)S(1)}, bf16[112,2048]{1,0:T(8,128)(2,1)S(1)}, u32[]{:S(2)}, u32[]{:S(2)}) collective-permute-start(bf16[112,2048]{1,0:T(8,128)(2,1)S(1)} %copy-done.49), channel_id=1, source_target_pairs={{0,28},{4,0},{8,4},{12,8},{16,12},{20,16},{24,20},{28,24},{1,29},{... | collective-permute-start | bytes 1376264 | tf_op jit(solution)/shard_map/ppermute | solution.py:84
  156.5 64.5 %collective-permute-start.3 = (bf16[112,2176]{1,0:T(8,128)(2,1)}, bf16[112,2176]{1,0:T(8,128)(2,1)}, u32[]{:S(2)}, u32[]{:S(2)}) collective-permute-start(bf16[112,2176]{1,0:T(8,128)(2,1)} %get-tuple-element.109), channel_id=1, source_target_pairs={{0,4},{4,8},{8,12},{12,16},{16,20},{20,24},{24,28},{28,0},{1,5},{5... | collective-permute-start | bytes 1462280 | tf_op jit(solution)/shard_map/ppermute | solution.py:84
  164.1 59.3 %collective-permute-start.4 = (bf16[112,2176]{1,0:T(8,128)(2,1)}, bf16[112,2176]{1,0:T(8,128)(2,1)}, u32[]{:S(2)}, u32[]{:S(2)}) collective-permute-start(bf16[112,2176]{1,0:T(8,128)(2,1)} %get-tuple-element.110), channel_id=1, source_target_pairs={{0,8},{4,12},{8,16},{12,20},{16,24},{20,28},{24,0},{28,4},{1,9},{5... | collective-permute-start | bytes 1462280 | tf_op jit(solution)/shard_map/ppermute | solution.py:84
  168.3 58.1 %collective-permute-start.5 = (bf16[112,2176]{1,0:T(8,128)(2,1)}, bf16[112,2176]{1,0:T(8,128)(2,1)}, u32[]{:S(2)}, u32[]{:S(2)}) collective-permute-start(bf16[112,2176]{1,0:T(8,128)(2,1)} %get-tuple-element.111), channel_id=1, source_target_pairs={{0,12},{4,16},{8,20},{12,24},{16,28},{20,0},{24,4},{28,8},{1,13},{... | collective-permute-start | bytes 1462280 | tf_op jit(solution)/shard_map/ppermute | solution.py:84
  170.4 57.8 %collective-permute-start.6 = (bf16[112,2176]{1,0:T(8,128)(2,1)}, bf16[112,2176]{1,0:T(8,128)(2,1)S(1)}, u32[]{:S(2)}, u32[]{:S(2)}) collective-permute-start(bf16[112,2176]{1,0:T(8,128)(2,1)} %get-tuple-element.112), channel_id=1, source_target_pairs={{0,16},{4,20},{8,24},{12,28},{16,0},{20,4},{24,8},{28,12},{1,17},{... | collective-permute-start | bytes 1462280 | tf_op jit(solution)/shard_map/ppermute | solution.py:84
  171.7 57.4 %collective-permute-start.7 = (bf16[112,2176]{1,0:T(8,128)(2,1)}, bf16[112,2176]{1,0:T(8,128)(2,1)S(1)}, u32[]{:S(2)}, u32[]{:S(2)}) collective-permute-start(bf16[112,2176]{1,0:T(8,128)(2,1)} %get-tuple-element.113), channel_id=1, source_target_pairs={{0,20},{4,24},{8,28},{12,0},{16,4},{20,8},{24,12},{28,16},{1,21},{... | collective-permute-start | bytes 1462280 | tf_op jit(solution)/shard_map/ppermute | solution.py:84
  221.1 23.0 %collective-permute-start.8 = (bf16[112,2176]{1,0:T(8,128)(2,1)}, bf16[112,2176]{1,0:T(8,128)(2,1)S(1)}, u32[]{:S(2)}, u32[]{:S(2)}) collective-permute-start(bf16[112,2176]{1,0:T(8,128)(2,1)} %get-tuple-element.114), channel_id=1, source_target_pairs={{0,24},{4,28},{8,0},{12,4},{16,8},{20,12},{24,16},{28,20},{1,25},{... | collective-permute-start | bytes 1462280 | tf_op jit(solution)/shard_map/ppermute | solution.py:84
  223.5 21.4 %collective-permute-start.9 = (bf16[112,2176]{1,0:T(8,128)(2,1)}, bf16[112,2176]{1,0:T(8,128)(2,1)S(1)}, u32[]{:S(2)}, u32[]{:S(2)}) collective-permute-start(bf16[112,2176]{1,0:T(8,128)(2,1)} %get-tuple-element.107), channel_id=1, source_target_pairs={{0,28},{4,0},{8,4},{12,8},{16,12},{20,16},{24,20},{28,24},{1,29},{... | collective-permute-start | bytes 1462280 | tf_op jit(solution)/shard_map/ppermute | solution.py:84
  294.7 23.6 %collective-permute-start.10 = (bf16[112,2048]{1,0:T(8,128)(2,1)S(1)}, bf16[112,2048]{1,0:T(8,128)(2,1)S(1)}, u32[]{:S(2)}, u32[]{:S(2)}) collective-permute-start(bf16[112,2048]{1,0:T(8,128)(2,1)S(1)} %get-tuple-element.137), channel_id=1, source_target_pairs={{0,28},{4,0},{8,4},{12,8},{16,12},{20,16},{24,20},{28,24},{1,29},{... | collective-permute-start | bytes 1376264 | tf_op jit(solution)/shard_map/ppermute | solution.py:84
  306.3 21.1 %collective-permute-start.11 = (bf16[112,2048]{1,0:T(8,128)(2,1)S(1)}, bf16[112,2048]{1,0:T(8,128)(2,1)S(1)}, u32[]{:S(2)}, u32[]{:S(2)}) collective-permute-start(bf16[112,2048]{1,0:T(8,128)(2,1)S(1)} %get-tuple-element.136), channel_id=1, source_target_pairs={{0,24},{4,28},{8,0},{12,4},{16,8},{20,12},{24,16},{28,20},{1,25},{... | collective-permute-start | bytes 1376264 | tf_op jit(solution)/shard_map/ppermute | solution.py:84
  313.0 24.1 %collective-permute-start.12 = (bf16[112,2048]{1,0:T(8,128)(2,1)S(1)}, bf16[112,2048]{1,0:T(8,128)(2,1)S(1)}, u32[]{:S(2)}, u32[]{:S(2)}) collective-permute-start(bf16[112,2048]{1,0:T(8,128)(2,1)S(1)} %get-tuple-element.135), channel_id=1, source_target_pairs={{0,20},{4,24},{8,28},{12,0},{16,4},{20,8},{24,12},{28,16},{1,21},{... | collective-permute-start | bytes 1376264 | tf_op jit(solution)/shard_map/ppermute | solution.py:84
  314.0 72.5 %collective-permute-start.13 = (bf16[112,2048]{1,0:T(8,128)(2,1)S(1)}, bf16[112,2048]{1,0:T(8,128)(2,1)S(1)}, u32[]{:S(2)}, u32[]{:S(2)}) collective-permute-start(bf16[112,2048]{1,0:T(8,128)(2,1)S(1)} %get-tuple-element.134), channel_id=1, source_target_pairs={{0,16},{4,20},{8,24},{12,28},{16,0},{20,4},{24,8},{28,12},{1,17},{... | collective-permute-start | bytes 1376264 | tf_op jit(solution)/shard_map/ppermute | solution.py:84
  316.5 70.0 %collective-permute-start.14 = (bf16[112,2048]{1,0:T(8,128)(2,1)S(1)}, bf16[112,2048]{1,0:T(8,128)(2,1)S(1)}, u32[]{:S(2)}, u32[]{:S(2)}) collective-permute-start(bf16[112,2048]{1,0:T(8,128)(2,1)S(1)} %get-tuple-element.133), channel_id=1, source_target_pairs={{0,12},{4,16},{8,20},{12,24},{16,28},{20,0},{24,4},{28,8},{1,13},{... | collective-permute-start | bytes 1376264 | tf_op jit(solution)/shard_map/ppermute | solution.py:84
  318.3 68.3 %collective-permute-start.15 = (bf16[112,2048]{1,0:T(8,128)(2,1)S(1)}, bf16[112,2048]{1,0:T(8,128)(2,1)S(1)}, u32[]{:S(2)}, u32[]{:S(2)}) collective-permute-start(bf16[112,2048]{1,0:T(8,128)(2,1)S(1)} %get-tuple-element.132), channel_id=1, source_target_pairs={{0,8},{4,12},{8,16},{12,20},{16,24},{20,28},{24,0},{28,4},{1,9},{5... | collective-permute-start | bytes 1376264 | tf_op jit(solution)/shard_map/ppermute | solution.py:84
  327.4 59.2 %collective-permute-start.16 = (bf16[112,2048]{1,0:T(8,128)(2,1)S(1)}, bf16[112,2048]{1,0:T(8,128)(2,1)S(1)}, u32[]{:S(2)}, u32[]{:S(2)}) collective-permute-start(bf16[112,2048]{1,0:T(8,128)(2,1)S(1)} %get-tuple-element.131), channel_id=1, source_target_pairs={{0,4},{4,8},{8,12},{12,16},{16,20},{20,24},{24,28},{28,0},{1,5},{5... | collective-permute-start | bytes 1376264 | tf_op jit(solution)/shard_map/ppermute | solution.py:84
  393.5 475.7 %reduce-scatter.10.cloned.1.call-start = ((), (), s32[]{:S(2)}) async-start(), calls=%async_computation.8 | async-start | bytes 7208960 | tf_op jit(solution)/shard_map/reduce_scatter | solution.py:573
  403.9 465.3 %reduce-scatter.12.cloned.1.call-start = ((), (), s32[]{:S(2)}) async-start(), calls=%async_computation.9 | async-start | bytes 7208960 | tf_op jit(solution)/shard_map/reduce_scatter | solution.py:574
  414.3 459.7 %reduce-scatter.14.cloned.1.call-start = ((), (), s32[]{:S(2)}) async-start(), calls=%async_computation.10 | async-start | bytes 7208960 | tf_op jit(solution)/shard_map/reduce_scatter | solution.py:572
  425.1 573.4 %reduce-scatter.8.cloned.1.call-start = ((), (), s32[]{:S(2)}) async-start(), calls=%async_computation.7 | async-start | bytes 19464192 | tf_op jit(solution)/shard_map/reduce_scatter | solution.py:556
  445.3 18.2 %collective-permute-start.24 = (bf16[112,2048]{1,0:T(8,128)(2,1)S(1)}, bf16[112,2048]{1,0:T(8,128)(2,1)S(1)}, u32[]{:S(2)}, u32[]{:S(2)}) collective-permute-start(bf16[112,2048]{1,0:T(8,128)(2,1)S(1)} %get-tuple-element.121), channel_id=1, source_target_pairs={{0,28},{4,0},{8,4},{12,8},{16,12},{20,16},{24,20},{28,24},{1,29},{... | collective-permute-start | bytes 1376264 | tf_op jit(solution)/shard_map/ppermute | solution.py:84
  445.4 20.8 %collective-permute-start.25 = (bf16[112,2048]{1,0:T(8,128)(2,1)S(1)}, bf16[112,2048]{1,0:T(8,128)(2,1)S(1)}, u32[]{:S(2)}, u32[]{:S(2)}) collective-permute-start(bf16[112,2048]{1,0:T(8,128)(2,1)S(1)} %get-tuple-element.120), channel_id=1, source_target_pairs={{0,24},{4,28},{8,0},{12,4},{16,8},{20,12},{24,16},{28,20},{1,25},{... | collective-permute-start | bytes 1376264 | tf_op jit(solution)/shard_map/ppermute | solution.py:84
  446.8 78.7 %copy-start.32 = (bf16[896,2048]{1,0:T(8,128)(2,1)S(1)}, bf16[896,2048]{1,0:T(8,128)(2,1)}, u32[]{:S(2)}) copy-start(bf16[896,2048]{1,0:T(8,128)(2,1)} %copy-done.31) | copy-start | bytes 11010052
  460.4 65.2 %copy-start.17 = (bf16[896,2048]{1,0:T(8,128)(2,1)S(1)}, bf16[896,2048]{1,0:T(8,128)(2,1)}, u32[]{:S(2)}) copy-start(bf16[896,2048]{1,0:T(8,128)(2,1)} %copy-done.16) | copy-start | bytes 11010052
  460.5 15.5 %collective-permute-start.26 = (bf16[112,2048]{1,0:T(8,128)(2,1)S(1)}, bf16[112,2048]{1,0:T(8,128)(2,1)S(1)}, u32[]{:S(2)}, u32[]{:S(2)}) collective-permute-start(bf16[112,2048]{1,0:T(8,128)(2,1)S(1)} %get-tuple-element.119), channel_id=1, source_target_pairs={{0,20},{4,24},{8,28},{12,0},{16,4},{20,8},{24,12},{28,16},{1,21},{... | collective-permute-start | bytes 1376264 | tf_op jit(solution)/shard_map/ppermute | solution.py:84
  460.6 65.0 %collective-permute-start.27 = (bf16[112,2048]{1,0:T(8,128)(2,1)S(1)}, bf16[112,2048]{1,0:T(8,128)(2,1)S(1)}, u32[]{:S(2)}, u32[]{:S(2)}) collective-permute-start(bf16[112,2048]{1,0:T(8,128)(2,1)S(1)} %get-tuple-element.118), channel_id=1, source_target_pairs={{0,16},{4,20},{8,24},{12,28},{16,0},{20,4},{24,8},{28,12},{1,17},{... | collective-permute-start | bytes 1376264 | tf_op jit(solution)/shard_map/ppermute | solution.py:84
  462.6 67.5 %collective-permute-start.28 = (bf16[112,2048]{1,0:T(8,128)(2,1)S(1)}, bf16[112,2048]{1,0:T(8,128)(2,1)S(1)}, u32[]{:S(2)}, u32[]{:S(2)}) collective-permute-start(bf16[112,2048]{1,0:T(8,128)(2,1)S(1)} %get-tuple-element.117), channel_id=1, source_target_pairs={{0,12},{4,16},{8,20},{12,24},{16,28},{20,0},{24,4},{28,8},{1,13},{... | collective-permute-start | bytes 1376264 | tf_op jit(solution)/shard_map/ppermute | solution.py:84
  463.5 67.7 %collective-permute-start.29 = (bf16[112,2048]{1,0:T(8,128)(2,1)S(1)}, bf16[112,2048]{1,0:T(8,128)(2,1)S(1)}, u32[]{:S(2)}, u32[]{:S(2)}) collective-permute-start(bf16[112,2048]{1,0:T(8,128)(2,1)S(1)} %get-tuple-element.116), channel_id=1, source_target_pairs={{0,8},{4,12},{8,16},{12,20},{16,24},{20,28},{24,0},{28,4},{1,9},{5... | collective-permute-start | bytes 1376264 | tf_op jit(solution)/shard_map/ppermute | solution.py:84
  466.2 65.0 %collective-permute-start.30 = (bf16[112,2048]{1,0:T(8,128)(2,1)S(1)}, bf16[112,2048]{1,0:T(8,128)(2,1)S(1)}, u32[]{:S(2)}, u32[]{:S(2)}) collective-permute-start(bf16[112,2048]{1,0:T(8,128)(2,1)S(1)} %get-tuple-element.115), channel_id=1, source_target_pairs={{0,4},{4,8},{8,12},{12,16},{16,20},{20,24},{24,28},{28,0},{1,5},{5... | collective-permute-start | bytes 1376264 | tf_op jit(solution)/shard_map/ppermute | solution.py:84
  547.0 3.3 collective-permute-start.31
  553.6 52.3 %copy-start.69 = (bf16[2048]{0:T(1024)(128)(2,1)S(1)}, bf16[2048]{0:T(1024)(128)(2,1)}, u32[]{:S(2)}) copy-start(bf16[2048]{0:T(1024)(128)(2,1)} %param.23) | copy-start | bytes 12292
  553.6 53.4 %copy-start.62 = (f32[640]{0:T(1024)S(1)}, f32[640]{0:T(1024)}, u32[]{:S(2)}) copy-start(f32[640]{0:T(1024)} %copy-done.61) | copy-start | bytes 7684
  553.6 54.3 %copy-start.71 = (f32[2048]{0:T(1024)S(1)}, f32[2048]{0:T(1024)}, u32[]{:S(2)}) copy-start(f32[2048]{0:T(1024)} %param.17) | copy-start | bytes 24580
  553.6 50.8 %collective-permute-start.32 = (bf16[640,1152]{1,0:T(8,128)(2,1)S(1)}, bf16[640,1152]{1,0:T(8,128)(2,1)S(1)}, u32[]{:S(2)}, u32[]{:S(2)}) collective-permute-start(bf16[640,1152]{1,0:T(8,128)(2,1)S(1)} %add_convert_fusion.3), channel_id=1, source_target_pairs={{0,2},{1,3},{2,0},{3,1},{4,6},{5,7},{6,4},{7,5},{8,10},{9,11},{10,... | collective-permute-start | bytes 4423688 | tf_op jit(solution)/shard_map/ppermute | solution.py:63
  605.9 4.8 collective-permute-start.33
  (86 other events, 521.3 us)
Sparse Core Ops, SparseCore 0:
  11.3 46.0 all-gather.9
  59.5 61.3 all-gather.7
  122.5 44.8 all-gather.5
  393.6 31.8 reduce-scatter.5
  428.1 54.8 reduce-scatter.9
  486.0 54.8 reduce-scatter.11
  543.6 76.8 reduce-scatter.13
  624.4 374.1 reduce-scatter.7

commit v3 on v2

--- a/solution.py
+++ b/solution.py
@@ -75,6 +75,19 @@
     return jnp.concatenate([jnp.where(low, two, other), jnp.where(low, other, two)], axis=1).astype(F32)
 
 
+def tp_scatter(x, n):
+    me = lax.axis_index("tp")
+    cols = x.shape[1] // n
+
+    def block(bits):
+        return lax.dynamic_slice_in_dim(x, (me ^ bits) * cols, cols, 1)
+
+    one = swap(jnp.concatenate([block(1), block(3)], axis=0).astype(BF), 1, n).astype(F32)
+    rows = x.shape[0]
+    two = swap((block(2) + one[rows:]).astype(BF), 2, n)
+    return block(0) + one[:rows] + two.astype(F32)
+
+
 def exchange(x, n, back=False):
     rows = x.shape[0] // n
     out = [x[:rows]]
@@ -130,9 +143,9 @@
 def tail_kernel(
     n,
     n_tp,
-    n1t,
+    n1,
     lg,
-    agt,
+    ag,
     ctx,
     w,
     h_cols,
@@ -176,8 +189,8 @@
     ep = lax.axis_index("ep")
     tp = lax.axis_index("tp")
     tokens, lw = ctx.shape
-    rows = n1t.shape[0] // n
-    width = n1t.shape[0]
+    rows = qkv_out.shape[1]
+    width = rows * n
     p = ring_place(ep, n)
     nxt = ring_member(lax.rem(p + 1, n), n)
     prv = ring_member(lax.rem(p + n - 1, n), n)
@@ -202,11 +215,10 @@
         return ring_member(lax.rem(p + 1 + step, n), n)
 
     def term(ring, owner):
-        at = pl.ds(pl.multiple_of(owner * rows, rows), rows)
         if ring == 1:
-            return jnp.dot(agt[at, :], ctx[...], preferred_element_type=F32)
+            return block_dot(ag, owner, rows, ctx[...])
         k = {0: 0, 2: 1, 3: 2}[ring]
-        return jnp.dot(n1t[at, :], lg[:, k * lw : (k + 1) * lw], preferred_element_type=F32)
+        return block_dot(n1, owner, rows, lg[:, k * lw : (k + 1) * lw])
 
     def ring_copy(ring, step, slot):
         return remote(
@@ -376,10 +388,12 @@
             ring_copy(ring, step, step % 2).wait_send()
 
 
-def tail(n, n_tp, n1t, lg, agt, ctx, w, h_cols, r_one, gain, mid_cols, bias, small):
-    width, tokens = n1t.shape
+def tail(n, n_tp, n1, lg, ag, ctx, w, h_cols, r_one, gain, mid_cols, bias, small):
+    tokens, width = n1.shape
     lw = ctx.shape[1]
     rows = width // n
+    if rows % 128:
+        n1, ag = n1.T, ag.T
     wide = small.shape[0]
     vmem = pl.BlockSpec(memory_space=pltpu.VMEM)
     dma = pltpu.SemaphoreType.DMA
@@ -428,7 +442,710 @@
         cost_estimate=pl.CostEstimate(
             flops=2 * tokens * width * 7 * lw, bytes_accessed=30 * 2**20, transcendentals=0
         ),
-    )(n1t, lg, agt, ctx, w, h_cols, r_one, gain, mid_cols, bias, small)
+    )(n1, lg, ag, ctx, w, h_cols, r_one, gain, mid_cols, bias, small)
+
+def cols_of(ref, owner, rows):
+    at = pl.ds(pl.multiple_of(owner * rows, rows), rows)
+    return ref[:, at] if rows % 128 == 0 else ref[at, :]
+
+
+def block_dot(ref, owner, rows, other):
+    dims = (((0,), (0,)), ((), ())) if rows % 128 == 0 else (((1,), (0,)), ((), ()))
+    return lax.dot_general(cols_of(ref, owner, rows), other, dims, preferred_element_type=F32)
+
+
+def middle_kernel(
+    n,
+    n_tp,
+    capp,
+    x_hbm,
+    u_hbm,
+    gu_a,
+    gu_c,
+    gu_b,
+    gu_own,
+    dn_a,
+    dn_c,
+    dn_b,
+    dn_own,
+    nt,
+    pg,
+    back,
+    o_hbm,
+    rg_hbm,
+    e_hbm,
+    gu_out,
+    w,
+    xb,
+    ub,
+    rgb,
+    ob,
+    eb,
+    rbs,
+    ring_recv,
+    ring_send,
+    w_sem,
+    x_sem,
+    u_sem,
+    out_sem,
+    ring_ss,
+    ring_rs,
+    back_ss,
+    back_rs,
+):
+    ep = lax.axis_index("ep")
+    gr = xb.shape[1]
+    width = u_hbm.shape[1]
+    units = w.shape[1]
+    quarter = units // 4
+    groups = x_hbm.shape[0] // gr
+    per = n // groups
+    rows = gu_out.shape[1]
+    half = ring_recv.shape[3]
+    p = ring_place(ep, n)
+    nxt = ring_member(lax.rem(p + 1, n), n)
+    prv = ring_member(lax.rem(p + n - 1, n), n)
+
+    w_in = [
+        pltpu.make_async_copy(ref, w.at[:2, i * quarter : (i + 1) * quarter, :], w_sem.at[i])
+        for i, ref in enumerate((gu_a, gu_c, gu_b, gu_own))
+    ] + [
+        pltpu.make_async_copy(ref, w.at[2, i * quarter : (i + 1) * quarter, :], w_sem.at[4 + i])
+        for i, ref in enumerate((dn_a, dn_c, dn_b, dn_own))
+    ]
+    for copy in w_in:
+        copy.start()
+
+    def x_copy(g):
+        at = pl.ds(pl.multiple_of(g * gr, gr), gr)
+        slot = lax.rem(g, 2)
+        return pltpu.make_async_copy(x_hbm.at[at, :], xb.at[slot], x_sem.at[slot])
+
+    def u_copy(g):
+        at = pl.ds(pl.multiple_of(g * gr, gr), gr)
+        slot = lax.rem(g, 2)
+        return pltpu.make_async_copy(u_hbm.at[at, :], ub.at[slot], u_sem.at[slot])
+
+    x_copy(0).start()
+    u_copy(0).start()
+
+    barrier = pltpu.get_barrier_semaphore()
+    for shift in range(1, n):
+        pl.semaphore_signal(
+            barrier, 1, device_id={"ep": lax.rem(ep + shift, n)}, device_id_type=pl.DeviceIdType.MESH
+        )
+    pl.semaphore_wait(barrier, n - 1)
+
+    piece = [(0, half), (half, units), (units, units + half), (units + half, 2 * units)]
+
+    def block_of(ring, step):
+        if ring < 2:
+            return ring_member(lax.rem(p + 2 * n - 1 - step, n), n)
+        return ring_member(lax.rem(p + 1 + step, n), n)
+
+    def term(ring, owner):
+        lo, hi = piece[ring]
+        return block_dot(nt, owner, rows, pg[:, lo:hi])
+
+    def ring_copy(ring, step, slot):
+        lo, hi = piece[ring]
+        return remote(
+            ring_send.at[ring, slot, :, : hi - lo],
+            ring_recv.at[ring, step, :, : hi - lo],
+            ring_ss.at[ring, slot],
+            ring_rs.at[ring, step],
+            "ep",
+            nxt if ring < 2 else prv,
+        )
+
+    def ring_step(step):
+        slot = lax.rem(step, 2)
+        for ring in (0, 2, 1, 3):
+            lo, hi = piece[ring]
+            mine = term(ring, block_of(ring, step))
+            ring_copy(ring, step - 1, slot).wait_recv()
+
+            @pl.when(step >= 2)
+            def _():
+                ring_copy(ring, step - 2, slot).wait_send()
+
+            ring_send[ring, slot, :, : hi - lo] = (
+                mine + ring_recv[ring, step - 1, :, : hi - lo].astype(F32)
+            ).astype(BF)
+            ring_copy(ring, step, slot).start()
+
+    for ring in (0, 2, 1, 3):
+        lo, hi = piece[ring]
+        ring_send[ring, 0, :, : hi - lo] = term(ring, block_of(ring, 0)).astype(BF)
+        ring_copy(ring, 0, 0).start()
+
+    for copy in w_in:
+        copy.wait()
+
+    nt_dims = (((1,), (1,)), ((), ()))
+
+    def saved(g):
+        at = pl.ds(pl.multiple_of(g * gr, gr), gr)
+        return (
+            pltpu.make_async_copy(rgb, rg_hbm.at[at, :], out_sem.at[0]),
+            pltpu.make_async_copy(ob, o_hbm.at[at, :], out_sem.at[1]),
+            pltpu.make_async_copy(eb, e_hbm.at[:, at, :], out_sem.at[2]),
+        )
+
+    def back_copy(r):
+        at = pl.ds(pl.multiple_of(r * capp, capp), capp)
+        return remote(
+            rbs.at[at, :], back.at[at, :], back_ss.at[r], back_rs.at[r], "ep", lax.rem(ep + n - r, n)
+        )
+
+    kept_copy = pltpu.make_async_copy(rbs.at[:capp, :], back.at[:capp, :], back_ss.at[0])
+
+    @pl.loop(0, groups)
+    def _(g):
+        slot = lax.rem(g, 2)
+
+        @pl.when(g + 1 < groups)
+        def _():
+            x_copy(g + 1).start()
+            u_copy(g + 1).start()
+
+        x_copy(g).wait()
+        u_copy(g).wait()
+
+        @pl.when(g >= 1)
+        def _():
+            for copy in saved(g - 1):
+                copy.wait()
+
+        gate = xb[slot, :, width : width + 1].astype(F32) + xb[slot, :, width + 1 : width + 2].astype(F32)
+        rgb[...] = (gate * ub[slot].astype(F32)).astype(BF)
+
+        def hidden(at):
+            x = xb[slot, :, :width]
+            g_pre = lax.dot_general(x, w[0, at, :], nt_dims, preferred_element_type=F32)
+            u_pre = lax.dot_general(x, w[1, at, :], nt_dims, preferred_element_type=F32)
+            grad = lax.dot_general(rgb[...], w[2, at, :], nt_dims, preferred_element_type=F32)
+            sig = jax.nn.sigmoid(g_pre)
+            eb[0, :, at] = (g_pre * sig * u_pre).astype(BF)
+            eb[1, :, at] = (grad * u_pre * sig * (1.0 + g_pre * (1.0 - sig))).astype(BF)
+            eb[2, :, at] = (grad * g_pre * sig).astype(BF)
+
+        @pl.loop(0, units // 256)
+        def _(c):
+            hidden(pl.ds(pl.multiple_of(c * 256, 256), 256))
+
+        if units % 256:
+            hidden(pl.ds(units // 256 * 256, units % 256))
+
+        def columns(c, total):
+            at = pl.ds(pl.multiple_of(c * 256, 256), 256)
+            out = jnp.dot(eb[0], w[2, :, at], preferred_element_type=F32)
+            ob[:, at] = out.astype(BF)
+            grad = jnp.dot(eb[1], w[0, :, at], preferred_element_type=F32) + jnp.dot(
+                eb[2], w[1, :, at], preferred_element_type=F32
+            )
+            rbs[pl.ds(pl.multiple_of(g * gr, gr), gr), at] = grad.astype(BF)
+            return total + jnp.sum(out * ub[slot, :, at].astype(F32), axis=1, keepdims=True)
+
+        total = lax.fori_loop(0, width // 256, columns, jnp.zeros((gr, 1), F32))
+        hi = total.astype(BF).astype(F32)
+        lane = lax.broadcasted_iota(jnp.int32, (gr, 128), 1)
+        rbs[pl.ds(pl.multiple_of(g * gr, gr), gr), width:] = jnp.where(
+            lane == 0, hi, jnp.where(lane == 1, total - hi, 0.0)
+        ).astype(BF)
+        for copy in saved(g):
+            copy.start()
+        for i in range(per):
+            r = g * per + i
+            if i == 0:
+
+                @pl.when(g == 0)
+                def _():
+                    kept_copy.start()
+
+                @pl.when(g > 0)
+                def _():
+                    back_copy(r).start()
+            else:
+                back_copy(r).start()
+        ring_step(g + 1)
+
+    for copy in saved(groups - 1):
+        copy.wait()
+
+    @pl.loop(groups + 1, n - 1)
+    def _(step):
+        ring_step(step)
+
+    for ring in (0, 2, 1, 3):
+        lo, hi = piece[ring]
+        mine = term(ring, ep)
+        ring_copy(ring, n - 2, 0).wait_recv()
+        base = (ring // 2) * units
+        gu_out[ring // 2, :, lo - base : hi - base] = mine + ring_recv[
+            ring, n - 2, :, : hi - lo
+        ].astype(F32)
+    for ring in range(4):
+        for step in (n - 3, n - 2):
+            ring_copy(ring, step, step % 2).wait_send()
+    kept_copy.wait()
+
+    @pl.loop(1, n)
+    def _(r):
+        back_copy(r).wait()
+
+
+def routed_expert(n, n_tp, capp, x, u, weights, nt, pg):
+    total, wide = x.shape
+    width = u.shape[1]
+    units = 4 * weights[-1].shape[0]
+    gr = total // 4
+    rows = width // n
+    half = (units // 128 + 1) // 2 * 128
+    vmem = pl.BlockSpec(memory_space=pltpu.VMEM)
+    hbm = pl.BlockSpec(memory_space=pl.ANY)
+    dma = pltpu.SemaphoreType.DMA
+    if rows % 128:
+        nt = nt.T
+    return pl.pallas_call(
+        functools.partial(middle_kernel, n, n_tp, capp),
+        out_shape=(
+            jax.ShapeDtypeStruct((total, wide), BF),
+            jax.ShapeDtypeStruct((total, width), BF),
+            jax.ShapeDtypeStruct((total, width), BF),
+            jax.ShapeDtypeStruct((3, total, units), BF),
+            jax.ShapeDtypeStruct((2, rows, units), F32),
+        ),
+        in_specs=[hbm] * 10 + [vmem] * 2,
+        out_specs=[hbm] * 4 + [vmem],
+        scratch_shapes=[
+            pltpu.VMEM((3, units, width), BF),
+            pltpu.VMEM((2, gr, wide), BF),
+            pltpu.VMEM((2, gr, width), BF),
+            pltpu.VMEM((gr, width), BF),
+            pltpu.VMEM((gr, width), BF),
+            pltpu.VMEM((3, gr, units), BF),
+            pltpu.VMEM((total, wide), BF),
+            pltpu.VMEM((4, n - 1, rows, half), BF),
+            pltpu.VMEM((4, 2, rows, half), BF),
+            dma((8,)),
+            dma((2,)),
+            dma((2,)),
+            dma((3,)),
+            dma((4, 2)),
+            dma((4, n - 1)),
+            dma((n,)),
+            dma((n,)),
+        ],
+        compiler_params=pltpu.CompilerParams(
+            collective_id=1, has_side_effects=True, vmem_limit_bytes=60 * 2**20
+        ),
+        cost_estimate=pl.CostEstimate(
+            flops=2 * total * width * 6 * units, bytes_accessed=40 * 2**20, transcendentals=0
+        ),
+    )(x, u, *weights, nt, pg)
+
+def front_kernel(
+    n,
+    n_tp,
+    capp,
+    hidden,
+    gain1,
+    gain2,
+    w,
+    bias,
+    cosine,
+    sine,
+    prefix,
+    ow,
+    up_sent,
+    gu_own,
+    dn_own,
+    up_rows,
+    gu_a,
+    dn_a,
+    dn_b,
+    n1,
+    qkv,
+    ctx,
+    mid,
+    nt,
+    core_send,
+    core_recv,
+    y_send,
+    y_recv,
+    summed,
+    up_ss,
+    up_rs,
+    w_ss,
+    w_rs,
+    core_ss,
+    core_rs,
+    y_ss,
+    y_rs,
+    g_ss,
+    g_rs,
+):
+    ep = lax.axis_index("ep")
+    tp = lax.axis_index("tp")
+    tokens, width = hidden.shape
+    lw = ctx.shape[1]
+    heads = lw // HEAD_DIM
+    core_peer, y_peer = flip(tp, 1), flip(tp, 2)
+    greet(n, n_tp, ep, tp)
+
+    def up_copy(r, way):
+        to = lax.rem(ep + r, n) if way == "out" else lax.rem(ep + n - r, n)
+        at = pl.ds(r * capp, capp)
+        return remote(up_sent.at[at, :], up_rows.at[at, :], up_ss.at[r], up_rs.at[r], "ep", to)
+
+    for r in range(1, n):
+        up_copy(r, "out").start()
+    kept = pltpu.make_async_copy(up_sent.at[:capp, :], up_rows.at[:capp, :], up_ss.at[0])
+    kept.start()
+    w_copies = [
+        remote(dn_own, dn_b, w_ss.at[0], w_rs.at[0], "tp", y_peer),
+        remote(dn_own, dn_a, w_ss.at[1], w_rs.at[1], "tp", core_peer),
+        remote(gu_own, gu_a, w_ss.at[2], w_rs.at[2], "tp", core_peer),
+    ]
+    for copy in w_copies:
+        copy.start()
+
+    @pl.loop(0, tokens // 64)
+    def _(m):
+        at = pl.ds(pl.multiple_of(m * 64, 64), 64)
+        h = hidden[at, :].astype(F32)
+        factor = lax.rsqrt(jnp.sum(h * h, axis=1, keepdims=True) * (1.0 / width) + EPSILON)
+        n1[at, :] = (h * factor * gain1[...]).astype(BF)
+
+    for k in range(3):
+
+        @pl.loop(0, lw // 256)
+        def _(c, k=k):
+            at = pl.ds(pl.multiple_of(c * 256, 256), 256)
+            x = jnp.dot(n1[...], w[k, :, at], preferred_element_type=F32) + bias[k : k + 1, at]
+            if k < 2:
+                x = jnp.concatenate(
+                    [
+                        x[:, i * HEAD_DIM : (i + 1) * HEAD_DIM] * cosine[...]
+                        + pltpu.roll(x[:, i * HEAD_DIM : (i + 1) * HEAD_DIM], HEAD_DIM // 2, 1) * sine[...]
+                        for i in range(256 // HEAD_DIM)
+                    ],
+                    axis=1,
+                )
+            qkv[k, :, at] = x.astype(BF)
+
+    @pl.loop(0, tokens // 128)
+    def _(m):
+        at = pl.ds(pl.multiple_of(m * 128, 128), 128)
+        row = lax.broadcasted_iota(jnp.int32, (128, tokens), 0) + m * 128
+        col = lax.broadcasted_iota(jnp.int32, (128, tokens), 1)
+        visible = (col <= row) | (col < prefix[...])
+        for i in range(heads):
+            lanes = slice(i * HEAD_DIM, (i + 1) * HEAD_DIM)
+            s = lax.dot_general(
+                qkv[0, at, lanes], qkv[1, :, lanes], (((1,), (1,)), ((), ())), preferred_element_type=F32
+            )
+            s = jnp.where(visible, s * HEAD_DIM ** (-0.5), -1e30)
+            e = jnp.exp(s - jnp.max(s, axis=1, keepdims=True))
+            e = e * (1.0 / jnp.sum(e, axis=1, keepdims=True))
+            ctx[at, lanes] = jnp.dot(
+                e.astype(BF), qkv[2, :, lanes], preferred_element_type=F32
+            ).astype(BF)
+
+    pieces = 4
+    half = width // 2
+    size = half // pieces
+    mine, theirs = (tp % 2) * half, (core_peer % 2) * half
+
+    def project(base, i):
+        at = pl.ds(pl.multiple_of(base + i * size, size), size)
+        return lax.dot_general(
+            ctx[...], ow[at, :], (((1,), (1,)), ((), ())), preferred_element_type=F32
+        )
+
+    def core_copy(i):
+        return remote(
+            core_send.at[i], core_recv.at[i], core_ss.at[i], core_rs.at[i], "tp", core_peer
+        )
+
+    def y_copy(i):
+        return remote(y_send.at[i], y_recv.at[i], y_ss.at[i], y_rs.at[i], "tp", y_peer)
+
+    def gather_copy(i, way):
+        slot = (tp % 2) if way == "out" else (core_peer % 2)
+        return remote(
+            summed.at[slot, i], summed.at[slot, i], g_ss.at[i], g_rs.at[i], "tp", core_peer
+        )
+
+    for i in range(pieces):
+        core_send[i] = project(theirs, i).astype(BF)
+        core_copy(i).start()
+    for i in range(pieces):
+        own = project(mine, i)
+        core_copy(i).wait_recv()
+        y_send[i] = (own + core_recv[i].astype(F32)).astype(BF)
+        y_copy(i).start()
+    for i in range(pieces):
+        y_copy(i).wait_recv()
+        summed[tp % 2, i] = (y_send[i].astype(F32) + y_recv[i].astype(F32)).astype(BF)
+        gather_copy(i, "out").start()
+    for i in range(pieces):
+        gather_copy(i, "in").wait_recv()
+
+    @pl.loop(0, tokens // 32)
+    def _(m):
+        at = pl.ds(pl.multiple_of(m * 32, 32), 32)
+        total = jnp.zeros((32, 1), F32)
+        for j in range(2):
+            for i in range(pieces):
+                lanes = slice(j * half + i * size, j * half + (i + 1) * size)
+                x = hidden[at, lanes].astype(F32) + summed[j, i, at, :].astype(F32)
+                mid[at, lanes] = x
+                total = total + jnp.sum(x * x, axis=1, keepdims=True)
+        factor = lax.rsqrt(total * (1.0 / width) + EPSILON)
+        nt[at, :] = (mid[at, :] * factor * gain2[...]).astype(BF)
+
+    for i in range(pieces):
+        core_copy(i).wait_send()
+        y_copy(i).wait_send()
+        gather_copy(i, "out").wait_send()
+    for copy in w_copies:
+        copy.wait()
+    kept.wait()
+    for r in range(1, n):
+        up_copy(r, "in").wait()
+
+
+def front(n, n_tp, capp, hidden, gain1, gain2, w, bias, cosine, sine, prefix, ow, up_sent, gu_own, dn_own):
+    tokens, width = hidden.shape
+    lw = ow.shape[1]
+    quarter = dn_own.shape[0]
+    vmem = pl.BlockSpec(memory_space=pltpu.VMEM)
+    hbm = pl.BlockSpec(memory_space=pl.ANY)
+    dma = pltpu.SemaphoreType.DMA
+    return pl.pallas_call(
+        functools.partial(front_kernel, n, n_tp, capp),
+        out_shape=(
+            jax.ShapeDtypeStruct(up_sent.shape, BF),
+            jax.ShapeDtypeStruct((2, quarter, width), BF),
+            jax.ShapeDtypeStruct((quarter, width), BF),
+            jax.ShapeDtypeStruct((quarter, width), BF),
+            jax.ShapeDtypeStruct((tokens, width), BF),
+            jax.ShapeDtypeStruct((3, tokens, lw), BF),
+            jax.ShapeDtypeStruct((tokens, lw), BF),
+            jax.ShapeDtypeStruct((tokens, width), F32),
+            jax.ShapeDtypeStruct((tokens, width), BF),
+        ),
+        in_specs=[vmem] * 9 + [hbm] * 3,
+        out_specs=[hbm] * 4 + [vmem] * 5,
+        scratch_shapes=[
+            pltpu.VMEM((4, tokens, width // 8), BF),
+            pltpu.VMEM((4, tokens, width // 8), BF),
+            pltpu.VMEM((4, tokens, width // 8), BF),
+            pltpu.VMEM((4, tokens, width // 8), BF),
+            pltpu.VMEM((2, 4, tokens, width // 8), BF),
+            dma((n,)),
+            dma((n,)),
+            dma((3,)),
+            dma((3,)),
+            dma((4,)),
+            dma((4,)),
+            dma((4,)),
+            dma((4,)),
+            dma((4,)),
+            dma((4,)),
+        ],
+        compiler_params=pltpu.CompilerParams(
+            collective_id=2, has_side_effects=True, vmem_limit_bytes=56 * 2**20
+        ),
+        cost_estimate=pl.CostEstimate(
+            flops=2 * tokens * width * 4 * lw, bytes_accessed=30 * 2**20, transcendentals=0
+        ),
+    )(hidden, gain1, gain2, w, bias, cosine, sine, prefix, ow, up_sent, gu_own, dn_own)
+
+
+def dispatch_kernel(
+    n,
+    n_tp,
+    capp,
+    n_exp,
+    nt,
+    place,
+    router,
+    cot,
+    sgu,
+    sdn,
+    gu_own,
+    dn_b,
+    x_rows,
+    gu_b,
+    gu_c,
+    dn_c,
+    probs,
+    gate,
+    og,
+    pg,
+    sh,
+    part,
+    sback,
+    x_send,
+    x_ss,
+    x_rs,
+    w_ss,
+    w_rs,
+):
+    ep = lax.axis_index("ep")
+    tp = lax.axis_index("tp")
+    tokens, width = nt.shape
+    units = sdn.shape[1]
+    total = place.shape[0]
+    core_peer, y_peer = flip(tp, 1), flip(tp, 2)
+    greet(n, n_tp, ep, tp)
+    w_y = remote(gu_own, gu_b, w_ss.at[0], w_rs.at[0], "tp", y_peer)
+    w_y.start()
+    w_on = remote(dn_b, dn_c, w_ss.at[1], w_rs.at[1], "tp", core_peer)
+    w_on.start()
+
+    logits = jnp.dot(nt[...], router[...], preferred_element_type=F32)
+    lane = lax.broadcasted_iota(jnp.int32, logits.shape, 1)
+    chosen = jnp.where(lane < n_exp, logits, -1e30)
+    e = jnp.exp(chosen - jnp.max(chosen, axis=1, keepdims=True))
+    prob = e / jnp.sum(e, axis=1, keepdims=True)
+    prob = jnp.where(lane == n_exp, jax.nn.sigmoid(logits), prob)
+    probs[...] = prob
+    hi = prob.astype(BF)
+    lo = (prob - hi.astype(F32)).astype(BF)
+
+    def x_copy(r, way):
+        to = lax.rem(ep + r, n) if way == "out" else lax.rem(ep + n - r, n)
+        at = pl.ds(pl.multiple_of(r * capp, capp), capp)
+        return remote(x_send.at[at, :], x_rows.at[at, :], x_ss.at[r], x_rs.at[r], "ep", to)
+
+    kept = pltpu.make_async_copy(x_send.at[:capp, :], x_rows.at[:capp, :], x_ss.at[0])
+
+    per = 1
+    while 2 * per * capp <= 128 and n % (2 * per) == 0:
+        per *= 2
+    size = per * capp
+
+    @pl.loop(0, n // per)
+    def _(b):
+        at = pl.ds(pl.multiple_of(b * size, size), size)
+        where = place[at, :]
+        x_send[at, :width] = jnp.dot(where, nt[...], preferred_element_type=F32).astype(BF)
+        row = lax.broadcasted_iota(jnp.int32, (size, 128), 0) + b * size
+        spot = lax.broadcasted_iota(jnp.int32, (size, 128), 1)
+        expert = lax.rem(row // capp + ep * (n_exp // n), n_exp)
+        pick = spot == expert
+        g_hi = jnp.sum(
+            jnp.where(pick, jnp.dot(where, hi, preferred_element_type=F32), 0.0), axis=1, keepdims=True
+        )
+        g_lo = jnp.sum(
+            jnp.where(pick, jnp.dot(where, lo, preferred_element_type=F32), 0.0), axis=1, keepdims=True
+        )
+        gate[at, :] = g_hi + g_lo
+        x_send[at, width:] = jnp.where(spot == 0, g_hi, jnp.where(spot == 1, g_lo, 0.0)).astype(BF)
+        for i in range(per):
+            r = b * per + i
+            if i == 0:
+
+                @pl.when(b == 0)
+                def _():
+                    kept.start()
+
+                @pl.when(b > 0)
+                def _():
+                    x_copy(r, "out").start()
+            else:
+                x_copy(r, "out").start()
+
+    @pl.loop(0, tokens // 64)
+    def _(m):
+        at = pl.ds(pl.multiple_of(m * 64, 64), 64)
+        og[at, :] = (probs[at, n_exp : n_exp + 1] * cot[at, :].astype(F32)).astype(BF)
+
+    def hidden(at, up_at):
+        g_pre = jnp.dot(nt[...], sgu[0, :, at], preferred_element_type=F32)
+        u_pre = jnp.dot(nt[...], sgu[1, :, at], preferred_element_type=F32)
+        grad = jnp.dot(og[...], sdn[:, at], preferred_element_type=F32)
+        sig = jax.nn.sigmoid(g_pre)
+        sh[:, at] = (g_pre * sig * u_pre).astype(BF)
+        pg[:, at] = (grad * u_pre * sig * (1.0 + g_pre * (1.0 - sig))).astype(BF)
+        pg[:, up_at] = (grad * g_pre * sig).astype(BF)
+
+    @pl.loop(0, units // 256)
+    def _(c):
+        hidden(
+            pl.ds(pl.multiple_of(c * 256, 256), 256),
+            pl.ds(pl.multiple_of(c * 256 + units, 128), 256),
+        )
+
+    if units % 256:
+        rest = units // 256 * 256
+        hidden(pl.ds(rest, units - rest), pl.ds(units + rest, units - rest))
+
+    w_y.wait()
+    w_far = remote(gu_b, gu_c, w_ss.at[2], w_rs.at[2], "tp", core_peer)
+    w_far.start()
+
+    nt_dims = (((1,), (1,)), ((), ()))
+
+    @pl.loop(0, width // 256)
+    def _(c):
+        at = pl.ds(pl.multiple_of(c * 256, 256), 256)
+        part[:, at] = lax.dot_general(sh[...], sdn[at, :], nt_dims, preferred_element_type=F32)
+        sback[:, at] = lax.dot_general(
+            pg[:, :units], sgu[0, at, :], nt_dims, preferred_element_type=F32
+        ) + lax.dot_general(pg[:, units:], sgu[1, at, :], nt_dims, preferred_element_type=F32)
+
+    w_on.wait()
+    w_far.wait()
+    kept.wait()
+
+    @pl.loop(1, n)
+    def _(r):
+        x_copy(r, "in").wait()
+
+
+def dispatch(n, n_tp, capp, n_exp, nt, place, router, cot, sgu, sdn, gu_own, dn_b):
+    tokens, width = nt.shape
+    units = sdn.shape[1]
+    total = place.shape[0]
+    vmem = pl.BlockSpec(memory_space=pltpu.VMEM)
+    hbm = pl.BlockSpec(memory_space=pl.ANY)
+    dma = pltpu.SemaphoreType.DMA
+    return pl.pallas_call(
+        functools.partial(dispatch_kernel, n, n_tp, capp, n_exp),
+        out_shape=(
+            jax.ShapeDtypeStruct((total, width + 128), BF),
+            jax.ShapeDtypeStruct(gu_own.shape, BF),
+            jax.ShapeDtypeStruct(gu_own.shape, BF),
+            jax.ShapeDtypeStruct(dn_b.shape, BF),
+            jax.ShapeDtypeStruct((tokens, 128), F32),
+            jax.ShapeDtypeStruct((total, 1), F32),
+            jax.ShapeDtypeStruct((tokens, width), BF),
+            jax.ShapeDtypeStruct((tokens, 2 * units), BF),
+            jax.ShapeDtypeStruct((tokens, units), BF),
+            jax.ShapeDtypeStruct((tokens, width), F32),
+            jax.ShapeDtypeStruct((tokens, width), F32),
+        ),
+        in_specs=[vmem] * 6 + [hbm] * 2,
+        out_specs=[hbm] * 4 + [vmem] * 7,
+        scratch_shapes=[
+            pltpu.VMEM((total, width + 128), BF),
+            dma((n,)),
+            dma((n,)),
+            dma((3,)),
+            dma((3,)),
+        ],
+        compiler_params=pltpu.CompilerParams(
+            collective_id=3, has_side_effects=True, vmem_limit_bytes=60 * 2**20
+        ),
+        cost_estimate=pl.CostEstimate(
+            flops=2 * tokens * width * 6 * units, bytes_accessed=40 * 2**20, transcendentals=0
+        ),
+    )(nt, place, router, cot, sgu, sdn, gu_own, dn_b)
 
 
 def body(
@@ -466,11 +1183,6 @@
     part_pad = -(-part // 16) * 16
     rows = n_exp * part_pad
 
-    gu_t = jnp.transpose(expert_gate_up[0], (1, 2, 0))
-    w_gate = lax.all_gather(gu_t[0], "tp", axis=0, tiled=True)
-    w_up = lax.all_gather(gu_t[1], "tp", axis=0, tiled=True)
-    w_down = lax.all_gather(jnp.transpose(expert_down[0], (1, 0)), "tp", axis=0, tiled=True)
-
     flat_route = routes.T.reshape(-1)
     flat_order = priority.T.reshape(-1)
     hits = (flat_route[:, None] == jnp.arange(n_exp, dtype=jnp.int32)[None, :]).astype(BF)
@@ -490,117 +1202,109 @@
     place = place.astype(BF)
 
     up_sent = mm(place, cotangent, 1, 0).astype(BF)
-    up_rows = exchange(up_sent, n_ep)
 
     upstream = cotangent.astype(F32)
     residual_in = hidden.astype(F32)
     factor_one = norm_factor(residual_in)
-    normed_one = (residual_in * factor_one * attn_gain).astype(BF)
-    linear = jnp.einsum("td,dkh->tkh", normed_one, qkv_weight, preferred_element_type=F32)
-    mixed_heads = (linear + qkv_bias[None]).reshape(tokens, 3, heads, head_size)
     cosine, sine_val = angle_tables(tokens, head_size)
-    queries = rotate_forward(mixed_heads[:, 0], cosine, sine_val).astype(BF)
-    key_rows = rotate_forward(mixed_heads[:, 1], cosine, sine_val).astype(BF)
-    value_rows = mixed_heads[:, 2].astype(BF)
-    scores = masked_scores(queries, key_rows, prefix[0], head_size)
-    row_max = jnp.max(scores, axis=-1, keepdims=True)
-    log_total = row_max + jnp.log(jnp.sum(jnp.exp(scores - row_max), axis=-1, keepdims=True))
-    attn_probs = jnp.exp(scores - log_total).astype(BF)
-    context = (
-        jnp.einsum("hqk,khd->qhd", attn_probs, value_rows, preferred_element_type=F32)
-        .astype(BF)
-        .reshape(tokens, local_width)
+    cos_all = jnp.concatenate([cosine[:, 0], cosine[:, 0]], axis=1)
+    sin_all = jnp.concatenate([-sine_val[:, 0], sine_val[:, 0]], axis=1)
+    w_t = jnp.transpose(qkv_weight, (1, 0, 2))
+    gu_own = jnp.transpose(expert_gate_up[0], (1, 2, 0))
+    dn_own = jnp.transpose(expert_down[0], (1, 0))
+    up_rows, gu_a, dn_a, dn_b, normed_one, qkv, context, middle, normed_two = front(
+        n_ep,
+        n_tp,
+        part_pad,
+        hidden,
+        attn_gain[None],
+        mlp_gain[None],
+        w_t,
+        qkv_bias,
+        cos_all,
+        sin_all,
+        jnp.broadcast_to(prefix[None], (1, tokens)),
+        out_weight,
+        up_sent,
+        gu_own,
+        dn_own,
     )
-    attn_out = tp_sum(mm(context, out_weight, 1, 1), n_tp)
-    middle = residual_in + attn_out
     factor_two = norm_factor(middle)
-    normed_two = (middle * factor_two * mlp_gain).astype(BF)
-
-    logits = mm(normed_two, router_weight, 1, 0)
-    router_probs = jax.nn.softmax(logits, axis=-1)
-    probs_hi = router_probs.astype(BF)
-    probs_lo = (router_probs - probs_hi.astype(F32)).astype(BF)
+
     row_expert = lax.rem(row_ids // part_pad + ep_i * expert_local, n_exp)
     own = (row_expert == jnp.arange(n_exp, dtype=jnp.int32)[None, :]).astype(F32)
-    sent_rows = mm(place, normed_two, 1, 0).astype(BF)
-    gate_hi = jnp.sum(mm(place, probs_hi, 1, 0) * own, axis=1, keepdims=True)
-    gate_lo = jnp.sum(mm(place, probs_lo, 1, 0) * own, axis=1, keepdims=True)
-    gate_sent = gate_hi + gate_lo
-    lane = jnp.arange(128, dtype=jnp.int32)[None, :]
-    gate_cols = jnp.where(lane == 0, gate_hi, jnp.where(lane == 1, gate_lo, 0.0)).astype(BF)
-    got = exchange(jnp.concatenate([sent_rows, gate_cols], axis=1), n_ep)
+    router_all = jnp.concatenate(
+        [router_weight, share_gate[:, None], jnp.zeros((width, 127 - n_exp), BF)], axis=1
+    )
+    got, gu_b, gu_c, dn_c, probs_all, gate_sent, shared_out_grad, pre_grad, shared_hidden, shared_part, shared_back = (
+        dispatch(
+            n_ep,
+            n_tp,
+            part_pad,
+            n_exp,
+            normed_two,
+            place,
+            router_all,
+            cotangent,
+            jnp.transpose(shared_gate_up, (1, 0, 2)),
+            shared_down,
+            gu_own,
+            dn_b,
+        )
+    )
+    router_probs = probs_all[:, :n_exp]
+    share_scale = probs_all[:, n_exp]
+    scale_grad_part = jnp.sum(upstream * shared_part, axis=1)
+    shared_down_grad = lax.psum_scatter(
+        mm(shared_out_grad, shared_hidden, 0, 0).astype(BF), "ep", scatter_dimension=0, tiled=True
+    ).astype(F32)
+
+    back_rows, e_out, row_grad, e_all, gu_grad = routed_expert(
+        n_ep,
+        n_tp,
+        part_pad,
+        got,
+        up_rows,
+        (gu_a, gu_c, gu_b, gu_own, dn_a, dn_c, dn_b, dn_own),
+        normed_two,
+        pre_grad,
+    )
+    shared_gate_up_grad = jnp.transpose(gu_grad, (1, 0, 2))
+    out_rows = exchange(e_out, n_ep, True)
     whole_rows = got[:, :width]
-    gate_row = got[:, width : width + 1].astype(F32) + got[:, width + 1 : width + 2].astype(F32)
-
-    gate_in = mm(normed_two, share_gate, 1, 0)
-    share_scale = jax.nn.sigmoid(gate_in)
-    shared_pre = jnp.einsum("td,dkf->tkf", normed_two, shared_gate_up, preferred_element_type=F32)
-    shared_hidden = (jax.nn.silu(shared_pre[:, 0]) * shared_pre[:, 1]).astype(BF)
-    shared_part = mm(shared_hidden, shared_down, 1, 1)
-    shared_out_grad = (share_scale[:, None] * upstream).astype(BF)
-    scale_grad_part = jnp.sum(upstream * shared_part, axis=1)
-    shared_hidden_grad = mm(shared_out_grad, shared_down, 1, 0)
-    sg, su = swiglu_backward(shared_hidden_grad, shared_pre[:, 0], shared_pre[:, 1])
-    shared_pre_grad = jnp.stack([sg, su], axis=1).astype(BF)
-    shared_back = jnp.einsum("tkf,dkf->td", shared_pre_grad, shared_gate_up, preferred_element_type=F32)
-    sg, su = sg.astype(BF), su.astype(BF)
-    slab = jnp.concatenate(
-        [
-            mm(normed_two, sg, 0, 0).astype(BF),
-            mm(normed_two, su, 0, 0).astype(BF),
-            mm(shared_out_grad, shared_hidden, 0, 0).astype(BF),
-        ],
-        axis=1,
-    )
-    slab, whole_rows, gate_row = lax.optimization_barrier((slab, whole_rows, gate_row))
-    shared_slab = lax.psum_scatter(slab, "ep", scatter_dimension=0, tiled=True).astype(F32)
-    sf = shared_hidden.shape[1]
-    shared_gate_up_grad = jnp.stack([shared_slab[:, :sf], shared_slab[:, sf : 2 * sf]], axis=1)
-    shared_down_grad = shared_slab[:, 2 * sf :]
-
-    e_gate = mm(whole_rows, w_gate, 1, 1)
-    e_up = mm(whole_rows, w_up, 1, 1)
-    e_hidden = (jax.nn.silu(e_gate) * e_up).astype(BF)
-    e_out = mm(e_hidden, w_down, 1, 0).astype(BF)
-    row_grad = (gate_row * up_rows.astype(F32)).astype(BF)
-    e_hidden_grad = mm(row_grad, w_down, 1, 1)
-    eg, eu = swiglu_backward(e_hidden_grad, e_gate, e_up)
-    eg, eu = eg.astype(BF), eu.astype(BF)
-    back_sent = (mm(eg, w_gate, 1, 0) + mm(eu, w_up, 1, 0)).astype(BF)
-    back_rows = exchange(back_sent, n_ep, True)
-    out_rows = exchange(e_out, n_ep, True)
-    d_down = lax.psum_scatter(mm(e_hidden, row_grad, 0, 0).astype(BF), "tp", scatter_dimension=0, tiled=True)
-    d_gate = lax.psum_scatter(mm(eg, whole_rows, 0, 0).astype(BF), "tp", scatter_dimension=0, tiled=True)
-    d_up = lax.psum_scatter(mm(eu, whole_rows, 0, 0).astype(BF), "tp", scatter_dimension=0, tiled=True)
-    expert_down_grad = jnp.transpose(d_down.astype(F32), (1, 0))[None]
-    expert_gate_up_grad = jnp.transpose(
-        jnp.stack([d_gate, d_up], axis=0).astype(F32), (2, 0, 1)
-    )[None]
+    quarter = dn_own.shape[0]
+    pairs = ((e_all[1], whole_rows), (e_all[2], whole_rows), (e_all[0], row_grad))
+    weight_grads = []
+    for left, right in pairs:
+        came = swap(mm(left[:, : 2 * quarter], right, 0, 0).astype(BF), 1, n_tp)
+        on = swap(
+            (
+                mm(left[:, 2 * quarter : 3 * quarter], right, 0, 0) + came[quarter:].astype(F32)
+            ).astype(BF),
+            2,
+            n_tp,
+        )
+        weight_grads.append(
+            mm(left[:, 3 * quarter :], right, 0, 0) + came[:quarter].astype(F32) + on.astype(F32)
+        )
+    expert_down_grad = jnp.transpose(weight_grads[2], (1, 0))[None]
+    expert_gate_up_grad = jnp.transpose(jnp.stack(weight_grads[:2], axis=0), (2, 0, 1))[None]
 
     weighted_place = (place.astype(F32) * gate_sent).astype(BF)
     routed = mm(weighted_place, out_rows, 0, 0)
-    out_cols = lax.psum_scatter(
-        (share_scale[:, None] * shared_part + routed).astype(BF), "tp", scatter_dimension=1, tiled=True
-    ).astype(F32)
+    out_cols = tp_scatter(share_scale[:, None] * shared_part + routed, n_tp)
     output = (lax.dynamic_slice_in_dim(middle, col_start, cols, 1) + out_cols).astype(BF)
-    gate_grad_row = jnp.sum(up_sent.astype(F32) * out_rows.astype(F32), axis=1, keepdims=True)
+    gate_grad_row = back_rows[:, width : width + 1].astype(F32) + back_rows[:, width + 1 : width + 2].astype(F32)
     prob_part = mm(place, (gate_grad_row * own).astype(BF), 0, 0)
-    pad = -(-(n_exp + 1) // 256) * 256 - n_exp - 1
-    summed = tp_sum(
+    few = tp_sum(
         jnp.concatenate(
-            [
-                shared_back + mm(place, back_rows, 0, 0),
-                prob_part,
-                scale_grad_part[:, None],
-                jnp.zeros((tokens, pad), F32),
-            ],
-            axis=1,
+            [prob_part, scale_grad_part[:, None], jnp.zeros((tokens, 256 - n_exp - 1), F32)], axis=1
         ),
         n_tp,
     )
-    normed_two_grad = summed[:, :width]
-    prob_grad = summed[:, width : width + n_exp]
-    scale_grad = summed[:, width + n_exp]
+    normed_two_grad = tp_sum(shared_back + mm(place, back_rows[:, :width], 0, 0), n_tp)
+    prob_grad = few[:, :n_exp]
+    scale_grad = few[:, n_exp]
     gate_in_grad = (scale_grad * share_scale * (1.0 - share_scale)).astype(BF)
     logit_grad = (
         router_probs * (prob_grad - jnp.sum(router_probs * prob_grad, axis=1, keepdims=True))
@@ -625,7 +1329,9 @@
 
     attn_grad = middle_grad.astype(BF)
     context_grad = mm(attn_grad, out_weight, 1, 0).astype(BF).reshape(tokens, heads, head_size)
-    attn_weights = jnp.exp(scores - log_total)
+    queries, key_rows, value_rows = (qkv[i].reshape(tokens, heads, head_size) for i in range(3))
+    scores = masked_scores(queries, key_rows, prefix[0], head_size)
+    attn_weights = jax.nn.softmax(scores, axis=-1)
     prob_grad_att = jnp.einsum("qhd,khd->hqk", context_grad, value_rows, preferred_element_type=F32)
     value_grad = jnp.einsum(
         "hqk,qhd->khd", attn_weights.astype(BF), context_grad, preferred_element_type=F32
@@ -646,11 +1352,11 @@
     qkv_grad, out_weight_grad, input_grad, gain_one, bias_sum, small_sum = tail(
         n_ep,
         n_tp,
-        normed_one.T,
+        normed_one,
         linear_grad,
-        attn_grad.T,
+        attn_grad,
         context,
-        jnp.transpose(qkv_weight, (1, 0, 2)),
+        w_t,
         lax.dynamic_slice_in_dim(hidden, col_start, cols, 1),
         factor_one,
         lax.dynamic_slice_in_dim(attn_gain, col_start, cols, 0)[None],

time: 1030 us -> 908 us (0.88)
  Pallas kernels: 198 us -> 525 us
  waiting for transfers between devices: 373 us -> 121 us
  matrix products: 207 us -> 89.6 us
  local copies, waits for them, and re-layouts: 96.5 us -> 60.2 us
  starting transfers between devices: 60 us -> 31.9 us
  other arithmetic: 72.4 us -> 58.2 us
    pallas_call x0 -> x3, Pallas kernels: none -> 398 us  [the longest x1 207 us: routed_expert(): pl.pallas_call(functools.partial(middle_kernel, n, n_tp, capp), out_shape...]
    reduce_scatter x5 -> x1, waiting for transfers between devices: 121 us -> 0.01 us  [body(): lax.psum_scatter(mm(shared_out_grad, shared_hidden, 0, 0).astype(BF), 'ep...]
    ppermute x28 -> x7, waiting for transfers between devices: 174 us -> 83 us  [exchange(): lax.ppermute(x[shift * rows:(shift + 1) * rows], 'ep', [(i, (i + step) %...]
    dot_general x28 -> x18, matrix products: 155 us -> 80.3 us  [mm(): lax.dot_general(a, b, (((ca,), (cb,)), ((), ())), preferred_element_type=...]
    pallas_call x1, Pallas kernels: 198 us -> 127 us  [tail(): pl.pallas_call(functools.partial(tail_kernel, n, n_tp), out_shape=(jax.Sh...]
    dot_general x5 -> x0, matrix products: 42.1 us -> none  [the longest x1 13.7 us: body(): jnp.einsum('td,dkf->tkf', normed_two, shared_gate_up, preferred_element_t...]
    ppermute x6 -> x14, waiting for transfers between devices: 76.5 us -> 38.4 us  [swap(): return lax.ppermute(x, 'tp', [(i, i ^ bit) for i in range(n)])]
    ppermute x28 -> x7, starting transfers between devices: 55.2 us -> 22.9 us  [exchange(): lax.ppermute(x[shift * rows:(shift + 1) * rows], 'ep', [(i, (i + step) %...]
  transfers between devices with their start and end apart: 42 -> 22, of which waited for: 15 -> 9; matrix products, arithmetic and copies ran while one was open for 30% -> 18% of each run, Pallas kernels for 19% -> 14%
where the time goes in v3:
time: 908 us; the launch traced here: 903 us
  Pallas kernels  525 us (58%)
  waiting for transfers between devices  121 us (13%)
  matrix products  89.6 us (10%)
  local copies, waits for them, and re-layouts  60.2 us (7%)
  other arithmetic  58.2 us (6%)
  starting transfers between devices  31.9 us (4%)
  between operations  16.2 us (2%)
    pallas_call x1, Pallas kernels, routed_expert(): pl.pallas_call(functools.partial(middle_kernel, n, n_tp, capp), out_shape...  207 us
    pallas_call x1, Pallas kernels, tail(): pl.pallas_call(functools.partial(tail_kernel, n, n_tp), out_shape=(jax.Sh...  127 us
    pallas_call x1, Pallas kernels, dispatch(): pl.pallas_call(functools.partial(dispatch_kernel, n, n_tp, capp, n_exp),...  111 us
    ppermute x7, waiting for transfers between devices, exchange(): lax.ppermute(x[shift * rows:(shift + 1) * rows], 'ep', [(i, (i + step) %...  83 us
    dot_general x18, matrix products, mm(): lax.dot_general(a, b, (((ca,), (cb,)), ((), ())), preferred_element_type=...  80.3 us
    pallas_call x1, Pallas kernels, front(): pl.pallas_call(functools.partial(front_kernel, n, n_tp, capp), out_shape=...  79.9 us
    ppermute x14, waiting for transfers between devices, swap(): return lax.ppermute(x, 'tp', [(i, i ^ bit) for i in range(n)])  38.4 us
    unnamed x127, local copies, waits for them, and re-layouts  29 us
  transfers between devices with their start and end apart: 22, of which 9 were waited for; matrix products, arithmetic and copies ran while one was open for 18% of the time, Pallas kernels for 14%

profile of v3, /device:TPU:0, one launch (start us, length us, event | category | flops | bytes accessed | tf_op | source)
XLA Modules:
  0.0 902.6 jit_solution(13733131237523534722)
XLA Ops:
  8.7 4.0 fusion.48
  14.8 6.7 convolution_convert_fusion.1.up_sent
  24.2 6.3 copy.130
  35.1 79.9 %shard_map.255 = (bf16[896,2048]{1,0:T(8,128)(2,1)}, bf16[2,352,2048]{2,1,0:T(8,128)(2,1)}, bf16[352,2048]{1,0:T(8,128)(2,1)}, bf16[352,2048]{1,0:T(8,128)(2,1)}...) custom-call(bf16[640,2048]{1,0:T(8,128)(2,1)} %hidden.1, ...), custom_call_target="tpu_custom_call" | custom-call | flops 5368709120 | bytes 31457280 | tf_op jit(solution)/shard_map/pallas_call | solution.py:927
  115.1 110.6 %shard_map.256 = (bf16[896,2176]{1,0:T(8,128)(2,1)}, bf16[2,352,2048]{2,1,0:T(8,128)(2,1)}, bf16[2,352,2048]{2,1,0:T(8,128)(2,1)}, bf16[352,2048]{1,0:T(8,128)(2...) custom-call(bf16[640,2048]{1,0:T(8,128)(2,1)} %get-tuple-element.45., ...), custom_call_target="tpu_custom_call" | custom-call | flops 22145925120 | bytes 41943040 | tf_op jit(solution)/shard_map/pallas_call | solution.py:1118
  225.7 207.2 %shard_map.257 = (bf16[896,2176]{1,0:T(8,128)(2,1)}, bf16[896,2048]{1,0:T(8,128)(2,1)}, bf16[896,2048]{1,0:T(8,128)(2,1)}, bf16[3,896,1408]{2,1,0:T(8,128)(2,1)}, f32[2,256,1408]{2,1,0:T(8,128)}) custom-call(bf16[896,2176]{1,0:T(8,128)(2,1)} %get-tuple-element.50.x_hbm, bf16[896,2048]{1,0:T(8,128)(2,1)} %get-tuple-element.51.u_hbm, ...), custom_call_target="tpu_custom_call" | custom-call | flops 31004295168 | bytes 41943040 | tf_op jit(solution)/shard_map/pallas_call | solution.py:710
  432.8 3.6 slice_bitcast_fusion
  437.1 4.6 convolution_convert_fusion.2
  442.0 4.5 convolution_convert_fusion.4
  446.7 4.5 convolution_convert_fusion.3
  452.9 3.1 fusion.5
  459.3 6.8 convolution_convert_fusion
  466.1 4.0 fusion.114
  470.1 5.3 collective-permute-start
  475.4 4.4 fusion.33
  479.9 4.8 fusion.28
  487.9 7.3 fusion.18
  505.7 5.8 copy.114
  515.8 4.5 collective-permute-done.13
  520.3 6.0 collective-permute-start.1
  528.4 16.3 %collective-permute-done.1 = bf16[112,2048]{1,0:T(8,128)(2,1)S(1)} collective-permute-done((bf16[112,2048]{1,0:T(8,128)(2,1)}, bf16[112,2048]{1,0:T(8,128)(2,1)S(1)}, u32[]{:S(2)}, u32[]{:S(2)}) %collective-permute-start.1) | collective-permute-done | bytes 458784 | tf_op jit(solution)/shard_map/ppermute | solution.py:97
  544.8 3.5 collective-permute-start.3
  549.1 3.5 collective-permute-done.2
  552.6 7.7 collective-permute-start.4
  561.0 34.8 %collective-permute-done.3 = bf16[112,2048]{1,0:T(8,128)(2,1)S(1)} collective-permute-done((bf16[112,2048]{1,0:T(8,128)(2,1)}, bf16[112,2048]{1,0:T(8,128)(2,1)S(1)}, u32[]{:S(2)}, u32[]{:S(2)}) %collective-permute-start.3) | collective-permute-done | bytes 458784 | tf_op jit(solution)/shard_map/ppermute | solution.py:97
  596.7 6.3 collective-permute-done.4
  604.1 6.1 collective-permute-done.5
  611.1 16.0 %collective-permute-done.6 = bf16[112,2048]{1,0:T(8,128)(2,1)S(1)} collective-permute-done((bf16[112,2048]{1,0:T(8,128)(2,1)S(1)}, bf16[112,2048]{1,0:T(8,128)(2,1)S(1)}, u32[]{:S(2)}, u32[]{:S(2)}) %collective-permute-start.6) | collective-permute-done | bytes 458784 | tf_op jit(solution)/shard_map/ppermute | solution.py:97
  629.0 5.3 multiply_add_fusion.1
  634.3 2.3 copy-done.6
  638.2 5.1 fusion.118
  643.3 5.6 fusion.59
  648.9 4.8 add_convert_fusion.4
  659.7 2.4 fusion.43
  666.4 33.3 %collective-permute-done.8 = bf16[640,512]{1,0:T(8,128)(2,1)} collective-permute-done((bf16[640,512]{1,0:T(8,128)(2,1)}, bf16[640,512]{1,0:T(8,128)(2,1)}, u32[]{:S(2)}, u32[]{:S(2)}) %collective-permute-start.8) | collective-permute-done | bytes 655392 | tf_op jit(solution)/shard_map/ppermute | solution.py:63
  699.7 3.3 fusion.46
  703.0 2.4 add_convert_fusion.3
  705.8 4.9 add_convert_fusion
  712.5 4.7 add_convert_fusion.2
  717.5 4.6 add_convert_fusion.1
  726.2 4.6 fusion.111
  740.9 2.5 constant_dynamic-slice_fusion.mid_cols
  745.5 127.4 %shard_map.258 = (f32[3,256,512]{2,1,0:T(8,128)}, f32[256,512]{1,0:T(8,128)}, bf16[640,512]{1,0:T(8,128)(2,1)}, f32[1,2048]{1,0:T(1,128)}, f32[1,1536]{1,0:T(1,128)}, /*index=5*/f32[16,2048]{1,0:T(8,128)}) custom-call(bf16[640,2048]{1,0:T(8,128)(2,1)} %get-tuple-element.59.n1, bf16[640,1536]{1,0:T(8,128)(2,1)} %pad_maximum_fusion.lg, ...), custom_call_target="tpu_custom_call" | custom-call | flops 9395240960 | bytes 31457280 | tf_op jit(solution)/shard_map/pallas_call | solution.py:400
  877.3 2.6 add_bitcast_fusion.2
  879.9 2.4 add_bitcast_fusion.1
  882.4 2.9 maximum_bitcast_fusion
  885.3 4.1 add_bitcast_fusion
  889.5 2.5 convert_element_type.234
  (246 shorter events, 80.9 us)
Async XLA Ops:
  7.2 882.3 %reduce-scatter.2.cloned.1.call-start = ((), (), s32[]{:S(2)}) async-start(), calls=%async_computation.1 | async-start | bytes 6488064 | tf_op jit(solution)/shard_map/reduce_scatter | solution.py:1258
  8.7 15.5 %slice-start.4 = ((s8[11534336]{0:T(1024)(128)(4,1)}), s8[3145728]{0:T(1024)(128)(4,1)S(1)}, s32[]{:S(2)}) async-start(s8[11534336]{0:T(1024)(128)(4,1)} %bitcast.85), calls=%async_computation.6 | async-start | bytes 6291456
  12.9 11.3 %slice-start.5 = ((s8[11534336]{0:T(1024)(128)(4,1)}), s8[4194304]{0:T(1024)(128)(4,1)S(1)}, s32[]{:S(2)}) async-start(s8[11534336]{0:T(1024)(128)(4,1)} %bitcast.85), calls=%async_computation.7 | async-start | bytes 8388608
  14.8 9.4 %slice-start.6 = ((s8[11534336]{0:T(1024)(128)(4,1)}), s8[4194304]{0:T(1024)(128)(4,1)S(1)}, s32[]{:S(2)}) async-start(s8[11534336]{0:T(1024)(128)(4,1)} %bitcast.85), calls=%async_computation.8 | async-start | bytes 8388608
  24.2 6.3 copy-start.33
  24.2 6.6 copy-start.32
  436.5 5.2 copy-start.17
  436.5 10.2 %copy-start.15 = (bf16[896,1408]{1,0:T(8,128)(2,1)}, bf16[896,1408]{1,0:T(8,128)(2,1)S(1)}, u32[]{:S(2)}) copy-start(bf16[896,1408]{1,0:T(8,128)(2,1)S(1)} %get-tuple-element.138) | copy-start | bytes 7569412
  441.7 263.8 %collective-permute-start.19 = (bf16[704,2048]{1,0:T(8,128)(2,1)}, bf16[704,2048]{1,0:T(8,128)(2,1)}, u32[]{:S(2)}, u32[]{:S(2)}) collective-permute-start(bf16[704,2048]{1,0:T(8,128)(2,1)} %convolution_convert_fusion.2), channel_id=1, source_target_pairs={{0,1},{1,0},{2,3},{3,2},{4,5},{5,4},{6,7},{7,6},{8,9},{9,8},{10,11... | collective-permute-start | bytes 8650760 | tf_op jit(solution)/shard_map/ppermute | solution.py:63
  446.5 266.0 %collective-permute-start.15 = (bf16[704,2048]{1,0:T(8,128)(2,1)}, bf16[704,2048]{1,0:T(8,128)(2,1)}, u32[]{:S(2)}, u32[]{:S(2)}) collective-permute-start(bf16[704,2048]{1,0:T(8,128)(2,1)} %convolution_convert_fusion.4), channel_id=1, source_target_pairs={{0,1},{1,0},{2,3},{3,2},{4,5},{5,4},{6,7},{7,6},{8,9},{9,8},{10,11... | collective-permute-start | bytes 8650760 | tf_op jit(solution)/shard_map/ppermute | solution.py:63
  446.7 6.2 copy-start.1
  451.2 266.3 %collective-permute-start.17 = (bf16[704,2048]{1,0:T(8,128)(2,1)}, bf16[704,2048]{1,0:T(8,128)(2,1)}, u32[]{:S(2)}, u32[]{:S(2)}) collective-permute-start(bf16[704,2048]{1,0:T(8,128)(2,1)} %convolution_convert_fusion.3), channel_id=1, source_target_pairs={{0,1},{1,0},{2,3},{3,2},{4,5},{5,4},{6,7},{7,6},{8,9},{9,8},{10,11... | collective-permute-start | bytes 8650760 | tf_op jit(solution)/shard_map/ppermute | solution.py:63
  459.1 53.6 %collective-permute-start.12 = (bf16[640,128]{1,0:T(8,128)(2,1)}, bf16[640,128]{1,0:T(8,128)(2,1)}, u32[]{:S(2)}, u32[]{:S(2)}) collective-permute-start(bf16[640,128]{1,0:T(8,128)(2,1)} %select_convert_fusion.2), channel_id=1, source_target_pairs={{0,1},{1,0},{2,3},{3,2},{4,5},{5,4},{6,7},{7,6},{8,9},{9,8},{10,11... | collective-permute-start | bytes 491528 | tf_op jit(solution)/shard_map/ppermute | solution.py:63
  466.1 9.3 %copy-start.40 = (bf16[896,2176]{1,0:T(8,128)(2,1)S(1)}, bf16[896,2176]{1,0:T(8,128)(2,1)}, u32[]{:S(2)}) copy-start(bf16[896,2176]{1,0:T(8,128)(2,1)} %get-tuple-element.50.x_hbm) | copy-start | bytes 11698180
  470.1 56.2 %collective-permute-start = (bf16[112,2048]{1,0:T(8,128)(2,1)}, bf16[112,2048]{1,0:T(8,128)(2,1)}, u32[]{:S(2)}, u32[]{:S(2)}) collective-permute-start(bf16[112,2048]{1,0:T(8,128)(2,1)} %get-tuple-element.148), channel_id=1, source_target_pairs={{0,28},{4,0},{8,4},{12,8},{16,12},{20,16},{24,20},{28,24},{1,29},{... | collective-permute-start | bytes 1376264 | tf_op jit(solution)/shard_map/ppermute | solution.py:97
  479.9 7.4 copy-start.3
  487.9 8.7 slice-start
  487.9 8.7 slice-start.1
  501.3 136.8 %copy-start.10 = (bf16[1,640,512]{1,2,0:T(8,128)(2,1)}, bf16[1,640,512]{1,2,0:T(8,128)(2,1)S(1)}, u32[]{:S(2)}) copy-start(bf16[1,640,512]{1,2,0:T(8,128)(2,1)S(1)} %copy.123) | copy-start | bytes 1966084
  505.7 5.8 copy-start.29
  505.7 7.0 copy-start.21
  505.7 123.3 %slice-start.9 = ((s8[5242880]{0:T(1024)(128)(4,1)}), s8[1048576]{0:T(1024)(128)(4,1)S(1)}, s32[]{:S(2)}) async-start(s8[5242880]{0:T(1024)(128)(4,1)} %bitcast.90), calls=%async_computation.11 | async-start | bytes 2097152
  511.7 91.2 %copy-start.28 = (bf16[112,2048]{1,0:T(8,128)(2,1)S(1)}, bf16[112,2048]{1,0:T(8,128)(2,1)}, u32[]{:S(2)}) copy-start(bf16[112,2048]{1,0:T(8,128)(2,1)} %get-tuple-element.142) | copy-start | bytes 1376260
  513.8 6.5 collective-permute-start.13
  520.3 24.4 %collective-permute-start.1 = (bf16[112,2048]{1,0:T(8,128)(2,1)}, bf16[112,2048]{1,0:T(8,128)(2,1)S(1)}, u32[]{:S(2)}, u32[]{:S(2)}) collective-permute-start(bf16[112,2048]{1,0:T(8,128)(2,1)} %get-tuple-element.147), channel_id=1, source_target_pairs={{0,24},{4,28},{8,0},{12,4},{16,8},{20,12},{24,16},{28,20},{1,25},{... | collective-permute-start | bytes 1376264 | tf_op jit(solution)/shard_map/ppermute | solution.py:97
  526.4 26.2 %collective-permute-start.2 = (bf16[112,2048]{1,0:T(8,128)(2,1)}, bf16[112,2048]{1,0:T(8,128)(2,1)S(1)}, u32[]{:S(2)}, u32[]{:S(2)}) collective-permute-start(bf16[112,2048]{1,0:T(8,128)(2,1)} %get-tuple-element.146), channel_id=1, source_target_pairs={{0,20},{4,24},{8,28},{12,0},{16,4},{20,8},{24,12},{28,16},{1,21},{... | collective-permute-start | bytes 1376264 | tf_op jit(solution)/shard_map/ppermute | solution.py:97
  526.5 102.5 %slice-start.10 = ((s8[5242880]{0:T(1024)(128)(4,1)}), s8[4194304]{0:T(1024)(128)(4,1)S(1)}, s32[]{:S(2)}) async-start(s8[5242880]{0:T(1024)(128)(4,1)} %bitcast.90), calls=%async_computation.12 | async-start | bytes 8388608
  544.8 51.1 %collective-permute-start.3 = (bf16[112,2048]{1,0:T(8,128)(2,1)}, bf16[112,2048]{1,0:T(8,128)(2,1)S(1)}, u32[]{:S(2)}, u32[]{:S(2)}) collective-permute-start(bf16[112,2048]{1,0:T(8,128)(2,1)} %get-tuple-element.145), channel_id=1, source_target_pairs={{0,16},{4,20},{8,24},{12,28},{16,0},{20,4},{24,8},{28,12},{1,17},{... | collective-permute-start | bytes 1376264 | tf_op jit(solution)/shard_map/ppermute | solution.py:97
  552.6 50.3 %collective-permute-start.4 = (bf16[112,2048]{1,0:T(8,128)(2,1)}, bf16[112,2048]{1,0:T(8,128)(2,1)S(1)}, u32[]{:S(2)}, u32[]{:S(2)}) collective-permute-start(bf16[112,2048]{1,0:T(8,128)(2,1)} %get-tuple-element.144), channel_id=1, source_target_pairs={{0,12},{4,16},{8,20},{12,24},{16,28},{20,0},{24,4},{28,8},{1,13},{... | collective-permute-start | bytes 1376264 | tf_op jit(solution)/shard_map/ppermute | solution.py:97
  561.0 67.5 %copy-start.4 = (f32[640,128]{1,0:T(8,128)S(1)}, f32[640,128]{1,0:T(8,128)}, u32[]{:S(2)}) copy-start(f32[640,128]{1,0:T(8,128)} %get-tuple-element.47) | copy-start | bytes 983044
  595.8 14.4 %collective-permute-start.5 = (bf16[112,2048]{1,0:T(8,128)(2,1)}, bf16[112,2048]{1,0:T(8,128)(2,1)S(1)}, u32[]{:S(2)}, u32[]{:S(2)}) collective-permute-start(bf16[112,2048]{1,0:T(8,128)(2,1)} %get-tuple-element.143), channel_id=1, source_target_pairs={{0,8},{4,12},{8,16},{12,20},{16,24},{20,28},{24,0},{28,4},{1,9},{5... | collective-permute-start | bytes 1376264 | tf_op jit(solution)/shard_map/ppermute | solution.py:97
  602.9 24.1 %collective-permute-start.6 = (bf16[112,2048]{1,0:T(8,128)(2,1)S(1)}, bf16[112,2048]{1,0:T(8,128)(2,1)S(1)}, u32[]{:S(2)}, u32[]{:S(2)}) collective-permute-start(bf16[112,2048]{1,0:T(8,128)(2,1)S(1)} %copy-done.28), channel_id=1, source_target_pairs={{0,4},{4,8},{8,12},{12,16},{16,20},{20,24},{24,28},{28,0},{1,5},{5... | collective-permute-start | bytes 1376264 | tf_op jit(solution)/shard_map/ppermute | solution.py:97
  610.2 38.7 %collective-permute-start.9 = (bf16[640,1024]{1,0:T(8,128)(2,1)}, bf16[640,1024]{1,0:T(8,128)(2,1)}, u32[]{:S(2)}, u32[]{:S(2)}) collective-permute-start(bf16[640,1024]{1,0:T(8,128)(2,1)} %select_convert_fusion), channel_id=1, source_target_pairs={{0,1},{1,0},{2,3},{3,2},{4,5},{5,4},{6,7},{7,6},{8,9},{9,8},{10,11... | collective-permute-start | bytes 3932168 | tf_op jit(solution)/shard_map/ppermute | solution.py:63
  627.1 1.4 collective-permute-start.14
  638.0 20.0 %collective-permute-start.7 = (bf16[1280,512]{1,0:T(8,128)(2,1)}, bf16[1280,512]{1,0:T(8,128)(2,1)}, u32[]{:S(2)}, u32[]{:S(2)}) collective-permute-start(bf16[1280,512]{1,0:T(8,128)(2,1)} %pad_maximum_fusion.1), channel_id=1, source_target_pairs={{0,1},{1,0},{2,3},{3,2},{4,5},{5,4},{6,7},{7,6},{8,9},{9,8},{10,11... | collective-permute-start | bytes 3932168 | tf_op jit(solution)/shard_map/ppermute | solution.py:63
  653.7 49.3 %collective-permute-start.10 = (bf16[640,1024]{1,0:T(8,128)(2,1)}, bf16[640,1024]{1,0:T(8,128)(2,1)}, u32[]{:S(2)}, u32[]{:S(2)}) collective-permute-start(bf16[640,1024]{1,0:T(8,128)(2,1)} %add_convert_fusion.4), channel_id=1, source_target_pairs={{0,2},{1,3},{2,0},{3,1},{4,6},{5,7},{6,4},{7,5},{8,10},{9,11},{10,... | collective-permute-start | bytes 3932168 | tf_op jit(solution)/shard_map/ppermute | solution.py:63
  662.1 37.6 %collective-permute-start.8 = (bf16[640,512]{1,0:T(8,128)(2,1)}, bf16[640,512]{1,0:T(8,128)(2,1)}, u32[]{:S(2)}, u32[]{:S(2)}) collective-permute-start(bf16[640,512]{1,0:T(8,128)(2,1)} %fusion.43), channel_id=1, source_target_pairs={{0,2},{1,3},{2,0},{3,1},{4,6},{5,7},{6,4},{7,5},{8,10},{9,11},{10,... | collective-permute-start | bytes 1966088 | tf_op jit(solution)/shard_map/ppermute | solution.py:63
  705.4 7.1 copy-start.41
  705.4 18.4 %collective-permute-start.11 = (bf16[640,1024]{1,0:T(8,128)(2,1)S(1)}, bf16[640,1024]{1,0:T(8,128)(2,1)S(1)}, u32[]{:S(2)}, u32[]{:S(2)}) collective-permute-start(bf16[640,1024]{1,0:T(8,128)(2,1)S(1)} %add_convert_fusion.3), channel_id=1, source_target_pairs={{0,1},{1,0},{2,3},{3,2},{4,5},{5,4},{6,7},{7,6},{8,9},{9,8},{10,11... | collective-permute-start | bytes 3932168 | tf_op jit(solution)/shard_map/ppermute | solution.py:63
  710.8 174.5 %collective-permute-start.20 = (bf16[352,2048]{1,0:T(8,128)(2,1)}, bf16[352,2048]{1,0:T(8,128)(2,1)}, u32[]{:S(2)}, u32[]{:S(2)}) collective-permute-start(bf16[352,2048]{1,0:T(8,128)(2,1)} %add_convert_fusion), channel_id=1, source_target_pairs={{0,2},{1,3},{2,0},{3,1},{4,6},{5,7},{6,4},{7,5},{8,10},{9,11},{10,... | collective-permute-start | bytes 4325384 | tf_op jit(solution)/shard_map/ppermute | solution.py:63
  712.5 11.4 %slice-start.2 = ((s8[5242880]{0:T(1024)(128)(4,1)}), s8[4194304]{0:T(1024)(128)(4,1)S(1)}, s32[]{:S(2)}) async-start(s8[5242880]{0:T(1024)(128)(4,1)} %bitcast.83), calls=%async_computation.4 | async-start | bytes 8388608
  717.2 6.8 slice-start.3
  717.2 160.1 %collective-permute-start.16 = (bf16[352,2048]{1,0:T(8,128)(2,1)}, bf16[352,2048]{1,0:T(8,128)(2,1)}, u32[]{:S(2)}, u32[]{:S(2)}) collective-permute-start(bf16[352,2048]{1,0:T(8,128)(2,1)} %add_convert_fusion.2), channel_id=1, source_target_pairs={{0,2},{1,3},{2,0},{3,1},{4,6},{5,7},{6,4},{7,5},{8,10},{9,11},{10,... | collective-permute-start | bytes 4325384 | tf_op jit(solution)/shard_map/ppermute | solution.py:63
  722.0 157.8 %collective-permute-start.18 = (bf16[352,2048]{1,0:T(8,128)(2,1)}, bf16[352,2048]{1,0:T(8,128)(2,1)}, u32[]{:S(2)}, u32[]{:S(2)}) collective-permute-start(bf16[352,2048]{1,0:T(8,128)(2,1)} %add_convert_fusion.1), channel_id=1, source_target_pairs={{0,2},{1,3},{2,0},{3,1},{4,6},{5,7},{6,4},{7,5},{8,10},{9,11},{10,... | collective-permute-start | bytes 4325384 | tf_op jit(solution)/shard_map/ppermute | solution.py:63
  724.0 8.7 slice-start.7
  726.2 6.6 slice-start.8
  745.5 131.7 %copy-start.8 = (f32[352,2048]{1,0:T(8,128)S(1)}, f32[352,2048]{1,0:T(8,128)}, u32[]{:S(2)}) copy-start(f32[352,2048]{1,0:T(8,128)} %fusion.33) | copy-start | bytes 8650756
  885.3 6.6 copy-start.25
  (31 other events, 81.9 us)
Sparse Core Ops, SparseCore 0:
  466.2 170.1 reduce-scatter.1

commit v4 on v3

--- a/solution.py
+++ b/solution.py
@@ -22,83 +22,12 @@
     return lax.rsqrt(jnp.mean(values * values, axis=-1, keepdims=True) + EPSILON)
 
 
-def swiglu_backward(hidden_grad, gate_pre, up_pre):
-    sig = jax.nn.sigmoid(gate_pre)
-    gate_grad = hidden_grad * up_pre * sig * (1.0 + gate_pre * (1.0 - sig))
-    up_grad = hidden_grad * gate_pre * sig
-    return gate_grad, up_grad
-
-
 def angle_tables(length, head_size):
     half_size = head_size // 2
     frequency = THETA ** (-jnp.arange(half_size, dtype=F32) * 2.0 / head_size)
     angles = jnp.arange(length, dtype=F32)[:, None] * frequency[None, :]
     return jnp.cos(angles)[:, None, :], jnp.sin(angles)[:, None, :]
 
-
-def rotate_forward(values, cosine, sine_val):
-    half = values.shape[-1] // 2
-    a, b = values[..., :half], values[..., half:]
-    return jnp.concatenate([a * cosine - b * sine_val, b * cosine + a * sine_val], axis=-1)
-
-
-def rotate_backward(grad_in, cosine, sine_val):
-    half = grad_in.shape[-1] // 2
-    a, b = grad_in[..., :half], grad_in[..., half:]
-    return jnp.concatenate([a * cosine + b * sine_val, b * cosine - a * sine_val], axis=-1)
-
-
-def masked_scores(queries, key_rows, prefix_len, head_size):
-    length = queries.shape[0]
-    scores = jnp.einsum(
-        "qhd,khd->hqk", queries, key_rows, preferred_element_type=F32
-    ) * head_size ** (-0.5)
-    row_index = jnp.arange(length, dtype=jnp.int32)[:, None]
-    col_index = jnp.arange(length, dtype=jnp.int32)[None, :]
-    visible = (col_index <= row_index) | (col_index < prefix_len)
-    return jnp.where(visible[None], scores, -1e30)
-
-
-def swap(x, bit, n):
-    return lax.ppermute(x, "tp", [(i, i ^ bit) for i in range(n)])
-
-
-def tp_sum(x, n):
-    half = x.shape[1] // 2
-    low = (lax.axis_index("tp") % 2) == 0
-    a, b = x[:, :half], x[:, half:]
-    mine = jnp.where(low, a, b)
-    theirs = jnp.where(low, b, a).astype(BF)
-    one = (mine.astype(F32) + swap(theirs, 1, n).astype(F32)).astype(BF)
-    two = (one.astype(F32) + swap(one, 2, n).astype(F32)).astype(BF)
-    other = swap(two, 1, n)
-    return jnp.concatenate([jnp.where(low, two, other), jnp.where(low, other, two)], axis=1).astype(F32)
-
-
-def tp_scatter(x, n):
-    me = lax.axis_index("tp")
-    cols = x.shape[1] // n
-
-    def block(bits):
-        return lax.dynamic_slice_in_dim(x, (me ^ bits) * cols, cols, 1)
-
-    one = swap(jnp.concatenate([block(1), block(3)], axis=0).astype(BF), 1, n).astype(F32)
-    rows = x.shape[0]
-    two = swap((block(2) + one[rows:]).astype(BF), 2, n)
-    return block(0) + one[:rows] + two.astype(F32)
-
-
-def exchange(x, n, back=False):
-    rows = x.shape[0] // n
-    out = [x[:rows]]
-    for shift in range(1, n):
-        step = n - shift if back else shift
-        out.append(
-            lax.ppermute(
-                x[shift * rows : (shift + 1) * rows], "ep", [(i, (i + step) % n) for i in range(n)]
-            )
-        )
-    return jnp.concatenate(out, axis=0)
 
 def ring_place(e, n):
     odd = e % 2
@@ -154,9 +83,14 @@
     mid_cols,
     bias,
     small,
+    o_rows,
+    place_t,
+    spart,
+    res_cols,
     qkv_out,
     o_out,
     in_out,
+    out_out,
     gain_out,
     bias_out,
     small_out,
@@ -175,6 +109,10 @@
     small_recv,
     gain_send,
     gain_recv,
+    out_send,
+    out_recv,
+    oy_send,
+    oy_recv,
     ring_ss,
     ring_rs,
     tp_ss,
@@ -329,15 +267,31 @@
     fourth = tp_copy(4, mean_send.at[1], mean_recv.at[1], y_peer)
     fourth.start()
 
+    def out_block(column):
+        at = pl.ds(pl.multiple_of(column * lw, lw), lw)
+        return spart[:, at].astype(F32) + jnp.dot(
+            place_t[...], o_rows[:, at], preferred_element_type=F32
+        )
+
+    fifth = [tp_copy(5 + i, out_send.at[i], out_recv.at[i], core_peer) for i in range(2)]
+    for i in range(2):
+        out_send[i] = out_block((core_peer % 2) + 2 * i).astype(BF)
+        fifth[i].start()
+
     ring_step(4, False)
 
+    for copy in fifth:
+        copy.wait()
+    oy_send[...] = (out_block((tp % 2) + 2 * other) + out_recv[other].astype(F32)).astype(BF)
+    sixth = tp_copy(7, oy_send, oy_recv, y_peer)
+    sixth.start()
     fourth.wait()
     for m in range(0, tokens, 128):
         at = slice(m, m + 128)
         mean = (mean_send[1, at, :1] + mean_recv[1, at, :1]) * (1.0 / width)
         r = r_one[at, :]
         in_out[at, :] = (
-            mid_cols[at, :]
+            mid_cols[at, :].astype(F32)
             + r * part_own[at, :] * gain[...]
             - h_cols[at, :].astype(F32) * (r * r * r) * mean
         ).astype(BF)
@@ -360,7 +314,13 @@
     for shift in range(1, n_tp):
         gain_copy(shift, "out").start()
 
-    @pl.loop(5, n - 1)
+    ring_step(5, False)
+
+    own = out_block(tp) + res_cols[...] + out_recv[tp // 2].astype(F32)
+    sixth.wait()
+    out_out[...] = (own + oy_recv[...].astype(F32)).astype(BF)
+
+    @pl.loop(6, n - 1)
     def _(step):
         ring_step(step, False)
 
@@ -388,7 +348,7 @@
             ring_copy(ring, step, step % 2).wait_send()
 
 
-def tail(n, n_tp, n1, lg, ag, ctx, w, h_cols, r_one, gain, mid_cols, bias, small):
+def tail(n, n_tp, n1, lg, ag, ctx, w, h_cols, r_one, gain, mid_cols, bias, small, o_rows, place_t, spart, res_cols):
     tokens, width = n1.shape
     lw = ctx.shape[1]
     rows = width // n
@@ -403,12 +363,13 @@
             jax.ShapeDtypeStruct((3, rows, lw), F32),
             jax.ShapeDtypeStruct((rows, lw), F32),
             jax.ShapeDtypeStruct((tokens, lw), BF),
+            jax.ShapeDtypeStruct((tokens, lw), BF),
             jax.ShapeDtypeStruct((1, width), F32),
             jax.ShapeDtypeStruct((1, 3 * lw), F32),
             jax.ShapeDtypeStruct((wide, width), F32),
         ),
-        in_specs=[vmem] * 11,
-        out_specs=[vmem] * 6,
+        in_specs=[vmem] * 15,
+        out_specs=[vmem] * 7,
         scratch_shapes=[
             pltpu.VMEM((4, n - 1, rows, lw), BF),
             pltpu.VMEM((4, 2, rows, lw), BF),
@@ -425,10 +386,14 @@
             pltpu.VMEM((n, wide, width), BF),
             pltpu.VMEM((1, lw), F32),
             pltpu.VMEM((n_tp, 1, lw), F32),
+            pltpu.VMEM((2, tokens, lw), BF),
+            pltpu.VMEM((2, tokens, lw), BF),
+            pltpu.VMEM((tokens, lw), BF),
+            pltpu.VMEM((tokens, lw), BF),
             dma((4, 2)),
             dma((4, n - 1)),
-            dma((5,)),
-            dma((5,)),
+            dma((8,)),
+            dma((8,)),
             dma((n,)),
             dma((n,)),
             dma((n,)),
@@ -437,12 +402,12 @@
             dma((n_tp,)),
         ],
         compiler_params=pltpu.CompilerParams(
-            collective_id=0, has_side_effects=True, vmem_limit_bytes=56 * 2**20
+            collective_id=0, has_side_effects=True, vmem_limit_bytes=60 * 2**20
         ),
         cost_estimate=pl.CostEstimate(
             flops=2 * tokens * width * 7 * lw, bytes_accessed=30 * 2**20, transcendentals=0
         ),
-    )(n1, lg, ag, ctx, w, h_cols, r_one, gain, mid_cols, bias, small)
+    )(n1, lg, ag, ctx, w, h_cols, r_one, gain, mid_cols, bias, small, o_rows, place_t, spart, res_cols)
 
 def cols_of(ref, owner, rows):
     at = pl.ds(pl.multiple_of(owner * rows, rows), rows)
@@ -468,20 +433,26 @@
     dn_c,
     dn_b,
     dn_own,
+    gates,
     nt,
     pg,
+    og,
+    sh,
     back,
+    g_back,
     o_hbm,
-    rg_hbm,
-    e_hbm,
+    dw_recv,
+    dw_own,
+    dw_y,
     gu_out,
+    dn_out,
     w,
     xb,
     ub,
     rgb,
-    ob,
     eb,
     rbs,
+    gbs,
     ring_recv,
     ring_send,
     w_sem,
@@ -490,11 +461,19 @@
     out_sem,
     ring_ss,
     ring_rs,
+    free,
     back_ss,
     back_rs,
+    gate_ss,
+    gate_rs,
+    dw_ss,
+    dw_rs,
+    dw_sem,
 ):
     ep = lax.axis_index("ep")
-    gr = xb.shape[1]
+    tp = lax.axis_index("tp")
+    core_peer, y_peer = flip(tp, 1), flip(tp, 2)
+    gr = ub.shape[1]
     width = u_hbm.shape[1]
     units = w.shape[1]
     quarter = units // 4
@@ -516,27 +495,21 @@
     for copy in w_in:
         copy.start()
 
-    def x_copy(g):
-        at = pl.ds(pl.multiple_of(g * gr, gr), gr)
-        slot = lax.rem(g, 2)
-        return pltpu.make_async_copy(x_hbm.at[at, :], xb.at[slot], x_sem.at[slot])
+    x_in = pltpu.make_async_copy(x_hbm, xb, x_sem)
 
     def u_copy(g):
         at = pl.ds(pl.multiple_of(g * gr, gr), gr)
         slot = lax.rem(g, 2)
         return pltpu.make_async_copy(u_hbm.at[at, :], ub.at[slot], u_sem.at[slot])
 
-    x_copy(0).start()
+    x_in.start()
     u_copy(0).start()
-
-    barrier = pltpu.get_barrier_semaphore()
-    for shift in range(1, n):
-        pl.semaphore_signal(
-            barrier, 1, device_id={"ep": lax.rem(ep + shift, n)}, device_id_type=pl.DeviceIdType.MESH
-        )
-    pl.semaphore_wait(barrier, n - 1)
-
-    piece = [(0, half), (half, units), (units, units + half), (units + half, 2 * units)]
+    greet(n, n_tp, ep, tp)
+
+    edges = [0]
+    for ring in range(4):
+        edges.append(edges[-1] + (3 * units // 128 + 3 - ring) // 4 * 128)
+    wide_of = [edges[i + 1] - edges[i] for i in range(4)]
 
     def block_of(ring, step):
         if ring < 2:
@@ -544,53 +517,70 @@
         return ring_member(lax.rem(p + 1 + step, n), n)
 
     def term(ring, owner):
-        lo, hi = piece[ring]
-        return block_dot(nt, owner, rows, pg[:, lo:hi])
-
-    def ring_copy(ring, step, slot):
-        lo, hi = piece[ring]
+        lo, hi = edges[ring], edges[ring + 1]
+        parts = []
+        if lo < 2 * units:
+            parts.append(block_dot(nt, owner, rows, pg[:, lo : min(hi, 2 * units)]))
+        if hi > 2 * units:
+            parts.append(block_dot(og, owner, rows, sh[:, max(lo - 2 * units, 0) : hi - 2 * units]))
+        return parts[0] if len(parts) == 1 else jnp.concatenate(parts, axis=1)
+
+    def ring_copy(ring, slot):
         return remote(
-            ring_send.at[ring, slot, :, : hi - lo],
-            ring_recv.at[ring, step, :, : hi - lo],
+            ring_send.at[ring, slot, :, : wide_of[ring]],
+            ring_recv.at[ring, slot, :, : wide_of[ring]],
             ring_ss.at[ring, slot],
-            ring_rs.at[ring, step],
+            ring_rs.at[ring, slot],
             "ep",
             nxt if ring < 2 else prv,
         )
 
+    order = (0, 2, 1, 3)
+
     def ring_step(step):
-        slot = lax.rem(step, 2)
-        for ring in (0, 2, 1, 3):
-            lo, hi = piece[ring]
+        slot, last = lax.rem(step, 2), lax.rem(step + 1, 2)
+        for ring in order:
+            size = wide_of[ring]
             mine = term(ring, block_of(ring, step))
-            ring_copy(ring, step - 1, slot).wait_recv()
+            ring_copy(ring, last).wait_recv()
 
             @pl.when(step >= 2)
             def _():
-                ring_copy(ring, step - 2, slot).wait_send()
-
-            ring_send[ring, slot, :, : hi - lo] = (
-                mine + ring_recv[ring, step - 1, :, : hi - lo].astype(F32)
+                ring_copy(ring, slot).wait_send()
+
+            ring_send[ring, slot, :, :size] = (
+                mine + ring_recv[ring, last, :, :size].astype(F32)
             ).astype(BF)
-            ring_copy(ring, step, slot).start()
-
-    for ring in (0, 2, 1, 3):
-        lo, hi = piece[ring]
-        ring_send[ring, 0, :, : hi - lo] = term(ring, block_of(ring, 0)).astype(BF)
-        ring_copy(ring, 0, 0).start()
+
+            @pl.when(step <= n - 3)
+            def _():
+                pl.semaphore_signal(
+                    free.at[ring],
+                    1,
+                    device_id={"ep": prv if ring < 2 else nxt},
+                    device_id_type=pl.DeviceIdType.MESH,
+                )
+
+            @pl.when(step >= 2)
+            def _():
+                pl.semaphore_wait(free.at[ring], 1)
+
+            ring_copy(ring, slot).start()
+
+    for ring in order:
+        ring_send[ring, 0, :, : wide_of[ring]] = term(ring, block_of(ring, 0)).astype(BF)
+        ring_copy(ring, 0).start()
 
     for copy in w_in:
         copy.wait()
-
-    nt_dims = (((1,), (1,)), ((), ()))
+    x_in.wait()
+
+    nt_dims, first_dims = (((1,), (1,)), ((), ())), (((0,), (0,)), ((), ()))
 
     def saved(g):
         at = pl.ds(pl.multiple_of(g * gr, gr), gr)
-        return (
-            pltpu.make_async_copy(rgb, rg_hbm.at[at, :], out_sem.at[0]),
-            pltpu.make_async_copy(ob, o_hbm.at[at, :], out_sem.at[1]),
-            pltpu.make_async_copy(eb, e_hbm.at[:, at, :], out_sem.at[2]),
-        )
+        slot = lax.rem(g, 2)
+        return pltpu.make_async_copy(ub.at[slot], o_hbm.at[at, :], out_sem.at[slot])
 
     def back_copy(r):
         at = pl.ds(pl.multiple_of(r * capp, capp), capp)
@@ -600,35 +590,40 @@
 
     kept_copy = pltpu.make_async_copy(rbs.at[:capp, :], back.at[:capp, :], back_ss.at[0])
 
+    def gate_copy(r):
+        return remote(
+            gbs.at[r], g_back.at[r], gate_ss.at[r], gate_rs.at[r], "ep", lax.rem(ep + n - r, n)
+        )
+
+    g_kept = pltpu.make_async_copy(gbs.at[0], g_back.at[0], gate_ss.at[0])
+    gbs[...] = jnp.zeros_like(gbs)
+
     @pl.loop(0, groups)
     def _(g):
         slot = lax.rem(g, 2)
+        mine = pl.ds(pl.multiple_of(g * gr, gr), gr)
+        u_copy(g).wait()
+
+        @pl.when(g >= 1)
+        def _():
+            saved(g - 1).wait()
 
         @pl.when(g + 1 < groups)
         def _():
-            x_copy(g + 1).start()
             u_copy(g + 1).start()
 
-        x_copy(g).wait()
-        u_copy(g).wait()
-
-        @pl.when(g >= 1)
-        def _():
-            for copy in saved(g - 1):
-                copy.wait()
-
-        gate = xb[slot, :, width : width + 1].astype(F32) + xb[slot, :, width + 1 : width + 2].astype(F32)
-        rgb[...] = (gate * ub[slot].astype(F32)).astype(BF)
+        gate = jnp.concatenate([gate_column(gates, g * per + i, capp) for i in range(per)], axis=0)
+        rgb[mine, :] = (gate * ub[slot].astype(F32)).astype(BF)
 
         def hidden(at):
-            x = xb[slot, :, :width]
+            x = xb[mine, :]
             g_pre = lax.dot_general(x, w[0, at, :], nt_dims, preferred_element_type=F32)
             u_pre = lax.dot_general(x, w[1, at, :], nt_dims, preferred_element_type=F32)
-            grad = lax.dot_general(rgb[...], w[2, at, :], nt_dims, preferred_element_type=F32)
+            grad = lax.dot_general(rgb[mine, :], w[2, at, :], nt_dims, preferred_element_type=F32)
             sig = jax.nn.sigmoid(g_pre)
-            eb[0, :, at] = (g_pre * sig * u_pre).astype(BF)
-            eb[1, :, at] = (grad * u_pre * sig * (1.0 + g_pre * (1.0 - sig))).astype(BF)
-            eb[2, :, at] = (grad * g_pre * sig).astype(BF)
+            eb[2, mine, at] = (g_pre * sig * u_pre).astype(BF)
+            eb[0, mine, at] = (grad * u_pre * sig * (1.0 + g_pre * (1.0 - sig))).astype(BF)
+            eb[1, mine, at] = (grad * g_pre * sig).astype(BF)
 
         @pl.loop(0, units // 256)
         def _(c):
@@ -639,22 +634,26 @@
 
         def columns(c, total):
             at = pl.ds(pl.multiple_of(c * 256, 256), 256)
-            out = jnp.dot(eb[0], w[2, :, at], preferred_element_type=F32)
-            ob[:, at] = out.astype(BF)
-            grad = jnp.dot(eb[1], w[0, :, at], preferred_element_type=F32) + jnp.dot(
-                eb[2], w[1, :, at], preferred_element_type=F32
+            out = jnp.dot(eb[2, mine, :], w[2, :, at], preferred_element_type=F32)
+            grad = jnp.dot(eb[0, mine, :], w[0, :, at], preferred_element_type=F32) + jnp.dot(
+                eb[1, mine, :], w[1, :, at], preferred_element_type=F32
             )
-            rbs[pl.ds(pl.multiple_of(g * gr, gr), gr), at] = grad.astype(BF)
-            return total + jnp.sum(out * ub[slot, :, at].astype(F32), axis=1, keepdims=True)
+            rbs[mine, at] = grad.astype(BF)
+            total = total + jnp.sum(out * ub[slot, :, at].astype(F32), axis=1, keepdims=True)
+            ub[slot, :, at] = out.astype(BF)
+            return total
 
         total = lax.fori_loop(0, width // 256, columns, jnp.zeros((gr, 1), F32))
         hi = total.astype(BF).astype(F32)
         lane = lax.broadcasted_iota(jnp.int32, (gr, 128), 1)
-        rbs[pl.ds(pl.multiple_of(g * gr, gr), gr), width:] = jnp.where(
-            lane == 0, hi, jnp.where(lane == 1, total - hi, 0.0)
-        ).astype(BF)
-        for copy in saved(g):
-            copy.start()
+        terms = jnp.where(lane == 0, hi, jnp.where(lane == 1, total - hi, 0.0)).astype(BF)
+        pick = (
+            lax.broadcasted_iota(jnp.int32, (16, 128), 0) == lax.broadcasted_iota(jnp.int32, (16, 128), 1)
+        ).astype(F32).astype(BF)
+        turned = lax.dot_general(pick, terms, nt_dims, preferred_element_type=F32).astype(BF)
+        for i in range(per):
+            gbs[g * per + i, :, :capp] = turned[:, i * capp : (i + 1) * capp]
+        saved(g).start()
         for i in range(per):
             r = g * per + i
             if i == 0:
@@ -662,88 +661,207 @@
                 @pl.when(g == 0)
                 def _():
                     kept_copy.start()
+                    g_kept.start()
 
                 @pl.when(g > 0)
                 def _():
                     back_copy(r).start()
+                    gate_copy(r).start()
             else:
                 back_copy(r).start()
-        ring_step(g + 1)
-
-    for copy in saved(groups - 1):
-        copy.wait()
-
-    @pl.loop(groups + 1, n - 1)
+                gate_copy(r).start()
+
+        @pl.when(lax.rem(g, 2) == 1)
+        def _():
+            ring_step((g + 1) // 2)
+
+    def weight_rows(at):
+        for k in range(3):
+            for c in range(0, width, 512):
+                w[k, at, c : c + 512] = lax.dot_general(
+                    eb[k, :, at],
+                    (rgb if k == 2 else xb)[:, c : c + 512],
+                    first_dims,
+                    preferred_element_type=F32,
+                ).astype(BF)
+
+    @pl.loop(0, units // 256)
+    def _(c):
+        weight_rows(pl.ds(pl.multiple_of(c * 256, 256), 256))
+
+    if units % 256:
+        weight_rows(pl.ds(units // 256 * 256, units % 256))
+
+    dw_core = remote(
+        w.at[:, : 2 * quarter, :], dw_recv, dw_ss.at[0], dw_rs.at[0], "tp", core_peer
+    )
+    dw_core.start()
+    ring_step(groups // 2 + 1)
+    dw_core.wait()
+    dw_in = pltpu.make_async_copy(dw_recv, w.at[:, : 2 * quarter, :], dw_sem.at[0])
+    dw_in.start()
+    dw_in.wait()
+    for k in range(3):
+
+        @pl.loop(0, quarter // 32)
+        def _(c, k=k):
+            far = pl.ds(pl.multiple_of(2 * quarter + c * 32, 32), 32)
+            came = pl.ds(pl.multiple_of(quarter + c * 32, 32), 32)
+            w[k, far, :] = (w[k, far, :].astype(F32) + w[k, came, :].astype(F32)).astype(BF)
+
+    dw_far = remote(
+        w.at[:, 2 * quarter : 3 * quarter, :], dw_y, dw_ss.at[1], dw_rs.at[1], "tp", y_peer
+    )
+    dw_far.start()
+    for k in range(3):
+
+        @pl.loop(0, quarter // 32)
+        def _(c, k=k):
+            far = pl.ds(pl.multiple_of(3 * quarter + c * 32, 32), 32)
+            came = pl.ds(pl.multiple_of(c * 32, 32), 32)
+            w[k, far, :] = (w[k, far, :].astype(F32) + w[k, came, :].astype(F32)).astype(BF)
+
+    dw_keep = pltpu.make_async_copy(w.at[:, 3 * quarter :, :], dw_own, dw_sem.at[1])
+    dw_keep.start()
+
+    @pl.loop(groups // 2 + 2, n - 1)
     def _(step):
         ring_step(step)
 
-    for ring in (0, 2, 1, 3):
-        lo, hi = piece[ring]
+    for ring in order:
         mine = term(ring, ep)
-        ring_copy(ring, n - 2, 0).wait_recv()
-        base = (ring // 2) * units
-        gu_out[ring // 2, :, lo - base : hi - base] = mine + ring_recv[
-            ring, n - 2, :, : hi - lo
-        ].astype(F32)
+        ring_copy(ring, n % 2).wait_recv()
+        done = mine + ring_recv[ring, n % 2, :, : wide_of[ring]].astype(F32)
+        lo, hi = edges[ring], edges[ring + 1]
+        for k, out in enumerate((gu_out.at[0], gu_out.at[1], dn_out)):
+            a, b = max(lo, k * units), min(hi, (k + 1) * units)
+            if a < b:
+                out[:, a - k * units : b - k * units] = done[:, a - lo : b - lo].astype(BF)
     for ring in range(4):
-        for step in (n - 3, n - 2):
-            ring_copy(ring, step, step % 2).wait_send()
+        for slot in range(2):
+            ring_copy(ring, slot).wait_send()
+    g_kept.wait()
     kept_copy.wait()
+    saved(groups - 1).wait()
+    dw_keep.wait()
+    dw_far.wait()
 
     @pl.loop(1, n)
     def _(r):
         back_copy(r).wait()
-
-
-def routed_expert(n, n_tp, capp, x, u, weights, nt, pg):
-    total, wide = x.shape
-    width = u.shape[1]
+        gate_copy(r).wait()
+
+
+def routed_expert(n, n_tp, capp, x, u, weights, gates, nt, pg, og, sh):
+    total, width = x.shape
     units = 4 * weights[-1].shape[0]
     gr = total // 4
     rows = width // n
-    half = (units // 128 + 1) // 2 * 128
+    half = (3 * units // 128 + 3) // 4 * 128
     vmem = pl.BlockSpec(memory_space=pltpu.VMEM)
     hbm = pl.BlockSpec(memory_space=pl.ANY)
     dma = pltpu.SemaphoreType.DMA
     if rows % 128:
-        nt = nt.T
+        nt, og = nt.T, og.T
     return pl.pallas_call(
         functools.partial(middle_kernel, n, n_tp, capp),
         out_shape=(
-            jax.ShapeDtypeStruct((total, wide), BF),
             jax.ShapeDtypeStruct((total, width), BF),
+            jax.ShapeDtypeStruct((n, 16, 128), BF),
             jax.ShapeDtypeStruct((total, width), BF),
-            jax.ShapeDtypeStruct((3, total, units), BF),
-            jax.ShapeDtypeStruct((2, rows, units), F32),
+            jax.ShapeDtypeStruct((3, units // 2, width), BF),
+            jax.ShapeDtypeStruct((3, units // 4, width), BF),
+            jax.ShapeDtypeStruct((3, units // 4, width), BF),
+            jax.ShapeDtypeStruct((2, rows, units), BF),
+            jax.ShapeDtypeStruct((rows, units), BF),
         ),
-        in_specs=[hbm] * 10 + [vmem] * 2,
-        out_specs=[hbm] * 4 + [vmem],
+        in_specs=[hbm] * 10 + [vmem] * 5,
+        out_specs=[hbm] * 6 + [vmem] * 2,
         scratch_shapes=[
             pltpu.VMEM((3, units, width), BF),
-            pltpu.VMEM((2, gr, wide), BF),
+            pltpu.VMEM((total, width), BF),
             pltpu.VMEM((2, gr, width), BF),
-            pltpu.VMEM((gr, width), BF),
-            pltpu.VMEM((gr, width), BF),
-            pltpu.VMEM((3, gr, units), BF),
-            pltpu.VMEM((total, wide), BF),
-            pltpu.VMEM((4, n - 1, rows, half), BF),
+            pltpu.VMEM((total, width), BF),
+            pltpu.VMEM((3, total, units), BF),
+            pltpu.VMEM((total, width), BF),
+            pltpu.VMEM((n, 16, 128), BF),
+            pltpu.VMEM((4, 2, rows, half), BF),
             pltpu.VMEM((4, 2, rows, half), BF),
             dma((8,)),
+            dma,
             dma((2,)),
             dma((2,)),
-            dma((3,)),
             dma((4, 2)),
-            dma((4, n - 1)),
+            dma((4, 2)),
+            pltpu.SemaphoreType.REGULAR((4,)),
             dma((n,)),
             dma((n,)),
+            dma((n,)),
+            dma((n,)),
+            dma((2,)),
+            dma((2,)),
+            dma((2,)),
         ],
         compiler_params=pltpu.CompilerParams(
-            collective_id=1, has_side_effects=True, vmem_limit_bytes=60 * 2**20
+            collective_id=1, has_side_effects=True, vmem_limit_bytes=63 * 2**20
         ),
         cost_estimate=pl.CostEstimate(
             flops=2 * total * width * 6 * units, bytes_accessed=40 * 2**20, transcendentals=0
         ),
-    )(x, u, *weights, nt, pg)
+    )(x, u, *weights, gates, nt, pg, og, sh)
+
+
+def tp_total(
+    project, between, tp, core_send, core_recv, y_send, y_recv, summed,
+    core_ss, core_rs, y_ss, y_rs, g_ss, g_rs,
+):
+    core_peer, y_peer = flip(tp, 1), flip(tp, 2)
+    pieces, size = core_send.shape[0], core_send.shape[2]
+    half = pieces * size
+
+    def core_copy(i):
+        return remote(core_send.at[i], core_recv.at[i], core_ss.at[i], core_rs.at[i], "tp", core_peer)
+
+    def y_copy(i):
+        return remote(y_send.at[i], y_recv.at[i], y_ss.at[i], y_rs.at[i], "tp", y_peer)
+
+    def gather_copy(i, slot):
+        return remote(summed.at[slot, i], summed.at[slot, i], g_ss.at[i], g_rs.at[i], "tp", core_peer)
+
+    me, other = tp % 2, core_peer % 2
+    for i in range(pieces):
+        core_send[i] = project(other * half, i, size).astype(BF)
+        core_copy(i).start()
+        own = project(me * half, i, size)
+        core_copy(i).wait_recv()
+        y_send[i] = (own + core_recv[i].astype(F32)).astype(BF)
+        y_copy(i).start()
+    between()
+    for i in range(pieces):
+        y_copy(i).wait_recv()
+        summed[me, i] = (y_send[i].astype(F32) + y_recv[i].astype(F32)).astype(BF)
+        gather_copy(i, me).start()
+    for i in range(pieces):
+        gather_copy(i, other).wait_recv()
+    for i in range(pieces):
+        core_copy(i).wait_send()
+        y_copy(i).wait_send()
+        gather_copy(i, me).wait_send()
+
+
+def blocks_at_once(n, capp):
+    per = 1
+    while 2 * per * capp <= 128 and n % (2 * per) == 0:
+        per *= 2
+    return per
+
+
+def gate_column(tiles, r, capp):
+    ones = jnp.ones((16, 128), BF)
+    return lax.dot_general(
+        tiles[r, :, :capp], ones, (((0,), (0,)), ((), ())), preferred_element_type=F32
+    )[:, :1]
+
 
 def front_kernel(
     n,
@@ -758,7 +876,8 @@
     sine,
     prefix,
     ow,
-    up_sent,
+    place,
+    cot,
     gu_own,
     dn_own,
     up_rows,
@@ -770,6 +889,7 @@
     ctx,
     mid,
     nt,
+    up_sent,
     core_send,
     core_recv,
     y_send,
@@ -796,13 +916,30 @@
 
     def up_copy(r, way):
         to = lax.rem(ep + r, n) if way == "out" else lax.rem(ep + n - r, n)
-        at = pl.ds(r * capp, capp)
+        at = pl.ds(pl.multiple_of(r * capp, capp), capp)
         return remote(up_sent.at[at, :], up_rows.at[at, :], up_ss.at[r], up_rs.at[r], "ep", to)
 
-    for r in range(1, n):
-        up_copy(r, "out").start()
     kept = pltpu.make_async_copy(up_sent.at[:capp, :], up_rows.at[:capp, :], up_ss.at[0])
-    kept.start()
+    per = blocks_at_once(n, capp)
+    size = per * capp
+
+    @pl.loop(0, n // per)
+    def _(b):
+        at = pl.ds(pl.multiple_of(b * size, size), size)
+        up_sent[at, :] = jnp.dot(place[at, :], cot[...], preferred_element_type=F32).astype(BF)
+        for i in range(per):
+            if i == 0:
+
+                @pl.when(b == 0)
+                def _():
+                    kept.start()
+
+                @pl.when(b > 0)
+                def _():
+                    up_copy(b * per, "out").start()
+            else:
+                up_copy(b * per + i, "out").start()
+
     w_copies = [
         remote(dn_own, dn_b, w_ss.at[0], w_rs.at[0], "tp", y_peer),
         remote(dn_own, dn_a, w_ss.at[1], w_rs.at[1], "tp", core_peer),
@@ -853,45 +990,19 @@
                 e.astype(BF), qkv[2, :, lanes], preferred_element_type=F32
             ).astype(BF)
 
-    pieces = 4
-    half = width // 2
-    size = half // pieces
-    mine, theirs = (tp % 2) * half, (core_peer % 2) * half
-
-    def project(base, i):
+    pieces, size = core_send.shape[0], core_send.shape[2]
+    half = pieces * size
+
+    def project(base, i, size):
         at = pl.ds(pl.multiple_of(base + i * size, size), size)
         return lax.dot_general(
             ctx[...], ow[at, :], (((1,), (1,)), ((), ())), preferred_element_type=F32
         )
 
-    def core_copy(i):
-        return remote(
-            core_send.at[i], core_recv.at[i], core_ss.at[i], core_rs.at[i], "tp", core_peer
-        )
-
-    def y_copy(i):
-        return remote(y_send.at[i], y_recv.at[i], y_ss.at[i], y_rs.at[i], "tp", y_peer)
-
-    def gather_copy(i, way):
-        slot = (tp % 2) if way == "out" else (core_peer % 2)
-        return remote(
-            summed.at[slot, i], summed.at[slot, i], g_ss.at[i], g_rs.at[i], "tp", core_peer
-        )
-
-    for i in range(pieces):
-        core_send[i] = project(theirs, i).astype(BF)
-        core_copy(i).start()
-    for i in range(pieces):
-        own = project(mine, i)
-        core_copy(i).wait_recv()
-        y_send[i] = (own + core_recv[i].astype(F32)).astype(BF)
-        y_copy(i).start()
-    for i in range(pieces):
-        y_copy(i).wait_recv()
-        summed[tp % 2, i] = (y_send[i].astype(F32) + y_recv[i].astype(F32)).astype(BF)
-        gather_copy(i, "out").start()
-    for i in range(pieces):
-        gather_copy(i, "in").wait_recv()
+    tp_total(
+        project, lambda: None, tp, core_send, core_recv, y_send, y_recv, summed,
+        core_ss, core_rs, y_ss, y_rs, g_ss, g_rs,
+    )
 
     @pl.loop(0, tokens // 32)
     def _(m):
@@ -906,10 +1017,6 @@
         factor = lax.rsqrt(total * (1.0 / width) + EPSILON)
         nt[at, :] = (mid[at, :] * factor * gain2[...]).astype(BF)
 
-    for i in range(pieces):
-        core_copy(i).wait_send()
-        y_copy(i).wait_send()
-        gather_copy(i, "out").wait_send()
     for copy in w_copies:
         copy.wait()
     kept.wait()
@@ -917,7 +1024,7 @@
         up_copy(r, "in").wait()
 
 
-def front(n, n_tp, capp, hidden, gain1, gain2, w, bias, cosine, sine, prefix, ow, up_sent, gu_own, dn_own):
+def front(n, n_tp, capp, hidden, gain1, gain2, w, bias, cosine, sine, prefix, ow, place, cot, gu_own, dn_own):
     tokens, width = hidden.shape
     lw = ow.shape[1]
     quarter = dn_own.shape[0]
@@ -927,7 +1034,7 @@
     return pl.pallas_call(
         functools.partial(front_kernel, n, n_tp, capp),
         out_shape=(
-            jax.ShapeDtypeStruct(up_sent.shape, BF),
+            jax.ShapeDtypeStruct((n * capp, width), BF),
             jax.ShapeDtypeStruct((2, quarter, width), BF),
             jax.ShapeDtypeStruct((quarter, width), BF),
             jax.ShapeDtypeStruct((quarter, width), BF),
@@ -937,9 +1044,10 @@
             jax.ShapeDtypeStruct((tokens, width), F32),
             jax.ShapeDtypeStruct((tokens, width), BF),
         ),
-        in_specs=[vmem] * 9 + [hbm] * 3,
+        in_specs=[vmem] * 11 + [hbm] * 2,
         out_specs=[hbm] * 4 + [vmem] * 5,
         scratch_shapes=[
+            pltpu.VMEM((n * capp, width), BF),
             pltpu.VMEM((4, tokens, width // 8), BF),
             pltpu.VMEM((4, tokens, width // 8), BF),
             pltpu.VMEM((4, tokens, width // 8), BF),
@@ -962,7 +1070,7 @@
         cost_estimate=pl.CostEstimate(
             flops=2 * tokens * width * 4 * lw, bytes_accessed=30 * 2**20, transcendentals=0
         ),
-    )(hidden, gain1, gain2, w, bias, cosine, sine, prefix, ow, up_sent, gu_own, dn_own)
+    )(hidden, gain1, gain2, w, bias, cosine, sine, prefix, ow, place, cot, gu_own, dn_own)
 
 
 def dispatch_kernel(
@@ -979,6 +1087,7 @@
     gu_own,
     dn_b,
     x_rows,
+    g_rows,
     gu_b,
     gu_c,
     dn_c,
@@ -989,9 +1098,13 @@
     sh,
     part,
     sback,
+    sgrad,
     x_send,
+    g_send,
     x_ss,
     x_rs,
+    gate_ss,
+    gate_rs,
     w_ss,
     w_rs,
 ):
@@ -1007,6 +1120,37 @@
     w_on = remote(dn_b, dn_c, w_ss.at[1], w_rs.at[1], "tp", core_peer)
     w_on.start()
 
+    def x_copy(r, way):
+        to = lax.rem(ep + r, n) if way == "out" else lax.rem(ep + n - r, n)
+        at = pl.ds(pl.multiple_of(r * capp, capp), capp)
+        return remote(x_send.at[at, :], x_rows.at[at, :], x_ss.at[r], x_rs.at[r], "ep", to)
+
+    def gate_copy(r, way):
+        to = lax.rem(ep + r, n) if way == "out" else lax.rem(ep + n - r, n)
+        return remote(g_send.at[r], g_rows.at[r], gate_ss.at[r], gate_rs.at[r], "ep", to)
+
+    kept = pltpu.make_async_copy(x_send.at[:capp, :], x_rows.at[:capp, :], x_ss.at[0])
+    g_kept = pltpu.make_async_copy(g_send.at[0], g_rows.at[0], gate_ss.at[0])
+    per = blocks_at_once(n, capp)
+    size = per * capp
+
+    @pl.loop(0, n // per)
+    def _(b):
+        at = pl.ds(pl.multiple_of(b * size, size), size)
+        x_send[at, :] = jnp.dot(place[at, :], nt[...], preferred_element_type=F32).astype(BF)
+        for i in range(per):
+            if i == 0:
+
+                @pl.when(b == 0)
+                def _():
+                    kept.start()
+
+                @pl.when(b > 0)
+                def _():
+                    x_copy(b * per, "out").start()
+            else:
+                x_copy(b * per + i, "out").start()
+
     logits = jnp.dot(nt[...], router[...], preferred_element_type=F32)
     lane = lax.broadcasted_iota(jnp.int32, logits.shape, 1)
     chosen = jnp.where(lane < n_exp, logits, -1e30)
@@ -1016,49 +1160,35 @@
     probs[...] = prob
     hi = prob.astype(BF)
     lo = (prob - hi.astype(F32)).astype(BF)
-
-    def x_copy(r, way):
-        to = lax.rem(ep + r, n) if way == "out" else lax.rem(ep + n - r, n)
-        at = pl.ds(pl.multiple_of(r * capp, capp), capp)
-        return remote(x_send.at[at, :], x_rows.at[at, :], x_ss.at[r], x_rs.at[r], "ep", to)
-
-    kept = pltpu.make_async_copy(x_send.at[:capp, :], x_rows.at[:capp, :], x_ss.at[0])
-
-    per = 1
-    while 2 * per * capp <= 128 and n % (2 * per) == 0:
-        per *= 2
-    size = per * capp
-
-    @pl.loop(0, n // per)
-    def _(b):
-        at = pl.ds(pl.multiple_of(b * size, size), size)
-        where = place[at, :]
-        x_send[at, :width] = jnp.dot(where, nt[...], preferred_element_type=F32).astype(BF)
-        row = lax.broadcasted_iota(jnp.int32, (size, 128), 0) + b * size
-        spot = lax.broadcasted_iota(jnp.int32, (size, 128), 1)
-        expert = lax.rem(row // capp + ep * (n_exp // n), n_exp)
-        pick = spot == expert
+    g_send[...] = jnp.zeros_like(g_send)
+    across = (((0,), (1,)), ((), ()))
+
+    @pl.loop(0, n)
+    def _(r):
+        where = place[pl.ds(pl.multiple_of(r * capp, capp), capp), :]
+        expert = lax.rem(r + ep, n)
+        pick = lax.broadcasted_iota(jnp.int32, (128, capp), 0) == expert
         g_hi = jnp.sum(
-            jnp.where(pick, jnp.dot(where, hi, preferred_element_type=F32), 0.0), axis=1, keepdims=True
+            jnp.where(pick, lax.dot_general(hi, where, across, preferred_element_type=F32), 0.0),
+            axis=0,
+            keepdims=True,
         )
         g_lo = jnp.sum(
-            jnp.where(pick, jnp.dot(where, lo, preferred_element_type=F32), 0.0), axis=1, keepdims=True
+            jnp.where(pick, lax.dot_general(lo, where, across, preferred_element_type=F32), 0.0),
+            axis=0,
+            keepdims=True,
         )
-        gate[at, :] = g_hi + g_lo
-        x_send[at, width:] = jnp.where(spot == 0, g_hi, jnp.where(spot == 1, g_lo, 0.0)).astype(BF)
-        for i in range(per):
-            r = b * per + i
-            if i == 0:
-
-                @pl.when(b == 0)
-                def _():
-                    kept.start()
-
-                @pl.when(b > 0)
-                def _():
-                    x_copy(r, "out").start()
-            else:
-                x_copy(r, "out").start()
+        term = lax.broadcasted_iota(jnp.int32, (16, capp), 0)
+        g_send[r, :, :capp] = jnp.where(term == 0, g_hi, jnp.where(term == 1, g_lo, 0.0)).astype(BF)
+        gate[r] = g_hi + g_lo
+
+        @pl.when(r == 0)
+        def _():
+            g_kept.start()
+
+        @pl.when(r > 0)
+        def _():
+            gate_copy(r, "out").start()
 
     @pl.loop(0, tokens // 64)
     def _(m):
@@ -1091,20 +1221,27 @@
 
     nt_dims = (((1,), (1,)), ((), ()))
 
-    @pl.loop(0, width // 256)
-    def _(c):
+    share = probs[:, n_exp : n_exp + 1]
+
+    def columns(c, total):
         at = pl.ds(pl.multiple_of(c * 256, 256), 256)
-        part[:, at] = lax.dot_general(sh[...], sdn[at, :], nt_dims, preferred_element_type=F32)
+        out = lax.dot_general(sh[...], sdn[at, :], nt_dims, preferred_element_type=F32)
+        part[:, at] = (share * out).astype(BF)
         sback[:, at] = lax.dot_general(
             pg[:, :units], sgu[0, at, :], nt_dims, preferred_element_type=F32
         ) + lax.dot_general(pg[:, units:], sgu[1, at, :], nt_dims, preferred_element_type=F32)
+        return total + jnp.sum(cot[:, at].astype(F32) * out, axis=1, keepdims=True)
+
+    sgrad[...] = lax.fori_loop(0, width // 256, columns, jnp.zeros((tokens, 1), F32))
 
     w_on.wait()
     w_far.wait()
     kept.wait()
+    g_kept.wait()
 
     @pl.loop(1, n)
     def _(r):
+        gate_copy(r, "in").wait()
         x_copy(r, "in").wait()
 
 
@@ -1118,22 +1255,27 @@
     return pl.pallas_call(
         functools.partial(dispatch_kernel, n, n_tp, capp, n_exp),
         out_shape=(
-            jax.ShapeDtypeStruct((total, width + 128), BF),
+            jax.ShapeDtypeStruct((total, width), BF),
+            jax.ShapeDtypeStruct((n, 16, 128), BF),
             jax.ShapeDtypeStruct(gu_own.shape, BF),
             jax.ShapeDtypeStruct(gu_own.shape, BF),
             jax.ShapeDtypeStruct(dn_b.shape, BF),
             jax.ShapeDtypeStruct((tokens, 128), F32),
-            jax.ShapeDtypeStruct((total, 1), F32),
+            jax.ShapeDtypeStruct((n, 1, capp), F32),
             jax.ShapeDtypeStruct((tokens, width), BF),
             jax.ShapeDtypeStruct((tokens, 2 * units), BF),
             jax.ShapeDtypeStruct((tokens, units), BF),
+            jax.ShapeDtypeStruct((tokens, width), BF),
             jax.ShapeDtypeStruct((tokens, width), F32),
-            jax.ShapeDtypeStruct((tokens, width), F32),
+            jax.ShapeDtypeStruct((tokens, 1), F32),
         ),
         in_specs=[vmem] * 6 + [hbm] * 2,
-        out_specs=[hbm] * 4 + [vmem] * 7,
+        out_specs=[hbm] * 5 + [vmem] * 8,
         scratch_shapes=[
-            pltpu.VMEM((total, width + 128), BF),
+            pltpu.VMEM((total, width), BF),
+            pltpu.VMEM((n, 16, 128), BF),
+            dma((n,)),
+            dma((n,)),
             dma((n,)),
             dma((n,)),
             dma((3,)),
@@ -1146,6 +1288,244 @@
             flops=2 * tokens * width * 6 * units, bytes_accessed=40 * 2**20, transcendentals=0
         ),
     )(nt, place, router, cot, sgu, sdn, gu_own, dn_b)
+
+def backward_kernel(
+    n,
+    n_tp,
+    capp,
+    n_exp,
+    back,
+    g_back,
+    place_t,
+    sback,
+    sgrad,
+    probs,
+    router,
+    nt,
+    mid,
+    cot,
+    gain2,
+    qkv,
+    ow,
+    cosine,
+    sine,
+    prefix,
+    o_sent,
+    o_rows,
+    ag,
+    lg,
+    bias,
+    small,
+    core_send,
+    core_recv,
+    y_send,
+    y_recv,
+    summed,
+    few_send,
+    few_recv,
+    ng,
+    cg,
+    dk,
+    dv,
+    o_ss,
+    o_rs,
+    core_ss,
+    core_rs,
+    y_ss,
+    y_rs,
+    g_ss,
+    g_rs,
+    few_ss,
+    few_rs,
+):
+    ep = lax.axis_index("ep")
+    tp = lax.axis_index("tp")
+    tokens, width = nt.shape
+    total = back.shape[0]
+    lw = ow.shape[1]
+    heads = lw // HEAD_DIM
+    core_peer, y_peer = flip(tp, 1), flip(tp, 2)
+    greet(n, n_tp, ep, tp)
+
+    def o_copy(r):
+        at = pl.ds(pl.multiple_of(r * capp, capp), capp)
+        return remote(
+            o_sent.at[at, :], o_rows.at[at, :], o_ss.at[r], o_rs.at[r], "ep", lax.rem(ep + n - r, n)
+        )
+
+    kept = pltpu.make_async_copy(o_sent.at[:capp, :], o_rows.at[:capp, :], o_ss.at[0])
+
+    for r in range(1, n):
+        o_copy(r).start()
+    kept.start()
+
+    row = lax.broadcasted_iota(jnp.int32, (total, 128), 0)
+    spot = lax.broadcasted_iota(jnp.int32, (total, 128), 1)
+    expert = lax.rem(row // capp + ep * (n_exp // n), n_exp)
+    gg = jnp.concatenate([gate_column(g_back, r, capp) for r in range(n)], axis=0)
+    few = jnp.dot(
+        place_t[...], jnp.where(spot == expert, gg, 0.0).astype(BF), preferred_element_type=F32
+    )
+    lane = lax.broadcasted_iota(jnp.int32, (tokens, 128), 1)
+    few_send[0] = jnp.where(lane == n_exp, sgrad[...], few).astype(BF)
+    few_core = remote(few_send.at[0], few_recv.at[0], few_ss.at[0], few_rs.at[0], "tp", core_peer)
+    few_core.start()
+
+    def project(base, i, size):
+        at = pl.ds(pl.multiple_of(base + i * size, size), size)
+        return sback[:, at] + jnp.dot(place_t[...], back[:, at], preferred_element_type=F32)
+
+    def between():
+        few_core.wait()
+        few_send[1] = (few_send[0].astype(F32) + few_recv[0].astype(F32)).astype(BF)
+        few_y = remote(few_send.at[1], few_recv.at[1], few_ss.at[1], few_rs.at[1], "tp", y_peer)
+        few_y.start()
+        few_y.wait()
+
+    tp_total(
+        project, between, tp, core_send, core_recv, y_send, y_recv, summed,
+        core_ss, core_rs, y_ss, y_rs, g_ss, g_rs,
+    )
+
+    prob = jnp.where(lane < n_exp, probs[...], 0.0)
+    share = probs[:, n_exp : n_exp + 1]
+    grads = few_send[1].astype(F32) + few_recv[1].astype(F32)
+    inner = jnp.sum(prob * grads, axis=1, keepdims=True)
+    gate_in = grads * share * (1.0 - share)
+    few_send[0] = jnp.where(
+        lane < n_exp, prob * (grads - inner), jnp.where(lane == n_exp, gate_in, 0.0)
+    ).astype(BF)
+    pieces, size = summed.shape[1], summed.shape[3]
+    for j in range(2):
+        for i in range(pieces):
+            at = slice((j * pieces + i) * size, (j * pieces + i + 1) * size)
+            ng[:, at] = summed[j, i].astype(F32) + lax.dot_general(
+                few_send[0], router[at, :], (((1,), (1,)), ((), ())), preferred_element_type=F32
+            )
+
+    step = 32
+
+    def norm_rows(m, acc):
+        at = pl.ds(pl.multiple_of(m * step, step), step)
+        h = mid[at, :]
+        grad = ng[at, :]
+        factor = lax.rsqrt(jnp.sum(h * h, axis=1, keepdims=True) * (1.0 / width) + EPSILON)
+        scaled = grad * gain2[...]
+        mean = jnp.sum(scaled * h, axis=1, keepdims=True) * (1.0 / width)
+        ag[at, :] = (
+            cot[at, :].astype(F32) + factor * scaled - h * (factor * factor * factor) * mean
+        ).astype(BF)
+        return acc + jnp.sum((grad * h * factor).reshape(step // 8, 8, width), axis=0)
+
+    acc = lax.fori_loop(0, tokens // step, norm_rows, jnp.zeros((8, width), F32))
+
+    @pl.loop(0, lw // 256)
+    def _(c):
+        at = pl.ds(pl.multiple_of(c * 256, 256), 256)
+        cg[:, at] = jnp.dot(ag[...], ow[:, at], preferred_element_type=F32).astype(BF)
+
+    dk[...] = jnp.zeros_like(dk)
+    dv[...] = jnp.zeros_like(dv)
+    first_dims, last_dims = (((0,), (0,)), ((), ())), (((1,), (1,)), ((), ()))
+
+    def attend(m, sums):
+        at = pl.ds(pl.multiple_of(m * 128, 128), 128)
+        row = lax.broadcasted_iota(jnp.int32, (128, tokens), 0) + m * 128
+        col = lax.broadcasted_iota(jnp.int32, (128, tokens), 1)
+        visible = (col <= row) | (col < prefix[...])
+        parts = []
+        for i in range(heads):
+            lanes = slice(i * HEAD_DIM, (i + 1) * HEAD_DIM)
+            q, grad = qkv[0, at, lanes], cg[at, lanes]
+            s = lax.dot_general(q, qkv[1, :, lanes], last_dims, preferred_element_type=F32)
+            s = jnp.where(visible, s * HEAD_DIM ** (-0.5), -1e30)
+            e = jnp.exp(s - jnp.max(s, axis=1, keepdims=True))
+            e = e * (1.0 / jnp.sum(e, axis=1, keepdims=True))
+            dp = lax.dot_general(grad, qkv[2, :, lanes], last_dims, preferred_element_type=F32)
+            delta = jnp.sum(e * dp, axis=1, keepdims=True)
+            ds = (e * (dp - delta)).astype(BF)
+            dv[:, lanes] += lax.dot_general(e.astype(BF), grad, first_dims, preferred_element_type=F32)
+            dk[:, lanes] += lax.dot_general(ds, q, first_dims, preferred_element_type=F32)
+            dq = jnp.dot(ds, qkv[1, :, lanes], preferred_element_type=F32) * HEAD_DIM ** (-0.5)
+            dq = dq * cosine[at, :] - pltpu.roll(dq, HEAD_DIM // 2, 1) * sine[at, :]
+            lg[at, lanes] = dq.astype(BF)
+            parts.append(jnp.sum(dq.reshape(16, 8, HEAD_DIM), axis=0))
+        return sums + jnp.concatenate(parts, axis=1)
+
+    sums = lax.fori_loop(0, tokens // 128, attend, jnp.zeros((8, lw), F32))
+    bias[:, :lw] = jnp.sum(sums, axis=0, keepdims=True)
+    for i in range(heads):
+        lanes = slice(i * HEAD_DIM, (i + 1) * HEAD_DIM)
+        grad = dk[:, lanes] * HEAD_DIM ** (-0.5)
+        grad = grad * cosine[...] - pltpu.roll(grad, HEAD_DIM // 2, 1) * sine[...]
+        at = slice(lw + i * HEAD_DIM, lw + (i + 1) * HEAD_DIM)
+        lg[:, at] = grad.astype(BF)
+        bias[:, at] = jnp.sum(grad, axis=0, keepdims=True)
+    lg[:, 2 * lw :] = dv[...].astype(BF)
+    bias[:, 2 * lw :] = jnp.sum(dv[...], axis=0, keepdims=True)
+
+    wide = small.shape[0]
+    gain_row = jnp.sum(acc, axis=0, keepdims=True)
+    for c in range(0, width, 512):
+        at = slice(c, c + 512)
+        rows = lax.dot_general(few_send[0], nt[:, at], first_dims, preferred_element_type=F32)[:wide]
+        index = lax.broadcasted_iota(jnp.int32, rows.shape, 0)
+        small[:, at] = jnp.where(index == n_exp + 1, gain_row[:, at], rows).astype(BF)
+
+    kept.wait()
+    for r in range(1, n):
+        o_copy(r).wait()
+
+
+def backward(n, n_tp, capp, n_exp, back, g_back, place_t, sback, sgrad, probs, router, nt, mid, cot, gain2, qkv, ow, cosine, sine, prefix, o_sent):
+    tokens, width = nt.shape
+    lw = ow.shape[1]
+    wide = -(-(n_exp + 2) // 16) * 16
+    vmem = pl.BlockSpec(memory_space=pltpu.VMEM)
+    hbm = pl.BlockSpec(memory_space=pl.ANY)
+    dma = pltpu.SemaphoreType.DMA
+    piece = (4, tokens, width // 8)
+    return pl.pallas_call(
+        functools.partial(backward_kernel, n, n_tp, capp, n_exp),
+        out_shape=(
+            jax.ShapeDtypeStruct(o_sent.shape, BF),
+            jax.ShapeDtypeStruct((tokens, width), BF),
+            jax.ShapeDtypeStruct((tokens, 3 * lw), BF),
+            jax.ShapeDtypeStruct((1, 3 * lw), F32),
+            jax.ShapeDtypeStruct((wide, width), BF),
+        ),
+        in_specs=[vmem] * 16 + [hbm],
+        out_specs=[hbm] + [vmem] * 4,
+        scratch_shapes=[
+            pltpu.VMEM(piece, BF),
+            pltpu.VMEM(piece, BF),
+            pltpu.VMEM(piece, BF),
+            pltpu.VMEM(piece, BF),
+            pltpu.VMEM((2,) + piece, BF),
+            pltpu.VMEM((2, tokens, 128), BF),
+            pltpu.VMEM((2, tokens, 128), BF),
+            pltpu.VMEM((tokens, width), F32),
+            pltpu.VMEM((tokens, lw), BF),
+            pltpu.VMEM((tokens, lw), F32),
+            pltpu.VMEM((tokens, lw), F32),
+            dma((n,)),
+            dma((n,)),
+            dma((4,)),
+            dma((4,)),
+            dma((4,)),
+            dma((4,)),
+            dma((4,)),
+            dma((4,)),
+            dma((2,)),
+            dma((2,)),
+        ],
+        compiler_params=pltpu.CompilerParams(
+            collective_id=4, has_side_effects=True, vmem_limit_bytes=60 * 2**20
+        ),
+        cost_estimate=pl.CostEstimate(
+            flops=2 * tokens * width * 4 * lw, bytes_accessed=30 * 2**20, transcendentals=0
+        ),
+    )(back, g_back, place_t, sback, sgrad, probs, router, nt, mid, cot, gain2, qkv, ow, cosine, sine, prefix, o_sent)
 
 
 def body(
@@ -1200,16 +1580,20 @@
     for k in range(1, top):
         place = place | (dest[k][None, :] == row_ids)
     place = place.astype(BF)
-
-    up_sent = mm(place, cotangent, 1, 0).astype(BF)
-
-    upstream = cotangent.astype(F32)
+    dest_t = dest.T
+    place_t = dest_t[:, :1] == row_ids.T
+    for k in range(1, top):
+        place_t = place_t | (dest_t[:, k : k + 1] == row_ids.T)
+    place_t = place_t.astype(BF)
+
+
     residual_in = hidden.astype(F32)
     factor_one = norm_factor(residual_in)
     cosine, sine_val = angle_tables(tokens, head_size)
     cos_all = jnp.concatenate([cosine[:, 0], cosine[:, 0]], axis=1)
     sin_all = jnp.concatenate([-sine_val[:, 0], sine_val[:, 0]], axis=1)
     w_t = jnp.transpose(qkv_weight, (1, 0, 2))
+    prefix_row = jnp.broadcast_to(prefix[None], (1, tokens))
     gu_own = jnp.transpose(expert_gate_up[0], (1, 2, 0))
     dn_own = jnp.transpose(expert_down[0], (1, 0))
     up_rows, gu_a, dn_a, dn_b, normed_one, qkv, context, middle, normed_two = front(
@@ -1223,20 +1607,18 @@
         qkv_bias,
         cos_all,
         sin_all,
-        jnp.broadcast_to(prefix[None], (1, tokens)),
+        prefix_row,
         out_weight,
-        up_sent,
+        place,
+        cotangent,
         gu_own,
         dn_own,
     )
-    factor_two = norm_factor(middle)
-
-    row_expert = lax.rem(row_ids // part_pad + ep_i * expert_local, n_exp)
-    own = (row_expert == jnp.arange(n_exp, dtype=jnp.int32)[None, :]).astype(F32)
+
     router_all = jnp.concatenate(
         [router_weight, share_gate[:, None], jnp.zeros((width, 127 - n_exp), BF)], axis=1
     )
-    got, gu_b, gu_c, dn_c, probs_all, gate_sent, shared_out_grad, pre_grad, shared_hidden, shared_part, shared_back = (
+    got, gates, gu_b, gu_c, dn_c, probs_all, gate_sent, shared_out_grad, pre_grad, shared_hidden, scaled_part, shared_back, scale_grad = (
         dispatch(
             n_ep,
             n_tp,
@@ -1252,104 +1634,50 @@
             dn_b,
         )
     )
-    router_probs = probs_all[:, :n_exp]
-    share_scale = probs_all[:, n_exp]
-    scale_grad_part = jnp.sum(upstream * shared_part, axis=1)
-    shared_down_grad = lax.psum_scatter(
-        mm(shared_out_grad, shared_hidden, 0, 0).astype(BF), "ep", scatter_dimension=0, tiled=True
-    ).astype(F32)
-
-    back_rows, e_out, row_grad, e_all, gu_grad = routed_expert(
+    back_rows, back_gates, e_out, _, dw_own, dw_y, gu_grad, shared_down_grad = routed_expert(
         n_ep,
         n_tp,
         part_pad,
         got,
         up_rows,
         (gu_a, gu_c, gu_b, gu_own, dn_a, dn_c, dn_b, dn_own),
+        gates,
         normed_two,
         pre_grad,
+        shared_out_grad,
+        shared_hidden,
     )
-    shared_gate_up_grad = jnp.transpose(gu_grad, (1, 0, 2))
-    out_rows = exchange(e_out, n_ep, True)
-    whole_rows = got[:, :width]
-    quarter = dn_own.shape[0]
-    pairs = ((e_all[1], whole_rows), (e_all[2], whole_rows), (e_all[0], row_grad))
-    weight_grads = []
-    for left, right in pairs:
-        came = swap(mm(left[:, : 2 * quarter], right, 0, 0).astype(BF), 1, n_tp)
-        on = swap(
-            (
-                mm(left[:, 2 * quarter : 3 * quarter], right, 0, 0) + came[quarter:].astype(F32)
-            ).astype(BF),
-            2,
-            n_tp,
-        )
-        weight_grads.append(
-            mm(left[:, 3 * quarter :], right, 0, 0) + came[:quarter].astype(F32) + on.astype(F32)
-        )
-    expert_down_grad = jnp.transpose(weight_grads[2], (1, 0))[None]
-    expert_gate_up_grad = jnp.transpose(jnp.stack(weight_grads[:2], axis=0), (2, 0, 1))[None]
-
-    weighted_place = (place.astype(F32) * gate_sent).astype(BF)
-    routed = mm(weighted_place, out_rows, 0, 0)
-    out_cols = tp_scatter(share_scale[:, None] * shared_part + routed, n_tp)
-    output = (lax.dynamic_slice_in_dim(middle, col_start, cols, 1) + out_cols).astype(BF)
-    gate_grad_row = back_rows[:, width : width + 1].astype(F32) + back_rows[:, width + 1 : width + 2].astype(F32)
-    prob_part = mm(place, (gate_grad_row * own).astype(BF), 0, 0)
-    few = tp_sum(
-        jnp.concatenate(
-            [prob_part, scale_grad_part[:, None], jnp.zeros((tokens, 256 - n_exp - 1), F32)], axis=1
-        ),
+    shared_gate_up_grad = jnp.transpose(gu_grad, (1, 0, 2)).astype(F32)
+    shared_down_grad = shared_down_grad.astype(F32)
+    dw = dw_own.astype(F32) + dw_y.astype(F32)
+    expert_down_grad = jnp.transpose(dw[2], (1, 0))[None]
+    expert_gate_up_grad = jnp.transpose(dw[:2], (2, 0, 1))[None]
+
+    out_rows, attn_grad, linear_grad, bias_grad, small = backward(
+        n_ep,
         n_tp,
+        part_pad,
+        n_exp,
+        back_rows,
+        back_gates,
+        place_t,
+        shared_back,
+        scale_grad,
+        probs_all,
+        router_all,
+        normed_two,
+        middle,
+        cotangent,
+        mlp_gain[None],
+        qkv,
+        out_weight,
+        cos_all,
+        sin_all,
+        prefix_row,
+        e_out,
     )
-    normed_two_grad = tp_sum(shared_back + mm(place, back_rows[:, :width], 0, 0), n_tp)
-    prob_grad = few[:, :n_exp]
-    scale_grad = few[:, n_exp]
-    gate_in_grad = (scale_grad * share_scale * (1.0 - share_scale)).astype(BF)
-    logit_grad = (
-        router_probs * (prob_grad - jnp.sum(router_probs * prob_grad, axis=1, keepdims=True))
-    ).astype(BF)
-    normed_two_grad = (
-        normed_two_grad
-        + mm(logit_grad, router_weight, 1, 1)
-        + gate_in_grad.astype(F32)[:, None] * share_gate.astype(F32)[None, :]
-    )
-    small_two = mm(
-        jnp.concatenate([logit_grad, gate_in_grad[:, None]], axis=1), normed_two, 0, 0
-    )
-    mlp_gain_grad = jnp.sum(normed_two_grad * middle * factor_two, axis=0)
-    scaled = normed_two_grad * mlp_gain
-    middle_grad = upstream + factor_two * scaled - middle * (factor_two**3) * jnp.mean(
-        scaled * middle, axis=-1, keepdims=True
-    )
-    small_pad = -(-(n_exp + 2) // 16) * 16 - n_exp - 2
-    small = jnp.concatenate(
-        [small_two, mlp_gain_grad[None], jnp.zeros((small_pad, width), F32)], axis=0
-    ).astype(BF)
-
-    attn_grad = middle_grad.astype(BF)
-    context_grad = mm(attn_grad, out_weight, 1, 0).astype(BF).reshape(tokens, heads, head_size)
-    queries, key_rows, value_rows = (qkv[i].reshape(tokens, heads, head_size) for i in range(3))
-    scores = masked_scores(queries, key_rows, prefix[0], head_size)
-    attn_weights = jax.nn.softmax(scores, axis=-1)
-    prob_grad_att = jnp.einsum("qhd,khd->hqk", context_grad, value_rows, preferred_element_type=F32)
-    value_grad = jnp.einsum(
-        "hqk,qhd->khd", attn_weights.astype(BF), context_grad, preferred_element_type=F32
-    )
-    row_delta = jnp.sum(attn_weights * prob_grad_att, axis=-1, keepdims=True)
-    score_grad = (attn_weights * (prob_grad_att - row_delta)).astype(BF)
-    query_grad = jnp.einsum(
-        "hqk,khd->qhd", score_grad, key_rows, preferred_element_type=F32
-    ) * head_size ** (-0.5)
-    key_grad = jnp.einsum(
-        "hqk,qhd->khd", score_grad, queries, preferred_element_type=F32
-    ) * head_size ** (-0.5)
-    query_grad = rotate_backward(query_grad, cosine, sine_val)
-    key_grad = rotate_backward(key_grad, cosine, sine_val)
-    parts = [g.reshape(tokens, local_width) for g in (query_grad, key_grad, value_grad)]
-    bias_grad = jnp.concatenate([jnp.sum(g, axis=0) for g in parts])
-    linear_grad = jnp.concatenate([g.astype(BF) for g in parts], axis=1)
-    qkv_grad, out_weight_grad, input_grad, gain_one, bias_sum, small_sum = tail(
+    weighted_place = (place_t.astype(F32) * gate_sent.reshape(1, rows)).astype(BF)
+    qkv_grad, out_weight_grad, input_grad, output, gain_one, bias_sum, small_sum = tail(
         n_ep,
         n_tp,
         normed_one,
@@ -1360,9 +1688,13 @@
         lax.dynamic_slice_in_dim(hidden, col_start, cols, 1),
         factor_one,
         lax.dynamic_slice_in_dim(attn_gain, col_start, cols, 0)[None],
-        lax.dynamic_slice_in_dim(middle_grad, col_start, cols, 1),
-        bias_grad[None],
+        lax.dynamic_slice_in_dim(attn_grad, col_start, cols, 1),
+        bias_grad,
         small,
+        out_rows,
+        weighted_place,
+        scaled_part,
+        lax.dynamic_slice_in_dim(middle, col_start, cols, 1),
     )
     qkv_weight_grad = jnp.transpose(qkv_grad, (1, 0, 2))
     gain_one_sum = gain_one[0]

time: 908 us -> 734 us (0.81)
  Pallas kernels: 525 us -> 665 us
  waiting for transfers between devices: 121 us -> 0 us
  matrix products: 89.6 us -> 4.03 us
  other arithmetic: 58.2 us -> 18.8 us
  starting transfers between devices: 31.9 us -> 0 us
  local copies, waits for them, and re-layouts: 60.2 us -> 38.6 us
  between operations: 16.2 us -> 1.75 us
    ppermute x21 -> x0, waiting for transfers between devices: 121 us -> none  [the longest x7 83 us: exchange(): lax.ppermute(x[shift * rows:(shift + 1) * rows], 'ep', [(i, (i + step) %...]
    pallas_call x0 -> x1, Pallas kernels: none -> 115 us  [backward(): pl.pallas_call(functools.partial(backward_kernel, n, n_tp, capp, n_exp),...]
    dot_general x18 -> x1, matrix products: 80.3 us -> 4.03 us  [mm(): lax.dot_general(a, b, (((ca,), (cb,)), ((), ())), preferred_element_type=...]
    pallas_call x1, Pallas kernels: 207 us -> 247 us  [routed_expert(): pl.pallas_call(functools.partial(middle_kernel, n, n_tp, capp), out_shape...]
    ppermute x21 -> x0, starting transfers between devices: 31.9 us -> none  [the longest x7 22.9 us: exchange(): lax.ppermute(x[shift * rows:(shift + 1) * rows], 'ep', [(i, (i + step) %...]
    pallas_call x1, Pallas kernels: 127 us -> 105 us  [tail(): pl.pallas_call(functools.partial(tail_kernel, n, n_tp), out_shape=(jax.Sh...]
    convert_element_type x17 -> x4, other arithmetic: 26.9 us -> 5.88 us  [the longest x1 2.35 us: body(): (place_t.astype(F32) * gate_sent.reshape(1, rows)).astype(BF)]
    unnamed x127 -> x32, local copies, waits for them, and re-layouts: 29 us -> 19.5 us
  transfers between devices with their start and end apart: 22 -> 0, of which waited for: 9 -> 0; matrix products, arithmetic and copies ran while one was open for 18% -> 0% of each run, Pallas kernels for 14% -> 0%
where the time goes in v4:
time: 734 us; the launch traced here: 728 us
  Pallas kernels  665 us (91%)
  local copies, waits for them, and re-layouts  38.6 us (5%)
  other arithmetic  18.8 us (3%)
    pallas_call x1, Pallas kernels, routed_expert(): pl.pallas_call(functools.partial(middle_kernel, n, n_tp, capp), out_shape...  247 us
    pallas_call x1, Pallas kernels, backward(): pl.pallas_call(functools.partial(backward_kernel, n, n_tp, capp, n_exp),...  115 us
    pallas_call x1, Pallas kernels, dispatch(): pl.pallas_call(functools.partial(dispatch_kernel, n, n_tp, capp, n_exp),...  112 us
    pallas_call x1, Pallas kernels, tail(): pl.pallas_call(functools.partial(tail_kernel, n, n_tp), out_shape=(jax.Sh...  105 us
    pallas_call x1, Pallas kernels, front(): pl.pallas_call(functools.partial(front_kernel, n, n_tp, capp), out_shape=...  86.7 us
    unnamed x32, local copies, waits for them, and re-layouts  19.5 us

profile of v4, /device:TPU:0, one launch (start us, length us, event | category | flops | bytes accessed | tf_op | source)
XLA Modules:
  0.0 728.2 jit_solution(13658110087737579065)
XLA Ops:
  0.6 0.7 eq.135
  1.4 0.7 lt.36
  2.1 4.0 fusion.15
  6.2 0.0 copy-done.7
  6.3 1.9 fusion.10.place
  8.2 1.2 fusion.20
  9.4 1.1 pad_maximum_fusion
  11.2 0.6 broadcast_in_dim.42.prefix
  11.7 86.7 %shard_map.255 = (bf16[896,2048]{1,0:T(8,128)(2,1)}, bf16[2,352,2048]{2,1,0:T(8,128)(2,1)}, bf16[352,2048]{1,0:T(8,128)(2,1)}, bf16[352,2048]{1,0:T(8,128)(2,1)}...) custom-call(bf16[640,2048]{1,0:T(8,128)(2,1)} %hidden.1, ...), custom_call_target="tpu_custom_call" | custom-call | flops 5368709120 | bytes 31457280 | tf_op jit(solution)/shard_map/pallas_call | solution.py:1034
  98.4 0.0 copy-done.10
  98.4 0.3 broadcast_in_dim.49
  98.8 0.3 copy.32
  99.1 0.1 pad.2.clone
  99.2 1.1 maximum_maximum_fusion.router
  100.3 11.2 %copy.38 = bf16[2048,2,1408]{2,0,1:T(8,128)(2,1)} copy(bf16[2048,2,1408]{2,1,0:T(2,128)(2,1)} %param.24) | data formatting | bytes 23068672 | tf_op args[8]
  111.5 111.9 %shard_map.256 = (bf16[896,2048]{1,0:T(8,128)(2,1)}, bf16[8,16,128]{2,1,0:T(8,128)(2,1)}, bf16[2,352,2048]{2,1,0:T(8,128)(2,1)}, bf16[2,352,2048]{2,1,0:T(8,128)...) custom-call(bf16[640,2048]{1,0:T(8,128)(2,1)} %get-tuple-element.55., ...), custom_call_target="tpu_custom_call" | custom-call | flops 22145925120 | bytes 41943040 | tf_op jit(solution)/shard_map/pallas_call | solution.py:1255
  223.4 247.0 %shard_map.257 = (bf16[896,2048]{1,0:T(8,128)(2,1)}, bf16[8,16,128]{2,1,0:T(8,128)(2,1)}, bf16[896,2048]{1,0:T(8,128)(2,1)}, bf16[3,704,2048]{2,1,0:T(8,128)(2,1...) custom-call(bf16[896,2048]{1,0:T(8,128)(2,1)} %get-tuple-element.57., ...), custom_call_target="tpu_custom_call" | custom-call | flops 31004295168 | bytes 41943040 | tf_op jit(solution)/shard_map/pallas_call | solution.py:766
  470.3 5.5 convert_add_fusion
  475.9 2.9 slice_bitcast_fusion
  478.8 1.8 slice_bitcast_fusion.1
  480.6 2.1 fusion.14.place_t
  482.7 114.5 %shard_map.258 = (bf16[896,2048]{1,0:T(8,128)(2,1)}, bf16[640,2048]{1,0:T(8,128)(2,1)}, bf16[640,1536]{1,0:T(8,128)(2,1)}, f32[1,1536]{1,0:T(1,128)}, bf16[16,2048]{1,0:T(8,128)(2,1)}) custom-call(bf16[896,2048]{1,0:T(8,128)(2,1)} %get-tuple-element.68.back, bf16[8,16,128]{2,1,0:T(8,128)(2,1)} %get-tuple-element.69.g_back, bf16[640,896]{1,0:T(8,128)(2,1)} %fusion.14.place_t, ...), custom_call_target="tpu_custom_call" | custom-call | flops 5368709120 | bytes 31457280 | tf_op jit(solution)/shard_map/pallas_call | solution.py:1488
  597.2 0.0 copy-start
  597.3 2.1 constant_dynamic-slice_fusion.1.mid_cols
  599.4 0.5 broadcast.58
  599.9 0.7 reduce.20
  600.6 0.1 mul.71
  600.6 2.4 multiply_convert_fusion.place_t
  603.0 2.5 constant_dynamic-slice_fusion.res_cols
  605.5 0.0 copy-done
  605.5 0.9 constant_dynamic-slice_fusion.2.h_cols
  606.4 1.3 dynamic_slice.13
  607.7 0.6 multiply_reduce_fusion
  608.3 0.9 rsqrt.7.r_one
  609.2 105.0 %shard_map.259 = (f32[3,256,512]{2,1,0:T(8,128)}, f32[256,512]{1,0:T(8,128)}, bf16[640,512]{1,0:T(8,128)(2,1)}, bf16[640,512]{1,0:T(8,128)(2,1)}, f32[1,2048]{1,...) custom-call(bf16[640,2048]{1,0:T(8,128)(2,1)} %get-tuple-element.54.n1, bf16[640,1536]{1,0:T(8,128)(2,1)} %get-tuple-element.76.lg, ...), custom_call_target="tpu_custom_call" | custom-call | flops 9395240960 | bytes 31457280 | tf_op jit(solution)/shard_map/pallas_call | solution.py:360
  714.2 1.5 slice_bitcast_fusion.2
  715.7 1.5 fusion.27
  717.2 0.7 reduce.9
  718.0 0.6 reshape.71
  718.6 0.2 convert_bitcast_fusion
  718.8 3.8 copy.36
  722.6 1.2 convert_element_type.52
  723.8 0.8 copy.45
  724.6 0.8 copy.46
  725.5 0.0 copy-done.9
  725.5 0.6 copy.47
  726.1 1.1 copy.48
  727.2 0.8 copy.49
  (29 shorter events, 0.2 us)
Async XLA Ops:
  2.1 4.1 copy-start.7
  11.7 86.7 %copy-start.10 = (bf16[2048]{0:T(1024)(128)(2,1)S(1)}, bf16[2048]{0:T(1024)(128)(2,1)}, u32[]{:S(2)}) copy-start(bf16[2048]{0:T(1024)(128)(2,1)} %param.23) | copy-start | bytes 12292
  11.7 87.1 %copy-start.8 = (bf16[2048,8]{0,1:T(8,128)(2,1)S(1)}, bf16[2048,8]{0,1:T(8,128)(2,1)}, u32[]{:S(2)}) copy-start(bf16[2048,8]{0,1:T(8,128)(2,1)} %param.22) | copy-start | bytes 98308
  482.7 117.2 %copy-start.11 = (f32[8,1,112]{2,1,0:T(1,128)S(1)}, f32[8,1,112]{2,1,0:T(1,128)}, u32[]{:S(2)}) copy-start(f32[8,1,112]{2,1,0:T(1,128)} %get-tuple-element.82) | copy-start | bytes 10756
  597.2 8.2 %copy-start = (bf16[640,2048]{1,0:T(8,128)(2,1)S(1)}, bf16[640,2048]{1,0:T(8,128)(2,1)}, u32[]{:S(2)}) copy-start(bf16[640,2048]{1,0:T(8,128)(2,1)} %hidden.1) | copy-start | bytes 7864324
  609.2 109.4 %copy-start.2 = (bf16[2,256,1408]{2,1,0:T(8,128)(2,1)S(1)}, bf16[2,256,1408]{2,1,0:T(8,128)(2,1)}, u32[]{:S(2)}) copy-start(bf16[2,256,1408]{2,1,0:T(8,128)(2,1)} %get-tuple-element.91) | copy-start | bytes 4325380
  718.8 3.8 copy-start.3
  718.8 5.0 copy-start.5
  722.6 2.0 copy-start.4
  722.6 2.9 copy-start.9
  722.6 3.5 copy-start.1
  723.8 3.4 copy-start.6

commit v5 on v4

--- a/solution.py
+++ b/solution.py
@@ -2,6 +2,7 @@
 
 import jax
 import jax.numpy as jnp
+import numpy as np
 from jax import lax
 from jax.experimental import pallas as pl
 from jax.experimental.pallas import tpu as pltpu
@@ -18,15 +19,15 @@
     return lax.dot_general(a, b, (((ca,), (cb,)), ((), ())), preferred_element_type=F32)
 
 
-def norm_factor(values):
-    return lax.rsqrt(jnp.mean(values * values, axis=-1, keepdims=True) + EPSILON)
-
-
 def angle_tables(length, head_size):
     half_size = head_size // 2
-    frequency = THETA ** (-jnp.arange(half_size, dtype=F32) * 2.0 / head_size)
-    angles = jnp.arange(length, dtype=F32)[:, None] * frequency[None, :]
-    return jnp.cos(angles)[:, None, :], jnp.sin(angles)[:, None, :]
+    frequency = (THETA ** (-np.arange(half_size, dtype=np.float32) * 2.0 / head_size)).astype(np.float32)
+    angles = (np.arange(length, dtype=np.float32)[:, None] * frequency[None, :]).astype(np.float64)
+    cosine, sine_val = np.cos(angles), np.sin(angles)
+    return (
+        np.concatenate([cosine, cosine], axis=1).astype(np.float32),
+        np.concatenate([-sine_val, sine_val], axis=1).astype(np.float32),
+    )
 
 
 def ring_place(e, n):
@@ -77,16 +78,16 @@
     ag,
     ctx,
     w,
-    h_cols,
+    hidden,
     r_one,
-    gain,
-    mid_cols,
+    gain_all,
     bias,
     small,
     o_rows,
-    place_t,
+    weighted,
     spart,
-    res_cols,
+    mid,
+    ag_hbm,
     qkv_out,
     o_out,
     in_out,
@@ -94,6 +95,10 @@
     gain_out,
     bias_out,
     small_out,
+    h_cols,
+    res_cols,
+    ag_cols,
+    in_sem,
     ring_recv,
     ring_send,
     part_own,
@@ -105,8 +110,8 @@
     mean_recv,
     vec_send,
     vec_recv,
-    small_send,
     small_recv,
+    small_sum,
     gain_send,
     gain_recv,
     out_send,
@@ -127,6 +132,15 @@
     ep = lax.axis_index("ep")
     tp = lax.axis_index("tp")
     tokens, lw = ctx.shape
+    columns = pl.ds(pl.multiple_of(tp * lw, lw), lw)
+    col_in = [
+        pltpu.make_async_copy(hidden.at[:, columns], h_cols, in_sem.at[0]),
+        pltpu.make_async_copy(mid.at[:, columns], res_cols, in_sem.at[1]),
+        pltpu.make_async_copy(ag_hbm.at[:, columns], ag_cols, in_sem.at[2]),
+    ]
+    for copy in col_in:
+        copy.start()
+    gain = gain_all[:, columns]
     rows = qkv_out.shape[1]
     width = rows * n
     p = ring_place(ep, n)
@@ -135,17 +149,16 @@
     core_peer, y_peer = flip(tp, 1), flip(tp, 2)
     greet(n, n_tp, ep, tp)
 
-    def small_copy(shift):
-        to = lax.rem(ep + shift, n)
-        return remote(
-            small_send, small_recv.at[ep], small_ss.at[shift], small_rs.at[shift], "ep", to
-        )
-
-    def small_wait(shift):
-        came = lax.rem(ep + n - shift, n)
-        return remote(
-            small_send, small_recv.at[came], small_ss.at[shift], small_rs.at[shift], "ep", came
-        )
+    def small_copy(shift, turn, way):
+        to, came = lax.rem(ep + shift, n), lax.rem(ep + n - shift, n)
+        if turn == 0:
+            src, dst, arrived = small.at[to], small_recv.at[ep], small_recv.at[came]
+        else:
+            src, dst, arrived = small_sum, small_out.at[ep], small_out.at[came]
+        sems = small_ss.at[turn, shift], small_rs.at[turn, shift]
+        if way == 0:
+            return remote(src, dst, *sems, "ep", to)
+        return remote(src, arrived, *sems, "ep", came)
 
     def block_of(ring, step):
         if ring < 2:
@@ -209,10 +222,11 @@
 
     ring_step(1, True)
 
-    small_send[...] = small[...]
-    small_recv[ep] = small[...]
+    small_recv[ep] = small[ep]
     for shift in range(1, n):
-        small_copy(shift).start()
+        small_copy(shift, 0, 0).start()
+    for copy in col_in:
+        copy.wait()
 
     def put_own(m, total):
         part_own[m : m + 128, :] = total
@@ -238,7 +252,7 @@
         )
         part_own[at, :] = grad
         hid = h_cols[at, :].astype(F32)
-        mean = jnp.sum(grad * gain[...] * hid, axis=1, keepdims=True)
+        mean = jnp.sum(grad * gain * hid, axis=1, keepdims=True)
         mean_send[0, at, :] = jnp.broadcast_to(mean, (128, 128))
         col = jnp.sum(grad * hid * r_one[at, :], axis=0, keepdims=True)
         if m == 0:
@@ -270,7 +284,7 @@
     def out_block(column):
         at = pl.ds(pl.multiple_of(column * lw, lw), lw)
         return spart[:, at].astype(F32) + jnp.dot(
-            place_t[...], o_rows[:, at], preferred_element_type=F32
+            weighted[...], o_rows[:, at], preferred_element_type=F32
         )
 
     fifth = [tp_copy(5 + i, out_send.at[i], out_recv.at[i], core_peer) for i in range(2)]
@@ -280,6 +294,15 @@
 
     ring_step(4, False)
 
+    for shift in range(1, n):
+        small_copy(shift, 0, 1).wait()
+    total = small_recv[0].astype(F32)
+    for e in range(1, n):
+        total = total + small_recv[e].astype(F32)
+    small_sum[...] = total
+    small_out[ep] = total
+    for shift in range(1, n):
+        small_copy(shift, 1, 0).start()
     for copy in fifth:
         copy.wait()
     oy_send[...] = (out_block((tp % 2) + 2 * other) + out_recv[other].astype(F32)).astype(BF)
@@ -291,8 +314,8 @@
         mean = (mean_send[1, at, :1] + mean_recv[1, at, :1]) * (1.0 / width)
         r = r_one[at, :]
         in_out[at, :] = (
-            mid_cols[at, :].astype(F32)
-            + r * part_own[at, :] * gain[...]
+            ag_cols[at, :].astype(F32)
+            + r * part_own[at, :] * gain
             - h_cols[at, :].astype(F32) * (r * r * r) * mean
         ).astype(BF)
     for shift in range(1, n):
@@ -325,11 +348,7 @@
         ring_step(step, False)
 
     for shift in range(1, n):
-        small_wait(shift).wait()
-    total = small_recv[0].astype(F32)
-    for e in range(1, n):
-        total = total + small_recv[e].astype(F32)
-    small_out[...] = total
+        small_copy(shift, 1, 1).wait()
     for shift in range(1, n_tp):
         gain_copy(shift, "in").wait()
     for j in range(n_tp):
@@ -348,14 +367,16 @@
             ring_copy(ring, step, step % 2).wait_send()
 
 
-def tail(n, n_tp, n1, lg, ag, ctx, w, h_cols, r_one, gain, mid_cols, bias, small, o_rows, place_t, spart, res_cols):
+def tail(n, n_tp, n1, lg, ag, ctx, w, hidden, r_one, gain, bias, small, o_rows, weighted, spart, mid):
     tokens, width = n1.shape
     lw = ctx.shape[1]
     rows = width // n
+    ag_hbm = ag
     if rows % 128:
         n1, ag = n1.T, ag.T
-    wide = small.shape[0]
+    wide = small.shape[1]
     vmem = pl.BlockSpec(memory_space=pltpu.VMEM)
+    hbm = pl.BlockSpec(memory_space=pl.ANY)
     dma = pltpu.SemaphoreType.DMA
     return pl.pallas_call(
         functools.partial(tail_kernel, n, n_tp),
@@ -366,11 +387,15 @@
             jax.ShapeDtypeStruct((tokens, lw), BF),
             jax.ShapeDtypeStruct((1, width), F32),
             jax.ShapeDtypeStruct((1, 3 * lw), F32),
-            jax.ShapeDtypeStruct((wide, width), F32),
+            jax.ShapeDtypeStruct((n, wide, rows), F32),
         ),
-        in_specs=[vmem] * 15,
+        in_specs=[vmem] * 5 + [hbm] + [vmem] * 7 + [hbm] * 2,
         out_specs=[vmem] * 7,
         scratch_shapes=[
+            pltpu.VMEM((tokens, lw), BF),
+            pltpu.VMEM((tokens, lw), F32),
+            pltpu.VMEM((tokens, lw), BF),
+            dma((3,)),
             pltpu.VMEM((4, n - 1, rows, lw), BF),
             pltpu.VMEM((4, 2, rows, lw), BF),
             pltpu.VMEM((tokens, lw), F32),
@@ -382,8 +407,8 @@
             pltpu.VMEM((2, tokens, 128), F32),
             pltpu.VMEM((1, 4 * lw), F32),
             pltpu.VMEM((n, 1, 4 * lw), F32),
-            pltpu.VMEM((wide, width), BF),
-            pltpu.VMEM((n, wide, width), BF),
+            pltpu.VMEM((n, wide, rows), BF),
+            pltpu.VMEM((wide, rows), F32),
             pltpu.VMEM((1, lw), F32),
             pltpu.VMEM((n_tp, 1, lw), F32),
             pltpu.VMEM((2, tokens, lw), BF),
@@ -396,8 +421,8 @@
             dma((8,)),
             dma((n,)),
             dma((n,)),
-            dma((n,)),
-            dma((n,)),
+            dma((2, n)),
+            dma((2, n)),
             dma((n_tp,)),
             dma((n_tp,)),
         ],
@@ -407,7 +432,7 @@
         cost_estimate=pl.CostEstimate(
             flops=2 * tokens * width * 7 * lw, bytes_accessed=30 * 2**20, transcendentals=0
         ),
-    )(n1, lg, ag, ctx, w, h_cols, r_one, gain, mid_cols, bias, small, o_rows, place_t, spart, res_cols)
+    )(n1, lg, ag, ctx, w, hidden, r_one, gain, bias, small, o_rows, weighted, spart, mid, ag_hbm)
 
 def cols_of(ref, owner, rows):
     at = pl.ds(pl.multiple_of(owner * rows, rows), rows)
@@ -422,7 +447,7 @@
 def middle_kernel(
     n,
     n_tp,
-    capp,
+    shape,
     x_hbm,
     u_hbm,
     gu_a,
@@ -446,6 +471,7 @@
     dw_y,
     gu_out,
     dn_out,
+    zero,
     w,
     xb,
     ub,
@@ -474,6 +500,8 @@
     tp = lax.axis_index("tp")
     core_peer, y_peer = flip(tp, 1), flip(tp, 2)
     gr = ub.shape[1]
+    capp = shape[0]
+    zero[...] = jnp.zeros_like(zero)
     width = u_hbm.shape[1]
     units = w.shape[1]
     quarter = units // 4
@@ -582,13 +610,10 @@
         slot = lax.rem(g, 2)
         return pltpu.make_async_copy(ub.at[slot], o_hbm.at[at, :], out_sem.at[slot])
 
-    def back_copy(r):
-        at = pl.ds(pl.multiple_of(r * capp, capp), capp)
-        return remote(
-            rbs.at[at, :], back.at[at, :], back_ss.at[r], back_rs.at[r], "ep", lax.rem(ep + n - r, n)
-        )
-
-    kept_copy = pltpu.make_async_copy(rbs.at[:capp, :], back.at[:capp, :], back_ss.at[0])
+    def back_copies(r):
+        return block_copies(r, rbs, back, back_ss, back_rs, lax.rem(ep + n - r, n), shape, tp, zero)
+
+    kept_copy = pltpu.make_async_copy(rbs.at[:capp, :], back.at[:capp, :], back_ss.at[0, 0])
 
     def gate_copy(r):
         return remote(
@@ -665,10 +690,10 @@
 
                 @pl.when(g > 0)
                 def _():
-                    back_copy(r).start()
+                    each(back_copies(r), "start")
                     gate_copy(r).start()
             else:
-                back_copy(r).start()
+                each(back_copies(r), "start")
                 gate_copy(r).start()
 
         @pl.when(lax.rem(g, 2) == 1)
@@ -748,11 +773,11 @@
 
     @pl.loop(1, n)
     def _(r):
-        back_copy(r).wait()
+        each(back_copies(r), "wait")
         gate_copy(r).wait()
 
 
-def routed_expert(n, n_tp, capp, x, u, weights, gates, nt, pg, og, sh):
+def routed_expert(n, n_tp, shape, x, u, weights, gates, nt, pg, og, sh):
     total, width = x.shape
     units = 4 * weights[-1].shape[0]
     gr = total // 4
@@ -764,7 +789,7 @@
     if rows % 128:
         nt, og = nt.T, og.T
     return pl.pallas_call(
-        functools.partial(middle_kernel, n, n_tp, capp),
+        functools.partial(middle_kernel, n, n_tp, shape),
         out_shape=(
             jax.ShapeDtypeStruct((total, width), BF),
             jax.ShapeDtypeStruct((n, 16, 128), BF),
@@ -778,6 +803,7 @@
         in_specs=[hbm] * 10 + [vmem] * 5,
         out_specs=[hbm] * 6 + [vmem] * 2,
         scratch_shapes=[
+            pltpu.VMEM((max(shape[0] - shape[1], 16), width), BF),
             pltpu.VMEM((3, units, width), BF),
             pltpu.VMEM((total, width), BF),
             pltpu.VMEM((2, gr, width), BF),
@@ -794,8 +820,8 @@
             dma((4, 2)),
             dma((4, 2)),
             pltpu.SemaphoreType.REGULAR((4,)),
-            dma((n,)),
-            dma((n,)),
+            dma((2, n)),
+            dma((2, n)),
             dma((n,)),
             dma((n,)),
             dma((2,)),
@@ -856,6 +882,25 @@
     return per
 
 
+def block_copies(r, src, dst, ss, rs, to, shape, tp, zero):
+    capp, base, extra = shape
+    at = pl.ds(pl.multiple_of(r * capp, 16), base)
+    out = [(None, remote(src.at[at, :], dst.at[at, :], ss.at[0, r], rs.at[0, r], "ep", to))]
+    if base < capp:
+        at = pl.ds(pl.multiple_of(r * capp + base, 16), capp - base)
+        out.append((tp < extra, remote(src.at[at, :], dst.at[at, :], ss.at[1, r], rs.at[1, r], "ep", to)))
+        out.append((tp >= extra, pltpu.make_async_copy(zero, dst.at[at, :], ss.at[1, r])))
+    return out
+
+
+def each(copies, verb):
+    for condition, copy in copies:
+        if condition is None:
+            getattr(copy, verb)()
+        else:
+            pl.when(condition)(getattr(copy, verb))
+
+
 def gate_column(tiles, r, capp):
     ones = jnp.ones((16, 128), BF)
     return lax.dot_general(
@@ -866,7 +911,7 @@
 def front_kernel(
     n,
     n_tp,
-    capp,
+    shape,
     hidden,
     gain1,
     gain2,
@@ -889,6 +934,8 @@
     ctx,
     mid,
     nt,
+    factor_one,
+    zero,
     up_sent,
     core_send,
     core_recv,
@@ -914,12 +961,13 @@
     core_peer, y_peer = flip(tp, 1), flip(tp, 2)
     greet(n, n_tp, ep, tp)
 
-    def up_copy(r, way):
-        to = lax.rem(ep + r, n) if way == "out" else lax.rem(ep + n - r, n)
-        at = pl.ds(pl.multiple_of(r * capp, capp), capp)
-        return remote(up_sent.at[at, :], up_rows.at[at, :], up_ss.at[r], up_rs.at[r], "ep", to)
-
-    kept = pltpu.make_async_copy(up_sent.at[:capp, :], up_rows.at[:capp, :], up_ss.at[0])
+    capp = shape[0]
+    zero[...] = jnp.zeros_like(zero)
+
+    def up_copies(r):
+        return block_copies(r, up_sent, up_rows, up_ss, up_rs, lax.rem(ep + r, n), shape, tp, zero)
+
+    kept = pltpu.make_async_copy(up_sent.at[:capp, :], up_rows.at[:capp, :], up_ss.at[0, 0])
     per = blocks_at_once(n, capp)
     size = per * capp
 
@@ -936,9 +984,9 @@
 
                 @pl.when(b > 0)
                 def _():
-                    up_copy(b * per, "out").start()
+                    each(up_copies(b * per), "start")
             else:
-                up_copy(b * per + i, "out").start()
+                each(up_copies(b * per + i), "start")
 
     w_copies = [
         remote(dn_own, dn_b, w_ss.at[0], w_rs.at[0], "tp", y_peer),
@@ -953,6 +1001,7 @@
         at = pl.ds(pl.multiple_of(m * 64, 64), 64)
         h = hidden[at, :].astype(F32)
         factor = lax.rsqrt(jnp.sum(h * h, axis=1, keepdims=True) * (1.0 / width) + EPSILON)
+        factor_one[at, :] = factor
         n1[at, :] = (h * factor * gain1[...]).astype(BF)
 
     for k in range(3):
@@ -1021,10 +1070,10 @@
         copy.wait()
     kept.wait()
     for r in range(1, n):
-        up_copy(r, "in").wait()
-
-
-def front(n, n_tp, capp, hidden, gain1, gain2, w, bias, cosine, sine, prefix, ow, place, cot, gu_own, dn_own):
+        each(up_copies(r), "wait")
+
+
+def front(n, n_tp, shape, hidden, gain1, gain2, w, bias, cosine, sine, prefix, ow, place, cot, gu_own, dn_own):
     tokens, width = hidden.shape
     lw = ow.shape[1]
     quarter = dn_own.shape[0]
@@ -1032,9 +1081,9 @@
     hbm = pl.BlockSpec(memory_space=pl.ANY)
     dma = pltpu.SemaphoreType.DMA
     return pl.pallas_call(
-        functools.partial(front_kernel, n, n_tp, capp),
+        functools.partial(front_kernel, n, n_tp, shape),
         out_shape=(
-            jax.ShapeDtypeStruct((n * capp, width), BF),
+            jax.ShapeDtypeStruct((n * shape[0], width), BF),
             jax.ShapeDtypeStruct((2, quarter, width), BF),
             jax.ShapeDtypeStruct((quarter, width), BF),
             jax.ShapeDtypeStruct((quarter, width), BF),
@@ -1043,18 +1092,20 @@
             jax.ShapeDtypeStruct((tokens, lw), BF),
             jax.ShapeDtypeStruct((tokens, width), F32),
             jax.ShapeDtypeStruct((tokens, width), BF),
+            jax.ShapeDtypeStruct((tokens, 1), F32),
         ),
         in_specs=[vmem] * 11 + [hbm] * 2,
-        out_specs=[hbm] * 4 + [vmem] * 5,
+        out_specs=[hbm] * 4 + [vmem] * 6,
         scratch_shapes=[
-            pltpu.VMEM((n * capp, width), BF),
+            pltpu.VMEM((max(shape[0] - shape[1], 16), width), BF),
+            pltpu.VMEM((n * shape[0], width), BF),
             pltpu.VMEM((4, tokens, width // 8), BF),
             pltpu.VMEM((4, tokens, width // 8), BF),
             pltpu.VMEM((4, tokens, width // 8), BF),
             pltpu.VMEM((4, tokens, width // 8), BF),
             pltpu.VMEM((2, 4, tokens, width // 8), BF),
-            dma((n,)),
-            dma((n,)),
+            dma((2, n)),
+            dma((2, n)),
             dma((3,)),
             dma((3,)),
             dma((4,)),
@@ -1076,7 +1127,7 @@
 def dispatch_kernel(
     n,
     n_tp,
-    capp,
+    shape,
     n_exp,
     nt,
     place,
@@ -1086,19 +1137,23 @@
     sdn,
     gu_own,
     dn_b,
+    dest_t,
     x_rows,
     g_rows,
     gu_b,
     gu_c,
     dn_c,
     probs,
-    gate,
+    place_t,
+    weighted,
     og,
     pg,
     sh,
     part,
     sback,
     sgrad,
+    zero,
+    gate,
     x_send,
     g_send,
     x_ss,
@@ -1120,16 +1175,17 @@
     w_on = remote(dn_b, dn_c, w_ss.at[1], w_rs.at[1], "tp", core_peer)
     w_on.start()
 
-    def x_copy(r, way):
-        to = lax.rem(ep + r, n) if way == "out" else lax.rem(ep + n - r, n)
-        at = pl.ds(pl.multiple_of(r * capp, capp), capp)
-        return remote(x_send.at[at, :], x_rows.at[at, :], x_ss.at[r], x_rs.at[r], "ep", to)
+    capp = shape[0]
+    zero[...] = jnp.zeros_like(zero)
+
+    def x_copies(r):
+        return block_copies(r, x_send, x_rows, x_ss, x_rs, lax.rem(ep + r, n), shape, tp, zero)
 
     def gate_copy(r, way):
         to = lax.rem(ep + r, n) if way == "out" else lax.rem(ep + n - r, n)
         return remote(g_send.at[r], g_rows.at[r], gate_ss.at[r], gate_rs.at[r], "ep", to)
 
-    kept = pltpu.make_async_copy(x_send.at[:capp, :], x_rows.at[:capp, :], x_ss.at[0])
+    kept = pltpu.make_async_copy(x_send.at[:capp, :], x_rows.at[:capp, :], x_ss.at[0, 0])
     g_kept = pltpu.make_async_copy(g_send.at[0], g_rows.at[0], gate_ss.at[0])
     per = blocks_at_once(n, capp)
     size = per * capp
@@ -1147,9 +1203,9 @@
 
                 @pl.when(b > 0)
                 def _():
-                    x_copy(b * per, "out").start()
+                    each(x_copies(b * per), "start")
             else:
-                x_copy(b * per + i, "out").start()
+                each(x_copies(b * per + i), "start")
 
     logits = jnp.dot(nt[...], router[...], preferred_element_type=F32)
     lane = lax.broadcasted_iota(jnp.int32, logits.shape, 1)
@@ -1163,11 +1219,9 @@
     g_send[...] = jnp.zeros_like(g_send)
     across = (((0,), (1,)), ((), ()))
 
-    @pl.loop(0, n)
-    def _(r):
-        where = place[pl.ds(pl.multiple_of(r * capp, capp), capp), :]
-        expert = lax.rem(r + ep, n)
-        pick = lax.broadcasted_iota(jnp.int32, (128, capp), 0) == expert
+    for r in range(n):
+        where = place[r * capp : (r + 1) * capp, :]
+        pick = lax.broadcasted_iota(jnp.int32, (128, capp), 0) == lax.rem(r + ep, n)
         g_hi = jnp.sum(
             jnp.where(pick, lax.dot_general(hi, where, across, preferred_element_type=F32), 0.0),
             axis=0,
@@ -1180,14 +1234,10 @@
         )
         term = lax.broadcasted_iota(jnp.int32, (16, capp), 0)
         g_send[r, :, :capp] = jnp.where(term == 0, g_hi, jnp.where(term == 1, g_lo, 0.0)).astype(BF)
-        gate[r] = g_hi + g_lo
-
-        @pl.when(r == 0)
-        def _():
+        gate[:, r * capp : (r + 1) * capp] = g_hi + g_lo
+        if r == 0:
             g_kept.start()
-
-        @pl.when(r > 0)
-        def _():
+        else:
             gate_copy(r, "out").start()
 
     @pl.loop(0, tokens // 64)
@@ -1215,10 +1265,6 @@
         rest = units // 256 * 256
         hidden(pl.ds(rest, units - rest), pl.ds(units + rest, units - rest))
 
-    w_y.wait()
-    w_far = remote(gu_b, gu_c, w_ss.at[2], w_rs.at[2], "tp", core_peer)
-    w_far.start()
-
     nt_dims = (((1,), (1,)), ((), ()))
 
     share = probs[:, n_exp : n_exp + 1]
@@ -1234,6 +1280,19 @@
 
     sgrad[...] = lax.fori_loop(0, width // 256, columns, jnp.zeros((tokens, 1), F32))
 
+    @pl.loop(0, total // 128)
+    def _(c):
+        at = pl.ds(pl.multiple_of(c * 128, 128), 128)
+        spot = lax.broadcasted_iota(jnp.int32, (tokens, 128), 1) + c * 128
+        hit = dest_t[:, :1] == spot
+        for k in range(1, dest_t.shape[1]):
+            hit = hit | (dest_t[:, k : k + 1] == spot)
+        place_t[:, at] = jnp.where(hit, 1.0, 0.0).astype(BF)
+        weighted[:, at] = jnp.where(hit, gate[:, at], 0.0).astype(BF)
+
+    w_y.wait()
+    w_far = remote(gu_b, gu_c, w_ss.at[2], w_rs.at[2], "tp", core_peer)
+    w_far.start()
     w_on.wait()
     w_far.wait()
     kept.wait()
@@ -1242,10 +1301,10 @@
     @pl.loop(1, n)
     def _(r):
         gate_copy(r, "in").wait()
-        x_copy(r, "in").wait()
-
-
-def dispatch(n, n_tp, capp, n_exp, nt, place, router, cot, sgu, sdn, gu_own, dn_b):
+        each(x_copies(r), "wait")
+
+
+def dispatch(n, n_tp, shape, n_exp, nt, place, router, cot, sgu, sdn, gu_own, dn_b, dest_t):
     tokens, width = nt.shape
     units = sdn.shape[1]
     total = place.shape[0]
@@ -1253,7 +1312,7 @@
     hbm = pl.BlockSpec(memory_space=pl.ANY)
     dma = pltpu.SemaphoreType.DMA
     return pl.pallas_call(
-        functools.partial(dispatch_kernel, n, n_tp, capp, n_exp),
+        functools.partial(dispatch_kernel, n, n_tp, shape, n_exp),
         out_shape=(
             jax.ShapeDtypeStruct((total, width), BF),
             jax.ShapeDtypeStruct((n, 16, 128), BF),
@@ -1261,7 +1320,8 @@
             jax.ShapeDtypeStruct(gu_own.shape, BF),
             jax.ShapeDtypeStruct(dn_b.shape, BF),
             jax.ShapeDtypeStruct((tokens, 128), F32),
-            jax.ShapeDtypeStruct((n, 1, capp), F32),
+            jax.ShapeDtypeStruct((tokens, total), BF),
+            jax.ShapeDtypeStruct((tokens, total), BF),
             jax.ShapeDtypeStruct((tokens, width), BF),
             jax.ShapeDtypeStruct((tokens, 2 * units), BF),
             jax.ShapeDtypeStruct((tokens, units), BF),
@@ -1269,13 +1329,15 @@
             jax.ShapeDtypeStruct((tokens, width), F32),
             jax.ShapeDtypeStruct((tokens, 1), F32),
         ),
-        in_specs=[vmem] * 6 + [hbm] * 2,
-        out_specs=[hbm] * 5 + [vmem] * 8,
+        in_specs=[vmem] * 6 + [hbm] * 2 + [vmem],
+        out_specs=[hbm] * 5 + [vmem] * 9,
         scratch_shapes=[
+            pltpu.VMEM((max(shape[0] - shape[1], 16), width), BF),
+            pltpu.VMEM((1, total), F32),
             pltpu.VMEM((total, width), BF),
             pltpu.VMEM((n, 16, 128), BF),
-            dma((n,)),
-            dma((n,)),
+            dma((2, n)),
+            dma((2, n)),
             dma((n,)),
             dma((n,)),
             dma((3,)),
@@ -1287,12 +1349,12 @@
         cost_estimate=pl.CostEstimate(
             flops=2 * tokens * width * 6 * units, bytes_accessed=40 * 2**20, transcendentals=0
         ),
-    )(nt, place, router, cot, sgu, sdn, gu_own, dn_b)
+    )(nt, place, router, cot, sgu, sdn, gu_own, dn_b, dest_t)
 
 def backward_kernel(
     n,
     n_tp,
-    capp,
+    shape,
     n_exp,
     back,
     g_back,
@@ -1316,6 +1378,7 @@
     lg,
     bias,
     small,
+    zero,
     core_send,
     core_recv,
     y_send,
@@ -1347,16 +1410,16 @@
     core_peer, y_peer = flip(tp, 1), flip(tp, 2)
     greet(n, n_tp, ep, tp)
 
-    def o_copy(r):
-        at = pl.ds(pl.multiple_of(r * capp, capp), capp)
-        return remote(
-            o_sent.at[at, :], o_rows.at[at, :], o_ss.at[r], o_rs.at[r], "ep", lax.rem(ep + n - r, n)
-        )
-
-    kept = pltpu.make_async_copy(o_sent.at[:capp, :], o_rows.at[:capp, :], o_ss.at[0])
+    capp = shape[0]
+    zero[...] = jnp.zeros_like(zero)
+
+    def o_copies(r):
+        return block_copies(r, o_sent, o_rows, o_ss, o_rs, lax.rem(ep + n - r, n), shape, tp, zero)
+
+    kept = pltpu.make_async_copy(o_sent.at[:capp, :], o_rows.at[:capp, :], o_ss.at[0, 0])
 
     for r in range(1, n):
-        o_copy(r).start()
+        each(o_copies(r), "start")
     kept.start()
 
     row = lax.broadcasted_iota(jnp.int32, (total, 128), 0)
@@ -1464,20 +1527,20 @@
     lg[:, 2 * lw :] = dv[...].astype(BF)
     bias[:, 2 * lw :] = jnp.sum(dv[...], axis=0, keepdims=True)
 
-    wide = small.shape[0]
+    wide, span = small.shape[1:]
     gain_row = jnp.sum(acc, axis=0, keepdims=True)
-    for c in range(0, width, 512):
-        at = slice(c, c + 512)
-        rows = lax.dot_general(few_send[0], nt[:, at], first_dims, preferred_element_type=F32)[:wide]
-        index = lax.broadcasted_iota(jnp.int32, rows.shape, 0)
-        small[:, at] = jnp.where(index == n_exp + 1, gain_row[:, at], rows).astype(BF)
+    rows = lax.dot_general(few_send[0], nt[...], first_dims, preferred_element_type=F32)[:wide]
+    index = lax.broadcasted_iota(jnp.int32, rows.shape, 0)
+    rows = jnp.where(index == n_exp + 1, gain_row, rows).astype(BF)
+    for r in range(n):
+        small[r] = rows[:, r * span : (r + 1) * span]
 
     kept.wait()
     for r in range(1, n):
-        o_copy(r).wait()
-
-
-def backward(n, n_tp, capp, n_exp, back, g_back, place_t, sback, sgrad, probs, router, nt, mid, cot, gain2, qkv, ow, cosine, sine, prefix, o_sent):
+        each(o_copies(r), "wait")
+
+
+def backward(n, n_tp, shape, n_exp, back, g_back, place_t, sback, sgrad, probs, router, nt, mid, cot, gain2, qkv, ow, cosine, sine, prefix, o_sent):
     tokens, width = nt.shape
     lw = ow.shape[1]
     wide = -(-(n_exp + 2) // 16) * 16
@@ -1486,17 +1549,18 @@
     dma = pltpu.SemaphoreType.DMA
     piece = (4, tokens, width // 8)
     return pl.pallas_call(
-        functools.partial(backward_kernel, n, n_tp, capp, n_exp),
+        functools.partial(backward_kernel, n, n_tp, shape, n_exp),
         out_shape=(
             jax.ShapeDtypeStruct(o_sent.shape, BF),
             jax.ShapeDtypeStruct((tokens, width), BF),
             jax.ShapeDtypeStruct((tokens, 3 * lw), BF),
             jax.ShapeDtypeStruct((1, 3 * lw), F32),
-            jax.ShapeDtypeStruct((wide, width), BF),
+            jax.ShapeDtypeStruct((n, wide, width // n), BF),
         ),
         in_specs=[vmem] * 16 + [hbm],
         out_specs=[hbm] + [vmem] * 4,
         scratch_shapes=[
+            pltpu.VMEM((max(shape[0] - shape[1], 16), width), BF),
             pltpu.VMEM(piece, BF),
             pltpu.VMEM(piece, BF),
             pltpu.VMEM(piece, BF),
@@ -1508,8 +1572,8 @@
             pltpu.VMEM((tokens, lw), BF),
             pltpu.VMEM((tokens, lw), F32),
             pltpu.VMEM((tokens, lw), F32),
-            dma((n,)),
-            dma((n,)),
+            dma((2, n)),
+            dma((2, n)),
             dma((4,)),
             dma((4,)),
             dma((4,)),
@@ -1550,17 +1614,15 @@
     n_ep = lax.axis_size("ep")
     n_tp = lax.axis_size("tp")
     tp_i = lax.axis_index("tp")
-    cols = width // n_tp
-    col_start = tp_i * cols
-    head_size = HEAD_DIM
     local_width = qkv_weight.shape[2]
-    heads = local_width // head_size
     expert_local = expert_gate_up.shape[0]
     n_exp = expert_local * n_ep
     top = routes.shape[1]
     capacity = (5 * tokens * top + 4 * n_exp - 1) // (4 * n_exp)
-    part = -(-capacity // n_tp)
-    part_pad = -(-part // 16) * 16
+    tiles = -(-capacity // 16)
+    least, extra = 16 * (tiles // n_tp), tiles % n_tp
+    part_pad = least + (16 if extra else 0)
+    shape = (part_pad, least, extra)
     rows = n_exp * part_pad
 
     flat_route = routes.T.reshape(-1)
@@ -1570,8 +1632,8 @@
     counts = mm(smaller, hits, 1, 0)
     slot = jnp.sum(counts * hits.astype(F32), axis=1).astype(jnp.int32).reshape(top, tokens)
     kept = slot < capacity
-    in_part = slot - tp_i * part
-    mine = kept & (in_part >= 0) & (in_part < part)
+    in_part = slot - (tp_i * least + 16 * jnp.minimum(tp_i, extra))
+    mine = kept & (in_part >= 0) & (in_part < jnp.where(tp_i < extra, part_pad, least))
     ep_i = lax.axis_index("ep")
     hop = lax.rem(routes.T + n_exp - ep_i * expert_local, n_exp)
     dest = jnp.where(mine, hop * part_pad + in_part, -1)
@@ -1580,26 +1642,17 @@
     for k in range(1, top):
         place = place | (dest[k][None, :] == row_ids)
     place = place.astype(BF)
-    dest_t = dest.T
-    place_t = dest_t[:, :1] == row_ids.T
-    for k in range(1, top):
-        place_t = place_t | (dest_t[:, k : k + 1] == row_ids.T)
-    place_t = place_t.astype(BF)
-
-
-    residual_in = hidden.astype(F32)
-    factor_one = norm_factor(residual_in)
-    cosine, sine_val = angle_tables(tokens, head_size)
-    cos_all = jnp.concatenate([cosine[:, 0], cosine[:, 0]], axis=1)
-    sin_all = jnp.concatenate([-sine_val[:, 0], sine_val[:, 0]], axis=1)
+
+    cos_all, sin_all = angle_tables(tokens, HEAD_DIM)
     w_t = jnp.transpose(qkv_weight, (1, 0, 2))
+    sgu, hidden = lax.optimization_barrier((jnp.transpose(shared_gate_up, (1, 0, 2)), hidden))
     prefix_row = jnp.broadcast_to(prefix[None], (1, tokens))
     gu_own = jnp.transpose(expert_gate_up[0], (1, 2, 0))
     dn_own = jnp.transpose(expert_down[0], (1, 0))
-    up_rows, gu_a, dn_a, dn_b, normed_one, qkv, context, middle, normed_two = front(
+    up_rows, gu_a, dn_a, dn_b, normed_one, qkv, context, middle, normed_two, factor_one = front(
         n_ep,
         n_tp,
-        part_pad,
+        shape,
         hidden,
         attn_gain[None],
         mlp_gain[None],
@@ -1618,26 +1671,27 @@
     router_all = jnp.concatenate(
         [router_weight, share_gate[:, None], jnp.zeros((width, 127 - n_exp), BF)], axis=1
     )
-    got, gates, gu_b, gu_c, dn_c, probs_all, gate_sent, shared_out_grad, pre_grad, shared_hidden, scaled_part, shared_back, scale_grad = (
+    got, gates, gu_b, gu_c, dn_c, probs_all, place_t, weighted_place, shared_out_grad, pre_grad, shared_hidden, scaled_part, shared_back, scale_grad = (
         dispatch(
             n_ep,
             n_tp,
-            part_pad,
+            shape,
             n_exp,
             normed_two,
             place,
             router_all,
             cotangent,
-            jnp.transpose(shared_gate_up, (1, 0, 2)),
+            sgu,
             shared_down,
             gu_own,
             dn_b,
+            dest.T,
         )
     )
     back_rows, back_gates, e_out, _, dw_own, dw_y, gu_grad, shared_down_grad = routed_expert(
         n_ep,
         n_tp,
-        part_pad,
+        shape,
         got,
         up_rows,
         (gu_a, gu_c, gu_b, gu_own, dn_a, dn_c, dn_b, dn_own),
@@ -1649,14 +1703,13 @@
     )
     shared_gate_up_grad = jnp.transpose(gu_grad, (1, 0, 2)).astype(F32)
     shared_down_grad = shared_down_grad.astype(F32)
-    dw = dw_own.astype(F32) + dw_y.astype(F32)
-    expert_down_grad = jnp.transpose(dw[2], (1, 0))[None]
-    expert_gate_up_grad = jnp.transpose(dw[:2], (2, 0, 1))[None]
+    expert_down_grad = jnp.transpose(dw_own[2].astype(F32) + dw_y[2].astype(F32), (1, 0))[None]
+    expert_gate_up_grad = jnp.transpose(dw_own[:2].astype(F32) + dw_y[:2].astype(F32), (2, 0, 1))[None]
 
     out_rows, attn_grad, linear_grad, bias_grad, small = backward(
         n_ep,
         n_tp,
-        part_pad,
+        shape,
         n_exp,
         back_rows,
         back_gates,
@@ -1676,7 +1729,6 @@
         prefix_row,
         e_out,
     )
-    weighted_place = (place_t.astype(F32) * gate_sent.reshape(1, rows)).astype(BF)
     qkv_grad, out_weight_grad, input_grad, output, gain_one, bias_sum, small_sum = tail(
         n_ep,
         n_tp,
@@ -1685,17 +1737,17 @@
         attn_grad,
         context,
         w_t,
-        lax.dynamic_slice_in_dim(hidden, col_start, cols, 1),
+        hidden,
         factor_one,
-        lax.dynamic_slice_in_dim(attn_gain, col_start, cols, 0)[None],
-        lax.dynamic_slice_in_dim(attn_grad, col_start, cols, 1),
+        attn_gain[None],
         bias_grad,
         small,
         out_rows,
         weighted_place,
         scaled_part,
-        lax.dynamic_slice_in_dim(middle, col_start, cols, 1),
+        middle,
     )
+    small_sum = jnp.transpose(small_sum, (1, 0, 2)).reshape(-1, width)
     qkv_weight_grad = jnp.transpose(qkv_grad, (1, 0, 2))
     gain_one_sum = gain_one[0]
     bias_sum = bias_sum.reshape(3, local_width)

time: 734 us -> 678 us (0.924)
  Pallas kernels: 665 us -> 628 us
  local copies, waits for them, and re-layouts: 38.6 us -> 27.2 us
  other arithmetic: 18.8 us -> 11.3 us
    pallas_call x4, Pallas kernels: 560 us -> 530 us  [the longest x1 238 us: routed_expert(): pl.pallas_call(functools.partial(middle_kernel, n, n_tp, shape), out_shap...]
    unnamed x32 -> x37, local copies, waits for them, and re-layouts: 19.5 us -> 20.6 us
where the time goes in v5:
time: 678 us; the launch traced here: 673 us
  Pallas kernels  628 us (93%)
  local copies, waits for them, and re-layouts  27.2 us (4%)
  other arithmetic  11.3 us (2%)
    pallas_call x1, Pallas kernels, routed_expert(): pl.pallas_call(functools.partial(middle_kernel, n, n_tp, shape), out_shap...  238 us
    pallas_call x1, Pallas kernels, backward(): pl.pallas_call(functools.partial(backward_kernel, n, n_tp, shape, n_exp),...  106 us
    pallas_call x1, Pallas kernels, dispatch(): pl.pallas_call(functools.partial(dispatch_kernel, n, n_tp, shape, n_exp),...  98.9 us
    pallas_call x1, Pallas kernels, tail(): pl.pallas_call(functools.partial(tail_kernel, n, n_tp), out_shape=(jax.Sh...  97.8 us
    pallas_call x1, Pallas kernels, front(): pl.pallas_call(functools.partial(front_kernel, n, n_tp, shape), out_shape...  86.8 us
    unnamed x37, local copies, waits for them, and re-layouts  20.6 us

profile of v5, /device:TPU:0, one launch (start us, length us, event | category | flops | bytes accessed | tf_op | source)
XLA Modules:
  0.0 672.5 jit_solution(13025590521140622527)
XLA Ops:
  1.3 0.1 pad.2.clone
  1.4 0.6 broadcast_in_dim.37.prefix
  2.0 0.7 lt.33
  2.7 0.9 copy.36
  3.6 0.1 copy.37
  3.7 4.1 fusion.11
  7.8 0.0 copy-start.7
  7.8 0.0 copy-start.9
  7.8 0.2 copy.39
  8.1 0.2 copy.38
  8.3 0.2 fusion.17
  8.5 0.0 copy-start
  8.5 0.7 slice_reduce_fusion.3
  9.2 0.0 copy-done.7
  9.2 0.3 copy.42
  9.5 0.0 copy-done.9
  9.5 0.3 broadcast_in_dim.43
  9.8 1.1 maximum_maximum_fusion.router
  10.9 1.9 fusion.10.place
  12.8 11.4 %copy.46 = bf16[2048,2,1408]{2,0,1:T(8,128)(2,1)} copy(bf16[2048,2,1408]{2,1,0:T(2,128)(2,1)} %param.26) | data formatting | bytes 23068672 | tf_op args[8]
  24.3 0.0 copy-done
  24.3 86.8 %shard_map.273 = (bf16[896,2048]{1,0:T(8,128)(2,1)}, bf16[2,352,2048]{2,1,0:T(8,128)(2,1)}, bf16[352,2048]{1,0:T(8,128)(2,1)}, bf16[352,2048]{1,0:T(8,128)(2,1)}...) custom-call(bf16[640,2048]{1,0:T(8,128)(2,1)} %hidden.1, ...), custom_call_target="tpu_custom_call" | custom-call | flops 5368709120 | bytes 31457280 | tf_op jit(solution)/shard_map/pallas_call | solution.py:1083
  111.0 98.9 %shard_map.274 = (bf16[896,2048]{1,0:T(8,128)(2,1)}, bf16[8,16,128]{2,1,0:T(8,128)(2,1)}, bf16[2,352,2048]{2,1,0:T(8,128)(2,1)}, bf16[2,352,2048]{2,1,0:T(8,128)...) custom-call(bf16[640,2048]{1,0:T(8,128)(2,1)} %get-tuple-element.60., ...), custom_call_target="tpu_custom_call" | custom-call | flops 22145925120 | bytes 41943040 | tf_op jit(solution)/shard_map/pallas_call | solution.py:1314
  210.0 238.1 %shard_map.275 = (bf16[896,2048]{1,0:T(8,128)(2,1)}, bf16[8,16,128]{2,1,0:T(8,128)(2,1)}, bf16[896,2048]{1,0:T(8,128)(2,1)}, bf16[3,704,2048]{2,1,0:T(8,128)(2,1...) custom-call(bf16[896,2048]{1,0:T(8,128)(2,1)} %get-tuple-element.63., ...), custom_call_target="tpu_custom_call" | custom-call | flops 31004295168 | bytes 41943040 | tf_op jit(solution)/shard_map/pallas_call | solution.py:791
  448.1 106.4 %shard_map.276 = (bf16[896,2048]{1,0:T(8,128)(2,1)}, bf16[640,2048]{1,0:T(8,128)(2,1)}, bf16[640,1536]{1,0:T(8,128)(2,1)}, f32[1,1536]{1,0:T(1,128)}, bf16[8,16,256]{2,1,0:T(8,128)(2,1)}) custom-call(bf16[896,2048]{1,0:T(8,128)(2,1)} %get-tuple-element.74.back, bf16[8,16,128]{2,1,0:T(8,128)(2,1)} %get-tuple-element.75.g_back, ...), custom_call_target="tpu_custom_call" | custom-call | flops 5368709120 | bytes 31457280 | tf_op jit(solution)/shard_map/pallas_call | solution.py:1551
  554.5 0.0 copy-start.3
  554.5 97.8 %shard_map.277 = (f32[3,256,512]{2,1,0:T(8,128)}, f32[256,512]{1,0:T(8,128)}, bf16[640,512]{1,0:T(8,128)(2,1)}, bf16[640,512]{1,0:T(8,128)(2,1)}, f32[1,2048]{1,...) custom-call(bf16[640,2048]{1,0:T(8,128)(2,1)} %get-tuple-element.59.n1, bf16[640,1536]{1,0:T(8,128)(2,1)} %get-tuple-element.83.lg, ...), custom_call_target="tpu_custom_call" | custom-call | flops 9395240960 | bytes 31457280 | tf_op jit(solution)/shard_map/pallas_call | solution.py:381
  652.3 0.0 copy-start.2
  652.3 0.8 reduce.4
  653.2 0.6 reshape.51
  653.8 1.5 fusion.20
  655.3 1.5 slice.55
  656.8 0.0 copy-done.3
  656.8 1.2 convert_element_type.44
  658.0 0.0 copy-done.2
  658.0 0.2 convert_bitcast_fusion
  658.2 3.8 copy.44
  662.0 0.0 slice-done
  662.0 0.0 slice-done.2
  662.0 0.0 slice-done.1
  662.0 2.1 add_bitcast_fusion.1
  664.2 3.7 add_bitcast_fusion
  667.9 0.8 copy.53
  668.7 0.0 copy-done.4
  668.7 0.8 copy.54
  669.6 0.6 copy.55
  670.2 1.1 copy.56
  671.3 0.8 copy.57
  (22 shorter events, 0.1 us)
Async XLA Ops:
  7.8 1.4 copy-start.7
  7.8 1.7 copy-start.9
  8.5 15.8 %copy-start = (s32[4,640]{0,1:T(8,128)}, s32[4,640]{0,1:T(8,128)S(1)}, u32[]{:S(2)}) copy-start(s32[4,640]{0,1:T(8,128)S(1)} %fusion.17) | copy-start | bytes 30724
  554.5 102.3 %copy-start.3 = (bf16[256,1408]{1,0:T(8,128)(2,1)S(1)}, bf16[256,1408]{1,0:T(8,128)(2,1)}, u32[]{:S(2)}) copy-start(bf16[256,1408]{1,0:T(8,128)(2,1)} %get-tuple-element.100) | copy-start | bytes 2162692
  652.3 5.6 copy-start.2
  656.8 5.2 slice-start
  656.8 5.2 slice-start.2
  658.0 4.0 slice-start.1
  658.0 4.0 slice-start.3
  664.1 3.7 copy-start.5
  664.1 4.6 copy-start.4
  664.1 5.4 copy-start.8
  667.9 2.3 copy-start.1
  667.9 3.4 copy-start.6

commit v6 on v5

--- a/solution.py
+++ b/solution.py
@@ -901,6 +901,19 @@
             pl.when(condition)(getattr(copy, verb))
 
 
+SEND_ORDER = (4, 5, 6, 7, 2, 3, 1, 0)
+
+
+def send_order(i, n, ep):
+    if n != len(SEND_ORDER):
+        return (i + 1) % n
+    to = ep
+    for bit in (1, 2, 4):
+        if SEND_ORDER[i] & bit:
+            to = to + bit - 2 * bit * ((to // bit) % 2)
+    return lax.rem(to + n - ep, n)
+
+
 def gate_column(tiles, r, capp):
     ones = jnp.ones((16, 128), BF)
     return lax.dot_general(
@@ -925,6 +938,7 @@
     cot,
     gu_own,
     dn_own,
+    pairs,
     up_rows,
     gu_a,
     dn_a,
@@ -935,6 +949,11 @@
     mid,
     nt,
     factor_one,
+    split,
+    pair_in,
+    pair_out,
+    pair_si,
+    pair_so,
     zero,
     up_sent,
     core_send,
@@ -971,22 +990,15 @@
     per = blocks_at_once(n, capp)
     size = per * capp
 
-    @pl.loop(0, n // per)
-    def _(b):
+    for i in range(n // per):
+        b = send_order(i, n, ep) if per == 1 else i
         at = pl.ds(pl.multiple_of(b * size, size), size)
         up_sent[at, :] = jnp.dot(place[at, :], cot[...], preferred_element_type=F32).astype(BF)
-        for i in range(per):
-            if i == 0:
-
-                @pl.when(b == 0)
-                def _():
-                    kept.start()
-
-                @pl.when(b > 0)
-                def _():
-                    each(up_copies(b * per), "start")
+        for j in range(per):
+            if i == (n - 1 if per == 1 else 0) and j == 0:
+                kept.start()
             else:
-                each(up_copies(b * per + i), "start")
+                each(up_copies(b * per + j), "start")
 
     w_copies = [
         remote(dn_own, dn_b, w_ss.at[0], w_rs.at[0], "tp", y_peer),
@@ -995,6 +1007,38 @@
     ]
     for copy in w_copies:
         copy.start()
+
+    chunk = pair_in.shape[1]
+    chunks = pairs.shape[0] // chunk
+
+    def pair_load(i):
+        at, slot = pl.ds(pl.multiple_of(i * chunk, chunk), chunk), lax.rem(i, 2)
+        return pltpu.make_async_copy(pairs.at[at], pair_in.at[slot], pair_si.at[slot])
+
+    def pair_store(i):
+        at, slot = pl.ds(pl.multiple_of(i * chunk, chunk), chunk), lax.rem(i, 2)
+        return pltpu.make_async_copy(pair_out.at[slot], split.at[:, at, :], pair_so.at[slot])
+
+    def set_apart(first, last):
+        @pl.loop(first, last)
+        def _(i):
+            slot = lax.rem(i, 2)
+
+            @pl.when(i + 1 < chunks)
+            def _():
+                pair_load(i + 1).start()
+
+            pair_load(i).wait()
+
+            @pl.when(i >= 2)
+            def _():
+                pair_store(i - 2).wait()
+
+            pair_out[slot, 0] = pair_in[slot, :, 0, :]
+            pair_out[slot, 1] = pair_in[slot, :, 1, :]
+            pair_store(i).start()
+
+    pair_load(0).start()
 
     @pl.loop(0, tokens // 64)
     def _(m):
@@ -1049,7 +1093,7 @@
         )
 
     tp_total(
-        project, lambda: None, tp, core_send, core_recv, y_send, y_recv, summed,
+        project, lambda: set_apart(0, chunks * 11 // 16), tp, core_send, core_recv, y_send, y_recv, summed,
         core_ss, core_rs, y_ss, y_rs, g_ss, g_rs,
     )
 
@@ -1066,6 +1110,9 @@
         factor = lax.rsqrt(total * (1.0 / width) + EPSILON)
         nt[at, :] = (mid[at, :] * factor * gain2[...]).astype(BF)
 
+    set_apart(chunks * 11 // 16, chunks)
+    pair_store(chunks - 2).wait()
+    pair_store(chunks - 1).wait()
     for copy in w_copies:
         copy.wait()
     kept.wait()
@@ -1073,7 +1120,7 @@
         each(up_copies(r), "wait")
 
 
-def front(n, n_tp, shape, hidden, gain1, gain2, w, bias, cosine, sine, prefix, ow, place, cot, gu_own, dn_own):
+def front(n, n_tp, shape, hidden, gain1, gain2, w, bias, cosine, sine, prefix, ow, place, cot, gu_own, dn_own, pairs):
     tokens, width = hidden.shape
     lw = ow.shape[1]
     quarter = dn_own.shape[0]
@@ -1093,10 +1140,15 @@
             jax.ShapeDtypeStruct((tokens, width), F32),
             jax.ShapeDtypeStruct((tokens, width), BF),
             jax.ShapeDtypeStruct((tokens, 1), F32),
+            jax.ShapeDtypeStruct((2, width, pairs.shape[2]), BF),
         ),
-        in_specs=[vmem] * 11 + [hbm] * 2,
-        out_specs=[hbm] * 4 + [vmem] * 6,
+        in_specs=[vmem] * 11 + [hbm] * 3,
+        out_specs=[hbm] * 4 + [vmem] * 6 + [hbm],
         scratch_shapes=[
+            pltpu.VMEM((2, 128, 2, pairs.shape[2]), BF),
+            pltpu.VMEM((2, 2, 128, pairs.shape[2]), BF),
+            dma((2,)),
+            dma((2,)),
             pltpu.VMEM((max(shape[0] - shape[1], 16), width), BF),
             pltpu.VMEM((n * shape[0], width), BF),
             pltpu.VMEM((4, tokens, width // 8), BF),
@@ -1121,7 +1173,7 @@
         cost_estimate=pl.CostEstimate(
             flops=2 * tokens * width * 4 * lw, bytes_accessed=30 * 2**20, transcendentals=0
         ),
-    )(hidden, gain1, gain2, w, bias, cosine, sine, prefix, ow, place, cot, gu_own, dn_own)
+    )(hidden, gain1, gain2, w, bias, cosine, sine, prefix, ow, place, cot, gu_own, dn_own, pairs)
 
 
 def dispatch_kernel(
@@ -1190,22 +1242,15 @@
     per = blocks_at_once(n, capp)
     size = per * capp
 
-    @pl.loop(0, n // per)
-    def _(b):
+    for i in range(n // per):
+        b = send_order(i, n, ep) if per == 1 else i
         at = pl.ds(pl.multiple_of(b * size, size), size)
         x_send[at, :] = jnp.dot(place[at, :], nt[...], preferred_element_type=F32).astype(BF)
-        for i in range(per):
-            if i == 0:
-
-                @pl.when(b == 0)
-                def _():
-                    kept.start()
-
-                @pl.when(b > 0)
-                def _():
-                    each(x_copies(b * per), "start")
+        for j in range(per):
+            if i == (n - 1 if per == 1 else 0) and j == 0:
+                kept.start()
             else:
-                each(x_copies(b * per + i), "start")
+                each(x_copies(b * per + j), "start")
 
     logits = jnp.dot(nt[...], router[...], preferred_element_type=F32)
     lane = lax.broadcasted_iota(jnp.int32, logits.shape, 1)
@@ -1418,8 +1463,8 @@
 
     kept = pltpu.make_async_copy(o_sent.at[:capp, :], o_rows.at[:capp, :], o_ss.at[0, 0])
 
-    for r in range(1, n):
-        each(o_copies(r), "start")
+    for i in range(n - 1):
+        each(o_copies(send_order(i, n, ep)), "start")
     kept.start()
 
     row = lax.broadcasted_iota(jnp.int32, (total, 128), 0)
@@ -1645,11 +1690,10 @@
 
     cos_all, sin_all = angle_tables(tokens, HEAD_DIM)
     w_t = jnp.transpose(qkv_weight, (1, 0, 2))
-    sgu, hidden = lax.optimization_barrier((jnp.transpose(shared_gate_up, (1, 0, 2)), hidden))
     prefix_row = jnp.broadcast_to(prefix[None], (1, tokens))
     gu_own = jnp.transpose(expert_gate_up[0], (1, 2, 0))
     dn_own = jnp.transpose(expert_down[0], (1, 0))
-    up_rows, gu_a, dn_a, dn_b, normed_one, qkv, context, middle, normed_two, factor_one = front(
+    up_rows, gu_a, dn_a, dn_b, normed_one, qkv, context, middle, normed_two, factor_one, sgu = front(
         n_ep,
         n_tp,
         shape,
@@ -1666,6 +1710,7 @@
         cotangent,
         gu_own,
         dn_own,
+        shared_gate_up,
     )
 
     router_all = jnp.concatenate(

time: 678 us -> 671 us (0.990)
  local copies, waits for them, and re-layouts: 27.2 us -> 15.8 us
    unnamed x37 -> x36, local copies, waits for them, and re-layouts: 20.6 us -> 9.21 us
    pallas_call x1, Pallas kernels: 86.8 us -> 95.8 us  [front(): pl.pallas_call(functools.partial(front_kernel, n, n_tp, shape), out_shape...]
    pallas_call x1, Pallas kernels: 106 us -> 98.4 us  [backward(): pl.pallas_call(functools.partial(backward_kernel, n, n_tp, shape, n_exp),...]
where the time goes in v6:
time: 671 us; the launch traced here: 663 us
  Pallas kernels  629 us (94%)
  local copies, waits for them, and re-layouts  15.8 us (2%)
  other arithmetic  11.3 us (2%)
    pallas_call x1, Pallas kernels, routed_expert(): pl.pallas_call(functools.partial(middle_kernel, n, n_tp, shape), out_shap...  238 us
    pallas_call x1, Pallas kernels, tail(): pl.pallas_call(functools.partial(tail_kernel, n, n_tp), out_shape=(jax.Sh...  102 us
    pallas_call x1, Pallas kernels, backward(): pl.pallas_call(functools.partial(backward_kernel, n, n_tp, shape, n_exp),...  98.4 us
    pallas_call x1, Pallas kernels, front(): pl.pallas_call(functools.partial(front_kernel, n, n_tp, shape), out_shape...  95.8 us
    pallas_call x1, Pallas kernels, dispatch(): pl.pallas_call(functools.partial(dispatch_kernel, n, n_tp, shape, n_exp),...  94.4 us

profile of v6, /device:TPU:0, one launch (start us, length us, event | category | flops | bytes accessed | tf_op | source)
XLA Modules:
  0.0 662.5 jit_solution(14230356320630101106)
XLA Ops:
  1.3 0.1 pad.2.clone
  1.4 0.6 broadcast_in_dim.37.prefix
  2.0 0.7 lt.33
  2.7 0.9 copy.34
  3.6 0.1 copy.35
  3.7 4.1 fusion.11
  7.8 0.0 copy-start.7
  7.8 0.0 copy-start.9
  7.8 0.2 copy.37
  8.1 0.2 copy.36
  8.3 0.2 fusion.17
  8.5 0.0 copy-start
  8.5 0.7 slice_reduce_fusion.3
  9.2 0.0 copy-done.7
  9.2 0.3 copy.40
  9.5 0.0 copy-done.9
  9.5 0.3 broadcast_in_dim.43
  9.8 1.1 maximum_maximum_fusion.router
  10.9 1.9 fusion.10.place
  12.8 95.8 %shard_map.273 = (bf16[896,2048]{1,0:T(8,128)(2,1)}, bf16[2,352,2048]{2,1,0:T(8,128)(2,1)}, bf16[352,2048]{1,0:T(8,128)(2,1)}, bf16[352,2048]{1,0:T(8,128)(2,1)}...) custom-call(bf16[640,2048]{1,0:T(8,128)(2,1)} %hidden.3, ...), custom_call_target="tpu_custom_call" | custom-call | flops 5368709120 | bytes 31457280 | tf_op jit(solution)/shard_map/pallas_call | solution.py:1130
  108.7 0.0 copy-done
  108.7 94.4 %shard_map.274 = (bf16[896,2048]{1,0:T(8,128)(2,1)}, bf16[8,16,128]{2,1,0:T(8,128)(2,1)}, bf16[2,352,2048]{2,1,0:T(8,128)(2,1)}, bf16[2,352,2048]{2,1,0:T(8,128)...) custom-call(bf16[640,2048]{1,0:T(8,128)(2,1)} %get-tuple-element.58., ...), custom_call_target="tpu_custom_call" | custom-call | flops 22145925120 | bytes 41943040 | tf_op jit(solution)/shard_map/pallas_call | solution.py:1359
  203.1 238.5 %shard_map.275 = (bf16[896,2048]{1,0:T(8,128)(2,1)}, bf16[8,16,128]{2,1,0:T(8,128)(2,1)}, bf16[896,2048]{1,0:T(8,128)(2,1)}, bf16[3,704,2048]{2,1,0:T(8,128)(2,1...) custom-call(bf16[896,2048]{1,0:T(8,128)(2,1)} %get-tuple-element.61., ...), custom_call_target="tpu_custom_call" | custom-call | flops 31004295168 | bytes 41943040 | tf_op jit(solution)/shard_map/pallas_call | solution.py:791
  441.6 98.4 %shard_map.276 = (bf16[896,2048]{1,0:T(8,128)(2,1)}, bf16[640,2048]{1,0:T(8,128)(2,1)}, bf16[640,1536]{1,0:T(8,128)(2,1)}, f32[1,1536]{1,0:T(1,128)}, bf16[8,16,256]{2,1,0:T(8,128)(2,1)}) custom-call(bf16[896,2048]{1,0:T(8,128)(2,1)} %get-tuple-element.72.back, bf16[8,16,128]{2,1,0:T(8,128)(2,1)} %get-tuple-element.73.g_back, ...), custom_call_target="tpu_custom_call" | custom-call | flops 5368709120 | bytes 31457280 | tf_op jit(solution)/shard_map/pallas_call | solution.py:1596
  540.0 0.0 copy-start.3
  540.0 102.3 %shard_map.277 = (f32[3,256,512]{2,1,0:T(8,128)}, f32[256,512]{1,0:T(8,128)}, bf16[640,512]{1,0:T(8,128)(2,1)}, bf16[640,512]{1,0:T(8,128)(2,1)}, f32[1,2048]{1,...) custom-call(bf16[640,2048]{1,0:T(8,128)(2,1)} %get-tuple-element.57.n1, bf16[640,1536]{1,0:T(8,128)(2,1)} %get-tuple-element.81.lg, ...), custom_call_target="tpu_custom_call" | custom-call | flops 9395240960 | bytes 31457280 | tf_op jit(solution)/shard_map/pallas_call | solution.py:381
  642.3 0.0 copy-start.2
  642.3 0.8 reduce.4
  643.1 0.6 reshape.51
  643.7 1.5 fusion.20
  645.3 1.5 slice.55
  646.7 0.0 copy-done.3
  646.7 1.2 convert_element_type.44
  647.9 0.0 copy-done.2
  647.9 0.2 convert_bitcast_fusion
  648.1 3.8 copy.42
  651.9 0.0 slice-done
  651.9 0.0 slice-done.2
  651.9 0.0 slice-done.1
  651.9 0.0 slice-done.3
  652.0 2.1 add_bitcast_fusion.1
  654.1 3.7 add_bitcast_fusion
  657.8 0.8 copy.49
  658.7 0.0 copy-done.4
  658.7 0.8 copy.50
  659.5 0.6 copy.51
  660.1 1.1 copy.52
  661.3 0.8 copy.53
  (21 shorter events, 0.1 us)
Async XLA Ops:
  7.8 1.4 copy-start.7
  7.8 1.7 copy-start.9
  8.5 100.2 %copy-start = (s32[4,640]{0,1:T(8,128)}, s32[4,640]{0,1:T(8,128)S(1)}, u32[]{:S(2)}) copy-start(s32[4,640]{0,1:T(8,128)S(1)} %fusion.17) | copy-start | bytes 30724
  540.0 106.7 %copy-start.3 = (bf16[256,1408]{1,0:T(8,128)(2,1)S(1)}, bf16[256,1408]{1,0:T(8,128)(2,1)}, u32[]{:S(2)}) copy-start(bf16[256,1408]{1,0:T(8,128)(2,1)} %get-tuple-element.98) | copy-start | bytes 2162692
  642.3 5.6 copy-start.2
  646.7 5.2 slice-start
  646.7 5.2 slice-start.2
  647.9 4.0 slice-start.1
  647.9 4.0 slice-start.3
  654.1 3.7 copy-start.5
  654.1 4.6 copy-start.4
  654.1 5.4 copy-start.8
  657.8 2.3 copy-start.1
  657.8 3.4 copy-start.6

commit v7 on v6

--- a/solution.py
+++ b/solution.py
@@ -611,7 +611,7 @@
         return pltpu.make_async_copy(ub.at[slot], o_hbm.at[at, :], out_sem.at[slot])
 
     def back_copies(r):
-        return block_copies(r, rbs, back, back_ss, back_rs, lax.rem(ep + n - r, n), shape, tp, zero)
+        return block_copies(r, rbs, back, back_ss, back_rs, ep, tp, n, shape, zero, True)
 
     kept_copy = pltpu.make_async_copy(rbs.at[:capp, :], back.at[:capp, :], back_ss.at[0, 0])
 
@@ -820,8 +820,8 @@
             dma((4, 2)),
             dma((4, 2)),
             pltpu.SemaphoreType.REGULAR((4,)),
-            dma((2, n)),
-            dma((2, n)),
+            dma((3, n)),
+            dma((3, n)),
             dma((n,)),
             dma((n,)),
             dma((2,)),
@@ -882,23 +882,34 @@
     return per
 
 
-def block_copies(r, src, dst, ss, rs, to, shape, tp, zero):
-    capp, base, extra = shape
+def has_more(tp, source, expert, n_tp, extra):
+    return lax.rem(tp + 64 * n_tp - source - expert, n_tp) < extra
+
+
+def block_copies(r, src, dst, ss, rs, ep, tp, n, shape, zero, home):
+    capp, base, extra, n_tp = shape
+    on, back = lax.rem(ep + r, n), lax.rem(ep + n - r, n)
+    to, come = (back, on) if home else (on, back)
     at = pl.ds(pl.multiple_of(r * capp, 16), base)
-    out = [(None, remote(src.at[at, :], dst.at[at, :], ss.at[0, r], rs.at[0, r], "ep", to))]
+    out = [(None, None, remote(src.at[at, :], dst.at[at, :], ss.at[0, r], rs.at[0, r], "ep", to))]
     if base < capp:
         at = pl.ds(pl.multiple_of(r * capp + base, 16), capp - base)
-        out.append((tp < extra, remote(src.at[at, :], dst.at[at, :], ss.at[1, r], rs.at[1, r], "ep", to)))
-        out.append((tp >= extra, pltpu.make_async_copy(zero, dst.at[at, :], ss.at[1, r])))
+        sends, gets = has_more(tp, ep, to, n_tp, extra), has_more(tp, ep, come, n_tp, extra)
+        out.append((sends, gets, remote(src.at[at, :], dst.at[at, :], ss.at[1, r], rs.at[1, r], "ep", to)))
+        fill = jnp.logical_not(gets)
+        out.append((fill, None, pltpu.make_async_copy(zero, dst.at[at, :], ss.at[2, r])))
     return out
 
 
 def each(copies, verb):
-    for condition, copy in copies:
-        if condition is None:
+    for sends, gets, copy in copies:
+        if sends is None:
             getattr(copy, verb)()
+        elif gets is None or verb == "start":
+            pl.when(sends)(getattr(copy, verb))
         else:
-            pl.when(condition)(getattr(copy, verb))
+            pl.when(sends)(copy.wait_send)
+            pl.when(gets)(copy.wait_recv)
 
 
 SEND_ORDER = (4, 5, 6, 7, 2, 3, 1, 0)
@@ -984,7 +995,7 @@
     zero[...] = jnp.zeros_like(zero)
 
     def up_copies(r):
-        return block_copies(r, up_sent, up_rows, up_ss, up_rs, lax.rem(ep + r, n), shape, tp, zero)
+        return block_copies(r, up_sent, up_rows, up_ss, up_rs, ep, tp, n, shape, zero, False)
 
     kept = pltpu.make_async_copy(up_sent.at[:capp, :], up_rows.at[:capp, :], up_ss.at[0, 0])
     per = blocks_at_once(n, capp)
@@ -1156,8 +1167,8 @@
             pltpu.VMEM((4, tokens, width // 8), BF),
             pltpu.VMEM((4, tokens, width // 8), BF),
             pltpu.VMEM((2, 4, tokens, width // 8), BF),
-            dma((2, n)),
-            dma((2, n)),
+            dma((3, n)),
+            dma((3, n)),
             dma((3,)),
             dma((3,)),
             dma((4,)),
@@ -1231,7 +1242,7 @@
     zero[...] = jnp.zeros_like(zero)
 
     def x_copies(r):
-        return block_copies(r, x_send, x_rows, x_ss, x_rs, lax.rem(ep + r, n), shape, tp, zero)
+        return block_copies(r, x_send, x_rows, x_ss, x_rs, ep, tp, n, shape, zero, False)
 
     def gate_copy(r, way):
         to = lax.rem(ep + r, n) if way == "out" else lax.rem(ep + n - r, n)
@@ -1381,8 +1392,8 @@
             pltpu.VMEM((1, total), F32),
             pltpu.VMEM((total, width), BF),
             pltpu.VMEM((n, 16, 128), BF),
-            dma((2, n)),
-            dma((2, n)),
+            dma((3, n)),
+            dma((3, n)),
             dma((n,)),
             dma((n,)),
             dma((3,)),
@@ -1459,7 +1470,7 @@
     zero[...] = jnp.zeros_like(zero)
 
     def o_copies(r):
-        return block_copies(r, o_sent, o_rows, o_ss, o_rs, lax.rem(ep + n - r, n), shape, tp, zero)
+        return block_copies(r, o_sent, o_rows, o_ss, o_rs, ep, tp, n, shape, zero, True)
 
     kept = pltpu.make_async_copy(o_sent.at[:capp, :], o_rows.at[:capp, :], o_ss.at[0, 0])
 
@@ -1617,8 +1628,8 @@
             pltpu.VMEM((tokens, lw), BF),
             pltpu.VMEM((tokens, lw), F32),
             pltpu.VMEM((tokens, lw), F32),
-            dma((2, n)),
-            dma((2, n)),
+            dma((3, n)),
+            dma((3, n)),
             dma((4,)),
             dma((4,)),
             dma((4,)),
@@ -1667,7 +1678,7 @@
     tiles = -(-capacity // 16)
     least, extra = 16 * (tiles // n_tp), tiles % n_tp
     part_pad = least + (16 if extra else 0)
-    shape = (part_pad, least, extra)
+    shape = (part_pad, least, extra, n_tp)
     rows = n_exp * part_pad
 
     flat_route = routes.T.reshape(-1)
@@ -1677,9 +1688,14 @@
     counts = mm(smaller, hits, 1, 0)
     slot = jnp.sum(counts * hits.astype(F32), axis=1).astype(jnp.int32).reshape(top, tokens)
     kept = slot < capacity
-    in_part = slot - (tp_i * least + 16 * jnp.minimum(tp_i, extra))
-    mine = kept & (in_part >= 0) & (in_part < jnp.where(tp_i < extra, part_pad, least))
     ep_i = lax.axis_index("ep")
+    more = [has_more(j, ep_i, routes.T // expert_local, n_tp, extra) for j in range(n_tp)]
+    more.append(has_more(tp_i, ep_i, routes.T // expert_local, n_tp, extra))
+    start = tp_i * least
+    for j in range(n_tp):
+        start = start + 16 * (more[j] & (j < tp_i)).astype(jnp.int32)
+    in_part = slot - start
+    mine = kept & (in_part >= 0) & (in_part < least + 16 * more[-1].astype(jnp.int32))
     hop = lax.rem(routes.T + n_exp - ep_i * expert_local, n_exp)
     dest = jnp.where(mine, hop * part_pad + in_part, -1)
     row_ids = jnp.arange(rows, dtype=jnp.int32)[:, None]

time: 671 us -> 671 us (level)
  no operation moved by 1% of the time
where the time goes in v7:
time: 671 us; the launch traced here: 663 us
  Pallas kernels  629 us (94%)
  local copies, waits for them, and re-layouts  15.5 us (2%)
  other arithmetic  12 us (2%)
    pallas_call x1, Pallas kernels, routed_expert(): pl.pallas_call(functools.partial(middle_kernel, n, n_tp, shape), out_shap...  237 us
    pallas_call x1, Pallas kernels, tail(): pl.pallas_call(functools.partial(tail_kernel, n, n_tp), out_shape=(jax.Sh...  106 us
    pallas_call x1, Pallas kernels, backward(): pl.pallas_call(functools.partial(backward_kernel, n, n_tp, shape, n_exp),...  98 us
    pallas_call x1, Pallas kernels, front(): pl.pallas_call(functools.partial(front_kernel, n, n_tp, shape), out_shape...  95.9 us
    pallas_call x1, Pallas kernels, dispatch(): pl.pallas_call(functools.partial(dispatch_kernel, n, n_tp, shape, n_exp),...  91.8 us

profile of v7, /device:TPU:0, one launch (start us, length us, event | category | flops | bytes accessed | tf_op | source)
XLA Modules:
  0.0 662.8 jit_solution(14606391445725753125)
XLA Ops:
  1.3 0.1 pad.2.clone
  1.4 0.6 broadcast_in_dim.35.prefix
  2.0 0.7 lt.39
  2.7 0.9 copy.41
  3.6 0.1 copy.42
  3.7 0.0 copy-start.7
  3.7 4.0 fusion.11
  7.8 0.0 copy-start.9
  7.8 0.2 copy.43
  8.0 0.8 fusion.27
  8.8 0.0 copy-start
  8.8 0.7 slice_reduce_fusion.3
  9.5 0.0 copy-done.7
  9.5 0.3 copy.46
  9.8 0.0 copy-done.9
  9.8 0.3 broadcast_in_dim.40
  10.2 1.1 maximum_maximum_fusion.router
  11.3 1.9 fusion.10.place
  13.2 95.9 %shard_map.273 = (bf16[896,2048]{1,0:T(8,128)(2,1)}, bf16[2,352,2048]{2,1,0:T(8,128)(2,1)}, bf16[352,2048]{1,0:T(8,128)(2,1)}, bf16[352,2048]{1,0:T(8,128)(2,1)}...) custom-call(bf16[640,2048]{1,0:T(8,128)(2,1)} %hidden.3, ...), custom_call_target="tpu_custom_call" | custom-call | flops 5368709120 | bytes 31457280 | tf_op jit(solution)/shard_map/pallas_call | solution.py:1141
  109.2 0.0 copy-done
  109.2 91.8 %shard_map.274 = (bf16[896,2048]{1,0:T(8,128)(2,1)}, bf16[8,16,128]{2,1,0:T(8,128)(2,1)}, bf16[2,352,2048]{2,1,0:T(8,128)(2,1)}, bf16[2,352,2048]{2,1,0:T(8,128)...) custom-call(bf16[640,2048]{1,0:T(8,128)(2,1)} %get-tuple-element.58., ...), custom_call_target="tpu_custom_call" | custom-call | flops 22145925120 | bytes 41943040 | tf_op jit(solution)/shard_map/pallas_call | solution.py:1370
  200.9 237.4 %shard_map.275 = (bf16[896,2048]{1,0:T(8,128)(2,1)}, bf16[8,16,128]{2,1,0:T(8,128)(2,1)}, bf16[896,2048]{1,0:T(8,128)(2,1)}, bf16[3,704,2048]{2,1,0:T(8,128)(2,1...) custom-call(bf16[896,2048]{1,0:T(8,128)(2,1)} %get-tuple-element.61., ...), custom_call_target="tpu_custom_call" | custom-call | flops 31004295168 | bytes 41943040 | tf_op jit(solution)/shard_map/pallas_call | solution.py:791
  438.4 98.0 %shard_map.276 = (bf16[896,2048]{1,0:T(8,128)(2,1)}, bf16[640,2048]{1,0:T(8,128)(2,1)}, bf16[640,1536]{1,0:T(8,128)(2,1)}, f32[1,1536]{1,0:T(1,128)}, bf16[8,16,256]{2,1,0:T(8,128)(2,1)}) custom-call(bf16[896,2048]{1,0:T(8,128)(2,1)} %get-tuple-element.72.back, bf16[8,16,128]{2,1,0:T(8,128)(2,1)} %get-tuple-element.73.g_back, ...), custom_call_target="tpu_custom_call" | custom-call | flops 5368709120 | bytes 31457280 | tf_op jit(solution)/shard_map/pallas_call | solution.py:1607
  536.4 0.0 copy-start.3
  536.4 106.2 %shard_map.277 = (f32[3,256,512]{2,1,0:T(8,128)}, f32[256,512]{1,0:T(8,128)}, bf16[640,512]{1,0:T(8,128)(2,1)}, bf16[640,512]{1,0:T(8,128)(2,1)}, f32[1,2048]{1,...) custom-call(bf16[640,2048]{1,0:T(8,128)(2,1)} %get-tuple-element.57.n1, bf16[640,1536]{1,0:T(8,128)(2,1)} %get-tuple-element.81.lg, ...), custom_call_target="tpu_custom_call" | custom-call | flops 9395240960 | bytes 31457280 | tf_op jit(solution)/shard_map/pallas_call | solution.py:381
  642.6 0.0 copy-start.2
  642.6 0.8 reduce.4
  643.4 0.6 reshape.47
  644.0 1.5 fusion.31
  645.5 1.5 slice.55
  647.0 0.0 copy-done.3
  647.0 1.2 convert_element_type.52
  648.2 0.0 copy-done.2
  648.2 0.2 convert_bitcast_fusion
  648.4 3.8 copy.48
  652.2 0.0 slice-done
  652.2 0.0 slice-done.2
  652.2 0.0 slice-done.1
  652.2 0.0 slice-done.3
  652.2 2.1 add_bitcast_fusion.1
  654.4 3.7 add_bitcast_fusion
  658.1 0.0 copy-done.5
  658.1 0.8 copy.55
  659.0 0.8 copy.56
  659.8 0.6 copy.57
  660.4 0.0 copy-done.1
  660.4 1.1 copy.58
  661.6 0.8 copy.59
  (18 shorter events, 0.1 us)
Async XLA Ops:
  3.7 5.8 copy-start.7
  7.8 2.1 copy-start.9
  8.8 100.3 %copy-start = (s32[4,640]{0,1:T(8,128)}, s32[4,640]{0,1:T(8,128)S(1)}, u32[]{:S(2)}) copy-start(s32[4,640]{0,1:T(8,128)S(1)} %fusion.27) | copy-start | bytes 30724
  536.4 110.6 %copy-start.3 = (bf16[256,1408]{1,0:T(8,128)(2,1)S(1)}, bf16[256,1408]{1,0:T(8,128)(2,1)}, u32[]{:S(2)}) copy-start(bf16[256,1408]{1,0:T(8,128)(2,1)} %get-tuple-element.98) | copy-start | bytes 2162692
  642.6 5.6 copy-start.2
  647.0 5.2 slice-start
  647.0 5.2 slice-start.2
  648.2 4.0 slice-start.1
  648.2 4.0 slice-start.3
  654.4 3.7 copy-start.5
  654.4 4.6 copy-start.4
  654.4 5.4 copy-start.8
  658.1 2.3 copy-start.1
  658.1 3.4 copy-start.6

commit v8 on v7

--- a/solution.py
+++ b/solution.py
@@ -73,6 +73,7 @@
 def tail_kernel(
     n,
     n_tp,
+    ready,
     n1,
     lg,
     ag,
@@ -195,6 +196,8 @@
         ring_send[ring, 0] = term(ring, block_of(ring, 0)).astype(BF)
         ring_copy(ring, 0, 0).start()
 
+    ready()
+
     def part_block(column, store):
         for m in range(0, tokens, 128):
             total = None
@@ -378,8 +381,10 @@
     vmem = pl.BlockSpec(memory_space=pltpu.VMEM)
     hbm = pl.BlockSpec(memory_space=pl.ANY)
     dma = pltpu.SemaphoreType.DMA
+    operands = (n1, lg, ag, ctx, w, hidden, r_one, gain, bias, small, o_rows, weighted, spart, mid, ag_hbm)
+    late = (4, 10, 11, 12)
     return pl.pallas_call(
-        functools.partial(tail_kernel, n, n_tp),
+        fetch_late(functools.partial(tail_kernel, n, n_tp), late),
         out_shape=(
             jax.ShapeDtypeStruct((3, rows, lw), F32),
             jax.ShapeDtypeStruct((rows, lw), F32),
@@ -389,7 +394,7 @@
             jax.ShapeDtypeStruct((1, 3 * lw), F32),
             jax.ShapeDtypeStruct((n, wide, rows), F32),
         ),
-        in_specs=[vmem] * 5 + [hbm] + [vmem] * 7 + [hbm] * 2,
+        in_specs=specs(15, (4, 5, 10, 11, 12, 13, 14)),
         out_specs=[vmem] * 7,
         scratch_shapes=[
             pltpu.VMEM((tokens, lw), BF),
@@ -425,14 +430,16 @@
             dma((2, n)),
             dma((n_tp,)),
             dma((n_tp,)),
-        ],
+        ]
+        + late_scratch(operands, late),
         compiler_params=pltpu.CompilerParams(
             collective_id=0, has_side_effects=True, vmem_limit_bytes=60 * 2**20
         ),
         cost_estimate=pl.CostEstimate(
             flops=2 * tokens * width * 7 * lw, bytes_accessed=30 * 2**20, transcendentals=0
         ),
-    )(n1, lg, ag, ctx, w, hidden, r_one, gain, bias, small, o_rows, weighted, spart, mid, ag_hbm)
+    )(*operands)
+
 
 def cols_of(ref, owner, rows):
     at = pl.ds(pl.multiple_of(owner * rows, rows), rows)
@@ -912,6 +919,35 @@
             pl.when(gets)(copy.wait_recv)
 
 
+def fetch_late(kernel, late):
+    def wrapped(*refs):
+        refs, held, sems = refs[: -len(late) - 1], refs[-len(late) - 1 : -1], refs[-1]
+        copies = [pltpu.make_async_copy(refs[at], held[i], sems.at[i]) for i, at in enumerate(late)]
+        for copy in copies:
+            copy.start()
+
+        def ready():
+            for copy in copies:
+                copy.wait()
+
+        refs = list(refs)
+        for i, at in enumerate(late):
+            refs[at] = held[i]
+        kernel(ready, *refs)
+
+    return wrapped
+
+
+def late_scratch(operands, late):
+    return [pltpu.VMEM(operands[at].shape, operands[at].dtype) for at in late] + [
+        pltpu.SemaphoreType.DMA((len(late),))
+    ]
+
+
+def specs(count, apart):
+    return [pl.BlockSpec(memory_space=pl.ANY if i in apart else pltpu.VMEM) for i in range(count)]
+
+
 SEND_ORDER = (4, 5, 6, 7, 2, 3, 1, 0)
 
 
@@ -936,6 +972,7 @@
     n,
     n_tp,
     shape,
+    ready,
     hidden,
     gain1,
     gain2,
@@ -1050,6 +1087,7 @@
             pair_store(i).start()
 
     pair_load(0).start()
+    ready()
 
     @pl.loop(0, tokens // 64)
     def _(m):
@@ -1138,8 +1176,10 @@
     vmem = pl.BlockSpec(memory_space=pltpu.VMEM)
     hbm = pl.BlockSpec(memory_space=pl.ANY)
     dma = pltpu.SemaphoreType.DMA
+    operands = (hidden, gain1, gain2, w, bias, cosine, sine, prefix, ow, place, cot, gu_own, dn_own, pairs)
+    late = (0, 3, 8)
     return pl.pallas_call(
-        functools.partial(front_kernel, n, n_tp, shape),
+        fetch_late(functools.partial(front_kernel, n, n_tp, shape), late),
         out_shape=(
             jax.ShapeDtypeStruct((n * shape[0], width), BF),
             jax.ShapeDtypeStruct((2, quarter, width), BF),
@@ -1153,7 +1193,7 @@
             jax.ShapeDtypeStruct((tokens, 1), F32),
             jax.ShapeDtypeStruct((2, width, pairs.shape[2]), BF),
         ),
-        in_specs=[vmem] * 11 + [hbm] * 3,
+        in_specs=specs(14, (0, 3, 8, 11, 12, 13)),
         out_specs=[hbm] * 4 + [vmem] * 6 + [hbm],
         scratch_shapes=[
             pltpu.VMEM((2, 128, 2, pairs.shape[2]), BF),
@@ -1177,14 +1217,15 @@
             dma((4,)),
             dma((4,)),
             dma((4,)),
-        ],
+        ]
+        + late_scratch(operands, late),
         compiler_params=pltpu.CompilerParams(
             collective_id=2, has_side_effects=True, vmem_limit_bytes=56 * 2**20
         ),
         cost_estimate=pl.CostEstimate(
             flops=2 * tokens * width * 4 * lw, bytes_accessed=30 * 2**20, transcendentals=0
         ),
-    )(hidden, gain1, gain2, w, bias, cosine, sine, prefix, ow, place, cot, gu_own, dn_own, pairs)
+    )(*operands)
 
 
 def dispatch_kernel(
@@ -1192,6 +1233,7 @@
     n_tp,
     shape,
     n_exp,
+    ready,
     nt,
     place,
     router,
@@ -1263,6 +1305,8 @@
             else:
                 each(x_copies(b * per + j), "start")
 
+    ready()
+
     logits = jnp.dot(nt[...], router[...], preferred_element_type=F32)
     lane = lax.broadcasted_iota(jnp.int32, logits.shape, 1)
     chosen = jnp.where(lane < n_exp, logits, -1e30)
@@ -1367,8 +1411,10 @@
     vmem = pl.BlockSpec(memory_space=pltpu.VMEM)
     hbm = pl.BlockSpec(memory_space=pl.ANY)
     dma = pltpu.SemaphoreType.DMA
+    operands = (nt, place, router, cot, sgu, sdn, gu_own, dn_b, dest_t)
+    late = (2, 3, 4, 5)
     return pl.pallas_call(
-        functools.partial(dispatch_kernel, n, n_tp, shape, n_exp),
+        fetch_late(functools.partial(dispatch_kernel, n, n_tp, shape, n_exp), late),
         out_shape=(
             jax.ShapeDtypeStruct((total, width), BF),
             jax.ShapeDtypeStruct((n, 16, 128), BF),
@@ -1385,7 +1431,7 @@
             jax.ShapeDtypeStruct((tokens, width), F32),
             jax.ShapeDtypeStruct((tokens, 1), F32),
         ),
-        in_specs=[vmem] * 6 + [hbm] * 2 + [vmem],
+        in_specs=specs(9, (2, 3, 4, 5, 6, 7)),
         out_specs=[hbm] * 5 + [vmem] * 9,
         scratch_shapes=[
             pltpu.VMEM((max(shape[0] - shape[1], 16), width), BF),
@@ -1398,20 +1444,23 @@
             dma((n,)),
             dma((3,)),
             dma((3,)),
-        ],
+        ]
+        + late_scratch(operands, late),
         compiler_params=pltpu.CompilerParams(
             collective_id=3, has_side_effects=True, vmem_limit_bytes=60 * 2**20
         ),
         cost_estimate=pl.CostEstimate(
             flops=2 * tokens * width * 6 * units, bytes_accessed=40 * 2**20, transcendentals=0
         ),
-    )(nt, place, router, cot, sgu, sdn, gu_own, dn_b, dest_t)
+    )(*operands)
+
 
 def backward_kernel(
     n,
     n_tp,
     shape,
     n_exp,
+    ready,
     back,
     g_back,
     place_t,
@@ -1477,6 +1526,7 @@
     for i in range(n - 1):
         each(o_copies(send_order(i, n, ep)), "start")
     kept.start()
+    ready()
 
     row = lax.broadcasted_iota(jnp.int32, (total, 128), 0)
     spot = lax.broadcasted_iota(jnp.int32, (total, 128), 1)
@@ -1604,8 +1654,10 @@
     hbm = pl.BlockSpec(memory_space=pl.ANY)
     dma = pltpu.SemaphoreType.DMA
     piece = (4, tokens, width // 8)
+    operands = (back, g_back, place_t, sback, sgrad, probs, router, nt, mid, cot, gain2, qkv, ow, cosine, sine, prefix, o_sent)
+    late = (0, 2, 3, 6, 7, 8, 9, 11, 12)
     return pl.pallas_call(
-        functools.partial(backward_kernel, n, n_tp, shape, n_exp),
+        fetch_late(functools.partial(backward_kernel, n, n_tp, shape, n_exp), late),
         out_shape=(
             jax.ShapeDtypeStruct(o_sent.shape, BF),
             jax.ShapeDtypeStruct((tokens, width), BF),
@@ -1613,7 +1665,7 @@
             jax.ShapeDtypeStruct((1, 3 * lw), F32),
             jax.ShapeDtypeStruct((n, wide, width // n), BF),
         ),
-        in_specs=[vmem] * 16 + [hbm],
+        in_specs=specs(17, (0, 2, 3, 6, 7, 8, 9, 11, 12, 16)),
         out_specs=[hbm] + [vmem] * 4,
         scratch_shapes=[
             pltpu.VMEM((max(shape[0] - shape[1], 16), width), BF),
@@ -1638,14 +1690,15 @@
             dma((4,)),
             dma((2,)),
             dma((2,)),
-        ],
+        ]
+        + late_scratch(operands, late),
         compiler_params=pltpu.CompilerParams(
             collective_id=4, has_side_effects=True, vmem_limit_bytes=60 * 2**20
         ),
         cost_estimate=pl.CostEstimate(
             flops=2 * tokens * width * 4 * lw, bytes_accessed=30 * 2**20, transcendentals=0
         ),
-    )(back, g_back, place_t, sback, sgrad, probs, router, nt, mid, cot, gain2, qkv, ow, cosine, sine, prefix, o_sent)
+    )(*operands)
 
 
 def body(

time: 671 us -> 651 us (0.970)
  Pallas kernels: 629 us -> 609 us
    pallas_call x4, Pallas kernels: 392 us -> 372 us  [the longest x1 102 us: tail(): pl.pallas_call(fetch_late(functools.partial(tail_kernel, n, n_tp), late),...]
where the time goes in v8:
time: 651 us; the launch traced here: 643 us
  Pallas kernels  609 us (94%)
  local copies, waits for them, and re-layouts  15.5 us (2%)
  other arithmetic  12 us (2%)
    pallas_call x1, Pallas kernels, routed_expert(): pl.pallas_call(functools.partial(middle_kernel, n, n_tp, shape), out_shap...  237 us
    pallas_call x1, Pallas kernels, tail(): pl.pallas_call(fetch_late(functools.partial(tail_kernel, n, n_tp), late),...  102 us
    pallas_call x1, Pallas kernels, front(): pl.pallas_call(fetch_late(functools.partial(front_kernel, n, n_tp, shape)...  92.8 us
    pallas_call x1, Pallas kernels, backward(): pl.pallas_call(fetch_late(functools.partial(backward_kernel, n, n_tp, sha...  90.7 us
    pallas_call x1, Pallas kernels, dispatch(): pl.pallas_call(fetch_late(functools.partial(dispatch_kernel, n, n_tp, sha...  86 us

profile of v8, /device:TPU:0, one launch (start us, length us, event | category | flops | bytes accessed | tf_op | source)
XLA Modules:
  0.0 642.8 jit_solution(15862589099132076101)
XLA Ops:
  1.3 0.1 pad.2.clone
  1.4 0.6 broadcast_in_dim.35.refs_7_.refs_15_
  2.0 0.7 lt.39
  2.7 0.9 copy.41
  3.6 0.1 copy.42
  3.7 0.0 copy-start.7
  3.7 4.0 fusion.11
  7.8 0.0 copy-start.9
  7.8 0.2 copy.43
  8.0 0.8 fusion.27
  8.8 0.0 copy-start
  8.8 0.7 slice_reduce_fusion.3
  9.5 0.0 copy-done.7
  9.5 0.3 copy.46
  9.8 0.0 copy-done.9
  9.8 0.3 broadcast_in_dim.40
  10.2 1.1 maximum_maximum_fusion.refs_2_.refs_6_
  11.3 1.9 fusion.10.refs_9_.refs_1_
  13.2 92.8 %shard_map.273 = (bf16[896,2048]{1,0:T(8,128)(2,1)}, bf16[2,352,2048]{2,1,0:T(8,128)(2,1)}, bf16[352,2048]{1,0:T(8,128)(2,1)}, bf16[352,2048]{1,0:T(8,128)(2,1)}...) custom-call(bf16[640,2048]{1,0:T(8,128)(2,1)} %refs_5_.4, ...), custom_call_target="tpu_custom_call" | custom-call | flops 5368709120 | bytes 31457280 | tf_op jit(solution)/shard_map/pallas_call | solution.py:1181
  106.0 0.0 copy-done
  106.0 86.0 %shard_map.274 = (bf16[896,2048]{1,0:T(8,128)(2,1)}, bf16[8,16,128]{2,1,0:T(8,128)(2,1)}, bf16[2,352,2048]{2,1,0:T(8,128)(2,1)}, bf16[2,352,2048]{2,1,0:T(8,128)...) custom-call(bf16[640,2048]{1,0:T(8,128)(2,1)} %get-tuple-element.58., ...), custom_call_target="tpu_custom_call" | custom-call | flops 22145925120 | bytes 41943040 | tf_op jit(solution)/shard_map/pallas_call | solution.py:1416
  192.0 237.5 %shard_map.275 = (bf16[896,2048]{1,0:T(8,128)(2,1)}, bf16[8,16,128]{2,1,0:T(8,128)(2,1)}, bf16[896,2048]{1,0:T(8,128)(2,1)}, bf16[3,704,2048]{2,1,0:T(8,128)(2,1...) custom-call(bf16[896,2048]{1,0:T(8,128)(2,1)} %get-tuple-element.61., ...), custom_call_target="tpu_custom_call" | custom-call | flops 31004295168 | bytes 41943040 | tf_op jit(solution)/shard_map/pallas_call | solution.py:798
  429.5 90.7 %shard_map.276 = (bf16[896,2048]{1,0:T(8,128)(2,1)}, bf16[640,2048]{1,0:T(8,128)(2,1)}, bf16[640,1536]{1,0:T(8,128)(2,1)}, f32[1,1536]{1,0:T(1,128)}, bf16[8,16,256]{2,1,0:T(8,128)(2,1)}) custom-call(bf16[896,2048]{1,0:T(8,128)(2,1)} %get-tuple-element.72.refs_0_, bf16[8,16,128]{2,1,0:T(8,128)(2,1)} %get-tuple-element.73.refs_1_, ...), custom_call_target="tpu_custom_call" | custom-call | flops 5368709120 | bytes 31457280 | tf_op jit(solution)/shard_map/pallas_call | solution.py:1659
  520.2 0.0 copy-start.3
  520.2 102.4 %shard_map.277 = (f32[3,256,512]{2,1,0:T(8,128)}, f32[256,512]{1,0:T(8,128)}, bf16[640,512]{1,0:T(8,128)(2,1)}, bf16[640,512]{1,0:T(8,128)(2,1)}, f32[1,2048]{1,...) custom-call(bf16[640,2048]{1,0:T(8,128)(2,1)} %get-tuple-element.57.refs_0_, ...), custom_call_target="tpu_custom_call" | custom-call | flops 9395240960 | bytes 31457280 | tf_op jit(solution)/shard_map/pallas_call | solution.py:386
  622.6 0.0 copy-start.2
  622.6 0.8 reduce.4
  623.4 0.6 reshape.47
  624.1 1.5 fusion.31
  625.6 1.5 slice.55
  627.1 0.0 copy-done.3
  627.1 1.2 convert_element_type.52
  628.3 0.0 copy-done.2
  628.3 0.2 convert_bitcast_fusion
  628.5 3.8 copy.48
  632.3 0.0 slice-done
  632.3 0.0 slice-done.2
  632.3 0.0 slice-done.1
  632.3 0.0 slice-done.3
  632.3 2.1 add_bitcast_fusion.1
  634.4 3.7 add_bitcast_fusion
  638.2 0.0 copy-done.5
  638.2 0.8 copy.55
  639.0 0.0 copy-done.4
  639.0 0.8 copy.56
  639.9 0.6 copy.57
  640.5 1.1 copy.58
  641.6 0.8 copy.59
  (18 shorter events, 0.1 us)
Async XLA Ops:
  3.7 5.8 copy-start.7
  7.8 2.1 copy-start.9
  8.8 97.2 %copy-start = (s32[4,640]{0,1:T(8,128)}, s32[4,640]{0,1:T(8,128)S(1)}, u32[]{:S(2)}) copy-start(s32[4,640]{0,1:T(8,128)S(1)} %fusion.27) | copy-start | bytes 30724
  520.2 106.9 %copy-start.3 = (bf16[256,1408]{1,0:T(8,128)(2,1)S(1)}, bf16[256,1408]{1,0:T(8,128)(2,1)}, u32[]{:S(2)}) copy-start(bf16[256,1408]{1,0:T(8,128)(2,1)} %get-tuple-element.98) | copy-start | bytes 2162692
  622.6 5.6 copy-start.2
  627.1 5.2 slice-start
  627.1 5.2 slice-start.2
  628.3 4.0 slice-start.1
  628.3 4.0 slice-start.3
  634.4 3.7 copy-start.5
  634.4 4.6 copy-start.4
  634.4 5.4 copy-start.8
  638.2 2.3 copy-start.1
  638.2 3.4 copy-start.6

commit v9 on v8

--- a/solution.py
+++ b/solution.py
@@ -455,6 +455,7 @@
     n,
     n_tp,
     shape,
+    ready,
     x_hbm,
     u_hbm,
     gu_a,
@@ -541,6 +542,8 @@
     u_copy(0).start()
     greet(n, n_tp, ep, tp)
 
+    ready()
+
     edges = [0]
     for ring in range(4):
         edges.append(edges[-1] + (3 * units // 128 + 3 - ring) // 4 * 128)
@@ -795,8 +798,10 @@
     dma = pltpu.SemaphoreType.DMA
     if rows % 128:
         nt, og = nt.T, og.T
+    operands = (x, u, *weights, gates, nt, pg, og, sh)
+    late = (11, 12, 13, 14)
     return pl.pallas_call(
-        functools.partial(middle_kernel, n, n_tp, shape),
+        fetch_late(functools.partial(middle_kernel, n, n_tp, shape), late),
         out_shape=(
             jax.ShapeDtypeStruct((total, width), BF),
             jax.ShapeDtypeStruct((n, 16, 128), BF),
@@ -807,7 +812,7 @@
             jax.ShapeDtypeStruct((2, rows, units), BF),
             jax.ShapeDtypeStruct((rows, units), BF),
         ),
-        in_specs=[hbm] * 10 + [vmem] * 5,
+        in_specs=specs(15, (0, 1, 2, 3, 4, 5, 6, 7, 8, 9, 11, 12, 13, 14)),
         out_specs=[hbm] * 6 + [vmem] * 2,
         scratch_shapes=[
             pltpu.VMEM((max(shape[0] - shape[1], 16), width), BF),
@@ -834,14 +839,15 @@
             dma((2,)),
             dma((2,)),
             dma((2,)),
-        ],
+        ]
+        + late_scratch(operands, late),
         compiler_params=pltpu.CompilerParams(
             collective_id=1, has_side_effects=True, vmem_limit_bytes=63 * 2**20
         ),
         cost_estimate=pl.CostEstimate(
             flops=2 * total * width * 6 * units, bytes_accessed=40 * 2**20, transcendentals=0
         ),
-    )(x, u, *weights, gates, nt, pg, og, sh)
+    )(*operands)
 
 
 def tp_total(
@@ -1142,7 +1148,7 @@
         )
 
     tp_total(
-        project, lambda: set_apart(0, chunks * 11 // 16), tp, core_send, core_recv, y_send, y_recv, summed,
+        project, lambda: set_apart(0, chunks * 12 // 16), tp, core_send, core_recv, y_send, y_recv, summed,
         core_ss, core_rs, y_ss, y_rs, g_ss, g_rs,
     )
 
@@ -1159,7 +1165,7 @@
         factor = lax.rsqrt(total * (1.0 / width) + EPSILON)
         nt[at, :] = (mid[at, :] * factor * gain2[...]).astype(BF)
 
-    set_apart(chunks * 11 // 16, chunks)
+    set_apart(chunks * 12 // 16, chunks)
     pair_store(chunks - 2).wait()
     pair_store(chunks - 1).wait()
     for copy in w_copies:

time: 651 us -> 650 us (level)
  no operation moved by 1% of the time
where the time goes in v9:
time: 650 us; the launch traced here: 642 us
  Pallas kernels  608 us (94%)
  local copies, waits for them, and re-layouts  15.5 us (2%)
  other arithmetic  12 us (2%)
    pallas_call x1, Pallas kernels, routed_expert(): pl.pallas_call(fetch_late(functools.partial(middle_kernel, n, n_tp, shape...  240 us
    pallas_call x1, Pallas kernels, tail(): pl.pallas_call(fetch_late(functools.partial(tail_kernel, n, n_tp), late),...  102 us
    pallas_call x1, Pallas kernels, front(): pl.pallas_call(fetch_late(functools.partial(front_kernel, n, n_tp, shape)...  91.1 us
    pallas_call x1, Pallas kernels, backward(): pl.pallas_call(fetch_late(functools.partial(backward_kernel, n, n_tp, sha...  88.3 us
    pallas_call x1, Pallas kernels, dispatch(): pl.pallas_call(fetch_late(functools.partial(dispatch_kernel, n, n_tp, sha...  86 us

profile of v9, /device:TPU:0, one launch (start us, length us, event | category | flops | bytes accessed | tf_op | source)
XLA Modules:
  0.0 641.7 jit_solution(11634443549621485356)
XLA Ops:
  1.3 0.1 pad.2.clone
  1.4 0.6 broadcast_in_dim.35.refs_7_.refs_15_
  2.0 0.7 lt.39
  2.7 0.9 copy.41
  3.6 0.1 copy.42
  3.7 0.0 copy-start.7
  3.7 4.0 fusion.11
  7.8 0.0 copy-start.9
  7.8 0.2 copy.43
  8.0 0.8 fusion.27
  8.8 0.0 copy-start
  8.8 0.7 slice_reduce_fusion.3
  9.5 0.0 copy-done.7
  9.5 0.3 copy.46
  9.8 0.0 copy-done.9
  9.8 0.3 broadcast_in_dim.40
  10.2 1.1 maximum_maximum_fusion.refs_2_.refs_6_
  11.3 1.9 fusion.10.refs_9_.refs_1_
  13.2 91.1 %shard_map.273 = (bf16[896,2048]{1,0:T(8,128)(2,1)}, bf16[2,352,2048]{2,1,0:T(8,128)(2,1)}, bf16[352,2048]{1,0:T(8,128)(2,1)}, bf16[352,2048]{1,0:T(8,128)(2,1)}...) custom-call(bf16[640,2048]{1,0:T(8,128)(2,1)} %refs_5_.4, ...), custom_call_target="tpu_custom_call" | custom-call | flops 5368709120 | bytes 31457280 | tf_op jit(solution)/shard_map/pallas_call | solution.py:1187
  104.4 0.0 copy-done
  104.4 86.0 %shard_map.274 = (bf16[896,2048]{1,0:T(8,128)(2,1)}, bf16[8,16,128]{2,1,0:T(8,128)(2,1)}, bf16[2,352,2048]{2,1,0:T(8,128)(2,1)}, bf16[2,352,2048]{2,1,0:T(8,128)...) custom-call(bf16[640,2048]{1,0:T(8,128)(2,1)} %get-tuple-element.58., ...), custom_call_target="tpu_custom_call" | custom-call | flops 22145925120 | bytes 41943040 | tf_op jit(solution)/shard_map/pallas_call | solution.py:1422
  190.4 240.4 %shard_map.275 = (bf16[896,2048]{1,0:T(8,128)(2,1)}, bf16[8,16,128]{2,1,0:T(8,128)(2,1)}, bf16[896,2048]{1,0:T(8,128)(2,1)}, bf16[3,704,2048]{2,1,0:T(8,128)(2,1...) custom-call(bf16[896,2048]{1,0:T(8,128)(2,1)} %get-tuple-element.61., ...), custom_call_target="tpu_custom_call" | custom-call | flops 31004295168 | bytes 41943040 | tf_op jit(solution)/shard_map/pallas_call | solution.py:803
  430.8 88.3 %shard_map.276 = (bf16[896,2048]{1,0:T(8,128)(2,1)}, bf16[640,2048]{1,0:T(8,128)(2,1)}, bf16[640,1536]{1,0:T(8,128)(2,1)}, f32[1,1536]{1,0:T(1,128)}, bf16[8,16,256]{2,1,0:T(8,128)(2,1)}) custom-call(bf16[896,2048]{1,0:T(8,128)(2,1)} %get-tuple-element.72.refs_0_, bf16[8,16,128]{2,1,0:T(8,128)(2,1)} %get-tuple-element.73.refs_1_, ...), custom_call_target="tpu_custom_call" | custom-call | flops 5368709120 | bytes 31457280 | tf_op jit(solution)/shard_map/pallas_call | solution.py:1665
  519.1 0.0 copy-start.3
  519.1 102.3 %shard_map.277 = (f32[3,256,512]{2,1,0:T(8,128)}, f32[256,512]{1,0:T(8,128)}, bf16[640,512]{1,0:T(8,128)(2,1)}, bf16[640,512]{1,0:T(8,128)(2,1)}, f32[1,2048]{1,...) custom-call(bf16[640,2048]{1,0:T(8,128)(2,1)} %get-tuple-element.57.refs_0_, ...), custom_call_target="tpu_custom_call" | custom-call | flops 9395240960 | bytes 31457280 | tf_op jit(solution)/shard_map/pallas_call | solution.py:386
  621.5 0.0 copy-start.2
  621.5 0.8 reduce.4
  622.3 0.6 reshape.47
  622.9 1.5 fusion.31
  624.4 1.5 slice.55
  625.9 0.0 copy-done.3
  625.9 1.2 convert_element_type.52
  627.1 0.0 copy-done.2
  627.1 0.2 convert_bitcast_fusion
  627.3 3.8 copy.48
  631.1 0.0 slice-done
  631.1 0.0 slice-done.2
  631.1 0.0 slice-done.1
  631.1 0.0 slice-done.3
  631.2 2.1 add_bitcast_fusion.1
  633.3 3.7 add_bitcast_fusion
  637.0 0.0 copy-done.5
  637.0 0.8 copy.55
  637.9 0.0 copy-done.4
  637.9 0.8 copy.56
  638.7 0.6 copy.57
  639.3 1.1 copy.58
  640.5 0.8 copy.59
  (18 shorter events, 0.1 us)
Async XLA Ops:
  3.7 5.8 copy-start.7
  7.8 2.1 copy-start.9
  8.8 95.5 %copy-start = (s32[4,640]{0,1:T(8,128)}, s32[4,640]{0,1:T(8,128)S(1)}, u32[]{:S(2)}) copy-start(s32[4,640]{0,1:T(8,128)S(1)} %fusion.27) | copy-start | bytes 30724
  519.1 106.8 %copy-start.3 = (bf16[256,1408]{1,0:T(8,128)(2,1)S(1)}, bf16[256,1408]{1,0:T(8,128)(2,1)}, u32[]{:S(2)}) copy-start(bf16[256,1408]{1,0:T(8,128)(2,1)} %get-tuple-element.98) | copy-start | bytes 2162692
  621.5 5.6 copy-start.2
  625.9 5.2 slice-start
  625.9 5.2 slice-start.2
  627.1 4.0 slice-start.1
  627.1 4.0 slice-start.3
  633.3 3.7 copy-start.5
  633.3 4.6 copy-start.4
  633.3 5.4 copy-start.8
  637.0 2.3 copy-start.1
  637.0 3.4 copy-start.6
